TPU v7x, 32 devices: a whole 2x2x4 slice. The times are simulated.
32 devices in a mesh: rep: 4 (over z), shard: 8 (over y, x, core).
Axes of the slice: x: 2, y: 2, z: 4, core: 2. Of those that a mesh axis runs over, the one named last changes fastest.
Arguments:
- layer_input_state: bfloat16 [4096, 2048], P(('rep', 'shard')), may hold values from -6 to 6
- cotangent: bfloat16 [4096, 2048], P(('rep', 'shard')), may hold values from -6 to 6
- norm_gain_vectors: bfloat16 [2, 2048], replicated, may hold values from 0.5 to 1.5
- attention_router_weight: bfloat16 [2048, 4], replicated, may hold values from -0.09375 to 0.09375
- feed_router_weight: bfloat16 [2048, 4], replicated, may hold values from -0.09375 to 0.09375
- attention_query_weight: bfloat16 [4, 2048, 2048], P(None, 'shard'), may hold values from -0.125 to 0.125
- key_value_weight: bfloat16 [2, 2048, 2048], P(None, 'shard'), may hold values from -0.125 to 0.125
- attention_output_weight: bfloat16 [4, 2048, 2048], P(None, 'shard'), may hold values from -1 to 1
- feed_expert_weight: bfloat16 [4, 3, 2048, 5632], P(None, None, None, 'shard'), may hold values from -0.125 to 0.125
- attention_adapters: bfloat16 [2, 10, 2048, 128], P(None, None, 'shard'), may hold values from -0.25 to 0.25
- feed_adapter_width: bfloat16 [4, 3, 2048, 128], P(None, None, 'shard'), may hold values from -0.25 to 0.25
- feed_adapter_hidden: bfloat16 [4, 3, 128, 5632], P(None, None, None, 'shard'), may hold values from -0.15625 to 0.15625
- token_document: int32 [4, 1024], P('rep'), may hold values from 0 to 2, as said below
- document_adapter: int32 [4, 3], P('rep'), may hold values from 0 to 7
- attention_expert_pairs: int32 [4096, 2], P(('rep', 'shard')), may hold values from 0 to 3, all different within a row; in each aligned block of 128 rows (0 to 127, 128 to 255, ...) at most 80 rows name the same one
- feed_expert_pairs: int32 [4096, 2], P(('rep', 'shard')), may hold values from 0 to 3, all different within a row; in each aligned block of 128 rows (0 to 127, 128 to 255, ...) at most 80 rows name the same one
Outputs:
- layer_out: float32 [4096, 2048], P(('rep', 'shard'))
- grad_in: float32 [4096, 2048], P(('rep', 'shard'))
- attention_adapter_gradient: float32 [2, 10, 2048, 128], P(None, None, 'shard')
- grad_lora_ffn_d: float32 [4, 3, 2048, 128], P(None, None, 'shard')
- grad_lora_ffn_b: float32 [4, 3, 128, 5632], P(None, None, None, 'shard')
Inputs may be any that keep to these rules, and one draw needn't show every extreme that they name: `token_document`: in each stream the ids are 0 on a first run of fewer than 128 tokens, 2 on a last run of fewer than 128 tokens, and 1 between. `attention_expert_pairs`: each row names two different experts; among the 128 rows of one device no expert is named by more than 80 rows, a bound that some block reaches. `feed_expert_pairs`: each row names two different experts; among the 128 rows of one device no expert is named by more than 80 rows, a bound that some block reaches.
All inputs are finite; a program needn't handle non-finite values.
Results may differ from a plain program's by a relative error of at most 0.017.
Values may be sent and summed in bfloat16 or wider, within the bound.
No kernel may reach another device: no remote copies, remote signals or barrier semaphores. Data moves between devices by JAX's collectives and lax.ppermute only.
A program may use at most 768 MiB of HBM per device.

v0:
```python
from functools import partial
import math

import jax
import jax.numpy as jnp
from jax import lax
from jax.sharding import PartitionSpec as P

KVH = 16
HD = 128
ATTEND_EXPERTS = 4
FEED_EXPERTS = 4
RANK = 16
CAP = 80


epsilon = 1e-05
big_negative = -1e30


def rms_norm(gain, values):
    return values * lax.rsqrt(jnp.mean(values * values, axis=-1, keepdims=True) + epsilon) * gain


def rms_back(values, gain, grad):
    unused, backward_function = jax.vjp(partial(rms_norm, gain), values)
    return backward_function(grad)[0]


def rotation(place):
    freq = jnp.exp(-jnp.arange(HD // 2, dtype=jnp.float32) * (2.0 * math.log(10000.0) / HD))
    angles = place.astype(jnp.float32)[:, None] * freq[None, :]
    return (jnp.cos(angles), jnp.sin(angles))


def rotate(values, cosine, sine):
    row_count = values.shape[0]
    half_size = cosine.shape[1]
    shaped = values.reshape(row_count, -1, 2 * half_size)
    first_half = shaped[..., :half_size]
    second_half = shaped[..., half_size:]
    cos_b = cosine[:, None, :]
    sin_b = sine[:, None, :]
    turned = jnp.concatenate(
        [first_half * cos_b - second_half * sin_b, second_half * cos_b + first_half * sin_b],
        axis=-1,
    )
    return turned.reshape(row_count, -1)


def dispatch(routes, expert_count, capacity):
    flat_routes = routes.reshape(-1)
    member = (flat_routes[:, None] == jnp.arange(expert_count)[None, :]).astype(jnp.int32)
    place = jnp.sum((jnp.cumsum(member, axis=0) - 1) * member, axis=1)
    entry = jnp.arange(flat_routes.shape[0], dtype=jnp.int32)
    slot_token = (
        jnp.zeros((expert_count, capacity), jnp.int32).at[flat_routes, place].set(entry // 2)
    )
    slot_pick = jnp.zeros((expert_count, capacity), jnp.int32).at[flat_routes, place].set(entry % 2)
    slot_live = jnp.zeros((expert_count, capacity), jnp.float32).at[flat_routes, place].set(1.0)
    slot_index = (flat_routes * capacity + place).reshape(routes.shape)
    return (slot_token, slot_pick, slot_live, slot_index)


def combine(slot_values, slot_index, shares):
    flat_values = slot_values.reshape(-1, slot_values.shape[-1])
    picked = flat_values[slot_index]
    return (jnp.sum(shares[:, :, None] * picked, axis=1), picked)


def route_back(shares, grad_shares, routes, count):
    inner_grad = shares * (grad_shares - jnp.sum(shares * grad_shares, axis=1, keepdims=True))
    table = (routes[:, :, None] == jnp.arange(count)[None, None, :]).astype(jnp.float32)
    return jnp.sum(inner_grad[:, :, None] * table, axis=1)


def outer_sum(wide, narrow):
    return jnp.einsum("...nd,...na->...da", wide, narrow, preferred_element_type=jnp.float32)


def block_parts(
    query_heads, key_heads, value_heads, query_seg, query_pos, segments, block_len, step
):
    begin_offset = step * block_len
    key_block = lax.dynamic_slice_in_dim(key_heads, begin_offset, block_len, 0)
    value_block = lax.dynamic_slice_in_dim(value_heads, begin_offset, block_len, 0)
    seg_block = lax.dynamic_slice_in_dim(segments, begin_offset, block_len, 0)
    key_pos = begin_offset + jnp.arange(block_len, dtype=jnp.int32)
    raw_scores = jnp.einsum(
        "qhd,khd->hqk", query_heads, key_block, preferred_element_type=jnp.float32
    ) * HD ** (-0.5)
    allowed = (query_seg[:, None] == seg_block[None, :]) & (key_pos[None, :] <= query_pos[:, None])
    return (
        jnp.where(allowed[None], raw_scores, big_negative),
        key_block,
        value_block,
        begin_offset,
    )


def attend(query_rot, all_keys, all_values, query_seg, query_pos, segments):
    row_count = query_rot.shape[0]
    seq_len = all_keys.shape[0]
    block_len = min(512, seq_len)
    query_heads = query_rot.reshape(row_count, KVH, HD)
    key_heads = all_keys.reshape(seq_len, KVH, HD)
    value_heads = all_values.reshape(seq_len, KVH, HD)
    parts_at = partial(
        block_parts, query_heads, key_heads, value_heads, query_seg, query_pos, segments, block_len
    )

    def stats_step(step, carry):
        running_top, running_total = carry
        scores = parts_at(step)[0]
        new_top = jnp.maximum(running_top, jnp.max(scores, axis=-1))
        running_total = running_total * jnp.exp(running_top - new_top) + jnp.sum(
            jnp.exp(scores - new_top[..., None]), axis=-1
        )
        return (new_top, running_total)

    start_stats = (
        jnp.full((KVH, row_count), big_negative, jnp.float32),
        jnp.zeros((KVH, row_count), jnp.float32),
    )
    running_top, running_total = lax.fori_loop(0, seq_len // block_len, stats_step, start_stats)
    log_total = running_top + jnp.log(running_total)

    def mix_step(step, accum):
        scores, key_block, value_block, begin_offset = parts_at(step)
        probs = jnp.exp(scores - log_total[..., None]).astype(jnp.bfloat16)
        return accum + jnp.einsum(
            "hqk,khd->qhd", probs, value_block, preferred_element_type=jnp.float32
        )

    expert_mixture = lax.fori_loop(
        0, seq_len // block_len, mix_step, jnp.zeros((row_count, KVH, HD), jnp.float32)
    )
    return (expert_mixture.reshape(row_count, KVH * HD), log_total)


def attend_back(
    query_rot, all_keys, all_values, grad_mixed, log_total, query_seg, query_pos, segments
):
    row_count = query_rot.shape[0]
    seq_len = all_keys.shape[0]
    block_len = min(512, seq_len)
    scale = HD ** (-0.5)
    query_heads = query_rot.reshape(row_count, KVH, HD)
    key_heads = all_keys.reshape(seq_len, KVH, HD)
    value_heads = all_values.reshape(seq_len, KVH, HD)
    grad_heads = grad_mixed.reshape(row_count, KVH, HD)
    parts_at = partial(
        block_parts, query_heads, key_heads, value_heads, query_seg, query_pos, segments, block_len
    )

    def probs_at(step):
        scores, key_block, value_block, begin_offset = parts_at(step)
        probs = jnp.exp(scores - log_total[..., None])
        grad_probs = jnp.einsum(
            "qhd,khd->hqk", grad_heads, value_block, preferred_element_type=jnp.float32
        )
        return (probs, grad_probs, key_block, begin_offset)

    def delta_step(step, accum):
        probs, grad_probs, key_block, begin_offset = probs_at(step)
        return accum + jnp.sum(probs * grad_probs, axis=-1)

    delta = lax.fori_loop(
        0, seq_len // block_len, delta_step, jnp.zeros((KVH, row_count), jnp.float32)
    )

    def back_step(step, carry):
        grad_query, grad_keys, grad_values = carry
        probs, grad_probs, key_block, begin_offset = probs_at(step)
        grad_scores = (probs * (grad_probs - delta[..., None])).astype(jnp.bfloat16)
        grad_query = (
            grad_query
            + jnp.einsum("hqk,khd->qhd", grad_scores, key_block, preferred_element_type=jnp.float32)
            * scale
        )
        key_part = (
            jnp.einsum("hqk,qhd->khd", grad_scores, query_heads, preferred_element_type=jnp.float32)
            * scale
        )
        value_part = jnp.einsum(
            "hqk,qhd->khd",
            probs.astype(jnp.bfloat16),
            grad_heads,
            preferred_element_type=jnp.float32,
        )
        grad_keys = lax.dynamic_update_slice_in_dim(grad_keys, key_part, begin_offset, 0)
        grad_values = lax.dynamic_update_slice_in_dim(grad_values, value_part, begin_offset, 0)
        return (grad_query, grad_keys, grad_values)

    start_back = (
        jnp.zeros((row_count, KVH, HD), jnp.float32),
        jnp.zeros((seq_len, KVH, HD), jnp.float32),
        jnp.zeros((seq_len, KVH, HD), jnp.float32),
    )
    grad_query, grad_keys, grad_values = lax.fori_loop(
        0, seq_len // block_len, back_step, start_back
    )
    return (
        grad_query.reshape(row_count, -1),
        grad_keys.reshape(seq_len, -1),
        grad_values.reshape(seq_len, -1),
    )


def feed_hidden_units(
    input_token_rows, adapter_gate_space, adapter_up_space, weight_portion, adapter_portion
):
    gate_before_activation = jnp.dot(
        input_token_rows, weight_portion[0], preferred_element_type=jnp.float32
    ) + jnp.dot(adapter_gate_space, adapter_portion[0], preferred_element_type=jnp.float32)
    up_before_activation = jnp.dot(
        input_token_rows, weight_portion[1], preferred_element_type=jnp.float32
    ) + jnp.dot(adapter_up_space, adapter_portion[1], preferred_element_type=jnp.float32)
    return (
        gate_before_activation,
        up_before_activation,
        (jax.nn.silu(gate_before_activation) * up_before_activation).astype(jnp.bfloat16),
    )


def ffn_forward_piece(input_token_rows, adapter_gate_space, adapter_up_space, portion_list):
    weight_portion, adapter_portion = portion_list
    gate_before_activation, up_before_activation, hidden_activation = feed_hidden_units(
        input_token_rows, adapter_gate_space, adapter_up_space, weight_portion, adapter_portion
    )
    out_accum = jnp.einsum(
        "nf,df->nd", hidden_activation, weight_portion[2], preferred_element_type=jnp.float32
    )
    adapter_running_sum = jnp.einsum(
        "yh,ch->yc", hidden_activation, adapter_portion[2], preferred_element_type=jnp.float32
    )
    return (out_accum, adapter_running_sum)


def feed_backward_part(
    input_token_rows,
    adapter_gate_space,
    adapter_up_space,
    grad_out,
    gradient_adapter_space,
    portion_list,
):
    weight_portion, adapter_portion = portion_list
    gate_before_activation, up_before_activation, hidden_activation = feed_hidden_units(
        input_token_rows, adapter_gate_space, adapter_up_space, weight_portion, adapter_portion
    )
    grad_inner = jnp.dot(grad_out, weight_portion[2], preferred_element_type=jnp.float32) + jnp.dot(
        gradient_adapter_space, adapter_portion[2], preferred_element_type=jnp.float32
    )
    sigmoid_gate = jax.nn.sigmoid(gate_before_activation)
    gradient_gate_branch = (
        grad_inner
        * up_before_activation
        * sigmoid_gate
        * (1.0 + gate_before_activation * (1.0 - sigmoid_gate))
    ).astype(jnp.bfloat16)
    gradient_up_branch = (grad_inner * gate_before_activation * sigmoid_gate).astype(jnp.bfloat16)
    gradient_token_rows = jnp.einsum(
        "nf,df->nd", gradient_gate_branch, weight_portion[0], preferred_element_type=jnp.float32
    ) + jnp.einsum(
        "nf,df->nd", gradient_up_branch, weight_portion[1], preferred_element_type=jnp.float32
    )
    adapter_space_terms = jnp.concatenate(
        [
            jnp.einsum(
                "yh,ch->yc",
                gradient_gate_branch,
                adapter_portion[0],
                preferred_element_type=jnp.float32,
            ),
            jnp.einsum(
                "yh,ch->yc",
                gradient_up_branch,
                adapter_portion[1],
                preferred_element_type=jnp.float32,
            ),
        ],
        axis=-1,
    )
    adapter_contributions = jnp.stack(
        [
            jnp.einsum(
                "na,nf->af",
                adapter_gate_space,
                gradient_gate_branch,
                preferred_element_type=jnp.float32,
            ),
            jnp.einsum(
                "na,nf->af",
                adapter_up_space,
                gradient_up_branch,
                preferred_element_type=jnp.float32,
            ),
            jnp.einsum(
                "na,nf->af",
                gradient_adapter_space,
                hidden_activation,
                preferred_element_type=jnp.float32,
            ),
        ]
    )
    return (gradient_token_rows, adapter_space_terms, adapter_contributions)


def local(
    layer_input_state,
    cotangent,
    norm_gain_vectors,
    attention_router_weight,
    feed_router_weight,
    attention_query_weight,
    key_value_weight,
    attention_output_weight,
    feed_expert_weight,
    attention_adapters,
    feed_adapter_width,
    feed_adapter_hidden,
    token_document,
    document_adapter,
    attention_expert_pairs,
    feed_expert_pairs,
):
    tok_count = layer_input_state.shape[0]
    adapter_space_whole = attention_adapters.shape[3]
    shard_at = lax.axis_index("shard")
    segments = token_document[0]
    seq_len = segments.shape[0]
    doc_adapters = document_adapter[0]
    doc_count = doc_adapters.shape[0]
    doc_table = (segments[:, None] == jnp.arange(doc_count)[None, :]).astype(jnp.int32)
    doc_starts = jnp.sum(
        (segments[None, :] < jnp.arange(doc_count)[:, None]).astype(jnp.int32), axis=1
    )
    in_doc = jnp.arange(seq_len, dtype=jnp.int32) - jnp.sum(doc_table * doc_starts[None, :], axis=1)
    which_all = jnp.sum(doc_table * doc_adapters[None, :], axis=1)
    first_row = shard_at * tok_count
    my_doc = lax.dynamic_slice_in_dim(in_doc, first_row, tok_count)
    my_adapter = lax.dynamic_slice_in_dim(which_all, first_row, tok_count)
    choose_rows = (jnp.arange(adapter_space_whole) // RANK == my_adapter[:, None]).astype(
        jnp.float32
    )
    select_low = choose_rows.astype(jnp.bfloat16)
    cosine, sine = rotation(my_doc)
    token_total = layer_input_state.astype(jnp.float32)
    gain_one = norm_gain_vectors[0].astype(jnp.float32)
    gain_two = norm_gain_vectors[1].astype(jnp.float32)
    first_normalized = rms_norm(gain_one, token_total).astype(jnp.bfloat16)
    w_query, w_keyval, w_output = (
        lax.all_gather(attention_query_weight, "shard", axis=1, tiled=True),
        lax.all_gather(key_value_weight, "shard", axis=1, tiled=True),
        lax.all_gather(attention_output_weight, "shard", axis=1, tiled=True),
    )
    adapter_lower_complete, adapter_width_complete = (
        lax.all_gather(attention_adapters, "shard", axis=2, tiled=True),
        lax.all_gather(feed_adapter_width, "shard", axis=2, tiled=True),
    )
    adapter_key_space = (
        jnp.dot(
            first_normalized,
            adapter_lower_complete[0, ATTEND_EXPERTS],
            preferred_element_type=jnp.float32,
        )
        * choose_rows
    ).astype(jnp.bfloat16)
    adapter_value_space = (
        jnp.dot(
            first_normalized,
            adapter_lower_complete[0, ATTEND_EXPERTS + 1],
            preferred_element_type=jnp.float32,
        )
        * choose_rows
    ).astype(jnp.bfloat16)
    key_before_rotation = jnp.dot(
        first_normalized, w_keyval[0], preferred_element_type=jnp.float32
    ) + jnp.einsum(
        "dm,om->do",
        adapter_key_space,
        adapter_lower_complete[1, ATTEND_EXPERTS],
        preferred_element_type=jnp.float32,
    )
    value_before_mixing = jnp.dot(
        first_normalized, w_keyval[1], preferred_element_type=jnp.float32
    ) + jnp.einsum(
        "dm,om->do",
        adapter_value_space,
        adapter_lower_complete[1, ATTEND_EXPERTS + 1],
        preferred_element_type=jnp.float32,
    )
    key_rot = rotate(key_before_rotation, cosine, sine).astype(jnp.bfloat16)
    value_low = value_before_mixing.astype(jnp.bfloat16)
    all_keys, all_values = (
        lax.all_gather(key_rot, "shard", axis=0, tiled=True),
        lax.all_gather(value_low, "shard", axis=0, tiled=True),
    )
    logits_attn = jnp.dot(
        first_normalized, attention_router_weight, preferred_element_type=jnp.float32
    )
    share_attn = jax.nn.softmax(
        jnp.take_along_axis(logits_attn, attention_expert_pairs, axis=1), axis=1
    )
    tok_attn, pick_attn, live_attn, index_attn = dispatch(
        attention_expert_pairs, ATTEND_EXPERTS, CAP
    )
    rows_query = ATTEND_EXPERTS * CAP
    first_choice_input = first_normalized[tok_attn]
    slot_select = choose_rows[tok_attn]
    slot_select_low = slot_select.astype(jnp.bfloat16)
    slot_cos = cosine[tok_attn].reshape(rows_query, -1)
    slot_sin = sine[tok_attn].reshape(rows_query, -1)
    adapter_query_space = (
        jnp.einsum(
            "sjh,sho->sjo",
            first_choice_input,
            adapter_lower_complete[0, :ATTEND_EXPERTS],
            preferred_element_type=jnp.float32,
        )
        * slot_select
    ).astype(jnp.bfloat16)
    query_pre = jnp.einsum(
        "ecd,edh->ech", first_choice_input, w_query, preferred_element_type=jnp.float32
    ) + jnp.einsum(
        "tjw,tpw->tjp",
        adapter_query_space,
        adapter_lower_complete[1, :ATTEND_EXPERTS],
        preferred_element_type=jnp.float32,
    )
    query_rot = rotate(query_pre.reshape(rows_query, -1), slot_cos, slot_sin).astype(jnp.bfloat16)
    query_pos = first_row + tok_attn.reshape(-1)
    query_seg = segments[query_pos]
    mixed_f, log_total = attend(query_rot, all_keys, all_values, query_seg, query_pos, segments)
    expert_mixture = mixed_f.astype(jnp.bfloat16).reshape(ATTEND_EXPERTS, CAP, -1)
    adapter_output_space = (
        jnp.einsum(
            "irq,iqy->iry",
            expert_mixture,
            adapter_lower_complete[0, ATTEND_EXPERTS + 2 :],
            preferred_element_type=jnp.float32,
        )
        * slot_select
    ).astype(jnp.bfloat16)
    slot_attn = jnp.einsum(
        "ech,ehd->ecd", expert_mixture, w_output, preferred_element_type=jnp.float32
    ) + jnp.einsum(
        "hlr,htr->hlt",
        adapter_output_space,
        adapter_lower_complete[1, ATTEND_EXPERTS + 2 :],
        preferred_element_type=jnp.float32,
    )
    attn_sum, picked_attn = combine(slot_attn, index_attn, share_attn)
    attended = token_total + attn_sum
    second_normalized = rms_norm(gain_two, attended).astype(jnp.bfloat16)
    logits_ffn = jnp.dot(second_normalized, feed_router_weight, preferred_element_type=jnp.float32)
    share_ffn = jax.nn.softmax(jnp.take_along_axis(logits_ffn, feed_expert_pairs, axis=1), axis=1)
    tok_ffn, pick_ffn, live_ffn, index_ffn = dispatch(feed_expert_pairs, FEED_EXPERTS, CAP)
    second_choice_input = second_normalized[tok_ffn]
    select_two = choose_rows[tok_ffn]
    select_two_low = select_two.astype(jnp.bfloat16)
    adapter_gate_space = (
        jnp.einsum(
            "sjh,sho->sjo",
            second_choice_input,
            adapter_width_complete[:, 0],
            preferred_element_type=jnp.float32,
        )
        * select_two
    ).astype(jnp.bfloat16)
    adapter_up_space = (
        jnp.einsum(
            "sjh,sho->sjo",
            second_choice_input,
            adapter_width_complete[:, 1],
            preferred_element_type=jnp.float32,
        )
        * select_two
    ).astype(jnp.bfloat16)
    slot_outputs = []
    rank_downs = []
    for expert_number in range(FEED_EXPERTS):
        summed, down_partial = ffn_forward_piece(
            second_choice_input[expert_number],
            adapter_gate_space[expert_number],
            adapter_up_space[expert_number],
            (
                lax.all_gather(feed_expert_weight[expert_number], "shard", axis=2, tiled=True),
                lax.all_gather(feed_adapter_hidden[expert_number], "shard", axis=2, tiled=True),
            ),
        )
        adapter_down_space = (down_partial * select_two[expert_number]).astype(jnp.bfloat16)
        rank_downs.append(adapter_down_space)
        slot_outputs.append(
            summed
            + jnp.einsum(
                "pm,em->pe",
                adapter_down_space,
                adapter_width_complete[expert_number, 2],
                preferred_element_type=jnp.float32,
            )
        )
    slot_ffn = jnp.stack(slot_outputs)
    ffn_sum, picked_ffn = combine(slot_ffn, index_ffn, share_ffn)
    layer_out = attended + ffn_sum
    grad_out = cotangent.astype(jnp.float32)
    grad_share_ffn = jnp.sum(picked_ffn * grad_out[:, None, :], axis=-1)
    gradient_choice_feed = (
        live_ffn[..., None] * share_ffn[tok_ffn, pick_ffn][..., None] * grad_out[tok_ffn]
    ).astype(jnp.bfloat16)
    grad_normed_two = jnp.dot(
        route_back(share_ffn, grad_share_ffn, feed_expert_pairs, FEED_EXPERTS),
        feed_router_weight.astype(jnp.float32).T,
        precision=lax.Precision.HIGHEST,
    )
    grad_slot_rows = []
    grad_rank_gates = []
    grad_rank_ups = []
    gradient_upper_portions = []
    for expert_number in range(FEED_EXPERTS):
        grad_rank_down = (
            jnp.dot(
                gradient_choice_feed[expert_number],
                adapter_width_complete[expert_number, 2],
                preferred_element_type=jnp.float32,
            ).astype(jnp.bfloat16)
            * select_two_low[expert_number]
        )
        gradient_token_rows, gradient_adapter_spaces, gradient_adapter_upper = feed_backward_part(
            second_choice_input[expert_number],
            adapter_gate_space[expert_number],
            adapter_up_space[expert_number],
            gradient_choice_feed[expert_number],
            grad_rank_down,
            (
                lax.all_gather(feed_expert_weight[expert_number], "shard", axis=2, tiled=True),
                lax.all_gather(feed_adapter_hidden[expert_number], "shard", axis=2, tiled=True),
            ),
        )
        grad_rank_gate = (
            gradient_adapter_spaces[:, :adapter_space_whole].astype(jnp.bfloat16)
            * select_two_low[expert_number]
        )
        grad_rank_up = (
            gradient_adapter_spaces[:, adapter_space_whole:].astype(jnp.bfloat16)
            * select_two_low[expert_number]
        )
        gradient_token_rows = (
            gradient_token_rows
            + jnp.einsum(
                "pm,em->pe",
                grad_rank_gate,
                adapter_width_complete[expert_number, 0],
                preferred_element_type=jnp.float32,
            )
            + jnp.einsum(
                "pm,em->pe",
                grad_rank_up,
                adapter_width_complete[expert_number, 1],
                preferred_element_type=jnp.float32,
            )
        )
        grad_slot_rows.append(gradient_token_rows)
        grad_rank_gates.append(grad_rank_gate)
        grad_rank_ups.append(grad_rank_up)
        gradient_upper_portions.append(gradient_adapter_upper)
    grad_slot_two = jnp.stack(grad_slot_rows).reshape(FEED_EXPERTS * CAP, -1)
    grad_normed_two = grad_normed_two + jnp.sum(grad_slot_two[index_ffn], axis=1)
    grad_attended = grad_out + rms_back(attended, gain_two, grad_normed_two)
    grad_share_attn = jnp.sum(picked_attn * grad_attended[:, None, :], axis=-1)
    grad_slot_attn = (
        live_attn[..., None] * share_attn[tok_attn, pick_attn][..., None] * grad_attended[tok_attn]
    ).astype(jnp.bfloat16)
    grad_normed = jnp.dot(
        route_back(share_attn, grad_share_attn, attention_expert_pairs, ATTEND_EXPERTS),
        attention_router_weight.astype(jnp.float32).T,
        precision=lax.Precision.HIGHEST,
    )
    w_query, w_keyval, w_output = (
        lax.all_gather(attention_query_weight, "shard", axis=1, tiled=True),
        lax.all_gather(key_value_weight, "shard", axis=1, tiled=True),
        lax.all_gather(attention_output_weight, "shard", axis=1, tiled=True),
    )
    grad_rank_out = (
        jnp.einsum(
            "sjh,sho->sjo",
            grad_slot_attn,
            adapter_lower_complete[1, ATTEND_EXPERTS + 2 :],
            preferred_element_type=jnp.float32,
        ).astype(jnp.bfloat16)
        * slot_select_low
    )
    grad_mixed = (
        jnp.einsum("ecd,ehd->ech", grad_slot_attn, w_output, preferred_element_type=jnp.float32)
        + jnp.einsum(
            "tjw,tpw->tjp",
            grad_rank_out,
            adapter_lower_complete[0, ATTEND_EXPERTS + 2 :],
            preferred_element_type=jnp.float32,
        )
    ).astype(jnp.bfloat16)
    grad_query_rot, grad_keys_all, grad_values_all = attend_back(
        query_rot,
        all_keys,
        all_values,
        grad_mixed.reshape(rows_query, -1),
        log_total,
        query_seg,
        query_pos,
        segments,
    )
    grad_keys, grad_values = (
        lax.psum_scatter(grad_keys_all, "shard", scatter_dimension=0, tiled=True),
        lax.psum_scatter(grad_values_all, "shard", scatter_dimension=0, tiled=True),
    )
    gradient_key_before = rotate(grad_keys, cosine, -sine).astype(jnp.bfloat16)
    gradient_value_before = grad_values.astype(jnp.bfloat16)
    gradient_query_before = (
        rotate(grad_query_rot, slot_cos, -slot_sin)
        .astype(jnp.bfloat16)
        .reshape(ATTEND_EXPERTS, CAP, -1)
    )
    gradient_adapter_query = (
        jnp.einsum(
            "irq,iqy->iry",
            gradient_query_before,
            adapter_lower_complete[1, :ATTEND_EXPERTS],
            preferred_element_type=jnp.float32,
        ).astype(jnp.bfloat16)
        * slot_select_low
    )
    grad_slot_in = jnp.einsum(
        "ech,edh->ecd", gradient_query_before, w_query, preferred_element_type=jnp.float32
    ) + jnp.einsum(
        "hlr,htr->hlt",
        gradient_adapter_query,
        adapter_lower_complete[0, :ATTEND_EXPERTS],
        preferred_element_type=jnp.float32,
    )
    grad_normed = grad_normed + jnp.sum(
        grad_slot_in.reshape(ATTEND_EXPERTS * CAP, -1)[index_attn], axis=1
    )
    gradient_adapter_key = (
        jnp.dot(
            gradient_key_before,
            adapter_lower_complete[1, ATTEND_EXPERTS],
            preferred_element_type=jnp.float32,
        ).astype(jnp.bfloat16)
        * select_low
    )
    gradient_adapter_value = (
        jnp.dot(
            gradient_value_before,
            adapter_lower_complete[1, ATTEND_EXPERTS + 1],
            preferred_element_type=jnp.float32,
        ).astype(jnp.bfloat16)
        * select_low
    )
    grad_normed = (
        grad_normed
        + jnp.einsum(
            "nh,dh->nd", gradient_key_before, w_keyval[0], preferred_element_type=jnp.float32
        )
        + jnp.einsum(
            "nh,dh->nd", gradient_value_before, w_keyval[1], preferred_element_type=jnp.float32
        )
    )
    grad_normed = (
        grad_normed
        + jnp.einsum(
            "pm,em->pe",
            gradient_adapter_key,
            adapter_lower_complete[0, ATTEND_EXPERTS],
            preferred_element_type=jnp.float32,
        )
        + jnp.einsum(
            "pm,em->pe",
            gradient_adapter_value,
            adapter_lower_complete[0, ATTEND_EXPERTS + 1],
            preferred_element_type=jnp.float32,
        )
    )
    grad_in = grad_attended + rms_back(token_total, gain_one, grad_normed)
    stacked_gates = jnp.stack(grad_rank_gates)
    stacked_ups = jnp.stack(grad_rank_ups)
    stacked_downs = jnp.stack(rank_downs)
    grad_query_down = outer_sum(first_choice_input, gradient_adapter_query)
    grad_out_down = outer_sum(expert_mixture, grad_rank_out)
    grad_query_up = outer_sum(gradient_query_before, adapter_query_space)
    grad_out_up = outer_sum(grad_slot_attn, adapter_output_space)
    grad_key_down = outer_sum(first_normalized, gradient_adapter_key)
    grad_value_down = outer_sum(first_normalized, gradient_adapter_value)
    grad_key_up = outer_sum(gradient_key_before, adapter_key_space)
    grad_value_up = outer_sum(gradient_value_before, adapter_value_space)
    gradient_gate_through_down = outer_sum(second_choice_input, stacked_gates)
    gradient_up_through_down = outer_sum(second_choice_input, stacked_ups)
    gradient_down_through_up = outer_sum(gradient_choice_feed, stacked_downs)
    adapter_down_matrices = jnp.concatenate(
        [grad_query_down, grad_key_down[None], grad_value_down[None], grad_out_down], axis=0
    )
    adapter_up_matrices = jnp.concatenate(
        [grad_query_up, grad_key_up[None], grad_value_up[None], grad_out_up], axis=0
    )
    attention_adapter_gradient = jnp.stack([adapter_down_matrices, adapter_up_matrices])
    gradient_adapter_lower = jnp.stack(
        [gradient_gate_through_down, gradient_up_through_down, gradient_down_through_up], axis=1
    )
    grad_attn_own, grad_d_own = (
        lax.psum_scatter(attention_adapter_gradient, "shard", scatter_dimension=2, tiled=True),
        lax.psum_scatter(gradient_adapter_lower, "shard", scatter_dimension=2, tiled=True),
    )
    gradient_adapter_upper = jnp.stack(gradient_upper_portions)
    gradient_upper_local = lax.psum_scatter(
        gradient_adapter_upper, "shard", scatter_dimension=3, tiled=True
    )
    grad_attn_own, grad_d_own, gradient_upper_local = lax.psum(
        (grad_attn_own, grad_d_own, gradient_upper_local), "rep"
    )
    return (layer_out, grad_in, grad_attn_own, grad_d_own, gradient_upper_local)


def solution(mesh):
    in_specs = (
        P(("rep", "shard"), None),
        P(("rep", "shard"), None),
        P(),
        P(),
        P(),
        P(None, "shard", None),
        P(None, "shard", None),
        P(None, "shard", None),
        P(None, None, None, "shard"),
        P(None, None, "shard", None),
        P(None, None, "shard", None),
        P(None, None, None, "shard"),
        P("rep", None),
        P("rep", None),
        P(("rep", "shard"), None),
        P(("rep", "shard"), None),
    )
    out_specs = (
        P(("rep", "shard"), None),
        P(("rep", "shard"), None),
        P(None, None, "shard", None),
        P(None, None, "shard", None),
        P(None, None, None, "shard"),
    )
    return jax.shard_map(local, mesh=mesh, in_specs=in_specs, out_specs=out_specs, check_vma=False)
```

profile of v0, /device:TPU:0, one launch (start us, length us, event | category | flops | bytes accessed | tf_op | source)
XLA Modules:
  0.0 3447.9 jit_solution(8699480621904216333)
XLA Ops:
  11.6 64.3 %all-gather.26.cloned.1.call-done = bf16[2,10,2048,128]{3,2,1,0:T(8,128)(2,1)} async-done(((bf16[2,10,256,128]{3,2,1,0:T(8,128)(2,1)}), bf16[2,10,2048,128]{3,2,1,0:T(8,128)(2,1)}) %all-gather.26.cloned.1.call-update) | async-done | bytes 10485776 | tf_op jit(solution)/shard_map/all_gather | solution.py:359
  77.3 90.4 %all-gather.24.cloned.1.call-done = bf16[2,2048,2048]{2,1,0:T(8,128)(2,1)} async-done(((bf16[2,256,2048]{2,1,0:T(8,128)(2,1)}), bf16[2,2048,2048]{2,1,0:T(8,128)(2,1)}) %all-gather.24.cloned.1.call-update) | async-done | bytes 16777232 | tf_op jit(solution)/shard_map/all_gather | solution.py:355
  187.3 22.7 fusion.248
  332.5 83.0 %all-gather.32.cloned.1.call-done = bf16[4,2048,2048]{2,1,0:T(8,128)(2,1)} async-done(((bf16[4,256,2048]{2,1,0:T(8,128)(2,1)}), bf16[4,2048,2048]{2,1,0:T(8,128)(2,1)}) %all-gather.32.cloned.1.call-update) | async-done | bytes 33554448 | tf_op jit(solution)/shard_map/all_gather | solution.py:354
  415.5 16.2 convolution_add_fusion.15
  435.7 27.3 while.62
  463.0 17.0 while.63
  494.9 83.2 %all-gather.34.cloned.1.call-done = bf16[4,2048,2048]{2,1,0:T(8,128)(2,1)} async-done(((bf16[4,256,2048]{2,1,0:T(8,128)(2,1)}), bf16[4,2048,2048]{2,1,0:T(8,128)(2,1)}) %all-gather.34.cloned.1.call-update) | async-done | bytes 33554448 | tf_op jit(solution)/shard_map/all_gather | solution.py:356
  578.1 18.3 convolution_add_fusion.14
  636.0 303.3 %all-gather.50.cloned.1.call-done = bf16[1,3,2048,5632]{2,3,1,0:T(8,128)(2,1)} async-done(((bf16[1,3,2048,704]{2,3,1,0:T(8,128)(2,1)}), bf16[1,3,2048,5632]{2,3,1,0:T(8,128)(2,1)}) %all-gather.50.cloned.1.call-update) | async-done | bytes 69206032 | tf_op jit(solution)/shard_map/all_gather | solution.py:489
  964.8 13.0 fusion.84
  986.6 16.8 fusion.80
  1004.5 287.6 %all-gather.46.cloned.1.call-done = bf16[1,3,2048,5632]{2,3,1,0:T(8,128)(2,1)} async-done(((bf16[1,3,2048,704]{2,3,1,0:T(8,128)(2,1)}), bf16[1,3,2048,5632]{2,3,1,0:T(8,128)(2,1)}) %all-gather.46.cloned.1.call-update) | async-done | bytes 69206032 | tf_op jit(solution)/shard_map/all_gather | solution.py:489
  1292.1 12.9 fusion.75
  1305.0 17.8 fusion.77
  1335.5 270.3 %all-gather.42.cloned.1.call-done = bf16[1,3,2048,5632]{2,3,1,0:T(8,128)(2,1)} async-done(((bf16[1,3,2048,704]{2,3,1,0:T(8,128)(2,1)}), bf16[1,3,2048,5632]{2,3,1,0:T(8,128)(2,1)}) %all-gather.42.cloned.1.call-update) | async-done | bytes 69206032 | tf_op jit(solution)/shard_map/all_gather | solution.py:489
  1605.8 13.1 fusion.69
  1664.9 19.3 all-gather.44.cloned.1.call-done
  1696.2 16.2 fusion.68
  1712.4 285.3 %all-gather.38.cloned.1.call-done = bf16[1,3,2048,5632]{2,3,1,0:T(8,128)(2,1)} async-done(((bf16[1,3,2048,704]{2,3,1,0:T(8,128)(2,1)}), bf16[1,3,2048,5632]{2,3,1,0:T(8,128)(2,1)}) %all-gather.38.cloned.1.call-update) | async-done | bytes 69206032 | tf_op jit(solution)/shard_map/all_gather | solution.py:489
  2023.1 13.1 fusion.66
  2190.6 17.6 fusion.90
  2210.4 15.8 while.64
  2234.9 101.8 %while.65 = (s32[]{:T(128)}, f32[320,16,128]{2,0,1:T(8,128)}, f32[1024,16,128]{0,2,1:T(8,128)}, f32[1024,16,128]{0,2,1:T(8,128)}, bf16[1024,16,128]{2,0,1:T(8,12...) while((s32[]{:T(128)}, f32[320,16,128]{2,0,1:T(8,128)}, ...), condition=%wide.region_41.43_spmd.clone, body=%wide.region_40.42_spmd.clone.sunk | while | flops 3385164288 | bytes 207143760 | solution.py:200
  2380.9 19.1 pad_maximum_fusion
  2400.0 38.1 %copy.229 = f32[4,3,128,5632]{2,0,1,3:T(4,128)} copy(f32[4,3,128,5632]{3,2,1,0:T(8,128)} %pad_maximum_fusion) | data formatting | bytes 69206016 | tf_op jit(solution)/shard_map/stack | solution.py:713
  2469.8 13.5 reduce-scatter.7.cloned.1.call-done
  2513.7 382.9 %all-reduce.5.cloned.1.call-done = f32[4,3,128,5632]{2,0,1,3:T(4,128)} async-done(((f32[4,3,128,5632]{2,0,1,3:T(4,128)}), f32[4,3,128,5632]{2,0,1,3:T(4,128)}) %all-reduce.5.cloned.1.call-update) | async-done | bytes 34603024
  2901.7 90.9 %reduce-scatter.11.cloned.1.call-done = f32[4,3,256,128]{3,2,0,1:T(8,128)} async-done(((f32[4,3,2048,128]{3,2,0,1:T(8,128)}), f32[4,3,256,128]{3,2,0,1:T(8,128)}) %reduce-scatter.11.cloned.1.call-update) | async-done | bytes 1572880 | tf_op jit(solution)/shard_map/reduce_scatter | solution.py:711
  2992.6 139.5 %reduce-scatter.9.cloned.1.call-done = f32[2,10,256,128]{3,2,1,0:T(8,128)} async-done(((f32[2,10,2048,128]{3,2,1,0:T(8,128)}), f32[2,10,256,128]{3,2,1,0:T(8,128)}) %reduce-scatter.9.cloned.1.call-update) | async-done | bytes 2621456 | tf_op jit(solution)/shard_map/reduce_scatter | solution.py:710
  3136.0 17.9 convolution_add_fusion.12
  3183.3 248.5 %all-reduce.7.cloned.1.call-done = (f32[2,10,256,128]{3,2,1,0:T(8,128)}, f32[4,3,256,128]{3,2,0,1:T(8,128)}, f32[4,3,128,704]{2,0,1,3:T(4,128)}) async-done(((f32[2,10,256,128]{3,2,1,0:T(8,128)}, f32[4,3,256,128]{3,2,0,1:T(8,128)}, f32[4,3,128,704]{2,0,1,3:T(4,128)}), (f32[2,10,256,128]{3,2,1,0:T(8,128)}, f32[4,3,256,128]{3,2,0,1:T(8,128)}, f32[4,3,128,704]{2,0,1,3:T(4,128)})) %all-reduce.7.cloned.1.call-update) | async-done | bytes 8519696 | tf_op jit(solution)/shard_map/psum | solution.py:717
  (824 shorter events, 814.1 us)
Async XLA Ops:
  7.2 601.4 %copy-start = (bf16[2048,4]{0,1:T(4,128)(2,1)S(1)}, bf16[2048,4]{0,1:T(4,128)(2,1)}, u32[]{:S(2)}) copy-start(bf16[2048,4]{0,1:T(4,128)(2,1)} %param.30) | copy-start | bytes 49156
  7.2 68.7 %all-gather.26.cloned.1.call-start = ((), (), s32[]{:S(2)}) async-start(), calls=%async_computation.5 | async-start | bytes 11796480 | tf_op jit(solution)/shard_map/all_gather | solution.py:359
  8.0 159.8 %all-gather.24.cloned.1.call-start = ((), (), s32[]{:S(2)}) async-start(), calls=%async_computation.4 | async-start | bytes 18874368 | tf_op jit(solution)/shard_map/all_gather | solution.py:355
  8.7 311.5 %all-gather.30.cloned.1.call-start = ((), (), s32[]{:S(2)}) async-start(), calls=%async_computation.7 | async-start | bytes 4718592 | tf_op jit(solution)/shard_map/all_gather | solution.py:397
  9.1 208.3 %copy-start.185 = (s32[128]{0:T(128)}, s32[128]{0:T(128)S(1)}, u32[]{:S(2)}) copy-start(s32[128]{0:T(128)S(1)} %and_select_fusion.4) | copy-start | bytes 1540
  10.8 235.7 %copy-start.25 = (f32[128,64]{1,0:T(8,128)}, f32[128,64]{1,0:T(8,128)S(1)}, u32[]{:S(2)}) copy-start(f32[128,64]{1,0:T(8,128)S(1)} %get-tuple-element.1179) | copy-start | bytes 98308
  11.6 241.0 %copy-start.13 = (bf16[128,2048]{1,0:T(8,128)(2,1)}, bf16[128,2048]{1,0:T(8,128)(2,1)S(1)}, u32[]{:S(2)}) copy-start(bf16[128,2048]{1,0:T(8,128)(2,1)S(1)} %fusion.179) | copy-start | bytes 1572868
  176.2 151.1 %all-gather.28.cloned.1.call-start = ((), (), s32[]{:S(2)}) async-start(), calls=%async_computation.6 | async-start | bytes 4718592 | tf_op jit(solution)/shard_map/all_gather | solution.py:398
  184.5 231.1 %all-gather.32.cloned.1.call-start = ((), (), s32[]{:S(2)}) async-start(), calls=%async_computation.8 | async-start | bytes 37748736 | tf_op jit(solution)/shard_map/all_gather | solution.py:354
  185.1 393.0 %all-gather.34.cloned.1.call-start = ((), (), s32[]{:S(2)}) async-start(), calls=%async_computation.9 | async-start | bytes 37748736 | tf_op jit(solution)/shard_map/all_gather | solution.py:356
  185.7 439.9 %all-gather.36.cloned.1.call-start = ((), (), s32[]{:S(2)}) async-start(), calls=%async_computation.10 | async-start | bytes 7077888 | tf_op jit(solution)/shard_map/all_gather | solution.py:360
  187.2 752.1 %all-gather.50.cloned.1.call-start = ((), (), s32[]{:S(2)}) async-start(), calls=%async_computation.21 | async-start | bytes 77856768 | tf_op jit(solution)/shard_map/all_gather | solution.py:489
  210.0 768.6 %all-gather.52.cloned.1.call-start = ((), (), s32[]{:S(2)}) async-start(), calls=%async_computation.22 | async-start | bytes 4866048 | tf_op jit(solution)/shard_map/all_gather | solution.py:490
  213.0 1079.1 %all-gather.46.cloned.1.call-start = ((), (), s32[]{:S(2)}) async-start(), calls=%async_computation.19 | async-start | bytes 77856768 | tf_op jit(solution)/shard_map/all_gather | solution.py:489
  213.6 1392.2 %all-gather.42.cloned.1.call-start = ((), (), s32[]{:S(2)}) async-start(), calls=%async_computation.17 | async-start | bytes 77856768 | tf_op jit(solution)/shard_map/all_gather | solution.py:489
  214.3 1430.6 %all-gather.48.cloned.1.call-start = ((), (), s32[]{:S(2)}) async-start(), calls=%async_computation.20 | async-start | bytes 4866048 | tf_op jit(solution)/shard_map/all_gather | solution.py:490
  214.9 1469.2 %all-gather.44.cloned.1.call-start = ((), (), s32[]{:S(2)}) async-start(), calls=%async_computation.18 | async-start | bytes 4866048 | tf_op jit(solution)/shard_map/all_gather | solution.py:490
  215.7 1782.0 %all-gather.38.cloned.1.call-start = ((), (), s32[]{:S(2)}) async-start(), calls=%async_computation.15 | async-start | bytes 77856768 | tf_op jit(solution)/shard_map/all_gather | solution.py:489
  216.2 1820.5 %all-gather.40.cloned.1.call-start = ((), (), s32[]{:S(2)}) async-start(), calls=%async_computation.16 | async-start | bytes 4866048 | tf_op jit(solution)/shard_map/all_gather | solution.py:490
  216.8 2250.0 %reduce-scatter.5.cloned.1.call-start = ((), (), s32[]{:S(2)}) async-start(), calls=%async_computation.11 | async-start | bytes 9437184 | tf_op jit(solution)/shard_map/reduce_scatter | solution.py:614
  608.6 1401.8 %copy-start.37 = (bf16[320,2048]{1,0:T(8,128)(2,1)}, bf16[320,2048]{1,0:T(8,128)(2,1)S(1)}, u32[]{:S(2)}) copy-start(bf16[320,2048]{1,0:T(8,128)(2,1)S(1)} %gather_fusion.6) | copy-start | bytes 3932164
  618.1 1405.0 %copy-start.39 = (bf16[4,80,2048]{2,1,0:T(8,128)(2,1)}, bf16[4,80,2048]{2,1,0:T(8,128)(2,1)S(1)}, u32[]{:S(2)}) copy-start(bf16[4,80,2048]{2,1,0:T(8,128)(2,1)S(1)} %multiply_convert_fusion.1) | copy-start | bytes 3932164
  627.8 1409.0 %copy-start.104 = (bf16[4,80,128]{2,1,0:T(8,128)(2,1)}, bf16[4,80,128]{2,1,0:T(8,128)(2,1)S(1)}, u32[]{:S(2)}) copy-start(bf16[4,80,128]{2,1,0:T(8,128)(2,1)S(1)} %fusion.136) | copy-start | bytes 245764
  630.0 1409.4 %copy-start.106 = (bf16[4,80,128]{2,1,0:T(8,128)(2,1)}, bf16[4,80,128]{2,1,0:T(8,128)(2,1)S(1)}, u32[]{:S(2)}) copy-start(bf16[4,80,128]{2,1,0:T(8,128)(2,1)S(1)} %fusion.135) | copy-start | bytes 245764
  631.4 352.6 %copy-start.168 = (bf16[80,128]{1,0:T(8,128)(2,1)}, bf16[80,128]{1,0:T(8,128)(2,1)S(1)}, u32[]{:S(2)}) copy-start(bf16[80,128]{1,0:T(8,128)(2,1)S(1)} %fusion.166) | copy-start | bytes 61444
  632.7 1017.7 %copy-start.170 = (bf16[80,128]{1,0:T(8,128)(2,1)}, bf16[80,128]{1,0:T(8,128)(2,1)S(1)}, u32[]{:S(2)}) copy-start(bf16[80,128]{1,0:T(8,128)(2,1)S(1)} %fusion.165) | copy-start | bytes 61444
  634.0 1055.6 %copy-start.164 = (bf16[80,128]{1,0:T(8,128)(2,1)}, bf16[80,128]{1,0:T(8,128)(2,1)S(1)}, u32[]{:S(2)}) copy-start(bf16[80,128]{1,0:T(8,128)(2,1)S(1)} %fusion.164) | copy-start | bytes 61444
  2336.8 146.5 %reduce-scatter.7.cloned.1.call-start = ((), (), s32[]{:S(2)}) async-start(), calls=%async_computation.12 | async-start | bytes 9437184 | tf_op jit(solution)/shard_map/reduce_scatter | solution.py:615
  2337.4 559.3 %all-reduce.5.cloned.1.call-start = ((), (), s32[]{:S(2)}) async-start(), calls=%async_computation.23 | async-start | bytes 69206016
  2438.2 554.4 %reduce-scatter.11.cloned.1.call-start = ((), (), s32[]{:S(2)}) async-start(), calls=%async_computation.14 | async-start | bytes 14155776 | tf_op jit(solution)/shard_map/reduce_scatter | solution.py:711
  2447.6 684.5 %reduce-scatter.9.cloned.1.call-start = ((), (), s32[]{:S(2)}) async-start(), calls=%async_computation.13 | async-start | bytes 23592960 | tf_op jit(solution)/shard_map/reduce_scatter | solution.py:710
  2511.9 920.0 %all-reduce.7.cloned.1.call-start = ((), (), s32[]{:S(2)}) async-start(), calls=%async_computation.24 | async-start | bytes 17039360 | tf_op jit(solution)/shard_map/psum | solution.py:717
  (197 other events, 2197.1 us)
Sparse Core Ops, SparseCore 0:
  10.0 65.9 all-gather.25
  77.9 89.8 all-gather.23
  176.3 37.4 all-gather.29
  216.1 36.7 all-gather.27
  254.6 160.8 all-gather.31
  417.3 160.7 all-gather.33
  580.0 45.5 all-gather.35
  627.5 311.7 all-gather.49
  941.2 37.2 all-gather.51
  980.3 311.7 all-gather.45
  1294.0 311.7 all-gather.41
  1607.6 37.2 all-gather.47
  1646.8 37.2 all-gather.43
  1685.9 311.7 all-gather.37
  1999.4 37.2 all-gather.39
  2336.9 71.3 reduce-scatter.4
  2412.0 71.2 reduce-scatter.6
  2486.9 409.7 all-reduce.4
  2900.2 92.3 reduce-scatter.10
  2996.1 135.9 reduce-scatter.8
  3135.4 296.3 all-reduce.6
where the time goes:
time: 3460 us; the launch traced here: 3450 us
  waiting for transfers between devices  2380 us (69%)
  matrix products  627 us (18%)
  local copies, waits for them, and re-layouts  303 us (9%)
  other arithmetic  119 us (3%)
    all_gather x4, waiting for transfers between devices, local(): lax.all_gather(feed_expert_weight[expert_number], 'shard', axis=2, tiled=...  1150 us
    unnamed x22, waiting for transfers between devices  390 us
    psum x1, waiting for transfers between devices, local(): lax.psum((grad_attn_own, grad_d_own, gradient_upper_local), 'rep')  249 us
    reduce_scatter x1, waiting for transfers between devices, local(): lax.psum_scatter(attention_adapter_gradient, 'shard', scatter_dimension=2...  139 us
    reduce_scatter x1, waiting for transfers between devices, local(): lax.psum_scatter(gradient_adapter_lower, 'shard', scatter_dimension=2, ti...  90.9 us
    all_gather x1, waiting for transfers between devices, local(): lax.all_gather(key_value_weight, 'shard', axis=1, tiled=True)  90.4 us
    all_gather x1, waiting for transfers between devices, local(): lax.all_gather(attention_output_weight, 'shard', axis=1, tiled=True)  83.2 us
    all_gather x1, waiting for transfers between devices, local(): lax.all_gather(attention_query_weight, 'shard', axis=1, tiled=True)  83 us
  transfers between devices with their start and end apart: 21, of which 18 were waited for; matrix products, arithmetic and copies ran while one was open for 21% of the time, Pallas kernels for 0%

commit v1 on v0

v1 whole, which is shorter than its diff:
```python
from functools import partial
import math

import jax
import jax.numpy as jnp
from jax import lax
from jax.experimental import pallas as pl
from jax.experimental.pallas import tpu as pltpu
from jax.sharding import PartitionSpec as P

HD = 128
RANK = 16
CAP = 80
EXPERTS = 4
CHUNK = 256
EPS = 1e-05
NEG = -1e30
F32 = jnp.float32
BF16 = jnp.bfloat16


def ein(spec, a, b):
    return jnp.einsum(spec, a, b, preferred_element_type=F32)


def rms_norm(gain, values):
    return values * lax.rsqrt(jnp.mean(values * values, axis=-1, keepdims=True) + EPS) * gain


def rms_back(values, gain, grad):
    unused, backward_function = jax.vjp(partial(rms_norm, gain), values)
    return backward_function(grad)[0]


def masks_of(n):
    return list(range(0, n, 2)) + list(range(1, n, 2))


def swap(x, n, d):
    return lax.ppermute(x, "shard", [(i, i ^ d) for i in range(n)])


def gather_blocks(x, n):
    if n == 8:
        half = x.shape[0] // 2
        y0, x1 = swap(x[:half], n, 4), swap(x[half:], n, 2)
        y1, x0 = swap(x[half:], n, 4), swap(x[:half], n, 2)
        d0, d1 = swap(y0, n, 2), swap(x1, n, 4)
        mine = [[x], [x0, x1], [y0, y1], [d0, d1]]
    else:
        mine = [[x]] + [[swap(x, n, d)] for d in range(2, n, 2)]
    mine = [p[0] if len(p) == 1 else jnp.concatenate(p) for p in mine]
    return jnp.stack(mine + [swap(p, n, 1) for p in mine])


def gather_small(x, n):
    out, d = x[None], 1
    while d < n:
        out = jnp.concatenate([out, swap(out, n, d)])
        d *= 2
    return jnp.stack([out[m] for m in masks_of(n)])


def sum_small(x, n):
    bits, d = n.bit_length() - 1, 1
    lead = x.ndim - 1
    x = x.reshape(x.shape[:lead] + (2,) * bits + (x.shape[lead] // n,))
    for k in range(bits):
        got = swap(x, n, d)
        x = x + jnp.flip(got, lead if k == 0 else lead + bits - k)
        d *= 2
    return x.reshape(x.shape[:lead] + (-1,))


def reduce_blocks(parts, n):
    h = n // 2
    near, far = parts[:h], parts[h:]
    got = swap(far, n, 1)
    q = near.astype(F32) + got.astype(F32)
    if n == 8:
        half = parts.shape[1] // 2
        low = q.astype(BF16)
        ra = swap(jnp.stack([low[1, :half], low[3, :half]]), n, 2).astype(F32)
        rb = swap(jnp.stack([low[2, half:], low[3, half:]]), n, 4).astype(F32)
        a0, a2 = q[0, :half] + ra[0], q[2, :half] + ra[1]
        b0, b1 = q[0, half:] + rb[0], q[1, half:] + rb[1]
        a0 = a0 + swap(a2.astype(BF16), n, 4).astype(F32)
        b0 = b0 + swap(b1.astype(BF16), n, 2).astype(F32)
        return jnp.concatenate([a0, b0])
    total = q[0]
    for i in range(1, h):
        total = total + swap(q[i].astype(BF16), n, 2 * i).astype(F32)
    return total


def reorder(stacked, me, n):
    where = position(me, n)
    return jnp.concatenate([lax.dynamic_slice_in_dim(stacked, where[j], 1, 0) for j in range(n)])


def position(me, n):
    mask = jnp.arange(n, dtype=jnp.int32) ^ me
    return jnp.where(mask % 2 == 0, mask // 2, n // 2 + mask // 2)


def reshard(w, me, n, axis):
    width = w.shape[-1] // n
    pieces = []
    for m in masks_of(n):
        piece = lax.dynamic_slice_in_dim(w, (me ^ m) * width, width, w.ndim - 1)
        pieces.append(piece if m == 0 else swap(piece, n, m))
    whole = reorder(jnp.stack(pieces), me, n)
    whole = jnp.moveaxis(whole, 0, axis)
    return whole.reshape(w.shape[:axis] + (n * w.shape[axis], width))


def turn(v, cos, sin):
    return v * cos + pltpu.roll(v, HD // 2, 1) * sin


def attend_kernel(
    where, qp, cs, sn, lo, hi, kp, vv, ct, st, mixed, qr, kr, lse, k_abs, v_abs, scores, mx, tot, acc
):
    b = pl.program_id(1)
    n, rows = kp.shape[0], qp.shape[0] * qp.shape[1]
    tok = kp.shape[1]

    @pl.when(b == 0)
    def start():
        def one(j, carry):
            at = where[j]
            k = turn(kp[at], ct[at], st[at]).astype(BF16)
            kr[at] = k
            begin = pl.multiple_of(j * tok, tok)
            k_abs[pl.ds(begin, tok), :] = k
            v_abs[pl.ds(begin, tok), :] = vv[at]
            return carry

        lax.fori_loop(0, n, one, 0)

    def flat(r):
        return r[...].reshape(rows, r.shape[-1])

    q = turn(flat(qp), flat(cs), flat(sn)).astype(BF16)
    qr[...] = q.reshape(qr.shape)
    first, last = flat(lo), flat(hi)
    count = (b * tok + tok + CHUNK - 1) // CHUNK
    mx[...] = jnp.full(mx.shape, NEG, F32)

    def score(j, carry):
        begin = pl.multiple_of(j * CHUNK, CHUNK)
        s = lax.dot_general(
            q, k_abs[pl.ds(begin, CHUNK), :], (((1,), (1,)), ((), ())), preferred_element_type=F32
        ) * HD ** (-0.5)
        at = begin + lax.broadcasted_iota(jnp.int32, s.shape, 1)
        s = jnp.where((at >= first) & (at <= last), s, NEG)
        scores[:, pl.ds(begin, CHUNK)] = s
        mx[...] = jnp.maximum(mx[...], jnp.maximum(s[:, :HD], s[:, HD:]))
        return carry

    lax.fori_loop(0, count, score, 0)
    top = jnp.max(mx[...], axis=1, keepdims=True)
    tot[...] = jnp.zeros(tot.shape, F32)
    acc[...] = jnp.zeros(acc.shape, F32)

    def mix(j, carry):
        begin = pl.multiple_of(j * CHUNK, CHUNK)
        p = jnp.exp(scores[:, pl.ds(begin, CHUNK)] - top)
        tot[...] += p[:, :HD] + p[:, HD:]
        acc[...] += jnp.dot(
            p.astype(BF16), v_abs[pl.ds(begin, CHUNK), :], preferred_element_type=F32
        )
        return carry

    lax.fori_loop(0, count, mix, 0)
    total = jnp.sum(tot[...], axis=1, keepdims=True)
    mixed[...] = (acc[...] / total).astype(BF16).reshape(mixed.shape)
    lse[...] = jnp.broadcast_to(top + jnp.log(total), (rows, HD)).reshape(lse.shape)


def attend_back_kernel(
    where, qr, gm, mixed, lse, cs, sn, lo, hi, kr, vv, ct, st, gq, gk, gv, k_abs, v_abs, dk, dv, dq
):
    b = pl.program_id(1)
    n, rows = kr.shape[0], qr.shape[0] * qr.shape[1]
    tok = kr.shape[1]
    scale = HD ** (-0.5)

    @pl.when(b == 0)
    def start():
        def one(j, carry):
            at = where[j]
            begin = pl.multiple_of(j * tok, tok)
            k_abs[pl.ds(begin, tok), :] = kr[at]
            v_abs[pl.ds(begin, tok), :] = vv[at]
            return carry

        lax.fori_loop(0, n, one, 0)
        dk[...] = jnp.zeros(dk.shape, F32)
        dv[...] = jnp.zeros(dv.shape, F32)

    def flat(r):
        return r[...].reshape(rows, r.shape[-1])

    q, g = flat(qr), flat(gm)
    delta = jnp.sum(flat(mixed).astype(F32) * g.astype(F32), axis=1, keepdims=True)
    log_total = flat(lse)[:, :1]
    first, last = flat(lo), flat(hi)
    count = (b * tok + tok + CHUNK - 1) // CHUNK
    dq[...] = jnp.zeros(dq.shape, F32)
    nt = (((1,), (1,)), ((), ()))
    tn = (((0,), (0,)), ((), ()))

    def step(j, carry):
        begin = pl.multiple_of(j * CHUNK, CHUNK)
        here = pl.ds(begin, CHUNK)
        k, v = k_abs[here, :], v_abs[here, :]
        s = lax.dot_general(q, k, nt, preferred_element_type=F32) * scale
        at = begin + lax.broadcasted_iota(jnp.int32, s.shape, 1)
        p = jnp.where((at >= first) & (at <= last), jnp.exp(s - log_total), 0.0)
        dp = lax.dot_general(g, v, nt, preferred_element_type=F32)
        ds = (p * (dp - delta)).astype(BF16)
        dq[...] += jnp.dot(ds, k, preferred_element_type=F32)
        dk[here, :] += lax.dot_general(ds, q, tn, preferred_element_type=F32)
        dv[here, :] += lax.dot_general(p.astype(BF16), g, tn, preferred_element_type=F32)
        return carry

    lax.fori_loop(0, count, step, 0)
    gq[...] = turn(dq[...] * scale, flat(cs), -flat(sn)).astype(BF16).reshape(gq.shape)

    @pl.when(b == n - 1)
    def finish():
        def one(j, carry):
            at = where[j]
            here = pl.ds(pl.multiple_of(j * tok, tok), tok)
            gk[at] = turn(dk[here, :] * scale, ct[at], -st[at]).astype(BF16)
            gv[at] = dv[here, :].astype(BF16)
            return carry

        lax.fori_loop(0, n, one, 0)


def slot_spec(width, per_head, n):
    if per_head:
        return pl.BlockSpec((EXPERTS, None, CAP, width), lambda h, b, where: (0, where[b], 0, h))
    return pl.BlockSpec((EXPERTS, None, CAP, width), lambda h, b, where: (0, where[b], 0, 0))


def token_spec(n, tok, per_head):
    if per_head:
        return pl.BlockSpec((n, tok, HD), lambda h, b, where: (0, 0, h))
    return pl.BlockSpec((n, tok, HD), lambda h, b, where: (0, 0, 0))


def attend(where, q_pre, cos_slot, sin_slot, lo, hi, k_pre, v, cos_tok, sin_tok):
    n, tok, own = k_pre.shape
    heads, seq, rows = own // HD, n * tok, EXPERTS * CAP
    qs, ss, one = slot_spec(HD, True, n), slot_spec(HD, False, n), slot_spec(1, False, n)
    kh, ks = token_spec(n, tok, True), token_spec(n, tok, False)
    slots = (EXPERTS, n, CAP, own)
    return pl.pallas_call(
        attend_kernel,
        grid_spec=pltpu.PrefetchScalarGridSpec(
            num_scalar_prefetch=1,
            grid=(heads, n),
            in_specs=[qs, ss, ss, one, one, kh, kh, ks, ks],
            out_specs=[qs, qs, kh, qs],
            scratch_shapes=[
                pltpu.VMEM((seq, HD), BF16),
                pltpu.VMEM((seq, HD), BF16),
                pltpu.VMEM((rows, seq + CHUNK), F32),
                pltpu.VMEM((rows, HD), F32),
                pltpu.VMEM((rows, HD), F32),
                pltpu.VMEM((rows, HD), F32),
            ],
        ),
        out_shape=[
            jax.ShapeDtypeStruct(slots, BF16),
            jax.ShapeDtypeStruct(slots, BF16),
            jax.ShapeDtypeStruct((n, tok, own), BF16),
            jax.ShapeDtypeStruct(slots, F32),
        ],
        compiler_params=pltpu.CompilerParams(vmem_limit_bytes=48 << 20),
        cost_estimate=pl.CostEstimate(
            flops=3 * rows * seq * own * n, bytes_accessed=16 << 20, transcendentals=rows * seq * n
        ),
        name="attend",
    )(where, q_pre, cos_slot, sin_slot, lo, hi, k_pre, v, cos_tok, sin_tok)


def attend_back(where, q_rot, gm, mixed, lse, cos_slot, sin_slot, lo, hi, k_rot, v, cos_tok, sin_tok):
    n, tok, own = k_rot.shape
    heads, seq, rows = own // HD, n * tok, EXPERTS * CAP
    qs, ss, one = slot_spec(HD, True, n), slot_spec(HD, False, n), slot_spec(1, False, n)
    kh, ks = token_spec(n, tok, True), token_spec(n, tok, False)
    return pl.pallas_call(
        attend_back_kernel,
        grid_spec=pltpu.PrefetchScalarGridSpec(
            num_scalar_prefetch=1,
            grid=(heads, n),
            in_specs=[qs, qs, qs, qs, ss, ss, one, one, kh, kh, ks, ks],
            out_specs=[qs, kh, kh],
            scratch_shapes=[
                pltpu.VMEM((seq, HD), BF16),
                pltpu.VMEM((seq, HD), BF16),
                pltpu.VMEM((seq, HD), F32),
                pltpu.VMEM((seq, HD), F32),
                pltpu.VMEM((rows, HD), F32),
            ],
        ),
        out_shape=[
            jax.ShapeDtypeStruct((EXPERTS, n, CAP, own), BF16),
            jax.ShapeDtypeStruct((n, tok, own), BF16),
            jax.ShapeDtypeStruct((n, tok, own), BF16),
        ],
        compiler_params=pltpu.CompilerParams(vmem_limit_bytes=48 << 20),
        cost_estimate=pl.CostEstimate(
            flops=7 * rows * seq * own * n, bytes_accessed=16 << 20, transcendentals=rows * seq * n
        ),
        name="attend_back",
    )(where, q_rot, gm, mixed, lse, cos_slot, sin_slot, lo, hi, k_rot, v, cos_tok, sin_tok)


def members(routes):
    names = jnp.arange(EXPERTS, dtype=jnp.int32)[None, :, None]
    member = (routes[:, :1] == names) | (routes[:, 1:] == names)
    tok = routes.shape[-1]
    before = (jnp.arange(tok)[:, None] < jnp.arange(tok)[None, :]).astype(BF16)
    rank = ein("met,tu->meu", member.astype(BF16), before).astype(jnp.int32)
    slots = jnp.arange(CAP, dtype=jnp.int32)[None, None, :, None]
    chosen = member[:, :, None, :] & (rank[:, :, None, :] == slots)
    return member, chosen


def shares_of(normed, router, member):
    logits = ein("mtd,de->met", normed, router)
    return jax.nn.softmax(jnp.where(member, logits, -jnp.inf), axis=1)


def pick_slots(chosen, values):
    return jnp.sum(jnp.where(chosen, values[:, :, None, :], 0), axis=-1).transpose(1, 0, 2)


def dispatch(chosen, tokens):
    slots = jnp.einsum("mect,mtd->emcd", chosen.astype(BF16), tokens, preferred_element_type=BF16)
    return slots.reshape(EXPERTS, -1, tokens.shape[-1])


def combine(chosen, slots, n):
    slots = slots.reshape(EXPERTS, n, CAP, -1)
    return ein("mect,emcd->mtd", chosen.astype(BF16), slots)


def route_back(share, grad_share, router):
    grad = share * (grad_share - jnp.sum(share * grad_share, axis=0, keepdims=True))
    return jnp.einsum(
        "et,de->td", grad, router.astype(F32), precision=lax.Precision.HIGHEST
    )


def live_rank(rank, select):
    e, k, s = rank.shape
    return jnp.sum(rank.reshape(e, k // RANK, RANK, s) * select[:, :, None, :], axis=1)


def spread(live, select):
    e, k, s = live.shape
    return (live[:, None] * select[:, :, None, :]).reshape(e, -1, s)


def local(
    n,
    reps,
    layer_input_state,
    cotangent,
    norm_gain_vectors,
    attention_router_weight,
    feed_router_weight,
    attention_query_weight,
    key_value_weight,
    attention_output_weight,
    feed_expert_weight,
    attention_adapters,
    feed_adapter_width,
    feed_adapter_hidden,
    token_document,
    document_adapter,
    attention_expert_pairs,
    feed_expert_pairs,
):
    tok, wide = layer_input_state.shape
    own = wide // n
    columns = attention_adapters.shape[3]
    me = lax.axis_index("shard")
    order = jnp.array(masks_of(n), jnp.int32) ^ me
    where = position(me, n)
    segments = token_document[0]
    seq = segments.shape[0]
    docs = document_adapter[0]
    doc_count = docs.shape[0]

    routes = jnp.concatenate([attention_expert_pairs.T, feed_expert_pairs.T])
    routes = gather_small(routes, n)
    x = layer_input_state.astype(F32)
    gain_one = norm_gain_vectors[0].astype(F32)
    gain_two = norm_gain_vectors[1].astype(F32)
    normed_own = rms_norm(gain_one, x).astype(BF16)
    normed = gather_blocks(normed_own, n)
    w_kv = reshard(key_value_weight, me, n, 1)
    w_query = reshard(attention_query_weight, me, n, 1)

    def one_hot(which):
        at = which[:, None] * RANK + jnp.arange(RANK)[None, :]
        return (at.reshape(-1)[:, None] == jnp.arange(columns)[None, :]).astype(BF16)

    pick = one_hot(docs)
    attn_small = ein("kc,pmwc->pmkw", pick, attention_adapters).astype(BF16)
    width_small = ein("kc,pmwc->pmkw", pick, feed_adapter_width).astype(BF16)
    hidden_small = ein("kc,epcf->epkf", pick, feed_adapter_hidden).astype(BF16)

    def gather_small_maps(maps):
        whole = reorder(gather_blocks(maps, n), me, n)
        return jnp.moveaxis(whole, 0, 2).reshape(maps.shape[0], maps.shape[1], -1)

    a_in = gather_small_maps(attn_small[0, : EXPERTS + 2])
    b_out = gather_small_maps(attn_small[1, EXPERTS + 2 :])
    width_all = gather_small_maps(width_small.reshape(EXPERTS * 3, -1, own))
    width_all = width_all.reshape(EXPERTS, 3, -1, wide)
    b_in, a_out = attn_small[1, : EXPERTS + 2], attn_small[0, EXPERTS + 2 :]
    grads_out_all = gather_blocks(cotangent, n)

    begins = jnp.sum((segments[None, :] < jnp.arange(doc_count)[:, None]).astype(jnp.int32), axis=1)
    doc = segments.reshape(n, tok)[order]
    place = order[:, None] * tok + jnp.arange(tok, dtype=jnp.int32)[None, :]
    doc_table = doc[None] == jnp.arange(doc_count, dtype=jnp.int32)[:, None, None]
    begin = jnp.sum(jnp.where(doc_table, begins[:, None, None], 0), axis=0)
    freq = jnp.exp(-jnp.arange(HD // 2, dtype=F32) * (2.0 * math.log(10000.0) / HD))
    angles = (place - begin).astype(F32)[..., None] * freq
    cos, sin = jnp.cos(angles), jnp.sin(angles)
    cos_tok = jnp.concatenate([cos, cos], axis=-1)
    sin_tok = jnp.concatenate([-sin, sin], axis=-1)
    select_tok = doc_table.astype(F32).reshape(1, doc_count, seq)

    def slot_facts(chosen):
        chose = chosen[:, :, None] & doc_table.transpose(1, 0, 2)[:, None, :, None, :]
        select = jnp.any(chose, axis=-1).astype(F32)
        return select.transpose(1, 2, 0, 3).reshape(EXPERTS, doc_count, n * CAP)

    member_a, chosen_a = members(routes[:, :2])
    member_f, chosen_f = members(routes[:, 2:])
    select_a, select_f = slot_facts(chosen_a), slot_facts(chosen_f)
    lo = pick_slots(chosen_a, begin[:, None])[..., None]
    hi = pick_slots(chosen_a, place[:, None])[..., None]

    def spread_table(table):
        return jnp.einsum(
            "mect,mtd->emcd", chosen_a.astype(F32), table, precision=lax.Precision.HIGHEST
        )

    cos_slot, sin_slot = spread_table(cos_tok), spread_table(sin_tok)

    def to_rank(maps, rows, select):
        e, k, s = maps.shape[0], maps.shape[1], rows.shape[1]
        rank = ein("ekd,esd->eks", maps, rows).reshape(e, doc_count, -1, s)
        return (rank * select[:, :, None, :]).reshape(e, k, s).astype(BF16)

    share_a = shares_of(normed, attention_router_weight, member_a)
    share_a_slot = pick_slots(chosen_a, share_a).reshape(EXPERTS, -1)
    rows_a = dispatch(chosen_a, normed)
    rank_q = to_rank(a_in[:EXPERTS], rows_a, select_a)
    q_pre = ein("esd,edh->esh", rows_a, w_query) + ein("eks,ekh->esh", rank_q, b_in[:EXPERTS])
    flat = normed.reshape(1, seq, wide)
    rank_kv = to_rank(a_in[EXPERTS:], jnp.broadcast_to(flat, (2, seq, wide)), select_tok)
    kv_pre = ein("sd,pdh->psh", flat[0], w_kv) + ein("pks,pkh->psh", rank_kv, b_in[EXPERTS:])
    k_pre = kv_pre[0].reshape(n, tok, own)
    values = kv_pre[1].astype(BF16).reshape(n, tok, own)
    mixed, q_rot, k_rot, lse = attend(
        where,
        q_pre.reshape(EXPERTS, n, CAP, own),
        cos_slot,
        sin_slot,
        lo,
        hi,
        k_pre,
        values,
        cos_tok,
        sin_tok,
    )
    mixed_rows = mixed.reshape(EXPERTS, n * CAP, own)
    rank_o = to_rank(a_out, mixed_rows, select_a)
    out_rows = ein("esh,ehd->esd", mixed_rows, attention_output_weight)
    out_rows = (out_rows + ein("eks,ekd->esd", rank_o, b_out)) * share_a_slot[..., None]
    attended = x + reduce_blocks(combine(chosen_a, out_rows.astype(BF16), n).astype(BF16), n)

    normed_two = gather_blocks(rms_norm(gain_two, attended).astype(BF16), n)
    share_f = shares_of(normed_two, feed_router_weight, member_f)
    share_f_slot = pick_slots(chosen_f, share_f).reshape(EXPERTS, -1)
    rows_f = dispatch(chosen_f, normed_two)
    rows_g = dispatch(chosen_f, grads_out_all)
    rank_gate = to_rank(width_all[:, 0], rows_f, select_f)
    rank_up = to_rank(width_all[:, 1], rows_f, select_f)
    back_down = to_rank(width_all[:, 2], rows_g, select_f)
    gate = ein("esd,edf->esf", rows_f, feed_expert_weight[:, 0])
    gate = gate + ein("eks,ekf->esf", rank_gate, hidden_small[:, 0])
    up = ein("esd,edf->esf", rows_f, feed_expert_weight[:, 1])
    up = up + ein("eks,ekf->esf", rank_up, hidden_small[:, 1])
    grad_inner = ein("esd,edf->esf", rows_g, feed_expert_weight[:, 2])
    grad_inner = grad_inner + ein("eks,ekf->esf", back_down, hidden_small[:, 2])
    sig = jax.nn.sigmoid(gate)
    inner_f = gate * sig * up
    inner = inner_f.astype(BF16)
    grad_share_f = jnp.sum(inner_f * grad_inner, axis=-1)
    scaled = grad_inner * share_f_slot[..., None]
    grad_gate = (scaled * up * sig * (1.0 + gate * (1.0 - sig))).astype(BF16)
    grad_up = (scaled * gate * sig).astype(BF16)
    back_gate = to_rank(hidden_small[:, 0], grad_gate, select_f)
    back_up = to_rank(hidden_small[:, 1], grad_up, select_f)
    grad_rows_f = ein("esf,edf->esd", grad_gate, feed_expert_weight[:, 0])
    grad_rows_f = grad_rows_f + ein("esf,edf->esd", grad_up, feed_expert_weight[:, 1])
    grad_rows_f = grad_rows_f + ein("eks,ekd->esd", back_gate, width_all[:, 0])
    grad_rows_f = grad_rows_f + ein("eks,ekd->esd", back_up, width_all[:, 1])
    grad_two_own = reduce_blocks(combine(chosen_f, grad_rows_f.astype(BF16), n).astype(BF16), n)
    rank_down = to_rank(hidden_small[:, 2], inner, select_f)
    ffn_rows = ein("esf,edf->esd", inner, feed_expert_weight[:, 2])
    ffn_rows = (ffn_rows + ein("eks,ekd->esd", rank_down, width_all[:, 2])) * share_f_slot[..., None]
    layer_out = attended + reduce_blocks(combine(chosen_f, ffn_rows.astype(BF16), n).astype(BF16), n)

    def own_tokens(chosen, slot_values):
        first = slot_values.reshape(EXPERTS, n, CAP)[:, 0]
        return jnp.sum(jnp.where(chosen[0], first[:, :, None], 0.0), axis=1)

    grad_share_f = sum_small(grad_share_f, n)
    grads_out = cotangent.astype(F32)
    grad_two_own = grad_two_own + route_back(
        share_f[0], own_tokens(chosen_f, grad_share_f), feed_router_weight
    )
    grad_attended = grads_out + rms_back(attended, gain_two, grad_two_own)

    grads_two = gather_blocks(grad_attended.astype(BF16), n)
    rows_ga = dispatch(chosen_a, grads_two)
    back_out = to_rank(b_out, rows_ga, select_a)
    grad_mixed = ein("esd,ehd->esh", rows_ga, attention_output_weight)
    grad_mixed = grad_mixed + ein("eks,ekh->esh", back_out, a_out)
    grad_share_a = sum_small(jnp.sum(mixed_rows.astype(F32) * grad_mixed, axis=-1), n)
    grad_mixed = (grad_mixed * share_a_slot[..., None]).astype(BF16)
    gq, gk, gv = attend_back(
        where,
        q_rot,
        grad_mixed.reshape(EXPERTS, n, CAP, own),
        mixed,
        lse,
        cos_slot,
        sin_slot,
        lo,
        hi,
        k_rot,
        values,
        cos_tok,
        sin_tok,
    )
    gq = gq.reshape(EXPERTS, n * CAP, own)
    gkv = jnp.stack([gk, gv]).reshape(2, seq, own)
    back_q = to_rank(b_in[:EXPERTS], gq, select_a)
    back_kv = to_rank(b_in[EXPERTS:], gkv, select_tok)
    grad_rows_a = ein("esh,edh->esd", gq, w_query) + ein("eks,ekd->esd", back_q, a_in[:EXPERTS])
    grad_normed = combine(chosen_a, grad_rows_a.astype(BF16), n).reshape(seq, wide)
    grad_normed = grad_normed + ein("sh,dh->sd", gkv[0], w_kv[0]) + ein("sh,dh->sd", gkv[1], w_kv[1])
    grad_normed = grad_normed + ein("pks,pkd->sd", back_kv, a_in[EXPERTS:])
    grad_normed = reduce_blocks(grad_normed.astype(BF16).reshape(n, tok, wide), n)
    grad_normed = grad_normed + route_back(
        share_a[0], own_tokens(chosen_a, grad_share_a), attention_router_weight
    )
    grad_in = grad_attended + rms_back(x, gain_one, grad_normed)

    def whole_rank(rank, select):
        live = live_rank(rank.astype(F32), select)
        return spread(sum_small(live.astype(BF16), n).astype(F32), select)

    def mine(rows):
        return lax.dynamic_slice_in_dim(rows, me * own, own, rows.ndim - 1)

    def grads(spec, rank, rows):
        return ein(spec, rank.astype(BF16), rows).astype(BF16)

    eks = "eks,esw->ekw"
    share_a_row, share_f_row = share_a_slot[:, None, :], share_f_slot[:, None, :]
    whole = [whole_rank(r, select_f) for r in (back_gate, back_up, rank_down)]
    rows_f_own, rows_g_own = mine(rows_f), mine(rows_g)
    width_grad = jnp.stack(
        [
            grads(eks, whole[0], rows_f_own),
            grads(eks, whole[1], rows_f_own),
            grads(eks, whole[2] * share_f_row, rows_g_own),
        ],
        axis=1,
    )
    hidden_grad = jnp.stack(
        [
            grads(eks, rank_gate, grad_gate),
            grads(eks, rank_up, grad_up),
            grads(eks, back_down * share_f_row, inner),
        ],
        axis=1,
    )
    whole_q = whole_rank(back_q, select_a)
    whole_kv = whole_rank(back_kv, select_tok)
    whole_o = whole_rank(rank_o, select_a)
    own_flat = mine(flat[0])
    attn_grad = jnp.stack(
        [
            jnp.concatenate(
                [
                    grads(eks, whole_q, mine(rows_a)),
                    grads("pks,sw->pkw", whole_kv, own_flat),
                    grads(eks, back_out * share_a_row, mixed_rows),
                ]
            ),
            jnp.concatenate(
                [
                    grads(eks, rank_q, gq),
                    grads(eks, rank_kv, gkv),
                    grads(eks, whole_o * share_a_row, mine(rows_ga)),
                ]
            ),
        ]
    )
    picks = lax.all_gather(document_adapter, "rep", axis=0, tiled=True)
    picks = jax.vmap(one_hot)(picks)

    def all_streams(g):
        return lax.all_gather(g, "rep", axis=0)

    attn_out = ein("rpmkw,rkc->pmwc", all_streams(attn_grad), picks)
    width_out = ein("rpmkw,rkc->pmwc", all_streams(width_grad), picks)
    hidden_out = ein("rpmkw,rkc->pmcw", all_streams(hidden_grad), picks)
    return (layer_out, grad_in, attn_out, width_out, hidden_out)


def solution(mesh):
    in_specs = (
        P(("rep", "shard"), None),
        P(("rep", "shard"), None),
        P(),
        P(),
        P(),
        P(None, "shard", None),
        P(None, "shard", None),
        P(None, "shard", None),
        P(None, None, None, "shard"),
        P(None, None, "shard", None),
        P(None, None, "shard", None),
        P(None, None, None, "shard"),
        P("rep", None),
        P("rep", None),
        P(("rep", "shard"), None),
        P(("rep", "shard"), None),
    )
    out_specs = (
        P(("rep", "shard"), None),
        P(("rep", "shard"), None),
        P(None, None, "shard", None),
        P(None, None, "shard", None),
        P(None, None, None, "shard"),
    )
    body = partial(local, mesh.shape["shard"], mesh.shape["rep"])
    return jax.shard_map(body, mesh=mesh, in_specs=in_specs, out_specs=out_specs, check_vma=False)
```

time: 3460 us -> 1080 us (0.31)
  waiting for transfers between devices: 2380 us -> 195 us
  matrix products: 627 us -> 398 us
  starting transfers between devices: 2.05 us -> 117 us
  local copies, waits for them, and re-layouts: 303 us -> 190 us
  Pallas kernels: 0 us -> 67.2 us
  other arithmetic: 119 us -> 61 us
    all_gather x15 -> x3, waiting for transfers between devices: 1500 us -> 8.63 us  [all_streams(): return lax.all_gather(g, 'rep', axis=0)]
    unnamed x22 -> x3, waiting for transfers between devices: 390 us -> 0.05 us
    psum x1 -> x0, waiting for transfers between devices: 249 us -> none  [local(): lax.psum((grad_attn_own, grad_d_own, gradient_upper_local), 'rep')]
    reduce_scatter x4 -> x0, waiting for transfers between devices: 244 us -> none  [the longest x1 139 us: local(): lax.psum_scatter(attention_adapter_gradient, 'shard', scatter_dimension=2...]
    dot_general x135 -> x69, matrix products: 627 us -> 391 us  [the longest x61 354 us: ein(): return jnp.einsum(spec, a, b, preferred_element_type=F32)]
    ppermute x0 -> x131, waiting for transfers between devices: none -> 186 us  [swap(): return lax.ppermute(x, 'shard', [(i, i ^ d) for i in range(n)])]
    ppermute x0 -> x131, starting transfers between devices: none -> 117 us  [swap(): return lax.ppermute(x, 'shard', [(i, i ^ d) for i in range(n)])]
    scatter x6 -> x0, local copies, waits for them, and re-layouts: 68.7 us -> none  [the longest x4 45.8 us: dispatch(): jnp.zeros((expert_count, capacity), jnp.int32).at[flat_routes, place]]
  transfers between devices with their start and end apart: 21 -> 134, of which waited for: 18 -> 53; matrix products, arithmetic and copies ran while one was open for 21% -> 44% of each run, Pallas kernels for 0% -> 6%
where the time goes in v1:
time: 1080 us; the launch traced here: 1070 us
  matrix products  398 us (37%)
  waiting for transfers between devices  195 us (18%)
  local copies, waits for them, and re-layouts  190 us (18%)
  starting transfers between devices  117 us (11%)
  Pallas kernels  67.2 us (6%)
  other arithmetic  61 us (6%)
  between operations  32.6 us (3%)
  blocking collectives  11.8 us (1%)
    dot_general x61, matrix products, ein(): return jnp.einsum(spec, a, b, preferred_element_type=F32)  354 us
    ppermute x131, waiting for transfers between devices, swap(): return lax.ppermute(x, 'shard', [(i, i ^ d) for i in range(n)])  186 us
    ppermute x131, starting transfers between devices, swap(): return lax.ppermute(x, 'shard', [(i, i ^ d) for i in range(n)])  117 us
    unnamed x431, local copies, waits for them, and re-layouts  76 us
    transpose x4, local copies, waits for them, and re-layouts, dispatch(): jnp.einsum('mect,mtd->emcd', chosen.astype(BF16), tokens, preferred_eleme...  40.6 us
    pallas_call x1, Pallas kernels, attend_back(): pl.pallas_call(attend_back_kernel, grid_spec=pltpu.PrefetchScalarGridSpec...  36 us
    pallas_call x1, Pallas kernels, attend(): pl.pallas_call(attend_kernel, grid_spec=pltpu.PrefetchScalarGridSpec(num_...  31.1 us
    dot_general x4, matrix products, dispatch(): jnp.einsum('mect,mtd->emcd', chosen.astype(BF16), tokens, preferred_eleme...  29.6 us
  transfers between devices with their start and end apart: 134, of which 53 were waited for; matrix products, arithmetic and copies ran while one was open for 44% of the time, Pallas kernels for 6%

profile of v1, /device:TPU:0, one launch (start us, length us, event | category | flops | bytes accessed | tf_op | source)
XLA Modules:
  0.0 1072.1 jit_solution(6660549096230687689)
XLA Ops:
  33.2 11.8 %all-gather.3 = s32[4,1,3]{2,1,0:T(1,128)S(1)} all-gather(s32[1,1,3]{2,1,0:T(1,128)S(1)} %bitcast.784), channel_id=1, replica_groups=mesh['rep'=4,'shard'=8] {'rep'}, dimensions={0}, use_global_device_ids=true | all-gather | bytes 60 | tf_op jit(solution)/shard_map/all_gather | solution.py:627
  197.1 7.6 collective-permute-done.36
  257.6 20.0 %collective-permute-done.14 = bf16[4,256,256]{2,1,0:T(8,128)(2,1)S(1)} collective-permute-done((bf16[4,256,256]{2,1,0:T(8,128)(2,1)S(1)}, bf16[4,256,256]{2,1,0:T(8,128)(2,1)S(1)}, u32[]{:S(2)}, u32[]{:S(2)}) %collective-permute-start.14) | collective-permute-done | bytes 524320 | tf_op jit(solution)/shard_map/ppermute | solution.py:40
  279.9 11.9 %collective-permute-done.17 = bf16[4,256,256]{2,1,0:T(8,128)(2,1)S(1)} collective-permute-done((bf16[4,256,256]{2,1,0:T(8,128)(2,1)S(1)}, bf16[4,256,256]{2,1,0:T(8,128)(2,1)S(1)}, u32[]{:S(2)}, u32[]{:S(2)}) %collective-permute-start.17) | collective-permute-done | bytes 524320 | tf_op jit(solution)/shard_map/ppermute | solution.py:40
  291.9 10.9 %collective-permute-start.82 = (bf16[64,2048]{1,0:T(8,128)(2,1)S(1)}, bf16[64,2048]{1,0:T(8,128)(2,1)S(1)}, u32[]{:S(2)}, u32[]{:S(2)}) collective-permute-start(bf16[64,2048]{1,0:T(8,128)(2,1)S(1)} %copy-done.105), channel_id=1, source_target_pairs={{0,4},{1,5},{2,6},{3,7},{4,0},{5,1},{6,2},{7,3},{8,12},{9,13},{10,... | collective-permute-start | bytes 786440 | tf_op jit(solution)/shard_map/ppermute | solution.py:40
  303.9 7.5 collective-permute-done.81
  342.0 7.9 convolution_bitcast_fusion.3
  355.7 10.2 copy.249
  380.5 31.1 %attend.1 = (bf16[4,8,80,256]{3,2,1,0:T(8,128)(2,1)S(1)}, bf16[4,8,80,256]{3,2,1,0:T(8,128)(2,1)S(1)}, bf16[8,128,256]{2,1,0:T(8,128)(2,1)S(1)}, f32[4,8,80,256]{3,2,1,0:T(8,128)}) custom-call(s32[8]{0:T(128)S(1)} %get-tuple-element.159.where, f32[4,8,80,256]{3,2,1,0:T(8,128)} %bitcast.722, f32[4,8,80,128]{3,2,1,0:T(8,128)} %convolution_bitcast_fusion.6.cs, ...), custom_call_target="tpu_custom_call" | custom-call | flops 2013265920 | bytes 16777216 | tf_op jit(solution)/shard_map/attend/pallas_call | solution.py:261
  413.2 8.5 fusion.272
  421.8 12.0 %multiply_convert_fusion.1 = bf16[4,640,2048]{2,1,0:T(8,128)(2,1)} fusion(f32[4,640,2048]{2,1,0:T(8,128)} %fusion.272, f32[4,640]{1,0:T(4,128)S(1)} %mul.560, bf16[4,48,640]{2,1,0:T(8,128)(2,1)S(1)} %fusion.72, bf16[4,48,2048]{2,1,0:T(8,128)(2,1)S(1)} %bitcast.727), kind=kOutput, calls=%fused_computation.6 | convolution fusion | flops 519045120 | bytes 32499712 | tf_op jit(solution)/shard_map/eks,ekd->esd/dot_general | solution.py:23
  464.6 8.4 collective-permute-done.48
  476.3 8.1 convolution_bitcast_fusion.1
  484.4 10.1 copy.282
  494.5 7.6 fusion.79
  542.9 10.1 copy.270
  553.0 7.6 fusion.77
  573.3 16.7 %fusion.8 = f32[4,640,704]{1,2,0:T(8,128)} fusion(bf16[4,640,2048]{2,1,0:T(8,128)(2,1)} %bitcast.703, bf16[4,3,2048,704]{2,3,1,0:T(8,128)(2,1)} %param.25), kind=kOutput, calls=%fused_computation.13 | convolution fusion | flops 7381975040 | bytes 29229056 | tf_op jit(solution)/shard_map/esd,edf->esf/dot_general | solution.py:23
  590.0 16.6 %fusion.45 = f32[4,640,704]{1,2,0:T(8,128)} fusion(f32[4,640,704]{1,2,0:T(8,128)} %fusion.185, bf16[4,640,2048]{2,1,0:T(8,128)(2,1)} %bitcast.704, bf16[4,3,2048,704]{2,3,1,0:T(8,128)(2,1)} %param.25), kind=kOutput, calls=%fused_computation.63 | convolution fusion | flops 7383777280 | bytes 36438016 | tf_op jit(solution)/shard_map/esd,edf->esf/dot_general | solution.py:23
  610.7 24.1 %multiply_reduce_fusion = (f32[4,640]{1,0:T(4,128)S(1)}, bf16[4,640,704]{1,2,0:T(8,128)(2,1)}, bf16[4,640,704]{1,2,0:T(8,128)(2,1)}, bf16[4,640,704]{1,2,0:T(8,128)(2,1)}) fusion(f32[4,640,704]{1,2,0:T(8,128)} %fusion.8, f32[4,640,704]{1,2,0:T(8,128)} %fusion.186, f32[4,640,704]{1,2,0:T(8,128)} %fusion.45, f32[4,640]{1,0:T(4,128)S(1)} %mul.579, ...), kind=kOutput, calls=%fused_computation.40 | convolution fusion | flops 7419819520 | bytes 61689856 | tf_op jit(solution)/shard_map/esd,edf->esf/dot_general | solution.py:23
  643.0 16.7 %fusion.6 = f32[4,640,2048]{2,1,0:T(8,128)} fusion(bf16[4,640,704]{1,2,0:T(8,128)(2,1)} %get-tuple-element.53, bf16[4,3,2048,704]{2,3,1,0:T(8,128)(2,1)} %param.25), kind=kOutput, calls=%fused_computation.11 | convolution fusion | flops 7381975040 | bytes 36110336 | tf_op jit(solution)/shard_map/esf,edf->esd/dot_general | solution.py:23
  659.7 16.2 %fusion.10 = f32[4,640,2048]{2,1,0:T(8,128)} fusion(bf16[4,640,704]{1,2,0:T(8,128)(2,1)} %get-tuple-element.52, bf16[4,3,2048,704]{2,3,1,0:T(8,128)(2,1)} %param.25), kind=kOutput, calls=%fused_computation.15 | convolution fusion | flops 7381975040 | bytes 36110336 | tf_op jit(solution)/shard_map/esf,edf->esd/dot_general | solution.py:23
  675.9 16.5 %fusion.4 = f32[4,640,2048]{2,1,0:T(8,128)} fusion(bf16[4,3,2048,704]{2,3,1,0:T(8,128)(2,1)} %param.25, bf16[4,640,704]{1,2,0:T(8,128)(2,1)} %get-tuple-element.47), kind=kOutput, calls=%fused_computation.9 | convolution fusion | flops 7381975040 | bytes 36110336 | tf_op jit(solution)/shard_map/esf,edf->esd/dot_general | solution.py:23
  692.7 11.0 %fusion.134 = f32[4,640,2048]{2,1,0:T(8,128)} fusion(bf16[4,48,640]{2,1,0:T(8,128)(2,1)S(1)} %fusion.80, bf16[4,3,48,2048]{3,2,1,0:T(8,128)(2,1)} %reshape_reshape.9), kind=kOutput, calls=%fused_computation.190 | convolution fusion | flops 503316480 | bytes 22003712 | tf_op jit(solution)/shard_map/eks,ekd->esd/dot_general | solution.py:23
  705.4 12.2 %multiply_convert_fusion = bf16[4,640,2048]{2,1,0:T(8,128)(2,1)} fusion(f32[4,640,2048]{2,1,0:T(8,128)} %fusion.4, f32[4,640]{1,0:T(4,128)S(1)} %mul.579, bf16[4,48,640]{2,1,0:T(8,128)(2,1)S(1)} %fusion.78, bf16[4,3,48,2048]{3,2,1,0:T(8,128)(2,1)} %reshape_reshape.9), kind=kOutput, calls=%fused_computation.5 | convolution fusion | flops 519045120 | bytes 32499712 | tf_op jit(solution)/shard_map/eks,ekd->esd/dot_general | solution.py:23
  728.6 24.9 %add_convert_fusion.1 = bf16[4,640,2048]{2,1,0:T(8,128)(2,1)} fusion(f32[4,640,2048]{2,1,0:T(8,128)} %fusion.134, f32[4,640,2048]{2,1,0:T(8,128)} %fusion.10, f32[4,640,2048]{2,1,0:T(8,128)} %fusion.6, bf16[4,48,640]{2,1,0:T(8,128)(2,1)S(1)} %fusion.81, bf16[4,3,48,2048]{3,2,1,0:T(8,128)(2,1)} %reshape_reshape.9), kind=kOutput, calls=%fused_computation.4 | convolution fusion | flops 524288000 | bytes 74432512 | tf_op jit(solution)/shard_map/eks,ekd->esd/dot_general | solution.py:23
  867.5 8.0 convolution_bitcast_fusion
  875.5 10.2 copy.284
  904.8 36.0 %attend_back.1 = (bf16[4,8,80,256]{3,2,1,0:T(8,128)(2,1)S(1)}, bf16[8,128,256]{2,1,0:T(8,128)(2,1)S(1)}, bf16[8,128,256]{2,1,0:T(8,128)(2,1)S(1)}) custom-call(s32[8]{0:T(128)S(1)} %copy-done.9, bf16[4,8,80,256]{3,2,1,0:T(8,128)(2,1)S(1)} %copy-done.11, bf16[4,8,80,256]{3,2,1,0:T(8,128)(2,1)} %bitcast.752, bf16[4,8,80,256]{3,2,1,0:T(8,128)(2,1)} %copy-done.2, ...), custom_call_target="tpu_custom_call" | custom-call | flops 4697620480 | bytes 16777216 | tf_op jit(solution)/shard_map/attend_back/pallas_call | solution.py:296
  942.4 8.8 fusion.274
  957.0 11.8 %add_convert_fusion = bf16[4,640,2048]{2,1,0:T(8,128)(2,1)} fusion(f32[4,640,2048]{2,1,0:T(8,128)} %fusion.274, bf16[4,48,640]{2,1,0:T(8,128)(2,1)S(1)} %fusion.73, bf16[4,48,2048]{2,1,0:T(8,128)(2,1)S(1)} %bitcast.730), kind=kOutput, calls=%fused_computation.3 | convolution fusion | flops 513802240 | bytes 32489472 | tf_op jit(solution)/shard_map/eks,ekd->esd/dot_general | solution.py:23
  1052.4 8.6 all-gather.8.cloned.1.call-done
  (972 shorter events, 610.0 us)
Async XLA Ops:
  7.2 1019.7 %all-gather.10.cloned.1.call-start = ((), (), s32[]{:S(2)}) async-start(), calls=%async_computation.1 | async-start | bytes 1474560 | tf_op jit(solution)/shard_map/all_gather | solution.py:631
  10.6 127.0 %collective-permute-start.64 = (bf16[6,48,256]{2,1,0:T(8,128)(2,1)}, bf16[6,48,256]{2,1,0:T(8,128)(2,1)}, u32[]{:S(2)}, u32[]{:S(2)}) collective-permute-start(bf16[6,48,256]{2,1,0:T(8,128)(2,1)} %bitcast.125), channel_id=1, source_target_pairs={{0,4},{1,5},{2,6},{3,7},{4,0},{5,1},{6,2},{7,3},{8,12},{9,13},{10,... | collective-permute-start | bytes 442376 | tf_op jit(solution)/shard_map/ppermute | solution.py:40
  13.5 119.3 %collective-permute-start.62 = (bf16[6,48,256]{2,1,0:T(8,128)(2,1)}, bf16[6,48,256]{2,1,0:T(8,128)(2,1)}, u32[]{:S(2)}, u32[]{:S(2)}) collective-permute-start(bf16[6,48,256]{2,1,0:T(8,128)(2,1)} %bitcast.125), channel_id=1, source_target_pairs={{0,2},{1,3},{2,0},{3,1},{4,6},{5,7},{6,4},{7,5},{8,10},{9,11},{10,... | collective-permute-start | bytes 442376 | tf_op jit(solution)/shard_map/ppermute | solution.py:40
  15.0 124.2 %collective-permute-start.65 = (bf16[6,48,256]{2,1,0:T(8,128)(2,1)}, bf16[6,48,256]{2,1,0:T(8,128)(2,1)}, u32[]{:S(2)}, u32[]{:S(2)}) collective-permute-start(bf16[6,48,256]{2,1,0:T(8,128)(2,1)} %bitcast.126), channel_id=1, source_target_pairs={{0,4},{1,5},{2,6},{3,7},{4,0},{5,1},{6,2},{7,3},{8,12},{9,13},{10,... | collective-permute-start | bytes 442376 | tf_op jit(solution)/shard_map/ppermute | solution.py:40
  15.5 119.7 %collective-permute-start.63 = (bf16[6,48,256]{2,1,0:T(8,128)(2,1)}, bf16[6,48,256]{2,1,0:T(8,128)(2,1)}, u32[]{:S(2)}, u32[]{:S(2)}) collective-permute-start(bf16[6,48,256]{2,1,0:T(8,128)(2,1)} %bitcast.126), channel_id=1, source_target_pairs={{0,2},{1,3},{2,0},{3,1},{4,6},{5,7},{6,4},{7,5},{8,10},{9,11},{10,... | collective-permute-start | bytes 442376 | tf_op jit(solution)/shard_map/ppermute | solution.py:40
  16.3 40.1 %collective-permute-start = (s32[1,4,128]{2,1,0:T(4,128)S(1)}, s32[1,4,128]{2,1,0:T(4,128)S(1)}, u32[]{:S(2)}, u32[]{:S(2)}) collective-permute-start(s32[1,4,128]{2,1,0:T(4,128)S(1)} %add_bitcast_fusion), channel_id=1, source_target_pairs={{0,1},{1,0},{2,3},{3,2},{4,5},{5,4},{6,7},{7,6},{8,9},{9,8},{10,11... | collective-permute-start | bytes 6152 | tf_op jit(solution)/shard_map/ppermute | solution.py:40
  130.7 76.9 %collective-permute-start.80 = (bf16[64,2048]{1,0:T(8,128)(2,1)}, bf16[64,2048]{1,0:T(8,128)(2,1)S(1)}, u32[]{:S(2)}, u32[]{:S(2)}) collective-permute-start(bf16[64,2048]{1,0:T(8,128)(2,1)} %get-tuple-element.114), channel_id=1, source_target_pairs={{0,4},{1,5},{2,6},{3,7},{4,0},{5,1},{6,2},{7,3},{8,12},{9,13},{10,... | collective-permute-start | bytes 786440 | tf_op jit(solution)/shard_map/ppermute | solution.py:40
  132.9 37.8 %collective-permute-start.78 = (bf16[64,2048]{1,0:T(8,128)(2,1)}, bf16[64,2048]{1,0:T(8,128)(2,1)S(1)}, u32[]{:S(2)}, u32[]{:S(2)}) collective-permute-start(bf16[64,2048]{1,0:T(8,128)(2,1)} %get-tuple-element.114), channel_id=1, source_target_pairs={{0,2},{1,3},{2,0},{3,1},{4,6},{5,7},{6,4},{7,5},{8,10},{9,11},{10,... | collective-permute-start | bytes 786440 | tf_op jit(solution)/shard_map/ppermute | solution.py:40
  135.3 70.5 %collective-permute-start.79 = (bf16[64,2048]{1,0:T(8,128)(2,1)}, bf16[64,2048]{1,0:T(8,128)(2,1)S(1)}, u32[]{:S(2)}, u32[]{:S(2)}) collective-permute-start(bf16[64,2048]{1,0:T(8,128)(2,1)} %get-tuple-element.115), channel_id=1, source_target_pairs={{0,4},{1,5},{2,6},{3,7},{4,0},{5,1},{6,2},{7,3},{8,12},{9,13},{10,... | collective-permute-start | bytes 786440 | tf_op jit(solution)/shard_map/ppermute | solution.py:40
  137.6 31.8 %collective-permute-start.77 = (bf16[64,2048]{1,0:T(8,128)(2,1)}, bf16[64,2048]{1,0:T(8,128)(2,1)S(1)}, u32[]{:S(2)}, u32[]{:S(2)}) collective-permute-start(bf16[64,2048]{1,0:T(8,128)(2,1)} %get-tuple-element.115), channel_id=1, source_target_pairs={{0,2},{1,3},{2,0},{3,1},{4,6},{5,7},{6,4},{7,5},{8,10},{9,11},{10,... | collective-permute-start | bytes 786440 | tf_op jit(solution)/shard_map/ppermute | solution.py:40
  168.4 273.3 %collective-permute-start.83 = (bf16[128,2048]{1,0:T(8,128)(2,1)}, bf16[128,2048]{1,0:T(8,128)(2,1)}, u32[]{:S(2)}, u32[]{:S(2)}) collective-permute-start(bf16[128,2048]{1,0:T(8,128)(2,1)} %param.18), channel_id=1, source_target_pairs={{0,1},{1,0},{2,3},{3,2},{4,5},{5,4},{6,7},{7,6},{8,9},{9,8},{10,11... | collective-permute-start | bytes 1572872 | tf_op jit(solution)/shard_map/ppermute | solution.py:40
  218.8 104.6 %collective-permute-start.9 = (bf16[128,2048]{1,0:T(8,128)(2,1)}, bf16[128,2048]{1,0:T(8,128)(2,1)}, u32[]{:S(2)}, u32[]{:S(2)}) collective-permute-start(bf16[128,2048]{1,0:T(8,128)(2,1)} %get-tuple-element.51), channel_id=1, source_target_pairs={{0,1},{1,0},{2,3},{3,2},{4,5},{5,4},{6,7},{7,6},{8,9},{9,8},{10,11... | collective-permute-start | bytes 1572872 | tf_op jit(solution)/shard_map/ppermute | solution.py:40
  218.8 30.4 %collective-permute-start.68 = (bf16[12,48,256]{2,1,0:T(8,128)(2,1)S(1)}, bf16[12,48,256]{2,1,0:T(8,128)(2,1)}, u32[]{:S(2)}, u32[]{:S(2)}) collective-permute-start(bf16[12,48,256]{2,1,0:T(8,128)(2,1)S(1)} %bitcast.740), channel_id=1, source_target_pairs={{0,1},{1,0},{2,3},{3,2},{4,5},{5,4},{6,7},{7,6},{8,9},{9,8},{10,11... | collective-permute-start | bytes 884744 | tf_op jit(solution)/shard_map/ppermute | solution.py:40
  291.8 169.1 %collective-permute-start.85 = (bf16[128,2048]{1,0:T(8,128)(2,1)}, bf16[128,2048]{1,0:T(8,128)(2,1)}, u32[]{:S(2)}, u32[]{:S(2)}) collective-permute-start(bf16[128,2048]{1,0:T(8,128)(2,1)} %constant_dynamic-update-slice_fusion.104), channel_id=1, source_target_pairs={{0,1},{1,0},{2,3},{3,2},{4,5},{5,4},{6,7},{7,6},{8,9},{9,8},{10,11... | collective-permute-start | bytes 1572872 | tf_op jit(solution)/shard_map/ppermute | solution.py:40
  321.8 132.1 %collective-permute-start.84 = (bf16[128,2048]{1,0:T(8,128)(2,1)}, bf16[128,2048]{1,0:T(8,128)(2,1)}, u32[]{:S(2)}, u32[]{:S(2)}) collective-permute-start(bf16[128,2048]{1,0:T(8,128)(2,1)} %constant_dynamic-update-slice_fusion.102), channel_id=1, source_target_pairs={{0,1},{1,0},{2,3},{3,2},{4,5},{5,4},{6,7},{7,6},{8,9},{9,8},{10,11... | collective-permute-start | bytes 1572872 | tf_op jit(solution)/shard_map/ppermute | solution.py:40
  328.8 116.1 %collective-permute-start.71 = (bf16[12,48,256]{2,1,0:T(8,128)(2,1)}, bf16[12,48,256]{2,1,0:T(8,128)(2,1)}, u32[]{:S(2)}, u32[]{:S(2)}) collective-permute-start(bf16[12,48,256]{2,1,0:T(8,128)(2,1)} %constant_dynamic-update-slice_fusion.84), channel_id=1, source_target_pairs={{0,1},{1,0},{2,3},{3,2},{4,5},{5,4},{6,7},{7,6},{8,9},{9,8},{10,11... | collective-permute-start | bytes 884744 | tf_op jit(solution)/shard_map/ppermute | solution.py:40
  329.7 133.1 %collective-permute-start.86 = (bf16[128,2048]{1,0:T(8,128)(2,1)}, bf16[128,2048]{1,0:T(8,128)(2,1)}, u32[]{:S(2)}, u32[]{:S(2)}) collective-permute-start(bf16[128,2048]{1,0:T(8,128)(2,1)} %constant_dynamic-update-slice_fusion.106), channel_id=1, source_target_pairs={{0,1},{1,0},{2,3},{3,2},{4,5},{5,4},{6,7},{7,6},{8,9},{9,8},{10,11... | collective-permute-start | bytes 1572872 | tf_op jit(solution)/shard_map/ppermute | solution.py:40
  474.6 27.6 %collective-permute-start.49 = (bf16[64,2048]{1,0:T(8,128)(2,1)}, bf16[64,2048]{1,0:T(8,128)(2,1)S(1)}, u32[]{:S(2)}, u32[]{:S(2)}) collective-permute-start(bf16[64,2048]{1,0:T(8,128)(2,1)} %get-tuple-element.78), channel_id=1, source_target_pairs={{0,4},{1,5},{2,6},{3,7},{4,0},{5,1},{6,2},{7,3},{8,12},{9,13},{10,... | collective-permute-start | bytes 786440 | tf_op jit(solution)/shard_map/ppermute | solution.py:40
  475.6 27.3 %collective-permute-start.51 = (bf16[64,2048]{1,0:T(8,128)(2,1)S(1)}, bf16[64,2048]{1,0:T(8,128)(2,1)}, u32[]{:S(2)}, u32[]{:S(2)}) collective-permute-start(bf16[64,2048]{1,0:T(8,128)(2,1)S(1)} %get-tuple-element.79), channel_id=1, source_target_pairs={{0,2},{1,3},{2,0},{3,1},{4,6},{5,7},{6,4},{7,5},{8,10},{9,11},{10,... | collective-permute-start | bytes 786440 | tf_op jit(solution)/shard_map/ppermute | solution.py:40
  692.5 35.1 %collective-permute-start.92 = (f32[4,2,2,2,80]{4,3,2,1,0:T(2,128)S(1)}, f32[4,2,2,2,80]{4,3,2,1,0:T(2,128)S(1)}, u32[]{:S(2)}, u32[]{:S(2)}) collective-permute-start(f32[4,2,2,2,80]{4,3,2,1,0:T(2,128)S(1)} %reshape.472), channel_id=1, source_target_pairs={{0,1},{1,0},{2,3},{3,2},{4,5},{5,4},{6,7},{7,6},{8,9},{9,8},{10,11... | collective-permute-start | bytes 30728 | tf_op jit(solution)/shard_map/ppermute | solution.py:40
  704.4 60.7 %collective-permute-start.128 = (bf16[4,16,2,2,2,80]{5,4,3,2,1,0:T(2,128)(2,1)S(1)}, bf16[4,16,2,2,2,80]{5,4,3,2,1,0:T(2,128)(2,1)S(1)}, u32[]{:S(2)}, u32[]{:S(2)}) collective-permute-start(bf16[4,16,2,2,2,80]{5,4,3,2,1,0:T(2,128)(2,1)S(1)} %convert_element_type.605), channel_id=1, source_target_pairs={{0,1},{1,0},{2,3},{3,2},{4,5},{5,4},{6,7},{7,6},{8,9},{9,8},{10,11... | collective-permute-start | bytes 245768 | tf_op jit(solution)/shard_map/ppermute | solution.py:40
  704.8 61.4 %collective-permute-start.125 = (bf16[4,16,2,2,2,80]{5,4,3,2,1,0:T(2,128)(2,1)S(1)}, bf16[4,16,2,2,2,80]{5,4,3,2,1,0:T(2,128)(2,1)S(1)}, u32[]{:S(2)}, u32[]{:S(2)}) collective-permute-start(bf16[4,16,2,2,2,80]{5,4,3,2,1,0:T(2,128)(2,1)S(1)} %convert_element_type.599), channel_id=1, source_target_pairs={{0,1},{1,0},{2,3},{3,2},{4,5},{5,4},{6,7},{7,6},{8,9},{9,8},{10,11... | collective-permute-start | bytes 245768 | tf_op jit(solution)/shard_map/ppermute | solution.py:40
  705.0 62.6 %collective-permute-start.122 = (bf16[4,16,2,2,2,80]{5,4,3,2,1,0:T(2,128)(2,1)S(1)}, bf16[4,16,2,2,2,80]{5,4,3,2,1,0:T(2,128)(2,1)S(1)}, u32[]{:S(2)}, u32[]{:S(2)}) collective-permute-start(bf16[4,16,2,2,2,80]{5,4,3,2,1,0:T(2,128)(2,1)S(1)} %convert_element_type.593), channel_id=1, source_target_pairs={{0,1},{1,0},{2,3},{3,2},{4,5},{5,4},{6,7},{7,6},{8,9},{9,8},{10,11... | collective-permute-start | bytes 245768 | tf_op jit(solution)/shard_map/ppermute | solution.py:40
  727.5 61.5 %collective-permute-start.72 = (bf16[4,128,2048]{2,1,0:T(8,128)(2,1)}, bf16[4,128,2048]{2,1,0:T(8,128)(2,1)}, u32[]{:S(2)}, u32[]{:S(2)}) collective-permute-start(bf16[4,128,2048]{2,1,0:T(8,128)(2,1)} %slice.618), channel_id=1, source_target_pairs={{0,1},{1,0},{2,3},{3,2},{4,5},{5,4},{6,7},{7,6},{8,9},{9,8},{10,11... | collective-permute-start | bytes 6291464 | tf_op jit(solution)/shard_map/ppermute | solution.py:40
  727.6 25.9 %collective-permute-start.93 = (f32[4,2,2,2,80]{4,3,2,1,0:T(2,128)S(1)}, f32[4,2,2,2,80]{4,3,2,1,0:T(2,128)S(1)}, u32[]{:S(2)}, u32[]{:S(2)}) collective-permute-start(f32[4,2,2,2,80]{4,3,2,1,0:T(2,128)S(1)} %reverse_add_fusion.9), channel_id=1, source_target_pairs={{0,2},{1,3},{2,0},{3,1},{4,6},{5,7},{6,4},{7,5},{8,10},{9,11},{10,... | collective-permute-start | bytes 30728 | tf_op jit(solution)/shard_map/ppermute | solution.py:40
  764.2 33.6 %collective-permute-start.87 = (bf16[4,128,2048]{2,1,0:T(8,128)(2,1)}, bf16[4,128,2048]{2,1,0:T(8,128)(2,1)}, u32[]{:S(2)}, u32[]{:S(2)}) collective-permute-start(bf16[4,128,2048]{2,1,0:T(8,128)(2,1)} %slice.630), channel_id=1, source_target_pairs={{0,1},{1,0},{2,3},{3,2},{4,5},{5,4},{6,7},{7,6},{8,9},{9,8},{10,11... | collective-permute-start | bytes 6291464 | tf_op jit(solution)/shard_map/ppermute | solution.py:40
  806.5 235.3 %all-gather.12.cloned.1.call-start = ((), (), s32[]{:S(2)}) async-start(), calls=%async_computation.2 | async-start | bytes 4423680 | tf_op jit(solution)/shard_map/all_gather | solution.py:631
  842.3 218.7 %all-gather.8.cloned.1.call-start = ((), (), s32[]{:S(2)}) async-start(), calls=%async_computation | async-start | bytes 2457600 | tf_op jit(solution)/shard_map/all_gather | solution.py:631
  951.8 43.5 %collective-permute-start.110 = (f32[4,2,2,2,80]{4,3,2,1,0:T(2,128)}, f32[4,2,2,2,80]{4,3,2,1,0:T(2,128)}, u32[]{:S(2)}, u32[]{:S(2)}) collective-permute-start(f32[4,2,2,2,80]{4,3,2,1,0:T(2,128)} %reshape.478), channel_id=1, source_target_pairs={{0,1},{1,0},{2,3},{3,2},{4,5},{5,4},{6,7},{7,6},{8,9},{9,8},{10,11... | collective-permute-start | bytes 30728 | tf_op jit(solution)/shard_map/ppermute | solution.py:40
  955.6 41.6 %collective-permute-start.116 = (bf16[2,16,2,2,2,128]{5,4,3,2,1,0:T(2,128)(2,1)S(1)}, bf16[2,16,2,2,2,128]{5,4,3,2,1,0:T(2,128)(2,1)}, u32[]{:S(2)}, u32[]{:S(2)}) collective-permute-start(bf16[2,16,2,2,2,128]{5,4,3,2,1,0:T(2,128)(2,1)S(1)} %convert_element_type.576), channel_id=1, source_target_pairs={{0,1},{1,0},{2,3},{3,2},{4,5},{5,4},{6,7},{7,6},{8,9},{9,8},{10,11... | collective-permute-start | bytes 196616 | tf_op jit(solution)/shard_map/ppermute | solution.py:40
  956.5 42.7 %collective-permute-start.119 = (bf16[4,16,2,2,2,80]{5,4,3,2,1,0:T(2,128)(2,1)}, bf16[4,16,2,2,2,80]{5,4,3,2,1,0:T(2,128)(2,1)}, u32[]{:S(2)}, u32[]{:S(2)}) collective-permute-start(bf16[4,16,2,2,2,80]{5,4,3,2,1,0:T(2,128)(2,1)} %convert_element_type.587), channel_id=1, source_target_pairs={{0,1},{1,0},{2,3},{3,2},{4,5},{5,4},{6,7},{7,6},{8,9},{9,8},{10,11... | collective-permute-start | bytes 245768 | tf_op jit(solution)/shard_map/ppermute | solution.py:40
  957.0 44.4 %collective-permute-start.113 = (bf16[4,16,2,2,2,80]{5,4,3,2,1,0:T(2,128)(2,1)}, bf16[4,16,2,2,2,80]{5,4,3,2,1,0:T(2,128)(2,1)}, u32[]{:S(2)}, u32[]{:S(2)}) collective-permute-start(bf16[4,16,2,2,2,80]{5,4,3,2,1,0:T(2,128)(2,1)} %convert_element_type.570), channel_id=1, source_target_pairs={{0,1},{1,0},{2,3},{3,2},{4,5},{5,4},{6,7},{7,6},{8,9},{9,8},{10,11... | collective-permute-start | bytes 245768 | tf_op jit(solution)/shard_map/ppermute | solution.py:40
  (256 other events, 5229.4 us)
Sparse Core Ops, SparseCore 0:
  806.6 27.9 all-gather.9
  842.4 67.0 all-gather.11
  1020.0 40.9 all-gather.7

commit v2 on v1

v2 whole, which is shorter than its diff:
```python
from functools import partial
import math

import jax
import jax.numpy as jnp
from jax import lax
from jax.experimental import pallas as pl
from jax.experimental.pallas import tpu as pltpu
from jax.sharding import PartitionSpec as P

HD = 128
RANK = 16
CAP = 80
EXPERTS = 4
CHUNK = 256
EPS = 1e-05
NEG = -1e30
F32 = jnp.float32
BF16 = jnp.bfloat16


def ein(spec, a, b):
    return jnp.einsum(spec, a, b, preferred_element_type=F32)


def rms_norm(gain, values):
    return values * lax.rsqrt(jnp.mean(values * values, axis=-1, keepdims=True) + EPS) * gain


def rms_back(values, gain, grad):
    unused, backward_function = jax.vjp(partial(rms_norm, gain), values)
    return backward_function(grad)[0]


NT = (((1,), (1,)), ((), ()))
TN = (((0,), (0,)), ((), ()))


def dot_nt(a, b):
    return lax.dot_general(a, b, NT, preferred_element_type=F32)


def dot_tn(a, b):
    return lax.dot_general(a, b, TN, preferred_element_type=F32)


def dot_nn(a, b):
    return jnp.dot(a, b, preferred_element_type=F32)


def swap(x, n, d):
    return lax.ppermute(x, "shard", [(i, i ^ d) for i in range(n)])


def tie(*values):
    return lax.optimization_barrier(values)


def across(x, n):
    return {d: swap(x, n, d) if d else x for d in range(0, n, 2)}


def from_sibling(pieces, n):
    other = {m ^ 1: swap(p, n, 1) for m, p in pieces.items()}
    return [p for unused, p in sorted({**pieces, **other}.items())]


def gather_small(x, me, n):
    out, d = x[None], 1
    while d < n:
        out = jnp.concatenate([out, swap(out, n, d)])
        d *= 2
    return out[jnp.arange(n) ^ me]


def sum_small(x, n):
    d = 1
    while d < n:
        x = x + swap(x, n, d)
        d *= 2
    return x


def halve(near, far, n):
    q = near.astype(F32) + swap(far, n, 1).astype(F32)
    return q[0], [q[i].astype(BF16) for i in range(1, n // 2)]


def collect(total, low, n):
    for i, part in enumerate(low):
        total = total + swap(part, n, 2 * i + 2).astype(F32)
    return total


def reshard(ws, me, n):
    rows, width = ws[0].shape[1], ws[0].shape[2] // n
    count = sum(w.shape[0] for w in ws)
    out = jnp.zeros((count, n * rows, width), ws[0].dtype)
    for m in sorted(range(n), key=lambda m: -m):
        piece = jnp.concatenate([lax.dynamic_slice_in_dim(w, (me ^ m) * width, width, 2) for w in ws])
        piece = swap(piece, n, m) if m else piece
        out = lax.dynamic_update_slice_in_dim(out, piece, (me ^ m) * rows, 1)
    return out


def pack_maps(maps, n, spare=None):
    count, k, own = maps.shape
    groups = -(-count // n)
    fill = groups * n - count
    flat = [maps[i] for i in range(count)]
    if fill:
        rest = jnp.zeros((k, fill * own), maps.dtype)
        if spare is not None:
            rest = rest.at[: spare.shape[0], : spare.shape[1]].set(spare)
        flat.append(rest)
    rows = [jnp.concatenate(flat[g * n : (g + 1) * n], axis=1) for g in range(groups)]
    return jnp.concatenate(rows) if groups > 1 else rows[0]


def fill_hot(key, hot):
    n, tok = key.shape
    slot = lax.broadcasted_iota(jnp.int32, (CAP, tok), 0)
    for b in range(n):
        one = jnp.where(slot == key[b : b + 1, :], 1.0, 0.0)
        hot[b * CAP : (b + 1) * CAP, :] = one.astype(BF16)


def block_of(b, size):
    return pl.ds(pl.multiple_of(b * size, 16), size)


def fill_rows(me, hot, xs, base, rows):
    tok = hot.shape[1]
    for m, x in enumerate(xs):
        here = block_of(me[0] ^ m, CAP)
        rows[here, :] = dot_nn(hot[here, :], x[pl.ds(base, tok), :]).astype(BF16)


def fill_map(me, xs, index, out):
    n, k = len(xs), out.shape[0]
    own = out.shape[1] // n
    group, column = index // n, index % n
    for m, x in enumerate(xs):
        part = x[block_of(group, k), pl.ds(pl.multiple_of(column * own, own), own)]
        out[:, pl.ds(pl.multiple_of((me[0] ^ m) * own, own), own)] = part


def fill_select(hot, select_tok, sel):
    for b in range(select_tok.shape[0]):
        here = pl.ds(b * CAP, CAP)
        sel[here, :] = dot_nn(hot[here, :], select_tok[b])


def fill_share(hot, share, col):
    for b in range(share.shape[0]):
        here = pl.ds(b * CAP, CAP)
        one = jnp.sum(hot[here, :].astype(F32) * share[b : b + 1, :], axis=1, keepdims=True)
        col[here, :] = jnp.broadcast_to(one, (CAP, col.shape[1]))


def scatter_add(me, hot, y, acc, at):
    tok = hot.shape[1]
    n = acc.shape[0] // tok
    for b in range(n):
        mask = me[0] ^ b
        there = block_of(mask // 2 + (mask % 2) * (n // 2), tok)
        acc[there, at] += dot_tn(hot[pl.ds(b * CAP, CAP), :], y[pl.ds(b * CAP, CAP), :])


def copy_out(acc, rows, near, far, sem):
    half = acc.shape[0] // 2
    for side, ref in enumerate((near, far)):
        rows[:half, :] = acc[side * half : (side + 1) * half, :].astype(BF16)
        copy = pltpu.make_async_copy(rows.at[pl.ds(0, half)], ref, sem)
        copy.start()
        copy.wait()


def write_out(acc, near, far):
    half = acc.shape[0] // 2
    near[...] = acc[:half, :].astype(BF16).reshape(near.shape)
    far[...] = acc[half:, :].astype(BF16).reshape(far.shape)


def live_rows(staged, first, k):
    total = staged[first : first + RANK]
    for d in range(1, k // RANK):
        total = total + staged[first + d * RANK : first + (d + 1) * RANK]
    return total


def lanes(e, size):
    return pl.ds(pl.multiple_of(e * size, 128), size)


def turn(v, cos, sin):
    return v * cos + pltpu.roll(v, HD // 2, 1) * sin


def turn_heads(v, table, sign):
    cos, sin = table[:, :HD], table[:, HD:]
    heads = [turn(v[:, h : h + HD], cos, sign * sin) for h in range(0, v.shape[1], HD)]
    return heads[0] if len(heads) == 1 else jnp.concatenate(heads, axis=1)


def qkv_kernel(n, *refs):
    me, xs, refs = refs[0], refs[1 : 1 + n], refs[1 + n :]
    key, select_tok, hi, lo, w, b_in, q, kv, rank_q, rank_kv, rows_own, tok_own, a_in, *refs = refs
    hot, rows, sel, table = refs
    i = pl.program_id(0)
    tok, k = hi.shape[1], b_in.shape[0]
    own = w.shape[1]
    mine = pl.ds(pl.multiple_of(me[0] * own, own), own)
    fill_map(me, xs, i, a_in)

    @pl.when(i < EXPERTS)
    def query():
        fill_hot(key, hot)
        fill_rows(me, hot, xs, k, rows)
        fill_select(hot, select_tok, sel)
        for b in range(n):
            here = pl.ds(b * CAP, CAP)
            table[here, :] = dot_nn(hot[here, :], hi[b]) + dot_nn(hot[here, :], lo[b])
        rank = (dot_nt(rows[...], a_in[...]) * sel[...]).astype(BF16)
        rank_q[...] = rank
        pre = dot_nn(rows[...], w[...]) + dot_nn(rank, b_in[...])
        q[...] = turn_heads(pre, table[...], 1.0).astype(BF16)
        rows_own[...] = rows[:, mine]

    @pl.when(i >= EXPERTS)
    def key_value():
        group = n // 2
        some = pl.ds(0, group * tok)
        for half in range(2):
            for j in range(group):
                m = half * group + j
                b = me[0] ^ m
                here = pl.ds(j * tok, tok)
                rows[here, :] = xs[m][pl.ds(k, tok), :]
                sel[here, :] = select_tok[b].astype(F32)
                table[here, :] = hi[b].astype(F32) + lo[b].astype(F32)
            rank = (dot_nt(rows[some, :], a_in[...]) * sel[some, :]).astype(BF16)
            pre = dot_nn(rows[some, :], w[...]) + dot_nn(rank, b_in[...])
            turned = turn_heads(pre, table[some, :], 1.0)
            done = jnp.where(i == EXPERTS, turned, pre).astype(BF16)
            for j in range(group):
                there = block_of(me[0] ^ (half * group + j), tok)
                here = slice(j * tok, (j + 1) * tok)
                rank_kv[there, :] = rank[here]
                kv[there, :] = done[here]
                tok_own[there, :] = rows[here, mine]


def attend_kernel(key, begin, q, k, v, mixed, lse, scores, mx, tot, acc):
    b = pl.program_id(1)
    tok = begin.shape[1]
    rows = q.shape[0] * q.shape[1]
    slot = lax.broadcasted_iota(jnp.int32, (CAP, tok), 0)
    token = b * tok + lax.broadcasted_iota(jnp.int32, (CAP, tok), 1)
    first, last = [], []
    for e in range(EXPERTS):
        chosen = slot == key[e : e + 1, :]
        first.append(jnp.sum(jnp.where(chosen, begin[...], 0), axis=1, keepdims=True))
        last.append(jnp.sum(jnp.where(chosen, token, 0), axis=1, keepdims=True))
    first, last = jnp.concatenate(first), jnp.concatenate(last)
    query = q[...].reshape(rows, HD)
    count = (b * tok + tok + CHUNK - 1) // CHUNK
    mx[...] = jnp.full(mx.shape, NEG, F32)

    def score(j, carry):
        start = pl.multiple_of(j * CHUNK, CHUNK)
        s = dot_nt(query, k[pl.ds(start, CHUNK), :]) * HD ** (-0.5)
        at = start + lax.broadcasted_iota(jnp.int32, s.shape, 1)
        s = jnp.where((at >= first) & (at <= last), s, NEG)
        scores[:, pl.ds(start, CHUNK)] = s
        mx[...] = jnp.maximum(mx[...], jnp.maximum(s[:, :HD], s[:, HD:]))
        return carry

    lax.fori_loop(0, count, score, 0)
    top = jnp.max(mx[...], axis=1, keepdims=True)
    tot[...] = jnp.zeros(tot.shape, F32)
    acc[...] = jnp.zeros(acc.shape, F32)

    def mix(j, carry):
        start = pl.multiple_of(j * CHUNK, CHUNK)
        p = jnp.exp(scores[:, pl.ds(start, CHUNK)] - top)
        tot[...] += p[:, :HD] + p[:, HD:]
        acc[...] += dot_nn(p.astype(BF16), v[pl.ds(start, CHUNK), :])
        return carry

    lax.fori_loop(0, count, mix, 0)
    total = jnp.sum(tot[...], axis=1, keepdims=True)
    mixed[...] = (acc[...] / total).astype(BF16).reshape(mixed.shape)
    lse[...] = jnp.broadcast_to(top + jnp.log(total), (rows, HD)).reshape(lse.shape)


def attend_back_kernel(key, begin, q, g, mixed, lse, k, v, gq, gk, gv, dq):
    b = pl.program_id(1)
    tok = begin.shape[1]
    rows = q.shape[0] * q.shape[1]
    scale = HD ** (-0.5)

    @pl.when(b == 0)
    def start():
        gk[...] = jnp.zeros(gk.shape, F32)
        gv[...] = jnp.zeros(gv.shape, F32)

    slot = lax.broadcasted_iota(jnp.int32, (CAP, tok), 0)
    token = b * tok + lax.broadcasted_iota(jnp.int32, (CAP, tok), 1)
    first, last = [], []
    for e in range(EXPERTS):
        chosen = slot == key[e : e + 1, :]
        first.append(jnp.sum(jnp.where(chosen, begin[...], 0), axis=1, keepdims=True))
        last.append(jnp.sum(jnp.where(chosen, token, 0), axis=1, keepdims=True))
    first, last = jnp.concatenate(first), jnp.concatenate(last)

    def flat(r):
        return r[...].reshape(rows, HD)

    query, grad = flat(q), flat(g)
    delta = jnp.sum(flat(mixed).astype(F32) * grad.astype(F32), axis=1, keepdims=True)
    log_total = flat(lse)[:, :1]
    count = (b * tok + tok + CHUNK - 1) // CHUNK
    dq[...] = jnp.zeros(dq.shape, F32)

    def step(j, carry):
        begin_at = pl.multiple_of(j * CHUNK, CHUNK)
        here = pl.ds(begin_at, CHUNK)
        kc, vc = k[here, :], v[here, :]
        s = dot_nt(query, kc) * scale
        at = begin_at + lax.broadcasted_iota(jnp.int32, s.shape, 1)
        p = jnp.where((at >= first) & (at <= last), jnp.exp(s - log_total), 0.0)
        dp = dot_nt(grad, vc)
        ds = (p * (dp - delta)).astype(BF16)
        dq[...] += dot_nn(ds, kc)
        gk[here, :] += dot_tn(ds, query) * scale
        gv[here, :] += dot_tn(p.astype(BF16), grad)
        return carry

    lax.fori_loop(0, count, step, 0)
    gq[...] = (dq[...] * scale).reshape(gq.shape)


def out_kernel(n, first, stride, *refs):
    me, xs, refs = refs[0], refs[1 : 1 + n], refs[1 + n :]
    x, key, share, select_tok, down, w, near, far, live, maps, hot, sel, col, part, stage, acc = refs
    e = pl.program_id(0)
    k, slots = down.shape[0], x.shape[0]

    @pl.when(e == 0)
    def start():
        acc[...] = jnp.zeros(acc.shape, F32)
        stage[...] = jnp.zeros(stage.shape, F32)

    fill_map(me, xs, first + stride * e, maps)
    fill_hot(key, hot)
    fill_select(hot, select_tok, sel)
    fill_share(hot, share, col)
    rank = dot_nt(x[...], down[...]) * sel[...]
    stage[:, :k] = rank
    live[:, lanes(e, slots)] = live_rows(stage[...].T, 0, k).astype(BF16)
    rank = rank.astype(BF16)
    width = part.shape[1]
    for c in range(0, w.shape[1], width):
        at = pl.ds(c, width)
        y = dot_nn(x[...], w[:, at]) + dot_nn(rank, maps[:, at])
        part[...] = (y * col[:, :1]).astype(BF16)
        scatter_add(me, hot, part, acc, at)

    @pl.when(e == EXPERTS - 1)
    def finish():
        write_out(acc, near, far)


def back_kernel(n, first, stride, *refs):
    me, xs, ms, refs = refs[0], refs[1 : 1 + n], refs[1 + n : 1 + 2 * n], refs[1 + 2 * n :]
    key, select_tok, w, small, h, rank, rows_own, maps, hot, rows, sel = refs
    fill_map(me, ms, first + stride * pl.program_id(0), maps)
    fill_hot(key, hot)
    fill_rows(me, hot, xs, 0, rows)
    fill_select(hot, select_tok, sel)
    low = (dot_nt(rows[...], maps[...]) * sel[...]).astype(BF16)
    rank[...] = low
    h[...] = dot_nt(rows[...], w[...]) + dot_nn(low, small[...])
    rows_own[...] = rows[:, lanes(me[0], rows_own.shape[1])]


def mixed_back_kernel(n, *refs):
    me, xs, ms, refs = refs[0], refs[1 : 1 + n], refs[1 + n : 1 + 2 * n], refs[1 + 2 * n :]
    key, share, select_tok, w, small, mixed, g, a_grad, dshare, rows_own, maps, *refs = refs
    hot, rows, sel, col, stage = refs
    e = pl.program_id(0)
    fill_map(me, ms, e, maps)
    k, own, slots = small.shape[0], mixed.shape[1], mixed.shape[0]

    @pl.when(e == 0)
    def start():
        stage[...] = jnp.zeros(stage.shape, F32)

    fill_hot(key, hot)
    fill_rows(me, hot, xs, 0, rows)
    fill_select(hot, select_tok, sel)
    fill_share(hot, share, col)
    low = (dot_nt(rows[...], maps[...]) * sel[...]).astype(BF16)
    h = dot_nt(rows[...], w[...]) + dot_nn(low, small[...])
    stage[:, :1] = jnp.sum(mixed[...].astype(F32) * h, axis=1, keepdims=True)
    dshare[:, lanes(e, slots)] = stage[...].T[:8]
    g[...] = (h * col[:, :1]).astype(BF16)
    scaled = (low.astype(F32) * col[:, :k]).astype(BF16)
    a_grad[...] = dot_tn(scaled, mixed[...]).astype(BF16)
    rows_own[...] = rows[:, lanes(me[0], own)]


def feed_kernel(n, first, stride, *refs):
    me, xs, ms, refs = refs[0], refs[1 : 1 + n], refs[1 + n : 1 + 2 * n], refs[1 + 2 * n :]
    key, share, select_tok, wg, wu, hid, h, back_down, *refs = refs
    near, far, inner, live, dshare, h_grad, rows_own, *refs = refs
    hot, rows, sel, col, stage, both, gate, up, gg, gu, part, acc, sem = refs
    e = pl.program_id(0)
    k, own, slots = hid.shape[1], rows_own.shape[1], rows.shape[0]

    @pl.when(e == 0)
    def start():
        acc[...] = jnp.zeros(acc.shape, F32)
        stage[...] = jnp.zeros(stage.shape, F32)

    fill_hot(key, hot)
    fill_rows(me, hot, xs, 0, rows)
    fill_select(hot, select_tok, sel)
    fill_share(hot, share, col)
    fill_map(me, ms, first + stride * e, both.at[:k])
    fill_map(me, ms, first + stride * e + 1, both.at[k:])
    ranks = dot_nt(rows[...], both[...])
    rank_gate = (ranks[:, :k] * sel[...]).astype(BF16)
    rank_up = (ranks[:, k:] * sel[...]).astype(BF16)
    gate[...] = dot_nt(rows[...], wg[...]) + dot_nn(rank_gate, hid[0])
    up[...] = dot_nt(rows[...], wu[...]) + dot_nn(rank_up, hid[1])

    def point(b, carry):
        r = block_of(b, CAP)
        a, u, hh, s = gate[r, :], up[r, :], h[r, :], col[r, :1]
        sig = jax.nn.sigmoid(a)
        act = a * sig
        value = act * u
        inner[r, :] = value.astype(BF16)
        stage[r, 2 * k : 2 * k + 1] = jnp.sum(value * hh, axis=1, keepdims=True)
        scaled = hh * s
        gg[r, :] = (scaled * u * sig * (1.0 + a * (1.0 - sig))).astype(BF16)
        gu[r, :] = (scaled * act).astype(BF16)
        return carry

    lax.fori_loop(0, slots // CAP, point, 0)
    stage[:, :k] = dot_nt(gg[...], hid[0]) * sel[...]
    stage[:, k : 2 * k] = dot_nt(gu[...], hid[1]) * sel[...]
    staged = stage[...].T
    live[:RANK, lanes(e, slots)] = live_rows(staged, 0, k).astype(BF16)
    live[RANK:, lanes(e, slots)] = live_rows(staged, k, k).astype(BF16)
    dshare[:, lanes(e, slots)] = staged[2 * k : 2 * k + 8]
    h_grad[0] = dot_tn(rank_gate, gg[...]).astype(BF16)
    h_grad[1] = dot_tn(rank_up, gu[...]).astype(BF16)
    scaled = (back_down[...].astype(F32) * col[:, :k]).astype(BF16)
    h_grad[2] = dot_tn(scaled, inner[...]).astype(BF16)
    rows_own[...] = rows[:, lanes(me[0], own)]
    back = stage[:, : 2 * k].astype(BF16)
    width = part.shape[1]
    for c in range(0, wg.shape[1], width):
        at = pl.ds(c, width)
        y = dot_nn(gg[...], wg[:, at]) + dot_nn(gu[...], wu[:, at]) + dot_nn(back, both[:, at])
        part[...] = y.astype(BF16)
        scatter_add(me, hot, part, acc, at)

    @pl.when(e == EXPERTS - 1)
    def finish():
        copy_out(acc, rows, near, far, sem)


def qkv_back_kernel(n, *refs):
    me, xs, refs = refs[0], refs[1 : 1 + n], refs[1 + n :]
    key, select_tok, hi, lo, w, b_in, gq, gk, gv, rank_q, rank_kv, near, far, live, b_grad, *refs = refs
    maps, hot, sel, table, part, stage, acc, some_g = refs
    i = pl.program_id(0)
    tok, k = hi.shape[1], b_in.shape[0]
    slots, wide = gq.shape[0], maps.shape[1]
    seq = n * tok
    width = part.shape[1]
    fill_map(me, xs, i, maps)

    @pl.when(i == 0)
    def start():
        acc[...] = jnp.zeros(acc.shape, F32)
        stage[...] = jnp.zeros(stage.shape, F32)

    @pl.when(i < EXPERTS)
    def query():
        fill_hot(key, hot)
        fill_select(hot, select_tok, sel)
        for b in range(n):
            here = pl.ds(b * CAP, CAP)
            table[here, :] = dot_nn(hot[here, :], hi[b]) + dot_nn(hot[here, :], lo[b])
        g = turn_heads(gq[...], table[...], -1.0).astype(BF16)
        rank = dot_nt(g, b_in[...]) * sel[...]
        stage[:slots, :k] = rank
        live[:, lanes(i, slots)] = live_rows(stage[:slots, :].T, 0, k).astype(BF16)
        b_grad[...] = dot_tn(rank_q[...], g).astype(BF16)
        rank = rank.astype(BF16)
        for c in range(0, wide, width):
            at = pl.ds(c, width)
            y = dot_nt(g, w[at, :]) + dot_nn(rank, maps[:, at])
            part[...] = y.astype(BF16)
            scatter_add(me, hot, part, acc, at)

    @pl.when(i >= EXPERTS)
    def key_value():
        group = n // 2
        size = group * tok
        some = pl.ds(0, size)
        total = jnp.zeros(b_grad.shape, F32)
        for half in range(2):
            there = pl.ds(half * size, size)
            for j in range(group):
                b = me[0] ^ (2 * j + half)
                here = pl.ds(j * tok, tok)
                sel[here, :] = select_tok[b].astype(F32)
                both = hi[b].astype(F32) + lo[b].astype(F32)
                turned = turn_heads(gk[block_of(b, tok), :], both, -1.0)
                some_g[here, :] = jnp.where(i == EXPERTS, turned, gv[block_of(b, tok), :]).astype(BF16)
                total = total + dot_tn(rank_kv[block_of(b, tok), :], some_g[here, :])
            g = some_g[...]
            rank = dot_nt(g, b_in[...]) * sel[some, :]
            for j in range(group):
                stage[block_of(me[0] ^ (2 * j + half), tok), :k] = rank[j * tok : (j + 1) * tok]
            rank = rank.astype(BF16)
            for c in range(0, wide, width):
                at = pl.ds(c, width)
                acc[there, at] += dot_nt(g, w[at, :]) + dot_nn(rank, maps[:, at])
        b_grad[...] = total.astype(BF16)
        begin = EXPERTS * slots + (i - EXPERTS) * seq
        there = pl.ds(pl.multiple_of(begin, 128), seq)
        live[:, there] = live_rows(stage[:seq, :].T, 0, k).astype(BF16)

    @pl.when(i == EXPERTS + 1)
    def finish():
        write_out(acc, near, far)


def chunk_of(slots, wide):
    width = wide // 2
    while slots * width > 640 * 1024:
        width //= 2
    return width


def whole(shape):
    zeros = (0,) * len(shape)
    return pl.BlockSpec(shape, lambda *at: zeros, pipeline_mode=pl.Buffered(1))


def by_expert(shape, at=lambda i: i):
    rest = (0,) * len(shape)
    return pl.BlockSpec((None,) + shape, lambda i, *unused: (at(i),) + rest)


def shaped(shape, dtype):
    return jax.ShapeDtypeStruct(shape, dtype)


def run(kernel, name, steps, ins, outs, scratch, args, flops, scalars=1):
    call = pl.pallas_call(
        kernel,
        grid_spec=pltpu.PrefetchScalarGridSpec(
            num_scalar_prefetch=scalars,
            grid=steps,
            in_specs=ins,
            out_specs=[o[0] for o in outs],
            scratch_shapes=[pltpu.VMEM(*one) if isinstance(one, tuple) else one for one in scratch],
        ),
        out_shape=[shaped(o[1], o[2]) for o in outs],
        compiler_params=pltpu.CompilerParams(vmem_limit_bytes=62 << 20),
        cost_estimate=pl.CostEstimate(
            flops=int(flops), bytes_accessed=32 << 20, transcendentals=1 << 20
        ),
        name=name,
    )
    return call(*args)


def last_expert(i):
    return jnp.minimum(i, EXPERTS - 1)


def from_expert(i):
    return jnp.maximum(i - EXPERTS, 0)


def rows_spec(x, rows=None):
    return whole((x.shape[0] if rows is None else rows, x.shape[1]))


def sides(n, tok, wide):
    shape = (n // 2, tok, wide)
    return [(whole(shape), shape, BF16)] * 2


def qkv(me, pieces, key, select_tok, hi, lo, w, b_in):
    n, tok, k = select_tok.shape
    wide, own, slots, seq = pieces[0].shape[1], w.shape[2], n * CAP, n * tok
    return run(
        partial(qkv_kernel, n),
        "qkv",
        (EXPERTS + 2,),
        [rows_spec(p) for p in pieces]
        + [by_expert((n, tok), last_expert), whole(select_tok.shape), whole(hi.shape),
           whole(lo.shape), by_expert((wide, own)), by_expert((k, own))],
        [
            (by_expert((slots, own), last_expert), (EXPERTS, slots, own), BF16),
            (by_expert((seq, own), from_expert), (2, seq, own), BF16),
            (by_expert((slots, k), last_expert), (EXPERTS, slots, k), BF16),
            (by_expert((seq, k), from_expert), (2, seq, k), BF16),
            (by_expert((slots, own), last_expert), (EXPERTS, slots, own), BF16),
            (whole((seq, own)), (seq, own), BF16),
        ],
        [((k, wide), BF16), ((slots, tok), BF16), ((max(slots, seq // 2), wide), BF16),
         ((max(slots, seq // 2), k), F32), ((max(slots, seq // 2), 2 * HD), F32)],
        (me, *pieces, key, select_tok, hi, lo, w, b_in),
        2 * wide * own * (EXPERTS * slots + 2 * seq) * 1.5,
    )


def attend(key, begin, q, k, v):
    n, tok = begin.shape[0], begin.shape[2]
    own, seq, rows = q.shape[2], n * tok, EXPERTS * CAP
    slot_spec = pl.BlockSpec((EXPERTS, None, CAP, HD), lambda h, b: (0, b, 0, h))
    all_spec = pl.BlockSpec((seq, HD), lambda h, b: (0, h))
    shape = (EXPERTS, n, CAP, own)
    mixed, lse = run(
        attend_kernel,
        "attend",
        (own // HD, n),
        [pl.BlockSpec((None, EXPERTS, tok), lambda h, b: (b, 0, 0)),
         pl.BlockSpec((None, 1, tok), lambda h, b: (b, 0, 0)), slot_spec, all_spec, all_spec],
        [(slot_spec, shape, BF16), (slot_spec, shape, F32)],
        [((rows, seq + CHUNK), F32), ((rows, HD), F32), ((rows, HD), F32), ((rows, HD), F32)],
        (key, begin, q.reshape(shape), k, v),
        3 * rows * seq * own * n,
        0,
    )
    return mixed.reshape(q.shape), lse


def attend_back(key, begin, q, g, mixed, lse, k, v):
    n, tok = begin.shape[0], begin.shape[2]
    own, seq, rows = q.shape[2], n * tok, EXPERTS * CAP
    slot_spec = pl.BlockSpec((EXPERTS, None, CAP, HD), lambda h, b: (0, b, 0, h))
    all_spec = pl.BlockSpec((seq, HD), lambda h, b: (0, h))
    shape = (EXPERTS, n, CAP, own)
    gq, gk, gv = run(
        attend_back_kernel,
        "attend_back",
        (own // HD, n),
        [pl.BlockSpec((None, EXPERTS, tok), lambda h, b: (b, 0, 0)),
         pl.BlockSpec((None, 1, tok), lambda h, b: (b, 0, 0)),
         slot_spec, slot_spec, slot_spec, slot_spec, all_spec, all_spec],
        [(slot_spec, shape, F32), (all_spec, (seq, own), F32), (all_spec, (seq, own), F32)],
        [((rows, HD), F32)],
        (key, begin, q.reshape(shape), g.reshape(shape), mixed.reshape(shape), lse, k, v),
        7 * rows * seq * own * n,
        0,
    )
    return gq.reshape(q.shape), gk, gv


def weight_spec(w, p=None):
    if p is None:
        return by_expert(w.shape[1:])
    return pl.BlockSpec((None, None) + w.shape[2:], lambda e, *unused: (e, p, 0, 0))


def project_out(name, me, x, key, share, select_tok, down, w, pieces, groups, first, stride, p=None):
    n, tok, k = select_tok.shape
    wide, slots, deep = pieces[0].shape[1], n * CAP, x.shape[2]
    down_spec = by_expert((k, deep)) if p is None else weight_spec(down, p)
    return run(
        partial(out_kernel, n, first, stride),
        name,
        (EXPERTS,),
        [rows_spec(m, groups * k) for m in pieces]
        + [by_expert((slots, deep)), by_expert((n, tok)), by_expert((n, tok)), whole(select_tok.shape),
           down_spec, weight_spec(w, p)],
        sides(n, tok, wide) + [(whole((RANK, EXPERTS * slots)), (RANK, EXPERTS * slots), BF16)],
        [((k, wide), BF16), ((slots, tok), BF16), ((slots, k), F32), ((slots, 128), F32),
         ((slots, chunk_of(slots, wide)), BF16), ((slots, 128), F32), ((n * tok, wide), F32)],
        (me, *pieces, x, key, share, select_tok, down, w),
        2 * wide * deep * EXPERTS * slots * 1.5,
    )


def feed_back_down(me, tokens, pieces, groups, first, stride, key, select_tok, w, small):
    n, tok, k = select_tok.shape
    wide, slots, deep = pieces[0].shape[1], n * CAP, w.shape[2]
    own = wide // n
    return run(
        partial(back_kernel, n, first, stride),
        "feed_down_back",
        (EXPERTS,),
        [rows_spec(m) for m in tokens] + [rows_spec(m, groups * k) for m in pieces]
        + [by_expert((n, tok)), whole(select_tok.shape), weight_spec(w, 2), weight_spec(small, 2)],
        [(by_expert((slots, deep)), (EXPERTS, slots, deep), F32),
         (by_expert((slots, k)), (EXPERTS, slots, k), BF16),
         (by_expert((slots, own)), (EXPERTS, slots, own), BF16)],
        [((k, wide), BF16), ((slots, tok), BF16), ((slots, wide), BF16), ((slots, k), F32)],
        (me, *tokens, *pieces, key, select_tok, w, small),
        2 * wide * deep * EXPERTS * slots * 1.3,
    )


def mixed_back(me, tokens, pieces, groups, key, share, select_tok, w, small, mixed):
    n, tok, k = select_tok.shape
    wide, slots, own = pieces[0].shape[1], n * CAP, w.shape[1]
    return run(
        partial(mixed_back_kernel, n),
        "mixed_back",
        (EXPERTS,),
        [rows_spec(m) for m in tokens] + [rows_spec(m, groups * k) for m in pieces]
        + [by_expert((n, tok)), by_expert((n, tok)), whole(select_tok.shape),
           weight_spec(w), by_expert((k, own)), by_expert((slots, own))],
        [(by_expert((slots, own)), (EXPERTS, slots, own), BF16),
         (by_expert((k, own)), (EXPERTS, k, own), BF16),
         (whole((8, EXPERTS * slots)), (8, EXPERTS * slots), F32),
         (by_expert((slots, own)), (EXPERTS, slots, own), BF16)],
        [((k, wide), BF16), ((slots, tok), BF16), ((slots, wide), BF16), ((slots, k), F32),
         ((slots, 128), F32), ((slots, 128), F32)],
        (me, *tokens, *pieces, key, share, select_tok, w, small, mixed),
        2 * wide * own * EXPERTS * slots * 1.5,
    )


def feed(me, tokens, pieces, groups, first, stride, key, share, select_tok, w, hid, h, back_down):
    n, tok, k = select_tok.shape
    wide, slots, deep = pieces[0].shape[1], n * CAP, w.shape[2]
    own = wide // n
    return run(
        partial(feed_kernel, n, first, stride),
        "feed",
        (EXPERTS,),
        [rows_spec(m) for m in tokens] + [rows_spec(m, groups * k) for m in pieces]
        + [by_expert((n, tok)), by_expert((n, tok)),
           whole(select_tok.shape), weight_spec(w, 0), weight_spec(w, 1), by_expert((3, k, deep)),
           by_expert((slots, deep)), by_expert((slots, k))],
        [(pl.BlockSpec(memory_space=pl.ANY), (n // 2 * tok, wide), BF16)] * 2
        + [(by_expert((slots, deep)), (EXPERTS, slots, deep), BF16),
           (whole((2 * RANK, EXPERTS * slots)), (2 * RANK, EXPERTS * slots), BF16),
           (whole((8, EXPERTS * slots)), (8, EXPERTS * slots), F32),
           (by_expert((3, k, deep)), (EXPERTS, 3, k, deep), BF16),
           (by_expert((slots, own)), (EXPERTS, slots, own), BF16)],
        [((slots, tok), BF16), ((slots, wide), BF16), ((slots, k), F32), ((slots, 128), F32),
         ((slots, 128), F32), ((2 * k, wide), BF16), ((slots, deep), F32), ((slots, deep), F32),
         ((slots, deep), BF16), ((slots, deep), BF16), ((slots, chunk_of(slots, wide)), BF16),
         ((n * tok, wide), F32), pltpu.SemaphoreType.DMA],
        (me, *tokens, *pieces, key, share, select_tok, w, w, hid, h, back_down),
        8 * wide * deep * EXPERTS * slots * 1.3,
    )


def qkv_back(me, pieces, key, select_tok, hi, lo, w, b_in, gq, gk, gv, rank_q, rank_kv):
    n, tok, k = select_tok.shape
    wide, own, slots, seq = pieces[0].shape[1], w.shape[2], n * CAP, n * tok
    total = EXPERTS * slots + 2 * seq
    most = max(slots, seq // 2)
    return run(
        partial(qkv_back_kernel, n),
        "qkv_back",
        (EXPERTS + 2,),
        [rows_spec(m, k) for m in pieces]
        + [by_expert((n, tok), last_expert), whole(select_tok.shape), whole(hi.shape),
           whole(lo.shape), by_expert((wide, own)), by_expert((k, own)),
           by_expert((slots, own), last_expert), whole((seq, own)), whole((seq, own)),
           by_expert((slots, k), last_expert), by_expert((seq, k), from_expert)],
        sides(n, tok, wide)
        + [(whole((RANK, total)), (RANK, total), BF16),
           (by_expert((k, own)), (EXPERTS + 2, k, own), BF16)],
        [((k, wide), BF16), ((slots, tok), BF16), ((most, k), F32), ((slots, 2 * HD), F32),
         ((slots, chunk_of(slots, wide)), BF16), ((max(slots, seq), 128), F32), ((seq, wide), F32),
         ((seq // 2, own), BF16)],
        (me, *pieces, key, select_tok, hi, lo, w, b_in, gq, gk, gv, rank_q, rank_kv),
        2 * wide * own * (EXPERTS * slots + 2 * seq) * 1.5,
    )


def members(routes):
    names = jnp.arange(EXPERTS, dtype=jnp.int32)[None, :, None]
    member = (routes[:, :1] == names) | (routes[:, 1:] == names)
    tok = routes.shape[-1]
    before = (jnp.arange(tok)[:, None] < jnp.arange(tok)[None, :]).astype(BF16)
    rank = ein("met,tu->meu", member.astype(BF16), before).astype(jnp.int32)
    return jnp.where(member, rank, -1)


def own_shares(normed, router, routes):
    names = jnp.arange(EXPERTS, dtype=jnp.int32)[:, None]
    member = (routes[:1] == names) | (routes[1:] == names)
    logits = ein("td,de->et", normed, router)
    return jax.nn.softmax(jnp.where(member, logits, -jnp.inf), axis=0)


def route_back(share, grad_share, router):
    grad = share * (grad_share - jnp.sum(share * grad_share, axis=0, keepdims=True))
    return jnp.einsum("et,de->td", grad, router.astype(F32), precision=lax.Precision.HIGHEST)


def local(
    n,
    reps,
    layer_input_state,
    cotangent,
    norm_gain_vectors,
    attention_router_weight,
    feed_router_weight,
    attention_query_weight,
    key_value_weight,
    attention_output_weight,
    feed_expert_weight,
    attention_adapters,
    feed_adapter_width,
    feed_adapter_hidden,
    token_document,
    document_adapter,
    attention_expert_pairs,
    feed_expert_pairs,
):
    tok, wide = layer_input_state.shape
    own, slots = wide // n, n * CAP
    columns = attention_adapters.shape[3]
    me = lax.axis_index("shard")
    me_ref = me.reshape(1).astype(jnp.int32)
    segments = token_document[0]
    seq = segments.shape[0]
    docs = document_adapter[0]
    doc_count = docs.shape[0]
    k = doc_count * RANK

    def one_hot(which):
        at = which[:, None] * RANK + jnp.arange(RANK)[None, :]
        return (at.reshape(-1)[:, None] == jnp.arange(columns)[None, :]).astype(BF16)

    pick = one_hot(docs)
    attn_small = ein("kc,pmwc->pmkw", pick, attention_adapters).astype(BF16)
    width_small = ein("kc,pmwc->pmkw", pick, feed_adapter_width).astype(BF16)
    hidden_small = ein("kc,epcf->epkf", pick, feed_adapter_hidden).astype(BF16)
    b_in, a_out = attn_small[1, : EXPERTS + 2], attn_small[0, EXPERTS + 2 :]

    x = layer_input_state.astype(F32)
    gain_one = norm_gain_vectors[0].astype(F32)
    gain_two = norm_gain_vectors[1].astype(F32)
    normed_own = rms_norm(gain_one, x).astype(BF16)
    routes = jnp.concatenate([attention_expert_pairs.T, feed_expert_pairs.T])
    own_a = own_shares(normed_own, attention_router_weight, routes[:2])
    own_hi = own_a.astype(BF16)
    own_lo = (own_a - lax.reduce_precision(own_a, 8, 7)).astype(BF16)
    spare = jnp.stack([routes.astype(BF16).reshape(-1), own_hi.reshape(-1), own_lo.reshape(-1)])
    first = jnp.concatenate([pack_maps(attn_small[0, : EXPERTS + 2], n, spare), normed_own])
    weights = [attention_query_weight, key_value_weight]
    if n == 8:
        cut = (first.shape[0] // 2 + 15) // 16 * 16
        y0, x1 = swap(first[:cut], n, 4), swap(first[cut:], n, 2)
        y1, x0 = swap(first[cut:], n, 4), swap(first[:cut], n, 2)
        y0, x1, *weights = tie(y0, x1, *weights)
        d0, d1 = swap(y0, n, 2), swap(x1, n, 4)
        chips = {0: first}
        for m, p in ((2, (x0, x1)), (4, (y0, y1)), (6, (d0, d1))):
            chips[m] = jnp.concatenate(p)
    else:
        chips = across(first, n)
    pieces = from_sibling(chips, n)
    w_in = reshard(weights, me, n)

    facts = jnp.stack([p[:3, (EXPERTS + 2) * own : (EXPERTS + 2) * own + EXPERTS * tok] for p in pieces])
    facts = facts[jnp.arange(n) ^ me].reshape(n, 3, EXPERTS, tok)
    routes = facts[:, 0].astype(jnp.int32)
    share_a = facts[:, 1].astype(F32) + facts[:, 2].astype(F32)

    second = jnp.concatenate([attn_small[1, EXPERTS + 2 :], width_small.reshape(-1, k, own)])
    groups = -(-second.shape[0] // n)
    second, cotangent_sent, w_in = tie(pack_maps(second, n), cotangent, w_in)
    map_chips, cotangent_chips = across(second, n), across(cotangent_sent, n)

    begins = jnp.sum((segments[None, :] < jnp.arange(doc_count)[:, None]).astype(jnp.int32), axis=1)
    doc = segments.reshape(n, tok)
    place = jnp.arange(seq, dtype=jnp.int32).reshape(n, tok)
    doc_table = doc[None] == jnp.arange(doc_count, dtype=jnp.int32)[:, None, None]
    begin = jnp.sum(jnp.where(doc_table, begins[:, None, None], 0), axis=0)
    freq = jnp.exp(-jnp.arange(HD // 2, dtype=F32) * (2.0 * math.log(10000.0) / HD))
    angles = (place - begin).astype(F32)[..., None] * freq
    cos, sin = jnp.cos(angles), jnp.sin(angles)
    table = jnp.concatenate([cos, cos, -sin, sin], axis=-1)
    table_hi = table.astype(BF16)
    table_lo = (table - lax.reduce_precision(table, 8, 7)).astype(BF16)
    chosen_doc = jnp.arange(k, dtype=jnp.int32)[None, None, :] // RANK
    select_tok = (doc[:, :, None] == chosen_doc).astype(BF16)
    select_row = doc_table.astype(F32).reshape(1, doc_count, seq)

    slot_a, slot_f = members(routes[:, :2]), members(routes[:, 2:])
    routes_f_own = feed_expert_pairs.T
    key_a, key_f = slot_a.transpose(1, 0, 2), slot_f.transpose(1, 0, 2)

    def slot_select(slot):
        hot = slot[:, :, None, :] == jnp.arange(CAP, dtype=jnp.int32)[None, None, :, None]
        chose = hot[:, :, None] & doc_table.transpose(1, 0, 2)[:, None, :, None, :]
        select = jnp.any(chose, axis=-1).astype(F32)
        return select.transpose(1, 2, 0, 3).reshape(EXPERTS, doc_count, slots)

    select_a, select_f = slot_select(slot_a), slot_select(slot_f)

    share_ae = share_a.transpose(1, 0, 2)
    q, kv, rank_q, rank_kv, rows_a_own, normed_own_columns = qkv(
        me_ref, pieces, key_a, select_tok, table_hi, table_lo, w_in, b_in
    )
    q, *sent = tie(q, *map_chips.values())
    maps = from_sibling(dict(zip(map_chips, sent)), n)
    mixed, lse = attend(slot_a, begin[:, None], q, kv[0], kv[1])
    mixed, *sent = tie(mixed, *cotangent_chips.values())
    grads_out_all = from_sibling(dict(zip(cotangent_chips, sent)), n)
    near, far, live_o = project_out(
        "attend_out", me_ref, mixed, key_a, share_ae, select_tok, a_out, attention_output_weight, maps, groups, 0, 1
    )
    attn_total, attn_low = halve(near, far, n)
    *attn_low, key_late = tie(*attn_low, key_f)

    w_feed = jnp.swapaxes(feed_expert_weight, 2, 3)
    grad_inner, back_down, rows_g_own = feed_back_down(
        me_ref, grads_out_all, maps, groups, EXPERTS + 2, 3, key_late, select_tok, w_feed, hidden_small
    )
    attn_total, grad_inner = tie(attn_total, grad_inner)
    attended = x + collect(attn_total, attn_low, n)
    normed_two_own = rms_norm(gain_two, attended).astype(BF16)
    normed_two = from_sibling(across(normed_two_own, n), n)
    own_f = own_shares(normed_two_own, feed_router_weight, routes_f_own)
    share_f = gather_small(own_f, me, n)
    share_fe = share_f.transpose(1, 0, 2)
    near, far, inner, live_f, dshare_f, hidden_grad, rows_f_own = feed(
        me_ref, normed_two, maps, groups, EXPERTS, 3, key_f, share_fe, select_tok, w_feed, hidden_small,
        grad_inner, back_down,
    )
    near, far = near.reshape(n // 2, tok, wide), far.reshape(n // 2, tok, wide)
    two_total, two_low = halve(near, far, n)
    *two_low, inner, dshare_f, docs_sent = tie(*two_low, inner, dshare_f, docs)
    near, far, live_d = project_out(
        "feed_out", me_ref, inner, key_f, share_fe, select_tok, hidden_small, w_feed, maps, groups, EXPERTS + 2, 3, 2
    )
    grad_two_own = collect(two_total, two_low, n)

    def own_tokens(slot, dshare):
        mine = lax.dynamic_slice_in_dim(dshare.reshape(EXPERTS, n, CAP), me, 1, 1)[:, 0]
        hot = lax.dynamic_slice_in_dim(slot, me, 1, 0)[0][:, None, :] == jnp.arange(CAP)[None, :, None]
        return jnp.sum(jnp.where(hot, mine[:, :, None], 0.0), axis=1)

    dshare_f = sum_small(dshare_f, n)[:1]
    grad_two_own = grad_two_own + route_back(own_f, own_tokens(slot_f, dshare_f), feed_router_weight)
    grad_attended = cotangent.astype(F32) + rms_back(attended, gain_two, grad_two_own)

    grad_sent, near, far = tie(grad_attended.astype(BF16), near, far)
    out_total, out_low = halve(near, far, n)
    chips = across(grad_sent, n)
    out_total, *sent = tie(out_total, *out_low, *chips.values())
    out_low, sent = sent[: n // 2 - 1], sent[n // 2 - 1 :]
    grads_two = from_sibling(dict(zip(chips, sent)), n)
    grad_mixed, a_out_grad, dshare_a, rows_ga_own = mixed_back(
        me_ref, grads_two, maps, groups, key_a, share_ae, select_tok, attention_output_weight, a_out, mixed
    )
    live_f, live_o = lax.psum((jnp.concatenate([live_f, live_d]), live_o), "shard")
    grad_mixed, *out_low = tie(grad_mixed, *out_low)
    gq, gk, gv = attend_back(slot_a, begin[:, None], q, grad_mixed, mixed, lse, kv[0], kv[1])
    gq, live_f, live_o = tie(gq, live_f, live_o)
    layer_out = attended + collect(out_total, out_low, n)
    near, far, live_in, b_in_grad = qkv_back(
        me_ref, pieces, key_a, select_tok, table_hi, table_lo, w_in, b_in, gq, gk, gv, rank_q, rank_kv
    )
    in_total, in_low = halve(near, far, n)
    *in_low, dshare_a, live_in, b_in_grad = tie(*in_low, dshare_a, live_in, b_in_grad)
    grad_normed = collect(in_total, in_low, n)
    dshare_a = sum_small(dshare_a, n)[:1]
    grad_normed = grad_normed + route_back(own_a, own_tokens(slot_a, dshare_a), attention_router_weight)
    grad_in = grad_attended + rms_back(x, gain_one, grad_normed)

    def spread(live, select):
        both = live.astype(F32)[:, None] * select[:, :, None, :]
        return both.reshape(live.shape[0], k, live.shape[2]).astype(BF16)

    def of_slots(live):
        return live.reshape(RANK, EXPERTS, slots).transpose(1, 0, 2)

    def grads(rank, rows):
        return ein("eks,esw->ekw", rank, rows).astype(BF16)

    def slot_row(share, slot):
        hot = slot[:, :, None, :] == jnp.arange(CAP, dtype=jnp.int32)[None, None, :, None]
        row = jnp.sum(jnp.where(hot, share[:, :, None, :], 0.0), axis=-1)
        return row.transpose(1, 0, 2).reshape(EXPERTS, 1, slots)

    scaled_f, scaled_a = select_f * slot_row(share_f, slot_f), select_a * slot_row(share_a, slot_a)
    width_grad = jnp.stack(
        [
            grads(spread(of_slots(live_f[:RANK]), select_f), rows_f_own),
            grads(spread(of_slots(live_f[RANK : 2 * RANK]), select_f), rows_f_own),
            grads(spread(of_slots(live_f[2 * RANK :]), scaled_f), rows_g_own),
        ],
        axis=1,
    )
    b_out_grad = grads(spread(of_slots(live_o), scaled_a), rows_ga_own)
    live_in = sum_small(live_in, n)
    live_kv = live_in[:, EXPERTS * slots :].reshape(RANK, 2, seq).transpose(1, 0, 2)
    a_in_grad = jnp.concatenate(
        [
            grads(spread(of_slots(live_in[:, : EXPERTS * slots]), select_a), rows_a_own),
            ein("pks,sw->pkw", spread(live_kv, select_row), normed_own_columns).astype(BF16),
        ]
    )

    def all_streams(g):
        mine = lax.axis_index("rep")
        out = lax.dynamic_update_slice_in_dim(jnp.zeros((reps,) + g.shape, g.dtype), g[None], mine, 0)
        for d in range(1, reps):
            got = lax.ppermute(g, "rep", [(i, i ^ d) for i in range(reps)])
            out = lax.dynamic_update_slice_in_dim(out, got[None], mine ^ d, 0)
        return out

    picks = jax.vmap(one_hot)(all_streams(docs_sent))
    hidden_out = ein("rpekf,rkc->pecf", lax.all_gather(hidden_grad, "rep"), picks)
    width_out = ein("rpmkw,rkc->pmwc", lax.all_gather(width_grad, "rep"), picks)
    early = all_streams(jnp.concatenate([a_out_grad, b_out_grad]))
    late_b, late_a = all_streams(b_in_grad), all_streams(a_in_grad)
    attn = jnp.concatenate([late_a, early[:, :EXPERTS], late_b, early[:, EXPERTS:]], axis=1)
    attn = attn.reshape(reps, 2, -1, k, own)
    attn_out = ein("rpmkw,rkc->pmwc", attn, picks)
    return (layer_out, grad_in, attn_out, width_out, hidden_out)


def solution(mesh):
    in_specs = (
        P(("rep", "shard"), None),
        P(("rep", "shard"), None),
        P(),
        P(),
        P(),
        P(None, "shard", None),
        P(None, "shard", None),
        P(None, "shard", None),
        P(None, None, None, "shard"),
        P(None, None, "shard", None),
        P(None, None, "shard", None),
        P(None, None, None, "shard"),
        P("rep", None),
        P("rep", None),
        P(("rep", "shard"), None),
        P(("rep", "shard"), None),
    )
    out_specs = (
        P(("rep", "shard"), None),
        P(("rep", "shard"), None),
        P(None, None, "shard", None),
        P(None, None, "shard", None),
        P(None, None, None, "shard"),
    )
    body = partial(local, mesh.shape["shard"], mesh.shape["rep"])
    return jax.shard_map(body, mesh=mesh, in_specs=in_specs, out_specs=out_specs, check_vma=False)
```

time: 1080 us -> 709 us (0.66)
  matrix products: 398 us -> 28.3 us
  Pallas kernels: 67.2 us -> 293 us
  local copies, waits for them, and re-layouts: 190 us -> 41.7 us
  starting transfers between devices: 117 us -> 74.6 us
  other arithmetic: 61 us -> 44.3 us
  between operations: 32.6 us -> 17.9 us
  blocking collectives: 11.8 us -> 0 us
    dot_general x61 -> x16, matrix products: 354 us -> 22.7 us  [ein(): return jnp.einsum(spec, a, b, preferred_element_type=F32)]
    pallas_call x2 -> x9, Pallas kernels: 67.2 us -> 293 us  [run(): return call(*args)]
    unnamed x431 -> x154, local copies, waits for them, and re-layouts: 76 us -> 6.4 us
    ppermute x131 -> x73, starting transfers between devices: 117 us -> 56 us  [swap(): return lax.ppermute(x, 'shard', [(i, i ^ d) for i in range(n)])]
    transpose x11 -> x2, local copies, waits for them, and re-layouts: 50 us -> 0.01 us  [slot_row(): return row.transpose(1, 0, 2).reshape(EXPERTS, 1, slots)]
    ppermute x0 -> x12, waiting for transfers between devices: none -> 37.4 us  [all_streams(): got = lax.ppermute(g, 'rep', [(i, i ^ d) for i in range(reps)])]
    dot_general x6 -> x0, matrix products: 33.3 us -> none  [the longest x4 29.6 us: dispatch(): jnp.einsum('mect,mtd->emcd', chosen.astype(BF16), tokens, preferred_eleme...]
    ppermute x131 -> x73, waiting for transfers between devices: 186 us -> 153 us  [swap(): return lax.ppermute(x, 'shard', [(i, i ^ d) for i in range(n)])]
  transfers between devices with their start and end apart: 134 -> 88, of which waited for: 53 -> 30; matrix products, arithmetic and copies ran while one was open for 44% -> 13% of each run, Pallas kernels for 6% -> 28%
where the time goes in v2:
time: 709 us; the launch traced here: 701 us
  Pallas kernels  293 us (41%)
  waiting for transfers between devices  202 us (28%)
  starting transfers between devices  74.6 us (11%)
  other arithmetic  44.3 us (6%)
  local copies, waits for them, and re-layouts  41.7 us (6%)
  matrix products  28.3 us (4%)
  between operations  17.9 us (3%)
    pallas_call x9, Pallas kernels, run(): return call(*args)  293 us
    ppermute x73, waiting for transfers between devices, swap(): return lax.ppermute(x, 'shard', [(i, i ^ d) for i in range(n)])  153 us
    ppermute x73, starting transfers between devices, swap(): return lax.ppermute(x, 'shard', [(i, i ^ d) for i in range(n)])  56 us
    ppermute x12, waiting for transfers between devices, all_streams(): got = lax.ppermute(g, 'rep', [(i, i ^ d) for i in range(reps)])  37.4 us
    dot_general x16, matrix products, ein(): return jnp.einsum(spec, a, b, preferred_element_type=F32)  22.7 us
    ppermute x12, starting transfers between devices, all_streams(): got = lax.ppermute(g, 'rep', [(i, i ^ d) for i in range(reps)])  18.4 us
  transfers between devices with their start and end apart: 88, of which 30 were waited for; matrix products, arithmetic and copies ran while one was open for 13% of the time, Pallas kernels for 28%

profile of v2, /device:TPU:0, one launch (start us, length us, event | category | flops | bytes accessed | tf_op | source)
XLA Modules:
  0.0 701.4 jit_solution(14798998008065608967)
XLA Ops:
  25.8 8.1 %collective-permute-done.3 = bf16[80,2048]{1,0:T(8,128)(2,1)} collective-permute-done((bf16[80,2048]{1,0:T(8,128)(2,1)}, bf16[80,2048]{1,0:T(8,128)(2,1)}, u32[]{:S(2)}, u32[]{:S(2)}) %collective-permute-start.3) | collective-permute-done | bytes 327712 | tf_op jit(solution)/shard_map/ppermute | solution.py:52
  45.7 19.0 %collective-permute-done.7 = bf16[96,2048]{1,0:T(8,128)(2,1)S(1)} collective-permute-done((bf16[96,2048]{1,0:T(8,128)(2,1)S(1)}, bf16[96,2048]{1,0:T(8,128)(2,1)S(1)}, u32[]{:S(2)}, u32[]{:S(2)}) %collective-permute-start.7) | collective-permute-done | bytes 393248 | tf_op jit(solution)/shard_map/ppermute | solution.py:52
  69.3 11.3 %collective-permute-done.11 = bf16[6,256,256]{2,1,0:T(8,128)(2,1)S(1)} collective-permute-done((bf16[6,256,256]{2,1,0:T(8,128)(2,1)S(1)}, bf16[6,256,256]{2,1,0:T(8,128)(2,1)S(1)}, u32[]{:S(2)}, u32[]{:S(2)}) %collective-permute-start.11) | collective-permute-done | bytes 786464 | tf_op jit(solution)/shard_map/ppermute | solution.py:52
  87.1 11.1 %collective-permute-done.12 = bf16[6,256,256]{2,1,0:T(8,128)(2,1)S(1)} collective-permute-done((bf16[6,256,256]{2,1,0:T(8,128)(2,1)S(1)}, bf16[6,256,256]{2,1,0:T(8,128)(2,1)S(1)}, u32[]{:S(2)}, u32[]{:S(2)}) %collective-permute-start.12) | collective-permute-done | bytes 786464 | tf_op jit(solution)/shard_map/ppermute | solution.py:52
  99.3 15.9 %collective-permute-done.13 = bf16[6,256,256]{2,1,0:T(8,128)(2,1)S(1)} collective-permute-done((bf16[6,256,256]{2,1,0:T(8,128)(2,1)S(1)}, bf16[6,256,256]{2,1,0:T(8,128)(2,1)S(1)}, u32[]{:S(2)}, u32[]{:S(2)}) %collective-permute-start.13) | collective-permute-done | bytes 786464 | tf_op jit(solution)/shard_map/ppermute | solution.py:52
  126.9 29.9 %qkv.1 = (bf16[4,640,256]{2,1,0:T(8,128)(2,1)}, bf16[2,1024,256]{2,1,0:T(8,128)(2,1)}, bf16[4,640,48]{2,1,0:T(8,128)(2,1)}, bf16[2,1024,48]{2,1,0:T(8,128)(2,1)}...) custom-call(s32[1]{0:T(128)} %bitcast.refs_0_, bf16[176,2048]{1,0:T(8,128)(2,1)} %copy-done.20, ...), custom_call_target="tpu_custom_call" | custom-call | flops 7247757312 | bytes 33554432 | tf_op jit(solution)/shard_map/qkv/pallas_call | solution.py:584
  162.9 28.6 %attend.1 = (bf16[4,8,80,256]{3,2,1,0:T(8,128)(2,1)}, f32[4,8,80,256]{3,2,1,0:T(8,128)}) custom-call(s32[8,4,128]{2,1,0:T(4,128)} %copy.169.key, s32[8,1,128]{2,1,0:T(1,128)} %bitcast.450, bf16[4,8,80,256]{3,2,1,0:T(8,128)(2,1)} %bitcast.476, bf16[1024,256]{1,0:T(8,128)(2,1)} %get-tuple-element.242.k, bf16[1024,256]{1,0:T(8,128)(2,1)} %get-tuple-element.241.v), custom_call_target="tpu_custom_call" | custom-call | flops 2013265920 | bytes 33554432 | tf_op jit(solution)/shard_map/attend/pallas_call | solution.py:584
  191.6 17.8 %attend_out.1 = (bf16[4,128,2048]{2,1,0:T(8,128)(2,1)}, bf16[4,128,2048]{2,1,0:T(8,128)(2,1)}, bf16[16,2560]{1,0:T(8,128)(2,1)}) custom-call(s32[1]{0:T(128)} %bitcast.refs_0_, bf16[96,2048]{1,0:T(8,128)(2,1)} %copy-done.11, bf16[96,2048]{1,0:T(8,128)(2,1)} %collective-permute-done.20.refs_2_.refs_10_, bf16[96,2048]{1,0:T(8,128)(2,1)} %copy-done.15, ...), custom_call_target="tpu_custom_call" | custom-call | flops 4026531840 | bytes 33554432 | tf_op jit(solution)/shard_map/attend_out/pallas_call | solution.py:584
  209.5 3.6 fusion.refs_20_.refs_22_.refs_13_
  223.5 27.7 %feed_down_back.1 = (f32[4,640,704]{2,1,0:T(8,128)}, bf16[4,640,48]{2,1,0:T(8,128)(2,1)}, bf16[4,640,256]{2,1,0:T(8,128)(2,1)}) custom-call(s32[1]{0:T(128)} %bitcast.refs_0_, bf16[128,2048]{1,0:T(8,128)(2,1)} %refs_1_, bf16[128,2048]{1,0:T(8,128)(2,1)} %copy-done.22, bf16[128,2048]{1,0:T(8,128)(2,1)} %collective-permute-done.24.refs_3_, ...), custom_call_target="tpu_custom_call" | custom-call | flops 9596567552 | bytes 33554432 | tf_op jit(solution)/shard_map/feed_down_back/pallas_call | solution.py:584
  259.2 11.0 %collective-permute-done.36.refs_3_ = bf16[128,2048]{1,0:T(8,128)(2,1)S(1)} collective-permute-done((bf16[128,2048]{1,0:T(8,128)(2,1)S(1)}, bf16[128,2048]{1,0:T(8,128)(2,1)S(1)}, u32[]{:S(2)}, u32[]{:S(2)}) %collective-permute-start.36) | collective-permute-done | bytes 524320 | tf_op jit(solution)/shard_map/ppermute | solution.py:52
  270.3 10.8 %collective-permute-done.38.refs_5_ = bf16[128,2048]{1,0:T(8,128)(2,1)} collective-permute-done((bf16[128,2048]{1,0:T(8,128)(2,1)S(1)}, bf16[128,2048]{1,0:T(8,128)(2,1)}, u32[]{:S(2)}, u32[]{:S(2)}) %collective-permute-start.38) | collective-permute-done | bytes 524320 | tf_op jit(solution)/shard_map/ppermute | solution.py:52
  291.5 77.7 %feed.1 = (bf16[512,2048]{1,0:T(8,128)(2,1)}, bf16[512,2048]{1,0:T(8,128)(2,1)}, bf16[4,640,704]{2,1,0:T(8,128)(2,1)}, bf16[32,2560]{1,0:T(8,128)(2,1)}, f32[8,2...) custom-call(s32[1]{0:T(128)} %bitcast.refs_0_, bf16[128,2048]{1,0:T(8,128)(2,1)} %copy-done.14, ...), custom_call_target="tpu_custom_call" | custom-call | flops 38386270208 | bytes 33554432 | tf_op jit(solution)/shard_map/feed/pallas_call | solution.py:584
  369.3 4.5 collective-permute-done.45
  373.8 5.2 fusion.94
  387.6 28.9 %feed_out.1 = (bf16[4,128,2048]{2,1,0:T(8,128)(2,1)}, bf16[4,128,2048]{2,1,0:T(8,128)(2,1)}, bf16[16,2560]{1,0:T(8,128)(2,1)}) custom-call(s32[1]{0:T(128)} %bitcast.refs_0_, bf16[96,2048]{1,0:T(8,128)(2,1)} %copy-done.11, bf16[96,2048]{1,0:T(8,128)(2,1)} %collective-permute-done.20.refs_2_.refs_10_, bf16[96,2048]{1,0:T(8,128)(2,1)} %copy-done.15, ...), custom_call_target="tpu_custom_call" | custom-call | flops 11072962560 | bytes 33554432 | tf_op jit(solution)/shard_map/feed_out/pallas_call | solution.py:584
  422.0 3.4 and_reduce_fusion
  439.1 7.1 %collective-permute-done.53.refs_3_ = bf16[128,2048]{1,0:T(8,128)(2,1)S(1)} collective-permute-done((bf16[128,2048]{1,0:T(8,128)(2,1)S(1)}, bf16[128,2048]{1,0:T(8,128)(2,1)S(1)}, u32[]{:S(2)}, u32[]{:S(2)}) %collective-permute-start.53) | collective-permute-done | bytes 524320 | tf_op jit(solution)/shard_map/ppermute | solution.py:52
  446.2 12.1 %collective-permute-done.54.refs_5_ = bf16[128,2048]{1,0:T(8,128)(2,1)S(1)} collective-permute-done((bf16[128,2048]{1,0:T(8,128)(2,1)S(1)}, bf16[128,2048]{1,0:T(8,128)(2,1)S(1)}, u32[]{:S(2)}, u32[]{:S(2)}) %collective-permute-start.54) | collective-permute-done | bytes 524320 | tf_op jit(solution)/shard_map/ppermute | solution.py:52
  475.2 21.4 %mixed_back.1 = (bf16[4,640,256]{2,1,0:T(8,128)(2,1)}, bf16[4,48,256]{2,1,0:T(8,128)(2,1)}, f32[8,2560]{1,0:T(8,128)}, bf16[4,640,256]{2,1,0:T(8,128)(2,1)}) custom-call(s32[1]{0:T(128)} %bitcast.refs_0_, bf16[128,2048]{1,0:T(8,128)(2,1)} %copy-done.25, bf16[128,2048]{1,0:T(8,128)(2,1)} %collective-permute-done.56.refs_2_, bf16[128,2048]{1,0:T(8,128)(2,1)} %copy-done.63, ...), custom_call_target="tpu_custom_call" | custom-call | flops 4026531840 | bytes 33554432 | tf_op jit(solution)/shard_map/mixed_back/pallas_call | solution.py:584
  496.6 33.8 %attend_back.1 = (f32[4,8,80,256]{3,2,1,0:T(8,128)}, f32[1024,256]{1,0:T(8,128)}, f32[1024,256]{1,0:T(8,128)}) custom-call(s32[8,4,128]{2,1,0:T(4,128)} %copy.169.key, s32[8,1,128]{2,1,0:T(1,128)} %bitcast.451, bf16[4,8,80,256]{3,2,1,0:T(8,128)(2,1)} %bitcast.477, bf16[4,8,80,256]{3,2,1,0:T(8,128)(2,1)} %bitcast.480, ...), custom_call_target="tpu_custom_call" | custom-call | flops 4697620480 | bytes 33554432 | tf_op jit(solution)/shard_map/attend_back/pallas_call | solution.py:584
  533.7 26.7 %qkv_back.1 = (bf16[4,128,2048]{2,1,0:T(8,128)(2,1)}, bf16[4,128,2048]{2,1,0:T(8,128)(2,1)}, bf16[16,4608]{1,0:T(8,128)(2,1)}, bf16[6,48,256]{2,1,0:T(8,128)(2,1)}) custom-call(s32[1]{0:T(128)} %bitcast.refs_0_, bf16[176,2048]{1,0:T(8,128)(2,1)} %copy-done.20, bf16[176,2048]{1,0:T(8,128)(2,1)} %collective-permute-done.refs_2_, bf16[176,2048]{1,0:T(8,128)(2,1)} %copy-done.29, ...), custom_call_target="tpu_custom_call" | custom-call | flops 7247757312 | bytes 33554432 | tf_op jit(solution)/shard_map/qkv_back/pallas_call | solution.py:584
  566.4 6.0 convolution_bitcast_fusion
  572.4 3.2 collective-permute-start.77
  578.4 22.2 %collective-permute-done.77 = bf16[8,48,256]{2,1,0:T(8,128)(2,1)S(1)} collective-permute-done((bf16[8,48,256]{2,1,0:T(8,128)(2,1)S(1)}, bf16[8,48,256]{2,1,0:T(8,128)(2,1)S(1)}, u32[]{:S(2)}, u32[]{:S(2)}) %collective-permute-start.77) | collective-permute-done | bytes 196640 | tf_op jit(solution)/shard_map/ppermute | solution.py:1022
  600.7 11.8 %all-gather.5.cloned.1.call-done = bf16[16,3,48,256]{3,2,0,1:T(8,128)(2,1)} async-done(((bf16[4,3,48,256]{3,2,0,1:T(8,128)(2,1)}), bf16[16,3,48,256]{3,2,0,1:T(8,128)(2,1)}) %all-gather.5.cloned.1.call-update) | async-done | bytes 1179664 | tf_op jit(solution)/shard_map/all_gather | solution.py:1028
  615.7 4.6 fusion.93
  628.9 6.5 collective-permute-done.80
  636.7 3.6 collective-permute-done.68
  647.9 6.3 collective-permute-done.71
  656.3 13.2 %collective-permute-done.72 = bf16[16,4608]{1,0:T(8,128)(2,1)S(1)} collective-permute-done((bf16[16,4608]{1,0:T(8,128)(2,1)S(1)}, bf16[16,4608]{1,0:T(8,128)(2,1)S(1)}, u32[]{:S(2)}, u32[]{:S(2)}) %collective-permute-start.72) | collective-permute-done | bytes 147488 | tf_op jit(solution)/shard_map/ppermute | solution.py:52
  669.5 3.4 collective-permute-start.66
  (517 shorter events, 187.0 us)
Async XLA Ops:
  8.1 522.3 %all-reduce.4.cloned.1.call-start = ((), (), s32[]{:S(2)}) async-start(), calls=%async_computation.2 | async-start | bytes 655360 | tf_op jit(solution)/shard_map/psum | solution.py:969
  36.2 32.3 %collective-permute-start.10 = (bf16[6,256,256]{2,1,0:T(8,128)(2,1)S(1)}, bf16[6,256,256]{2,1,0:T(8,128)(2,1)S(1)}, u32[]{:S(2)}, u32[]{:S(2)}) collective-permute-start(bf16[6,256,256]{2,1,0:T(8,128)(2,1)S(1)} %pad_maximum_fusion.3), channel_id=1, source_target_pairs={{0,7},{1,6},{2,5},{3,4},{4,3},{5,2},{6,1},{7,0},{8,15},{9,14},{10,... | collective-permute-start | bytes 2359304 | tf_op jit(solution)/shard_map/ppermute | solution.py:52
  41.0 39.7 %collective-permute-start.11 = (bf16[6,256,256]{2,1,0:T(8,128)(2,1)S(1)}, bf16[6,256,256]{2,1,0:T(8,128)(2,1)S(1)}, u32[]{:S(2)}, u32[]{:S(2)}) collective-permute-start(bf16[6,256,256]{2,1,0:T(8,128)(2,1)S(1)} %pad_maximum_fusion.4), channel_id=1, source_target_pairs={{0,6},{1,7},{2,4},{3,5},{4,2},{5,3},{6,0},{7,1},{8,14},{9,15},{10,... | collective-permute-start | bytes 2359304 | tf_op jit(solution)/shard_map/ppermute | solution.py:52
  64.7 33.5 %collective-permute-start.12 = (bf16[6,256,256]{2,1,0:T(8,128)(2,1)S(1)}, bf16[6,256,256]{2,1,0:T(8,128)(2,1)S(1)}, u32[]{:S(2)}, u32[]{:S(2)}) collective-permute-start(bf16[6,256,256]{2,1,0:T(8,128)(2,1)S(1)} %pad_maximum_fusion.5), channel_id=1, source_target_pairs={{0,5},{1,4},{2,7},{3,6},{4,1},{5,0},{6,3},{7,2},{8,13},{9,12},{10,... | collective-permute-start | bytes 2359304 | tf_op jit(solution)/shard_map/ppermute | solution.py:52
  65.6 49.5 %collective-permute-start.13 = (bf16[6,256,256]{2,1,0:T(8,128)(2,1)S(1)}, bf16[6,256,256]{2,1,0:T(8,128)(2,1)S(1)}, u32[]{:S(2)}, u32[]{:S(2)}) collective-permute-start(bf16[6,256,256]{2,1,0:T(8,128)(2,1)S(1)} %pad_maximum_fusion.6), channel_id=1, source_target_pairs={{0,4},{1,5},{2,6},{3,7},{4,0},{5,1},{6,2},{7,3},{8,12},{9,13},{10,... | collective-permute-start | bytes 2359304 | tf_op jit(solution)/shard_map/ppermute | solution.py:52
  67.0 49.0 %collective-permute-start.14 = (bf16[6,256,256]{2,1,0:T(8,128)(2,1)S(1)}, bf16[6,256,256]{2,1,0:T(8,128)(2,1)S(1)}, u32[]{:S(2)}, u32[]{:S(2)}) collective-permute-start(bf16[6,256,256]{2,1,0:T(8,128)(2,1)S(1)} %pad_maximum_fusion.7), channel_id=1, source_target_pairs={{0,3},{1,2},{2,1},{3,0},{4,7},{5,6},{6,5},{7,4},{8,11},{9,10},{10,... | collective-permute-start | bytes 2359304 | tf_op jit(solution)/shard_map/ppermute | solution.py:52
  68.5 48.6 %collective-permute-start.15 = (bf16[6,256,256]{2,1,0:T(8,128)(2,1)S(1)}, bf16[6,256,256]{2,1,0:T(8,128)(2,1)S(1)}, u32[]{:S(2)}, u32[]{:S(2)}) collective-permute-start(bf16[6,256,256]{2,1,0:T(8,128)(2,1)S(1)} %pad_maximum_fusion.8), channel_id=1, source_target_pairs={{0,2},{1,3},{2,0},{3,1},{4,6},{5,7},{6,4},{7,5},{8,10},{9,11},{10,... | collective-permute-start | bytes 2359304 | tf_op jit(solution)/shard_map/ppermute | solution.py:52
  80.6 37.3 %collective-permute-start.16 = (bf16[6,256,256]{2,1,0:T(8,128)(2,1)S(1)}, bf16[6,256,256]{2,1,0:T(8,128)(2,1)S(1)}, u32[]{:S(2)}, u32[]{:S(2)}) collective-permute-start(bf16[6,256,256]{2,1,0:T(8,128)(2,1)S(1)} %pad_maximum_fusion.9), channel_id=1, source_target_pairs={{0,1},{1,0},{2,3},{3,2},{4,5},{5,4},{6,7},{7,6},{8,9},{9,8},{10,11... | collective-permute-start | bytes 2359304 | tf_op jit(solution)/shard_map/ppermute | solution.py:52
  119.9 39.2 %collective-permute-start.17 = (bf16[96,2048]{1,0:T(8,128)(2,1)S(1)}, bf16[96,2048]{1,0:T(8,128)(2,1)S(1)}, u32[]{:S(2)}, u32[]{:S(2)}) collective-permute-start(bf16[96,2048]{1,0:T(8,128)(2,1)S(1)} %pad_maximum_fusion.10.refs_1_.refs_9_), channel_id=1, source_target_pairs={{0,2},{1,3},{2,0},{3,1},{4,6},{5,7},{6,4},{7,5},{8,10},{9,11},{10,... | collective-permute-start | bytes 1179656 | tf_op jit(solution)/shard_map/ppermute | solution.py:52
  121.1 40.1 %collective-permute-start.18 = (bf16[96,2048]{1,0:T(8,128)(2,1)S(1)}, bf16[96,2048]{1,0:T(8,128)(2,1)}, u32[]{:S(2)}, u32[]{:S(2)}) collective-permute-start(bf16[96,2048]{1,0:T(8,128)(2,1)S(1)} %pad_maximum_fusion.10.refs_1_.refs_9_), channel_id=1, source_target_pairs={{0,4},{1,5},{2,6},{3,7},{4,0},{5,1},{6,2},{7,3},{8,12},{9,13},{10,... | collective-permute-start | bytes 1179656 | tf_op jit(solution)/shard_map/ppermute | solution.py:52
  121.9 39.2 %collective-permute-start.19 = (bf16[96,2048]{1,0:T(8,128)(2,1)S(1)}, bf16[96,2048]{1,0:T(8,128)(2,1)}, u32[]{:S(2)}, u32[]{:S(2)}) collective-permute-start(bf16[96,2048]{1,0:T(8,128)(2,1)S(1)} %pad_maximum_fusion.10.refs_1_.refs_9_), channel_id=1, source_target_pairs={{0,6},{1,7},{2,4},{3,5},{4,2},{5,3},{6,0},{7,1},{8,14},{9,15},{10,... | collective-permute-start | bytes 1179656 | tf_op jit(solution)/shard_map/ppermute | solution.py:52
  123.4 38.4 %collective-permute-start.24 = (bf16[128,2048]{1,0:T(8,128)(2,1)S(1)}, bf16[128,2048]{1,0:T(8,128)(2,1)}, u32[]{:S(2)}, u32[]{:S(2)}) collective-permute-start(bf16[128,2048]{1,0:T(8,128)(2,1)S(1)} %copy-done.6), channel_id=1, source_target_pairs={{0,2},{1,3},{2,0},{3,1},{4,6},{5,7},{6,4},{7,5},{8,10},{9,11},{10,... | collective-permute-start | bytes 1572872 | tf_op jit(solution)/shard_map/ppermute | solution.py:52
  124.6 37.2 %collective-permute-start.25 = (bf16[128,2048]{1,0:T(8,128)(2,1)S(1)}, bf16[128,2048]{1,0:T(8,128)(2,1)}, u32[]{:S(2)}, u32[]{:S(2)}) collective-permute-start(bf16[128,2048]{1,0:T(8,128)(2,1)S(1)} %copy-done.6), channel_id=1, source_target_pairs={{0,4},{1,5},{2,6},{3,7},{4,0},{5,1},{6,2},{7,3},{8,12},{9,13},{10,... | collective-permute-start | bytes 1572872 | tf_op jit(solution)/shard_map/ppermute | solution.py:52
  159.1 32.4 %collective-permute-start.26 = (bf16[128,2048]{1,0:T(8,128)(2,1)S(1)}, bf16[128,2048]{1,0:T(8,128)(2,1)}, u32[]{:S(2)}, u32[]{:S(2)}) collective-permute-start(bf16[128,2048]{1,0:T(8,128)(2,1)S(1)} %copy-done.6), channel_id=1, source_target_pairs={{0,6},{1,7},{2,4},{3,5},{4,2},{5,3},{6,0},{7,1},{8,14},{9,15},{10,... | collective-permute-start | bytes 1572872 | tf_op jit(solution)/shard_map/ppermute | solution.py:52
  161.2 30.3 %collective-permute-start.20 = (bf16[96,2048]{1,0:T(8,128)(2,1)S(1)}, bf16[96,2048]{1,0:T(8,128)(2,1)}, u32[]{:S(2)}, u32[]{:S(2)}) collective-permute-start(bf16[96,2048]{1,0:T(8,128)(2,1)S(1)} %pad_maximum_fusion.10.refs_1_.refs_9_), channel_id=1, source_target_pairs={{0,1},{1,0},{2,3},{3,2},{4,5},{5,4},{6,7},{7,6},{8,9},{9,8},{10,11... | collective-permute-start | bytes 1179656 | tf_op jit(solution)/shard_map/ppermute | solution.py:52
  161.2 30.3 %collective-permute-start.21 = (bf16[96,2048]{1,0:T(8,128)(2,1)S(1)}, bf16[96,2048]{1,0:T(8,128)(2,1)}, u32[]{:S(2)}, u32[]{:S(2)}) collective-permute-start(bf16[96,2048]{1,0:T(8,128)(2,1)S(1)} %collective-permute-done.17.refs_3_.refs_11_), channel_id=1, source_target_pairs={{0,1},{1,0},{2,3},{3,2},{4,5},{5,4},{6,7},{7,6},{8,9},{9,8},{10,11... | collective-permute-start | bytes 1179656 | tf_op jit(solution)/shard_map/ppermute | solution.py:52
  161.7 29.8 %collective-permute-start.22 = (bf16[96,2048]{1,0:T(8,128)(2,1)}, bf16[96,2048]{1,0:T(8,128)(2,1)}, u32[]{:S(2)}, u32[]{:S(2)}) collective-permute-start(bf16[96,2048]{1,0:T(8,128)(2,1)} %collective-permute-done.18.refs_5_.refs_13_), channel_id=1, source_target_pairs={{0,1},{1,0},{2,3},{3,2},{4,5},{5,4},{6,7},{7,6},{8,9},{9,8},{10,11... | collective-permute-start | bytes 1179656 | tf_op jit(solution)/shard_map/ppermute | solution.py:52
  161.8 29.7 %collective-permute-start.23 = (bf16[96,2048]{1,0:T(8,128)(2,1)}, bf16[96,2048]{1,0:T(8,128)(2,1)}, u32[]{:S(2)}, u32[]{:S(2)}) collective-permute-start(bf16[96,2048]{1,0:T(8,128)(2,1)} %collective-permute-done.19.refs_7_.refs_15_), channel_id=1, source_target_pairs={{0,1},{1,0},{2,3},{3,2},{4,5},{5,4},{6,7},{7,6},{8,9},{9,8},{10,11... | collective-permute-start | bytes 1179656 | tf_op jit(solution)/shard_map/ppermute | solution.py:52
  219.2 33.3 %collective-permute-start.32 = (bf16[128,2048]{1,0:T(8,128)(2,1)}, bf16[128,2048]{1,0:T(8,128)(2,1)}, u32[]{:S(2)}, u32[]{:S(2)}) collective-permute-start(bf16[128,2048]{1,0:T(8,128)(2,1)} %get-tuple-element.130), channel_id=1, source_target_pairs={{0,2},{1,3},{2,0},{3,1},{4,6},{5,7},{6,4},{7,5},{8,10},{9,11},{10,... | collective-permute-start | bytes 1572872 | tf_op jit(solution)/shard_map/ppermute | solution.py:52
  221.1 31.4 %collective-permute-start.33 = (bf16[128,2048]{1,0:T(8,128)(2,1)}, bf16[128,2048]{1,0:T(8,128)(2,1)S(1)}, u32[]{:S(2)}, u32[]{:S(2)}) collective-permute-start(bf16[128,2048]{1,0:T(8,128)(2,1)} %get-tuple-element.131), channel_id=1, source_target_pairs={{0,4},{1,5},{2,6},{3,7},{4,0},{5,1},{6,2},{7,3},{8,12},{9,13},{10,... | collective-permute-start | bytes 1572872 | tf_op jit(solution)/shard_map/ppermute | solution.py:52
  222.0 31.3 %collective-permute-start.34 = (bf16[128,2048]{1,0:T(8,128)(2,1)}, bf16[128,2048]{1,0:T(8,128)(2,1)}, u32[]{:S(2)}, u32[]{:S(2)}) collective-permute-start(bf16[128,2048]{1,0:T(8,128)(2,1)} %get-tuple-element.132), channel_id=1, source_target_pairs={{0,6},{1,7},{2,4},{3,5},{4,2},{5,3},{6,0},{7,1},{8,14},{9,15},{10,... | collective-permute-start | bytes 1572872 | tf_op jit(solution)/shard_map/ppermute | solution.py:52
  258.9 32.6 %collective-permute-start.35 = (bf16[128,2048]{1,0:T(8,128)(2,1)S(1)}, bf16[128,2048]{1,0:T(8,128)(2,1)}, u32[]{:S(2)}, u32[]{:S(2)}) collective-permute-start(bf16[128,2048]{1,0:T(8,128)(2,1)S(1)} %multiply_convert_fusion.refs_1_), channel_id=1, source_target_pairs={{0,1},{1,0},{2,3},{3,2},{4,5},{5,4},{6,7},{7,6},{8,9},{9,8},{10,11... | collective-permute-start | bytes 1572872 | tf_op jit(solution)/shard_map/ppermute | solution.py:52
  382.4 34.4 %collective-permute-start.46 = (bf16[128,2048]{1,0:T(8,128)(2,1)}, bf16[128,2048]{1,0:T(8,128)(2,1)}, u32[]{:S(2)}, u32[]{:S(2)}) collective-permute-start(bf16[128,2048]{1,0:T(8,128)(2,1)} %get-tuple-element.139), channel_id=1, source_target_pairs={{0,2},{1,3},{2,0},{3,1},{4,6},{5,7},{6,4},{7,5},{8,10},{9,11},{10,... | collective-permute-start | bytes 1572872 | tf_op jit(solution)/shard_map/ppermute | solution.py:52
  383.6 33.2 %collective-permute-start.47 = (bf16[128,2048]{1,0:T(8,128)(2,1)}, bf16[128,2048]{1,0:T(8,128)(2,1)}, u32[]{:S(2)}, u32[]{:S(2)}) collective-permute-start(bf16[128,2048]{1,0:T(8,128)(2,1)} %get-tuple-element.140), channel_id=1, source_target_pairs={{0,4},{1,5},{2,6},{3,7},{4,0},{5,1},{6,2},{7,3},{8,12},{9,13},{10,... | collective-permute-start | bytes 1572872 | tf_op jit(solution)/shard_map/ppermute | solution.py:52
  384.5 32.4 %collective-permute-start.48 = (bf16[128,2048]{1,0:T(8,128)(2,1)}, bf16[128,2048]{1,0:T(8,128)(2,1)}, u32[]{:S(2)}, u32[]{:S(2)}) collective-permute-start(bf16[128,2048]{1,0:T(8,128)(2,1)} %get-tuple-element.141), channel_id=1, source_target_pairs={{0,6},{1,7},{2,4},{3,5},{4,2},{5,3},{6,0},{7,1},{8,14},{9,15},{10,... | collective-permute-start | bytes 1572872 | tf_op jit(solution)/shard_map/ppermute | solution.py:52
  427.1 139.3 %all-gather.7.cloned.1.call-start = ((), (), s32[]{:S(2)}) async-start(), calls=%async_computation.1 | async-start | bytes 4423680 | tf_op jit(solution)/shard_map/all_gather | solution.py:1027
  430.0 182.4 %all-gather.5.cloned.1.call-start = ((), (), s32[]{:S(2)}) async-start(), calls=%async_computation | async-start | bytes 1474560 | tf_op jit(solution)/shard_map/all_gather | solution.py:1028
  560.5 55.2 %collective-permute-start.63 = (bf16[4,128,2048]{2,1,0:T(8,128)(2,1)}, bf16[4,128,2048]{2,1,0:T(8,128)(2,1)}, u32[]{:S(2)}, u32[]{:S(2)}) collective-permute-start(bf16[4,128,2048]{2,1,0:T(8,128)(2,1)} %get-tuple-element.173), channel_id=1, source_target_pairs={{0,1},{1,0},{2,3},{3,2},{4,5},{5,4},{6,7},{7,6},{8,9},{9,8},{10,11... | collective-permute-start | bytes 6291464 | tf_op jit(solution)/shard_map/ppermute | solution.py:52
  576.7 106.6 %collective-permute-start.60 = (bf16[128,2048]{1,0:T(8,128)(2,1)}, bf16[128,2048]{1,0:T(8,128)(2,1)}, u32[]{:S(2)}, u32[]{:S(2)}) collective-permute-start(bf16[128,2048]{1,0:T(8,128)(2,1)} %get-tuple-element.158), channel_id=1, source_target_pairs={{0,2},{1,3},{2,0},{3,1},{4,6},{5,7},{6,4},{7,5},{8,10},{9,11},{10,... | collective-permute-start | bytes 1572872 | tf_op jit(solution)/shard_map/ppermute | solution.py:52
  576.8 108.3 %collective-permute-start.61 = (bf16[128,2048]{1,0:T(8,128)(2,1)}, bf16[128,2048]{1,0:T(8,128)(2,1)}, u32[]{:S(2)}, u32[]{:S(2)}) collective-permute-start(bf16[128,2048]{1,0:T(8,128)(2,1)} %get-tuple-element.159), channel_id=1, source_target_pairs={{0,4},{1,5},{2,6},{3,7},{4,0},{5,1},{6,2},{7,3},{8,12},{9,13},{10,... | collective-permute-start | bytes 1572872 | tf_op jit(solution)/shard_map/ppermute | solution.py:52
  640.3 37.2 %collective-permute-start.64 = (bf16[128,2048]{1,0:T(8,128)(2,1)}, bf16[128,2048]{1,0:T(8,128)(2,1)}, u32[]{:S(2)}, u32[]{:S(2)}) collective-permute-start(bf16[128,2048]{1,0:T(8,128)(2,1)} %get-tuple-element.177), channel_id=1, source_target_pairs={{0,2},{1,3},{2,0},{3,1},{4,6},{5,7},{6,4},{7,5},{8,10},{9,11},{10,... | collective-permute-start | bytes 1572872 | tf_op jit(solution)/shard_map/ppermute | solution.py:52
  642.7 34.9 %collective-permute-start.65 = (bf16[128,2048]{1,0:T(8,128)(2,1)}, bf16[128,2048]{1,0:T(8,128)(2,1)}, u32[]{:S(2)}, u32[]{:S(2)}) collective-permute-start(bf16[128,2048]{1,0:T(8,128)(2,1)} %get-tuple-element.178), channel_id=1, source_target_pairs={{0,4},{1,5},{2,6},{3,7},{4,0},{5,1},{6,2},{7,3},{8,12},{9,13},{10,... | collective-permute-start | bytes 1572872 | tf_op jit(solution)/shard_map/ppermute | solution.py:52
  (122 other events, 1554.5 us)
Sparse Core Ops, SparseCore 0:
  427.2 61.3 all-reduce.3
Sparse Core Ops, SparseCore 1:
  430.1 70.5 all-gather.6
  565.2 47.2 all-gather.4

commit v3 on v2

--- a/solution.py
+++ b/solution.py
@@ -66,11 +66,9 @@
 
 
 def gather_small(x, me, n):
-    out, d = x[None], 1
-    while d < n:
-        out = jnp.concatenate([out, swap(out, n, d)])
-        d *= 2
-    return out[jnp.arange(n) ^ me]
+    mine = jnp.stack(list(across(x, n).values()))
+    mask = jnp.arange(n) ^ me
+    return jnp.concatenate([mine, swap(mine, n, 1)])[mask // 2 + mask % 2 * (n // 2)]
 
 
 def sum_small(x, n):
@@ -84,6 +82,27 @@
 def halve(near, far, n):
     q = near.astype(F32) + swap(far, n, 1).astype(F32)
     return q[0], [q[i].astype(BF16) for i in range(1, n // 2)]
+
+
+def added(parts):
+    return sum([part.astype(F32) for part in parts[1:]], parts[0].astype(F32))
+
+
+def quarter(near, far, n):
+    q = near.astype(F32) + swap(far, n, 1).astype(F32)
+    cut = q.shape[1] // 2
+    qa, qb = q[:, :cut], q[:, cut:]
+    sent = [jnp.stack([qa[1], qa[3]]).astype(BF16), jnp.stack([qb[2], qb[3]]).astype(BF16)]
+    return [qa[0], qa[2], qb[0], qb[1]], sent
+
+
+def collect_quarters(kept, got, n):
+    a0, a2, b0, b1 = kept
+    ra, rb = got[0].astype(F32), got[1].astype(F32)
+    a2, b1 = (a2 + ra[1]).astype(BF16), (b1 + rb[1]).astype(BF16)
+    a0 = a0 + ra[0] + swap(a2, n, 4).astype(F32)
+    b0 = b0 + rb[0] + swap(b1, n, 2).astype(F32)
+    return jnp.concatenate([a0, b0])
 
 
 def collect(total, low, n):
@@ -205,13 +224,20 @@
 
 def qkv_kernel(n, *refs):
     me, xs, refs = refs[0], refs[1 : 1 + n], refs[1 + n :]
-    key, select_tok, hi, lo, w, b_in, q, kv, rank_q, rank_kv, rows_own, tok_own, a_in, *refs = refs
+    key, select_tok, hi, lo, w, b_in, q, kv, rank_q, rank_kv, rows_own, tok_own, a_in, wide_w, *refs = refs
     hot, rows, sel, table = refs
     i = pl.program_id(0)
-    tok, k = hi.shape[1], b_in.shape[0]
+    tok, k, slots = hi.shape[1], b_in.shape[0], hot.shape[0]
     own = w.shape[1]
     mine = pl.ds(pl.multiple_of(me[0] * own, own), own)
-    fill_map(me, xs, i, a_in)
+
+    @pl.when(i == 0)
+    def start():
+        a_in[...] = jnp.zeros(a_in.shape, BF16)
+
+    fill_map(me, xs, i, a_in.at[:k])
+    wide_w[:, :own] = w[...]
+    wide_w[:, own:] = a_in[...].T
 
     @pl.when(i < EXPERTS)
     def query():
@@ -221,11 +247,12 @@
         for b in range(n):
             here = pl.ds(b * CAP, CAP)
             table[here, :] = dot_nn(hot[here, :], hi[b]) + dot_nn(hot[here, :], lo[b])
-        rank = (dot_nt(rows[...], a_in[...]) * sel[...]).astype(BF16)
+        both = dot_nn(rows[:slots, :], wide_w[...])
+        rank = (both[:, own : own + k] * sel[:slots, :]).astype(BF16)
         rank_q[...] = rank
-        pre = dot_nn(rows[...], w[...]) + dot_nn(rank, b_in[...])
-        q[...] = turn_heads(pre, table[...], 1.0).astype(BF16)
-        rows_own[...] = rows[:, mine]
+        pre = both[:, :own] + dot_nn(rank, b_in[...])
+        q[...] = turn_heads(pre, table[:slots, :], 1.0).astype(BF16)
+        rows_own[...] = rows[:slots, mine]
 
     @pl.when(i >= EXPERTS)
     def key_value():
@@ -239,8 +266,9 @@
                 rows[here, :] = xs[m][pl.ds(k, tok), :]
                 sel[here, :] = select_tok[b].astype(F32)
                 table[here, :] = hi[b].astype(F32) + lo[b].astype(F32)
-            rank = (dot_nt(rows[some, :], a_in[...]) * sel[some, :]).astype(BF16)
-            pre = dot_nn(rows[some, :], w[...]) + dot_nn(rank, b_in[...])
+            both = dot_nn(rows[some, :], wide_w[...])
+            rank = (both[:, own : own + k] * sel[some, :]).astype(BF16)
+            pre = both[:, :own] + dot_nn(rank, b_in[...])
             turned = turn_heads(pre, table[some, :], 1.0)
             done = jnp.where(i == EXPERTS, turned, pre).astype(BF16)
             for j in range(group):
@@ -251,10 +279,8 @@
                 tok_own[there, :] = rows[here, mine]
 
 
-def attend_kernel(key, begin, q, k, v, mixed, lse, scores, mx, tot, acc):
-    b = pl.program_id(1)
+def limits(key, begin, b):
     tok = begin.shape[1]
-    rows = q.shape[0] * q.shape[1]
     slot = lax.broadcasted_iota(jnp.int32, (CAP, tok), 0)
     token = b * tok + lax.broadcasted_iota(jnp.int32, (CAP, tok), 1)
     first, last = [], []
@@ -262,41 +288,55 @@
         chosen = slot == key[e : e + 1, :]
         first.append(jnp.sum(jnp.where(chosen, begin[...], 0), axis=1, keepdims=True))
         last.append(jnp.sum(jnp.where(chosen, token, 0), axis=1, keepdims=True))
-    first, last = jnp.concatenate(first), jnp.concatenate(last)
-    query = q[...].reshape(rows, HD)
+    return jnp.concatenate(first), jnp.concatenate(last)
+
+
+def attend_kernel(key, begin, q, k, v, mixed, lse, scores, mx, tot, acc):
+    b = pl.program_id(0)
+    tok, own = begin.shape[1], q.shape[2]
+    rows = q.shape[0] * q.shape[1]
+    first, last = limits(key, begin, b)
+    query = q[...].reshape(rows, own)
+    heads = [slice(h, h + HD) for h in range(0, own, HD)]
     count = (b * tok + tok + CHUNK - 1) // CHUNK
     mx[...] = jnp.full(mx.shape, NEG, F32)
 
     def score(j, carry):
         start = pl.multiple_of(j * CHUNK, CHUNK)
-        s = dot_nt(query, k[pl.ds(start, CHUNK), :]) * HD ** (-0.5)
-        at = start + lax.broadcasted_iota(jnp.int32, s.shape, 1)
-        s = jnp.where((at >= first) & (at <= last), s, NEG)
-        scores[:, pl.ds(start, CHUNK)] = s
-        mx[...] = jnp.maximum(mx[...], jnp.maximum(s[:, :HD], s[:, HD:]))
+        here = pl.ds(start, CHUNK)
+        at = start + lax.broadcasted_iota(jnp.int32, (rows, CHUNK), 1)
+        seen = (at >= first) & (at <= last)
+        raw = [dot_nt(query[:, h], k[here, h]) for h in heads]
+        for i, h in enumerate(heads):
+            s = jnp.where(seen, raw[i] * HD ** (-0.5), NEG)
+            scores[i, :, here] = s
+            mx[:, h] = jnp.maximum(mx[:, h], jnp.maximum(s[:, :HD], s[:, HD:]))
         return carry
 
     lax.fori_loop(0, count, score, 0)
-    top = jnp.max(mx[...], axis=1, keepdims=True)
+    top = [jnp.max(mx[:, h], axis=1, keepdims=True) for h in heads]
     tot[...] = jnp.zeros(tot.shape, F32)
     acc[...] = jnp.zeros(acc.shape, F32)
 
     def mix(j, carry):
-        start = pl.multiple_of(j * CHUNK, CHUNK)
-        p = jnp.exp(scores[:, pl.ds(start, CHUNK)] - top)
-        tot[...] += p[:, :HD] + p[:, HD:]
-        acc[...] += dot_nn(p.astype(BF16), v[pl.ds(start, CHUNK), :])
+        here = pl.ds(pl.multiple_of(j * CHUNK, CHUNK), CHUNK)
+        for i, h in enumerate(heads):
+            p = jnp.exp(scores[i, :, here] - top[i])
+            tot[:, h] += p[:, :HD] + p[:, HD:]
+            acc[:, h] += dot_nn(p.astype(BF16), v[here, h])
         return carry
 
     lax.fori_loop(0, count, mix, 0)
-    total = jnp.sum(tot[...], axis=1, keepdims=True)
-    mixed[...] = (acc[...] / total).astype(BF16).reshape(mixed.shape)
-    lse[...] = jnp.broadcast_to(top + jnp.log(total), (rows, HD)).reshape(lse.shape)
+    for i, h in enumerate(heads):
+        total = jnp.sum(tot[:, h], axis=1, keepdims=True)
+        mixed[:, :, h] = (acc[:, h] / total).astype(BF16).reshape(EXPERTS, CAP, HD)
+        spread = jnp.broadcast_to(top[i] + jnp.log(total), (rows, HD))
+        lse[:, :, h] = spread.reshape(EXPERTS, CAP, HD)
 
 
 def attend_back_kernel(key, begin, q, g, mixed, lse, k, v, gq, gk, gv, dq):
-    b = pl.program_id(1)
-    tok = begin.shape[1]
+    b = pl.program_id(0)
+    tok, own = begin.shape[1], q.shape[2]
     rows = q.shape[0] * q.shape[1]
     scale = HD ** (-0.5)
 
@@ -305,36 +345,33 @@
         gk[...] = jnp.zeros(gk.shape, F32)
         gv[...] = jnp.zeros(gv.shape, F32)
 
-    slot = lax.broadcasted_iota(jnp.int32, (CAP, tok), 0)
-    token = b * tok + lax.broadcasted_iota(jnp.int32, (CAP, tok), 1)
-    first, last = [], []
-    for e in range(EXPERTS):
-        chosen = slot == key[e : e + 1, :]
-        first.append(jnp.sum(jnp.where(chosen, begin[...], 0), axis=1, keepdims=True))
-        last.append(jnp.sum(jnp.where(chosen, token, 0), axis=1, keepdims=True))
-    first, last = jnp.concatenate(first), jnp.concatenate(last)
+    first, last = limits(key, begin, b)
 
     def flat(r):
-        return r[...].reshape(rows, HD)
+        return r[...].reshape(rows, own)
 
     query, grad = flat(q), flat(g)
-    delta = jnp.sum(flat(mixed).astype(F32) * grad.astype(F32), axis=1, keepdims=True)
-    log_total = flat(lse)[:, :1]
+    heads = [slice(h, h + HD) for h in range(0, own, HD)]
+    product = flat(mixed).astype(F32) * grad.astype(F32)
+    delta = [jnp.sum(product[:, h], axis=1, keepdims=True) for h in heads]
+    logs = flat(lse)
+    log_total = [logs[:, h.start : h.start + 1] for h in heads]
     count = (b * tok + tok + CHUNK - 1) // CHUNK
     dq[...] = jnp.zeros(dq.shape, F32)
 
     def step(j, carry):
         begin_at = pl.multiple_of(j * CHUNK, CHUNK)
         here = pl.ds(begin_at, CHUNK)
-        kc, vc = k[here, :], v[here, :]
-        s = dot_nt(query, kc) * scale
-        at = begin_at + lax.broadcasted_iota(jnp.int32, s.shape, 1)
-        p = jnp.where((at >= first) & (at <= last), jnp.exp(s - log_total), 0.0)
-        dp = dot_nt(grad, vc)
-        ds = (p * (dp - delta)).astype(BF16)
-        dq[...] += dot_nn(ds, kc)
-        gk[here, :] += dot_tn(ds, query) * scale
-        gv[here, :] += dot_tn(p.astype(BF16), grad)
+        at = begin_at + lax.broadcasted_iota(jnp.int32, (rows, CHUNK), 1)
+        seen = (at >= first) & (at <= last)
+        raw = [dot_nt(query[:, h], k[here, h]) for h in heads]
+        dps = [dot_nt(grad[:, h], v[here, h]) for h in heads]
+        for i, h in enumerate(heads):
+            p = jnp.where(seen, jnp.exp(raw[i] * scale - log_total[i]), 0.0)
+            ds = (p * (dps[i] - delta[i])).astype(BF16)
+            dq[:, h] += dot_nn(ds, k[here, h])
+            gk[here, h] += dot_tn(ds, query[:, h]) * scale
+            gv[here, h] += dot_tn(p.astype(BF16), grad[:, h])
         return carry
 
     lax.fori_loop(0, count, step, 0)
@@ -375,13 +412,16 @@
 def back_kernel(n, first, stride, *refs):
     me, xs, ms, refs = refs[0], refs[1 : 1 + n], refs[1 + n : 1 + 2 * n], refs[1 + 2 * n :]
     key, select_tok, w, small, h, rank, rows_own, maps, hot, rows, sel = refs
-    fill_map(me, ms, first + stride * pl.program_id(0), maps)
+    deep = w.shape[0]
+    maps[:deep, :] = w[...]
+    fill_map(me, ms, first + stride * pl.program_id(0), maps.at[deep:])
     fill_hot(key, hot)
     fill_rows(me, hot, xs, 0, rows)
     fill_select(hot, select_tok, sel)
-    low = (dot_nt(rows[...], maps[...]) * sel[...]).astype(BF16)
+    both = dot_nt(rows[...], maps[...])
+    low = (both[:, deep:] * sel[...]).astype(BF16)
     rank[...] = low
-    h[...] = dot_nt(rows[...], w[...]) + dot_nn(low, small[...])
+    h[...] = both[:, :deep] + dot_nn(low, small[...])
     rows_own[...] = rows[:, lanes(me[0], rows_own.shape[1])]
 
 
@@ -390,8 +430,9 @@
     key, share, select_tok, w, small, mixed, g, a_grad, dshare, rows_own, maps, *refs = refs
     hot, rows, sel, col, stage = refs
     e = pl.program_id(0)
-    fill_map(me, ms, e, maps)
     k, own, slots = small.shape[0], mixed.shape[1], mixed.shape[0]
+    maps[:own, :] = w[...]
+    fill_map(me, ms, e, maps.at[own:])
 
     @pl.when(e == 0)
     def start():
@@ -401,8 +442,9 @@
     fill_rows(me, hot, xs, 0, rows)
     fill_select(hot, select_tok, sel)
     fill_share(hot, share, col)
-    low = (dot_nt(rows[...], maps[...]) * sel[...]).astype(BF16)
-    h = dot_nt(rows[...], w[...]) + dot_nn(low, small[...])
+    both = dot_nt(rows[...], maps[...])
+    low = (both[:, own:] * sel[...]).astype(BF16)
+    h = both[:, :own] + dot_nn(low, small[...])
     stage[:, :1] = jnp.sum(mixed[...].astype(F32) * h, axis=1, keepdims=True)
     dshare[:, lanes(e, slots)] = stage[...].T[:8]
     g[...] = (h * col[:, :1]).astype(BF16)
@@ -452,9 +494,11 @@
     lax.fori_loop(0, slots // CAP, point, 0)
     stage[:, :k] = dot_nt(gg[...], hid[0]) * sel[...]
     stage[:, k : 2 * k] = dot_nt(gu[...], hid[1]) * sel[...]
+    stage[:, 128 : 128 + k] = dot_nt(inner[...], hid[2]) * sel[...]
     staged = stage[...].T
     live[:RANK, lanes(e, slots)] = live_rows(staged, 0, k).astype(BF16)
-    live[RANK:, lanes(e, slots)] = live_rows(staged, k, k).astype(BF16)
+    live[RANK : 2 * RANK, lanes(e, slots)] = live_rows(staged, k, k).astype(BF16)
+    live[2 * RANK :, lanes(e, slots)] = live_rows(staged, 128, k).astype(BF16)
     dshare[:, lanes(e, slots)] = staged[2 * k : 2 * k + 8]
     h_grad[0] = dot_tn(rank_gate, gg[...]).astype(BF16)
     h_grad[1] = dot_tn(rank_up, gu[...]).astype(BF16)
@@ -474,20 +518,17 @@
         copy_out(acc, rows, near, far, sem)
 
 
-def qkv_back_kernel(n, *refs):
-    me, xs, refs = refs[0], refs[1 : 1 + n], refs[1 + n :]
-    key, select_tok, hi, lo, w, b_in, gq, gk, gv, rank_q, rank_kv, near, far, live, b_grad, *refs = refs
-    maps, hot, sel, table, part, stage, acc, some_g = refs
+def qkv_rank_kernel(
+    key, select_tok, hi, lo, b_in, gq, gk, gv, rank_q, rank_kv,
+    out_q, out_kv, back_q, back_kv, live, b_grad,
+    hot, sel, table, stage,
+):
     i = pl.program_id(0)
-    tok, k = hi.shape[1], b_in.shape[0]
-    slots, wide = gq.shape[0], maps.shape[1]
-    seq = n * tok
-    width = part.shape[1]
-    fill_map(me, xs, i, maps)
+    n, tok, k = hi.shape[0], hi.shape[1], b_in.shape[0]
+    slots, seq = gq.shape[0], gk.shape[0]
 
     @pl.when(i == 0)
     def start():
-        acc[...] = jnp.zeros(acc.shape, F32)
         stage[...] = jnp.zeros(stage.shape, F32)
 
     @pl.when(i < EXPERTS)
@@ -498,14 +539,50 @@
             here = pl.ds(b * CAP, CAP)
             table[here, :] = dot_nn(hot[here, :], hi[b]) + dot_nn(hot[here, :], lo[b])
         g = turn_heads(gq[...], table[...], -1.0).astype(BF16)
+        out_q[...] = g
         rank = dot_nt(g, b_in[...]) * sel[...]
         stage[:slots, :k] = rank
+        back_q[...] = rank.astype(BF16)
         live[:, lanes(i, slots)] = live_rows(stage[:slots, :].T, 0, k).astype(BF16)
         b_grad[...] = dot_tn(rank_q[...], g).astype(BF16)
-        rank = rank.astype(BF16)
+
+    @pl.when(i >= EXPERTS)
+    def key_value():
+        for b in range(n):
+            here = pl.ds(b * tok, tok)
+            both = hi[b].astype(F32) + lo[b].astype(F32)
+            turned = turn_heads(gk[here, :], both, -1.0)
+            out_kv[here, :] = jnp.where(i == EXPERTS, turned, gv[here, :]).astype(BF16)
+            stage[here, k : 2 * k] = select_tok[b].astype(F32)
+        g = out_kv[...]
+        rank = dot_nt(g, b_in[...]) * stage[:seq, k : 2 * k]
+        stage[:seq, :k] = rank
+        back_kv[...] = rank.astype(BF16)
+        b_grad[...] = dot_tn(rank_kv[...], g).astype(BF16)
+        begin = EXPERTS * slots + (i - EXPERTS) * seq
+        there = pl.ds(pl.multiple_of(begin, 128), seq)
+        live[:, there] = live_rows(stage[:seq, :].T, 0, k).astype(BF16)
+
+
+def qkv_back_kernel(n, *refs):
+    me, xs, refs = refs[0], refs[1 : 1 + n], refs[1 + n :]
+    key, w, gq, gkv, back_q, back_kv, near, far, maps, hot, part, acc, some_g, some_rank = refs
+    i = pl.program_id(0)
+    tok = hot.shape[1]
+    wide = maps.shape[1]
+    width = part.shape[1]
+    fill_map(me, xs, i, maps)
+
+    @pl.when(i == 0)
+    def start():
+        acc[...] = jnp.zeros(acc.shape, F32)
+
+    @pl.when(i < EXPERTS)
+    def query():
+        fill_hot(key, hot)
         for c in range(0, wide, width):
             at = pl.ds(c, width)
-            y = dot_nt(g, w[at, :]) + dot_nn(rank, maps[:, at])
+            y = dot_nt(gq[...], w[at, :]) + dot_nn(back_q[...], maps[:, at])
             part[...] = y.astype(BF16)
             scatter_add(me, hot, part, acc, at)
 
@@ -513,30 +590,15 @@
     def key_value():
         group = n // 2
         size = group * tok
-        some = pl.ds(0, size)
-        total = jnp.zeros(b_grad.shape, F32)
         for half in range(2):
             there = pl.ds(half * size, size)
             for j in range(group):
-                b = me[0] ^ (2 * j + half)
-                here = pl.ds(j * tok, tok)
-                sel[here, :] = select_tok[b].astype(F32)
-                both = hi[b].astype(F32) + lo[b].astype(F32)
-                turned = turn_heads(gk[block_of(b, tok), :], both, -1.0)
-                some_g[here, :] = jnp.where(i == EXPERTS, turned, gv[block_of(b, tok), :]).astype(BF16)
-                total = total + dot_tn(rank_kv[block_of(b, tok), :], some_g[here, :])
-            g = some_g[...]
-            rank = dot_nt(g, b_in[...]) * sel[some, :]
-            for j in range(group):
-                stage[block_of(me[0] ^ (2 * j + half), tok), :k] = rank[j * tok : (j + 1) * tok]
-            rank = rank.astype(BF16)
+                block = block_of(me[0] ^ (2 * j + half), tok)
+                some_g[j * tok : (j + 1) * tok, :] = gkv[block, :]
+                some_rank[j * tok : (j + 1) * tok, :] = back_kv[block, :]
             for c in range(0, wide, width):
                 at = pl.ds(c, width)
-                acc[there, at] += dot_nt(g, w[at, :]) + dot_nn(rank, maps[:, at])
-        b_grad[...] = total.astype(BF16)
-        begin = EXPERTS * slots + (i - EXPERTS) * seq
-        there = pl.ds(pl.multiple_of(begin, 128), seq)
-        live[:, there] = live_rows(stage[:seq, :].T, 0, k).astype(BF16)
+                acc[there, at] += dot_nt(some_g[...], w[at, :]) + dot_nn(some_rank[...], maps[:, at])
 
     @pl.when(i == EXPERTS + 1)
     def finish():
@@ -619,27 +681,32 @@
             (by_expert((slots, own), last_expert), (EXPERTS, slots, own), BF16),
             (whole((seq, own)), (seq, own), BF16),
         ],
-        [((k, wide), BF16), ((slots, tok), BF16), ((max(slots, seq // 2), wide), BF16),
+        [((128, wide), BF16), ((wide, own + 128), BF16), ((slots, tok), BF16),
+         ((max(slots, seq // 2), wide), BF16),
          ((max(slots, seq // 2), k), F32), ((max(slots, seq // 2), 2 * HD), F32)],
         (me, *pieces, key, select_tok, hi, lo, w, b_in),
         2 * wide * own * (EXPERTS * slots + 2 * seq) * 1.5,
     )
 
 
+def attend_specs(n, tok, own):
+    slot_spec = pl.BlockSpec((EXPERTS, None, CAP, own), lambda b: (0, b, 0, 0))
+    tokens = [pl.BlockSpec((None, EXPERTS, tok), lambda b: (b, 0, 0)),
+              pl.BlockSpec((None, 1, tok), lambda b: (b, 0, 0))]
+    return slot_spec, tokens, whole((n * tok, own)), (EXPERTS, n, CAP, own)
+
+
 def attend(key, begin, q, k, v):
     n, tok = begin.shape[0], begin.shape[2]
     own, seq, rows = q.shape[2], n * tok, EXPERTS * CAP
-    slot_spec = pl.BlockSpec((EXPERTS, None, CAP, HD), lambda h, b: (0, b, 0, h))
-    all_spec = pl.BlockSpec((seq, HD), lambda h, b: (0, h))
-    shape = (EXPERTS, n, CAP, own)
+    slot_spec, tokens, all_spec, shape = attend_specs(n, tok, own)
     mixed, lse = run(
         attend_kernel,
         "attend",
-        (own // HD, n),
-        [pl.BlockSpec((None, EXPERTS, tok), lambda h, b: (b, 0, 0)),
-         pl.BlockSpec((None, 1, tok), lambda h, b: (b, 0, 0)), slot_spec, all_spec, all_spec],
+        (n,),
+        tokens + [slot_spec, all_spec, all_spec],
         [(slot_spec, shape, BF16), (slot_spec, shape, F32)],
-        [((rows, seq + CHUNK), F32), ((rows, HD), F32), ((rows, HD), F32), ((rows, HD), F32)],
+        [((own // HD, rows, seq), F32), ((rows, own), F32), ((rows, own), F32), ((rows, own), F32)],
         (key, begin, q.reshape(shape), k, v),
         3 * rows * seq * own * n,
         0,
@@ -650,18 +717,14 @@
 def attend_back(key, begin, q, g, mixed, lse, k, v):
     n, tok = begin.shape[0], begin.shape[2]
     own, seq, rows = q.shape[2], n * tok, EXPERTS * CAP
-    slot_spec = pl.BlockSpec((EXPERTS, None, CAP, HD), lambda h, b: (0, b, 0, h))
-    all_spec = pl.BlockSpec((seq, HD), lambda h, b: (0, h))
-    shape = (EXPERTS, n, CAP, own)
+    slot_spec, tokens, all_spec, shape = attend_specs(n, tok, own)
     gq, gk, gv = run(
         attend_back_kernel,
         "attend_back",
-        (own // HD, n),
-        [pl.BlockSpec((None, EXPERTS, tok), lambda h, b: (b, 0, 0)),
-         pl.BlockSpec((None, 1, tok), lambda h, b: (b, 0, 0)),
-         slot_spec, slot_spec, slot_spec, slot_spec, all_spec, all_spec],
+        (n,),
+        tokens + [slot_spec] * 4 + [all_spec] * 2,
         [(slot_spec, shape, F32), (all_spec, (seq, own), F32), (all_spec, (seq, own), F32)],
-        [((rows, HD), F32)],
+        [((rows, own), F32)],
         (key, begin, q.reshape(shape), g.reshape(shape), mixed.reshape(shape), lse, k, v),
         7 * rows * seq * own * n,
         0,
@@ -707,7 +770,7 @@
         [(by_expert((slots, deep)), (EXPERTS, slots, deep), F32),
          (by_expert((slots, k)), (EXPERTS, slots, k), BF16),
          (by_expert((slots, own)), (EXPERTS, slots, own), BF16)],
-        [((k, wide), BF16), ((slots, tok), BF16), ((slots, wide), BF16), ((slots, k), F32)],
+        [((deep + k, wide), BF16), ((slots, tok), BF16), ((slots, wide), BF16), ((slots, k), F32)],
         (me, *tokens, *pieces, key, select_tok, w, small),
         2 * wide * deep * EXPERTS * slots * 1.3,
     )
@@ -727,7 +790,7 @@
          (by_expert((k, own)), (EXPERTS, k, own), BF16),
          (whole((8, EXPERTS * slots)), (8, EXPERTS * slots), F32),
          (by_expert((slots, own)), (EXPERTS, slots, own), BF16)],
-        [((k, wide), BF16), ((slots, tok), BF16), ((slots, wide), BF16), ((slots, k), F32),
+        [((own + k, wide), BF16), ((slots, tok), BF16), ((slots, wide), BF16), ((slots, k), F32),
          ((slots, 128), F32), ((slots, 128), F32)],
         (me, *tokens, *pieces, key, share, select_tok, w, small, mixed),
         2 * wide * own * EXPERTS * slots * 1.5,
@@ -748,12 +811,12 @@
            by_expert((slots, deep)), by_expert((slots, k))],
         [(pl.BlockSpec(memory_space=pl.ANY), (n // 2 * tok, wide), BF16)] * 2
         + [(by_expert((slots, deep)), (EXPERTS, slots, deep), BF16),
-           (whole((2 * RANK, EXPERTS * slots)), (2 * RANK, EXPERTS * slots), BF16),
+           (whole((3 * RANK, EXPERTS * slots)), (3 * RANK, EXPERTS * slots), BF16),
            (whole((8, EXPERTS * slots)), (8, EXPERTS * slots), F32),
            (by_expert((3, k, deep)), (EXPERTS, 3, k, deep), BF16),
            (by_expert((slots, own)), (EXPERTS, slots, own), BF16)],
         [((slots, tok), BF16), ((slots, wide), BF16), ((slots, k), F32), ((slots, 128), F32),
-         ((slots, 128), F32), ((2 * k, wide), BF16), ((slots, deep), F32), ((slots, deep), F32),
+         ((slots, 256), F32), ((2 * k, wide), BF16), ((slots, deep), F32), ((slots, deep), F32),
          ((slots, deep), BF16), ((slots, deep), BF16), ((slots, chunk_of(slots, wide)), BF16),
          ((n * tok, wide), F32), pltpu.SemaphoreType.DMA],
         (me, *tokens, *pieces, key, share, select_tok, w, w, hid, h, back_down),
@@ -761,27 +824,47 @@
     )
 
 
-def qkv_back(me, pieces, key, select_tok, hi, lo, w, b_in, gq, gk, gv, rank_q, rank_kv):
+def qkv_rank(key, select_tok, hi, lo, b_in, gq, gk, gv, rank_q, rank_kv):
     n, tok, k = select_tok.shape
-    wide, own, slots, seq = pieces[0].shape[1], w.shape[2], n * CAP, n * tok
+    own, slots, seq = gq.shape[2], n * CAP, n * tok
     total = EXPERTS * slots + 2 * seq
-    most = max(slots, seq // 2)
+    return run(
+        qkv_rank_kernel,
+        "qkv_rank",
+        (EXPERTS + 2,),
+        [by_expert((n, tok), last_expert), whole(select_tok.shape), whole(hi.shape),
+         whole(lo.shape), by_expert((k, own)),
+         by_expert((slots, own), last_expert), whole((seq, own)), whole((seq, own)),
+         by_expert((slots, k), last_expert), by_expert((seq, k), from_expert)],
+        [(by_expert((slots, own), last_expert), (EXPERTS, slots, own), BF16),
+         (by_expert((seq, own), from_expert), (2, seq, own), BF16),
+         (by_expert((slots, k), last_expert), (EXPERTS, slots, k), BF16),
+         (by_expert((seq, k), from_expert), (2, seq, k), BF16),
+         (whole((RANK, total)), (RANK, total), BF16),
+         (by_expert((k, own)), (EXPERTS + 2, k, own), BF16)],
+        [((slots, tok), BF16), ((slots, k), F32), ((slots, 2 * HD), F32), ((max(slots, seq), 128), F32)],
+        (key, select_tok, hi, lo, b_in, gq, gk, gv, rank_q, rank_kv),
+        4 * k * own * (EXPERTS * slots + 2 * seq),
+        0,
+    )
+
+
+def qkv_back(me, pieces, key, w, gq, gkv, back_q, back_kv):
+    n, tok = key.shape[1:]
+    k, own, slots, seq = back_q.shape[2], w.shape[2], n * CAP, n * tok
+    wide = pieces[0].shape[1]
     return run(
         partial(qkv_back_kernel, n),
         "qkv_back",
         (EXPERTS + 2,),
         [rows_spec(m, k) for m in pieces]
-        + [by_expert((n, tok), last_expert), whole(select_tok.shape), whole(hi.shape),
-           whole(lo.shape), by_expert((wide, own)), by_expert((k, own)),
-           by_expert((slots, own), last_expert), whole((seq, own)), whole((seq, own)),
+        + [by_expert((n, tok), last_expert), by_expert((wide, own)),
+           by_expert((slots, own), last_expert), by_expert((seq, own), from_expert),
            by_expert((slots, k), last_expert), by_expert((seq, k), from_expert)],
-        sides(n, tok, wide)
-        + [(whole((RANK, total)), (RANK, total), BF16),
-           (by_expert((k, own)), (EXPERTS + 2, k, own), BF16)],
-        [((k, wide), BF16), ((slots, tok), BF16), ((most, k), F32), ((slots, 2 * HD), F32),
-         ((slots, chunk_of(slots, wide)), BF16), ((max(slots, seq), 128), F32), ((seq, wide), F32),
-         ((seq // 2, own), BF16)],
-        (me, *pieces, key, select_tok, hi, lo, w, b_in, gq, gk, gv, rank_q, rank_kv),
+        sides(n, tok, wide),
+        [((k, wide), BF16), ((slots, tok), BF16), ((slots, chunk_of(slots, wide)), BF16),
+         ((seq, wide), F32), ((seq // 2, own), BF16), ((seq // 2, k), BF16)],
+        (me, *pieces, key, w, gq, gkv, back_q, back_kv),
         2 * wide * own * (EXPERTS * slots + 2 * seq) * 1.5,
     )
 
@@ -880,8 +963,8 @@
 
     second = jnp.concatenate([attn_small[1, EXPERTS + 2 :], width_small.reshape(-1, k, own)])
     groups = -(-second.shape[0] // n)
-    second, cotangent_sent, w_in = tie(pack_maps(second, n), cotangent, w_in)
-    map_chips, cotangent_chips = across(second, n), across(cotangent_sent, n)
+    second, w_in = tie(pack_maps(second, n), w_in)
+    map_chips = across(second, n)
 
     begins = jnp.sum((segments[None, :] < jnp.arange(doc_count)[:, None]).astype(jnp.int32), axis=1)
     doc = segments.reshape(n, tok)
@@ -910,19 +993,23 @@
 
     select_a, select_f = slot_select(slot_a), slot_select(slot_f)
 
+    def send(g):
+        return [lax.ppermute(g, "rep", [(i, i ^ d) for i in range(reps)]) if d else g for d in range(reps)]
+
     share_ae = share_a.transpose(1, 0, 2)
     q, kv, rank_q, rank_kv, rows_a_own, normed_own_columns = qkv(
         me_ref, pieces, key_a, select_tok, table_hi, table_lo, w_in, b_in
     )
-    q, *sent = tie(q, *map_chips.values())
+    q, cotangent_sent, *sent = tie(q, cotangent, *map_chips.values())
+    cotangent_chips = across(cotangent_sent, n)
     maps = from_sibling(dict(zip(map_chips, sent)), n)
     mixed, lse = attend(slot_a, begin[:, None], q, kv[0], kv[1])
-    mixed, *sent = tie(mixed, *cotangent_chips.values())
-    grads_out_all = from_sibling(dict(zip(cotangent_chips, sent)), n)
     near, far, live_o = project_out(
         "attend_out", me_ref, mixed, key_a, share_ae, select_tok, a_out, attention_output_weight, maps, groups, 0, 1
     )
+    near, far, *sent = tie(near, far, *cotangent_chips.values())
     attn_total, attn_low = halve(near, far, n)
+    grads_out_all = from_sibling(dict(zip(cotangent_chips, sent)), n)
     *attn_low, key_late = tie(*attn_low, key_f)
 
     w_feed = jnp.swapaxes(feed_expert_weight, 2, 3)
@@ -942,8 +1029,10 @@
     )
     near, far = near.reshape(n // 2, tok, wide), far.reshape(n // 2, tok, wide)
     two_total, two_low = halve(near, far, n)
-    *two_low, inner, dshare_f, docs_sent = tie(*two_low, inner, dshare_f, docs)
-    near, far, live_d = project_out(
+    *two_low, inner, dshare_f, live_f, live_o = tie(*two_low, inner, dshare_f, live_f, live_o)
+    live_f = jnp.concatenate([live_f, live_o])
+    live_f = live_f + swap(live_f, n, 1)
+    near, far, unused = project_out(
         "feed_out", me_ref, inner, key_f, share_fe, select_tok, hidden_small, w_feed, maps, groups, EXPERTS + 2, 3, 2
     )
     grad_two_own = collect(two_total, two_low, n)
@@ -963,23 +1052,15 @@
     out_total, *sent = tie(out_total, *out_low, *chips.values())
     out_low, sent = sent[: n // 2 - 1], sent[n // 2 - 1 :]
     grads_two = from_sibling(dict(zip(chips, sent)), n)
+    mixed_late, live_f = tie(mixed, live_f)
+    live_f_sent = list(across(live_f, n).values())
     grad_mixed, a_out_grad, dshare_a, rows_ga_own = mixed_back(
-        me_ref, grads_two, maps, groups, key_a, share_ae, select_tok, attention_output_weight, a_out, mixed
-    )
-    live_f, live_o = lax.psum((jnp.concatenate([live_f, live_d]), live_o), "shard")
-    grad_mixed, *out_low = tie(grad_mixed, *out_low)
-    gq, gk, gv = attend_back(slot_a, begin[:, None], q, grad_mixed, mixed, lse, kv[0], kv[1])
-    gq, live_f, live_o = tie(gq, live_f, live_o)
-    layer_out = attended + collect(out_total, out_low, n)
-    near, far, live_in, b_in_grad = qkv_back(
-        me_ref, pieces, key_a, select_tok, table_hi, table_lo, w_in, b_in, gq, gk, gv, rank_q, rank_kv
-    )
-    in_total, in_low = halve(near, far, n)
-    *in_low, dshare_a, live_in, b_in_grad = tie(*in_low, dshare_a, live_in, b_in_grad)
-    grad_normed = collect(in_total, in_low, n)
-    dshare_a = sum_small(dshare_a, n)[:1]
-    grad_normed = grad_normed + route_back(own_a, own_tokens(slot_a, dshare_a), attention_router_weight)
-    grad_in = grad_attended + rms_back(x, gain_one, grad_normed)
+        me_ref, grads_two, maps, groups, key_a, share_ae, select_tok, attention_output_weight, a_out, mixed_late
+    )
+    grad_mixed, *sent = tie(grad_mixed, *live_f_sent, *out_low)
+    live_f_sent, out_low = sent[: n // 2], sent[n // 2 :]
+    live_f = added(live_f_sent)
+    live_f, live_o = live_f[: 3 * RANK], live_f[3 * RANK :]
 
     def spread(live, select):
         both = live.astype(F32)[:, None] * select[:, :, None, :]
@@ -995,6 +1076,12 @@
         hot = slot[:, :, None, :] == jnp.arange(CAP, dtype=jnp.int32)[None, None, :, None]
         row = jnp.sum(jnp.where(hot, share[:, :, None, :], 0.0), axis=-1)
         return row.transpose(1, 0, 2).reshape(EXPERTS, 1, slots)
+
+    def by_stream(sent):
+        out = jnp.zeros((reps,) + sent[0].shape, sent[0].dtype)
+        for d, got in enumerate(sent):
+            out = lax.dynamic_update_slice_in_dim(out, got[None], lax.axis_index("rep") ^ d, 0)
+        return out
 
     scaled_f, scaled_a = select_f * slot_row(share_f, slot_f), select_a * slot_row(share_a, slot_a)
     width_grad = jnp.stack(
@@ -1006,29 +1093,52 @@
         axis=1,
     )
     b_out_grad = grads(spread(of_slots(live_o), scaled_a), rows_ga_own)
-    live_in = sum_small(live_in, n)
-    live_kv = live_in[:, EXPERTS * slots :].reshape(RANK, 2, seq).transpose(1, 0, 2)
+    noted = jnp.zeros((1, k, own), BF16).at[0, 0, :doc_count].set(docs.astype(BF16))
+    early_grad = jnp.concatenate([a_out_grad, b_out_grad, noted])
+    width_grad, early_grad, lse_late = tie(width_grad, early_grad, lse)
+    hidden_all, width_all = lax.all_gather(hidden_grad, "rep"), lax.all_gather(width_grad, "rep")
+    early_sent = send(early_grad)
+    gq, gk, gv = attend_back(slot_a, begin[:, None], q, grad_mixed, mixed, lse_late, kv[0], kv[1])
+    gq, *early_sent = tie(gq, *early_sent)
+    layer_out = attended + collect(out_total, out_low, n)
+    gq, gkv, back_q, back_kv, live_in, b_in_grad = qkv_rank(
+        key_a, select_tok, table_hi, table_lo, b_in, gq, gk, gv, rank_q, rank_kv
+    )
+    dshare_a = dshare_a[0].astype(BF16).reshape(RANK, -1)
+    spare = -dshare_a.shape[1] % 128
+    live_in = jnp.concatenate([live_in, jnp.pad(dshare_a, ((0, 0), (0, spare)))], axis=1)
+    live_in = live_in + swap(live_in, n, 1)
+    gq, live_in, b_in_grad = tie(gq, live_in, b_in_grad)
+    live_sent, late_b_sent = list(across(live_in, n).values()), send(b_in_grad)
+    near, far = qkv_back(me_ref, pieces, key_a, w_in, gq, gkv, back_q, back_kv)
+    near, far, *sent = tie(near, far, *live_sent, *late_b_sent)
+    live_sent, late_b_sent = sent[: n // 2], sent[n // 2 :]
+    in_total, in_low = (quarter if n == 8 else halve)(near, far, n)
+    *in_low, first_sent = tie(*in_low, live_sent[0])
+    in_got = [swap(part, n, 2 * i + 2) for i, part in enumerate(in_low)]
+    live_in = added([first_sent] + live_sent[1:])
+    width = EXPERTS * slots + 2 * seq
+    dshare_a = live_in[:, width : width + EXPERTS * slots // RANK]
+    live_kv = live_in[:, EXPERTS * slots : width].reshape(RANK, 2, seq).transpose(1, 0, 2)
     a_in_grad = jnp.concatenate(
         [
             grads(spread(of_slots(live_in[:, : EXPERTS * slots]), select_a), rows_a_own),
             ein("pks,sw->pkw", spread(live_kv, select_row), normed_own_columns).astype(BF16),
         ]
     )
-
-    def all_streams(g):
-        mine = lax.axis_index("rep")
-        out = lax.dynamic_update_slice_in_dim(jnp.zeros((reps,) + g.shape, g.dtype), g[None], mine, 0)
-        for d in range(1, reps):
-            got = lax.ppermute(g, "rep", [(i, i ^ d) for i in range(reps)])
-            out = lax.dynamic_update_slice_in_dim(out, got[None], mine ^ d, 0)
-        return out
-
-    picks = jax.vmap(one_hot)(all_streams(docs_sent))
-    hidden_out = ein("rpekf,rkc->pecf", lax.all_gather(hidden_grad, "rep"), picks)
-    width_out = ein("rpmkw,rkc->pmwc", lax.all_gather(width_grad, "rep"), picks)
-    early = all_streams(jnp.concatenate([a_out_grad, b_out_grad]))
-    late_b, late_a = all_streams(b_in_grad), all_streams(a_in_grad)
-    attn = jnp.concatenate([late_a, early[:, :EXPERTS], late_b, early[:, EXPERTS:]], axis=1)
+    a_in_grad, hidden_all, *in_got = tie(a_in_grad, hidden_all, *in_got)
+    late_a_sent = send(a_in_grad)
+    grad_normed = collect_quarters(in_total, in_got, n) if n == 8 else added([in_total] + in_got)
+    grad_normed = grad_normed + route_back(own_a, own_tokens(slot_a, dshare_a), attention_router_weight)
+    grad_normed, width_all = tie(grad_normed, width_all)
+    grad_in = grad_attended + rms_back(x, gain_one, grad_normed)
+
+    early = by_stream(early_sent)
+    picks = jax.vmap(one_hot)(early[:, 2 * EXPERTS, 0, :doc_count].astype(jnp.int32))
+    hidden_out = ein("rpekf,rkc->pecf", hidden_all, picks)
+    width_out = ein("rpmkw,rkc->pmwc", width_all, picks)
+    late_b, late_a = by_stream(late_b_sent), by_stream(late_a_sent)
+    attn = jnp.concatenate([late_a, early[:, :EXPERTS], late_b, early[:, EXPERTS : 2 * EXPERTS]], axis=1)
     attn = attn.reshape(reps, 2, -1, k, own)
     attn_out = ein("rpmkw,rkc->pmwc", attn, picks)
     return (layer_out, grad_in, attn_out, width_out, hidden_out)

time: 709 us -> 679 us (0.958)
  waiting for transfers between devices: 202 us -> 136 us
  local copies, waits for them, and re-layouts: 41.7 us -> 93.1 us
  Pallas kernels: 293 us -> 261 us
  starting transfers between devices: 74.6 us -> 91.1 us
    dynamic_update_slice x15 -> x12, local copies, waits for them, and re-layouts: 0.34 us -> 44.9 us  [by_stream(): lax.dynamic_update_slice_in_dim(out, got[None], lax.axis_index('rep') ^ d...]
    pallas_call x9 -> x10, Pallas kernels: 293 us -> 261 us  [run(): return call(*args)]
    ppermute x12 -> x9, waiting for transfers between devices: 37.4 us -> 9.07 us  [send(): lax.ppermute(g, 'rep', [(i, i ^ d) for i in range(reps)])]
    ppermute x73 -> x77, waiting for transfers between devices: 153 us -> 127 us  [swap(): return lax.ppermute(x, 'shard', [(i, i ^ d) for i in range(n)])]
    all_gather x1, waiting for transfers between devices: 11.8 us -> 0.02 us  [local(): lax.all_gather(width_grad, 'rep')]
    ppermute x12 -> x9, starting transfers between devices: 18.4 us -> 27.5 us  [send(): lax.ppermute(g, 'rep', [(i, i ^ d) for i in range(reps)])]
    ppermute x73 -> x77, starting transfers between devices: 56 us -> 63.5 us  [swap(): return lax.ppermute(x, 'shard', [(i, i ^ d) for i in range(n)])]
  transfers between devices with their start and end apart: 88 -> 88, of which waited for: 30 -> 24; matrix products, arithmetic and copies ran while one was open for 13% -> 21% of each run, Pallas kernels for 28% -> 27%
where the time goes in v3:
time: 679 us; the launch traced here: 670 us
  Pallas kernels  261 us (38%)
  waiting for transfers between devices  136 us (20%)
  local copies, waits for them, and re-layouts  93.1 us (14%)
  starting transfers between devices  91.1 us (13%)
  other arithmetic  45.1 us (7%)
  matrix products  26 us (4%)
  between operations  16.8 us (2%)
    pallas_call x10, Pallas kernels, run(): return call(*args)  261 us
    ppermute x77, waiting for transfers between devices, swap(): return lax.ppermute(x, 'shard', [(i, i ^ d) for i in range(n)])  127 us
    ppermute x77, starting transfers between devices, swap(): return lax.ppermute(x, 'shard', [(i, i ^ d) for i in range(n)])  63.5 us
    dynamic_update_slice x12, local copies, waits for them, and re-layouts, by_stream(): lax.dynamic_update_slice_in_dim(out, got[None], lax.axis_index('rep') ^ d...  44.9 us
    ppermute x9, starting transfers between devices, send(): lax.ppermute(g, 'rep', [(i, i ^ d) for i in range(reps)])  27.5 us
    dot_general x16, matrix products, ein(): return jnp.einsum(spec, a, b, preferred_element_type=F32)  22.7 us
  transfers between devices with their start and end apart: 88, of which 24 were waited for; matrix products, arithmetic and copies ran while one was open for 21% of the time, Pallas kernels for 27%

profile of v3, /device:TPU:0, one launch (start us, length us, event | category | flops | bytes accessed | tf_op | source)
XLA Modules:
  0.0 670.0 jit_solution(821537577266952796)
XLA Ops:
  26.0 8.0 %collective-permute-done.3 = bf16[80,2048]{1,0:T(8,128)(2,1)} collective-permute-done((bf16[80,2048]{1,0:T(8,128)(2,1)}, bf16[80,2048]{1,0:T(8,128)(2,1)}, u32[]{:S(2)}, u32[]{:S(2)}) %collective-permute-start.3) | collective-permute-done | bytes 327712 | tf_op jit(solution)/shard_map/ppermute | solution.py:52
  45.9 19.0 %collective-permute-done.7 = bf16[96,2048]{1,0:T(8,128)(2,1)S(1)} collective-permute-done((bf16[96,2048]{1,0:T(8,128)(2,1)S(1)}, bf16[96,2048]{1,0:T(8,128)(2,1)S(1)}, u32[]{:S(2)}, u32[]{:S(2)}) %collective-permute-start.7) | collective-permute-done | bytes 393248 | tf_op jit(solution)/shard_map/ppermute | solution.py:52
  69.1 11.8 %collective-permute-done.11 = bf16[6,256,256]{2,1,0:T(8,128)(2,1)S(1)} collective-permute-done((bf16[6,256,256]{2,1,0:T(8,128)(2,1)S(1)}, bf16[6,256,256]{2,1,0:T(8,128)(2,1)S(1)}, u32[]{:S(2)}, u32[]{:S(2)}) %collective-permute-start.11) | collective-permute-done | bytes 786464 | tf_op jit(solution)/shard_map/ppermute | solution.py:52
  87.3 11.1 %collective-permute-done.12 = bf16[6,256,256]{2,1,0:T(8,128)(2,1)S(1)} collective-permute-done((bf16[6,256,256]{2,1,0:T(8,128)(2,1)S(1)}, bf16[6,256,256]{2,1,0:T(8,128)(2,1)S(1)}, u32[]{:S(2)}, u32[]{:S(2)}) %collective-permute-start.12) | collective-permute-done | bytes 786464 | tf_op jit(solution)/shard_map/ppermute | solution.py:52
  99.5 15.9 %collective-permute-done.13 = bf16[6,256,256]{2,1,0:T(8,128)(2,1)S(1)} collective-permute-done((bf16[6,256,256]{2,1,0:T(8,128)(2,1)S(1)}, bf16[6,256,256]{2,1,0:T(8,128)(2,1)S(1)}, u32[]{:S(2)}, u32[]{:S(2)}) %collective-permute-start.13) | collective-permute-done | bytes 786464 | tf_op jit(solution)/shard_map/ppermute | solution.py:52
  126.4 24.6 %qkv.1 = (bf16[4,640,256]{2,1,0:T(8,128)(2,1)}, bf16[2,1024,256]{2,1,0:T(8,128)(2,1)}, bf16[4,640,48]{2,1,0:T(8,128)(2,1)}, bf16[2,1024,48]{2,1,0:T(8,128)(2,1)}...) custom-call(s32[1]{0:T(128)} %bitcast.refs_0_, bf16[176,2048]{1,0:T(8,128)(2,1)} %copy-done.24, ...), custom_call_target="tpu_custom_call" | custom-call | flops 7247757312 | bytes 33554432 | tf_op jit(solution)/shard_map/qkv/pallas_call | solution.py:646
  158.6 17.8 %attend.1 = (bf16[4,8,80,256]{3,2,1,0:T(8,128)(2,1)}, f32[4,8,80,256]{3,2,1,0:T(8,128)}) custom-call(s32[8,4,128]{2,1,0:T(4,128)} %copy.152.key, s32[8,1,128]{2,1,0:T(1,128)} %bitcast.449, bf16[4,8,80,256]{3,2,1,0:T(8,128)(2,1)} %bitcast.470, bf16[1024,256]{1,0:T(8,128)(2,1)} %get-tuple-element.321.k, bf16[1024,256]{1,0:T(8,128)(2,1)} %get-tuple-element.320.v), custom_call_target="tpu_custom_call" | custom-call | flops 2013265920 | bytes 33554432 | tf_op jit(solution)/shard_map/attend/pallas_call | solution.py:646
  176.4 17.8 %attend_out.1 = (bf16[4,128,2048]{2,1,0:T(8,128)(2,1)}, bf16[4,128,2048]{2,1,0:T(8,128)(2,1)}, bf16[16,2560]{1,0:T(8,128)(2,1)}) custom-call(s32[1]{0:T(128)} %bitcast.refs_0_, bf16[96,2048]{1,0:T(8,128)(2,1)} %copy-done.14, bf16[96,2048]{1,0:T(8,128)(2,1)} %copy-done.19, bf16[96,2048]{1,0:T(8,128)(2,1)} %copy-done.18, bf16[96,2048]{1,0:T(8,128)(2,1)} %copy-done.20, ...), custom_call_target="tpu_custom_call" | custom-call | flops 4026531840 | bytes 33554432 | tf_op jit(solution)/shard_map/attend_out/pallas_call | solution.py:646
  194.4 3.6 fusion.refs_20_.refs_22_.refs_13_
  208.4 22.0 %feed_down_back.1 = (f32[4,640,704]{2,1,0:T(8,128)}, bf16[4,640,48]{2,1,0:T(8,128)(2,1)}, bf16[4,640,256]{2,1,0:T(8,128)(2,1)}) custom-call(s32[1]{0:T(128)} %bitcast.refs_0_, bf16[128,2048]{1,0:T(8,128)(2,1)} %refs_1_, bf16[128,2048]{1,0:T(8,128)(2,1)} %copy-done.27, bf16[128,2048]{1,0:T(8,128)(2,1)} %collective-permute-done.24.refs_3_, ...), custom_call_target="tpu_custom_call" | custom-call | flops 9596567552 | bytes 33554432 | tf_op jit(solution)/shard_map/feed_down_back/pallas_call | solution.py:646
  240.7 18.6 %collective-permute-done.42 = f32[4,128]{1,0:T(4,128)S(1)} collective-permute-done((f32[4,128]{1,0:T(4,128)S(1)}, f32[4,128]{1,0:T(4,128)S(1)}, u32[]{:S(2)}, u32[]{:S(2)}) %collective-permute-start.42) | collective-permute-done | bytes 2080 | tf_op jit(solution)/shard_map/ppermute | solution.py:52
  267.7 79.1 %feed.1 = (bf16[512,2048]{1,0:T(8,128)(2,1)}, bf16[512,2048]{1,0:T(8,128)(2,1)}, bf16[4,640,704]{2,1,0:T(8,128)(2,1)}, bf16[48,2560]{1,0:T(8,128)(2,1)}, f32[8,2...) custom-call(s32[1]{0:T(128)} %bitcast.refs_0_, bf16[128,2048]{1,0:T(8,128)(2,1)} %copy-done.17, ...), custom_call_target="tpu_custom_call" | custom-call | flops 38386270208 | bytes 33554432 | tf_op jit(solution)/shard_map/feed/pallas_call | solution.py:646
  347.2 4.1 collective-permute-done.46
  351.4 5.2 fusion.103
  365.7 28.9 %feed_out.1 = (bf16[4,128,2048]{2,1,0:T(8,128)(2,1)}, bf16[4,128,2048]{2,1,0:T(8,128)(2,1)}, bf16[16,2560]{1,0:T(8,128)(2,1)}) custom-call(s32[1]{0:T(128)} %bitcast.refs_0_, bf16[96,2048]{1,0:T(8,128)(2,1)} %copy-done.14, bf16[96,2048]{1,0:T(8,128)(2,1)} %copy-done.19, bf16[96,2048]{1,0:T(8,128)(2,1)} %copy-done.18, bf16[96,2048]{1,0:T(8,128)(2,1)} %copy-done.20, ...), custom_call_target="tpu_custom_call" | custom-call | flops 11072962560 | bytes 33554432 | tf_op jit(solution)/shard_map/feed_out/pallas_call | solution.py:646
  399.0 3.4 and_reduce_fusion
  413.3 5.7 collective-permute-done.54.refs_3_
  419.0 11.7 %collective-permute-done.55.refs_5_ = bf16[128,2048]{1,0:T(8,128)(2,1)} collective-permute-done((bf16[128,2048]{1,0:T(8,128)(2,1)S(1)}, bf16[128,2048]{1,0:T(8,128)(2,1)}, u32[]{:S(2)}, u32[]{:S(2)}) %collective-permute-start.55) | collective-permute-done | bytes 524320 | tf_op jit(solution)/shard_map/ppermute | solution.py:52
  438.7 16.6 %mixed_back.1 = (bf16[4,640,256]{2,1,0:T(8,128)(2,1)}, bf16[4,48,256]{2,1,0:T(8,128)(2,1)}, f32[8,2560]{1,0:T(8,128)}, bf16[4,640,256]{2,1,0:T(8,128)(2,1)}) custom-call(s32[1]{0:T(128)} %bitcast.refs_0_, bf16[128,2048]{1,0:T(8,128)(2,1)} %copy-done.29, bf16[128,2048]{1,0:T(8,128)(2,1)} %collective-permute-done.57.refs_2_, bf16[128,2048]{1,0:T(8,128)(2,1)} %copy-done.80, ...), custom_call_target="tpu_custom_call" | custom-call | flops 4026531840 | bytes 33554432 | tf_op jit(solution)/shard_map/mixed_back/pallas_call | solution.py:646
  470.3 24.2 %attend_back.1 = (f32[4,8,80,256]{3,2,1,0:T(8,128)}, f32[1024,256]{1,0:T(8,128)}, f32[1024,256]{1,0:T(8,128)}) custom-call(s32[8,4,128]{2,1,0:T(4,128)} %copy.152.key, s32[8,1,128]{2,1,0:T(1,128)} %bitcast.450, bf16[4,8,80,256]{3,2,1,0:T(8,128)(2,1)} %bitcast.471, bf16[4,8,80,256]{3,2,1,0:T(8,128)(2,1)} %bitcast.474, ...), custom_call_target="tpu_custom_call" | custom-call | flops 4697620480 | bytes 33554432 | tf_op jit(solution)/shard_map/attend_back/pallas_call | solution.py:646
  495.0 3.5 collective-permute-done.70
  498.5 9.0 %qkv_rank.1 = (bf16[4,640,256]{2,1,0:T(8,128)(2,1)}, bf16[2,1024,256]{2,1,0:T(8,128)(2,1)}, bf16[4,640,48]{2,1,0:T(8,128)(2,1)}, bf16[2,1024,48]{2,1,0:T(8,128)(...) custom-call(s32[4,8,128]{2,1,0:T(8,128)} %get-tuple-element.368.refs_9_.refs_10_.refs_17_.key, ...), custom_call_target="tpu_custom_call" | custom-call | flops 226492416 | bytes 33554432 | tf_op jit(solution)/shard_map/qkv_rank/pallas_call | solution.py:646
  510.8 17.1 %collective-permute-start.75 = (bf16[6,48,256]{2,1,0:T(8,128)(2,1)}, bf16[6,48,256]{2,1,0:T(8,128)(2,1)S(1)}, u32[]{:S(2)}, u32[]{:S(2)}) collective-permute-start(bf16[6,48,256]{2,1,0:T(8,128)(2,1)} %get-tuple-element.263), channel_id=1, source_target_pairs={{0,8},{8,0},{16,24},{24,16},{1,9},{9,1},{17,25},{25,17},{2,10},{10... | collective-permute-start | bytes 442376 | tf_op jit(solution)/shard_map/ppermute | solution.py:997
  533.9 21.5 %qkv_back.1 = (bf16[4,128,2048]{2,1,0:T(8,128)(2,1)}, bf16[4,128,2048]{2,1,0:T(8,128)(2,1)}) custom-call(s32[1]{0:T(128)} %bitcast.refs_0_, bf16[176,2048]{1,0:T(8,128)(2,1)} %copy-done.24, bf16[176,2048]{1,0:T(8,128)(2,1)} %collective-permute-done.refs_2_, bf16[176,2048]{1,0:T(8,128)(2,1)} %copy-done.35, bf16[176,2048]{1,0:T(8,128)(2,1)} %copy-done.77, ...), custom_call_target="tpu_custom_call" | custom-call | flops 7247757312 | bytes 33554432 | tf_op jit(solution)/shard_map/qkv_back/pallas_call | solution.py:646
  563.4 11.8 %dynamic_update_slice.72 = bf16[4,9,48,256]{3,0,2,1:T(4,128)(2,1)S(1)} dynamic-update-slice(bf16[4,9,48,256]{3,0,2,1:T(4,128)(2,1)S(1)} %broadcast_in_dim.198, bf16[1,9,48,256]{3,0,2,1:T(2,128)(2,1)} %copy.174, s32[]{:T(128)S(6)} %select_n.184, s32[]{:T(128)} %constant.139.clone.1, s32[]{:T(128)} %constant.139.clone.1, s32[]{:T(128)} %constant.139.clone.1) | dynamic-update-slice | bytes 442372 | tf_op jit(solution)/shard_map/dynamic_update_slice | solution.py:1083
  575.2 10.3 %dynamic_update_slice.73 = bf16[4,9,48,256]{3,0,2,1:T(4,128)(2,1)S(1)} dynamic-update-slice(bf16[4,9,48,256]{3,0,2,1:T(4,128)(2,1)S(1)} %dynamic_update_slice.72, bf16[1,9,48,256]{3,0,2,1:T(2,128)(2,1)S(1)} %copy.175, s32[]{:T(128)S(6)} %select_n.185, s32[]{:T(128)} %constant.139.clone.1, s32[]{:T(128)} %constant.139.clone.1, s32[]{:T(128)} %constant.139.clone.1) | dynamic-update-slice | bytes 442372 | tf_op jit(solution)/shard_map/dynamic_update_slice | solution.py:1083
  585.6 10.3 %dynamic_update_slice.74 = bf16[4,9,48,256]{3,0,2,1:T(4,128)(2,1)S(1)} dynamic-update-slice(bf16[4,9,48,256]{3,0,2,1:T(4,128)(2,1)S(1)} %dynamic_update_slice.73, bf16[1,9,48,256]{3,0,2,1:T(2,128)(2,1)S(1)} %copy.176, s32[]{:T(128)S(6)} %select_n.186, s32[]{:T(128)} %constant.139.clone.1, s32[]{:T(128)} %constant.139.clone.1, s32[]{:T(128)} %constant.139.clone.1) | dynamic-update-slice | bytes 442372 | tf_op jit(solution)/shard_map/dynamic_update_slice | solution.py:1083
  595.9 10.6 %dynamic_update_slice.75 = bf16[4,9,48,256]{3,0,2,1:T(4,128)(2,1)S(1)} dynamic-update-slice(bf16[4,9,48,256]{3,0,2,1:T(4,128)(2,1)S(1)} %dynamic_update_slice.74, bf16[1,9,48,256]{3,0,2,1:T(2,128)(2,1)S(1)} %copy.177, s32[]{:T(128)S(6)} %select_n.187, s32[]{:T(128)} %constant.139.clone.1, s32[]{:T(128)} %constant.139.clone.1, s32[]{:T(128)} %constant.139.clone.1) | dynamic-update-slice | bytes 442372 | tf_op jit(solution)/shard_map/dynamic_update_slice | solution.py:1083
  609.4 4.5 convert_add_fusion.1
  621.9 7.9 %collective-permute-done.79 = bf16[2,64,2048]{2,1,0:T(8,128)(2,1)S(1)} collective-permute-done((bf16[2,64,2048]{2,1,0:T(8,128)(2,1)}, bf16[2,64,2048]{2,1,0:T(8,128)(2,1)S(1)}, u32[]{:S(2)}, u32[]{:S(2)}) %collective-permute-start.79) | collective-permute-done | bytes 524320 | tf_op jit(solution)/shard_map/ppermute | solution.py:52
  635.0 6.1 convolution_bitcast_fusion
  644.3 4.2 collective-permute-done.85
  (563 shorter events, 187.3 us)
Async XLA Ops:
  7.2 614.7 %all-gather.5.cloned.1.call-start = ((), (), s32[]{:S(2)}) async-start(), calls=%async_computation | async-start | bytes 4423680 | tf_op jit(solution)/shard_map/all_gather | solution.py:1099
  36.4 31.7 %collective-permute-start.10 = (bf16[6,256,256]{2,1,0:T(8,128)(2,1)S(1)}, bf16[6,256,256]{2,1,0:T(8,128)(2,1)S(1)}, u32[]{:S(2)}, u32[]{:S(2)}) collective-permute-start(bf16[6,256,256]{2,1,0:T(8,128)(2,1)S(1)} %pad_maximum_fusion.3), channel_id=1, source_target_pairs={{0,7},{1,6},{2,5},{3,4},{4,3},{5,2},{6,1},{7,0},{8,15},{9,14},{10,... | collective-permute-start | bytes 2359304 | tf_op jit(solution)/shard_map/ppermute | solution.py:52
  36.5 28.4 %collective-permute-start.8 = (bf16[80,2048]{1,0:T(8,128)(2,1)}, bf16[80,2048]{1,0:T(8,128)(2,1)S(1)}, u32[]{:S(2)}, u32[]{:S(2)}) collective-permute-start(bf16[80,2048]{1,0:T(8,128)(2,1)} %collective-permute-done.3), channel_id=1, source_target_pairs={{0,4},{1,5},{2,6},{3,7},{4,0},{5,1},{6,2},{7,3},{8,12},{9,13},{10,... | collective-permute-start | bytes 983048 | tf_op jit(solution)/shard_map/ppermute | solution.py:52
  41.2 39.7 %collective-permute-start.11 = (bf16[6,256,256]{2,1,0:T(8,128)(2,1)S(1)}, bf16[6,256,256]{2,1,0:T(8,128)(2,1)S(1)}, u32[]{:S(2)}, u32[]{:S(2)}) collective-permute-start(bf16[6,256,256]{2,1,0:T(8,128)(2,1)S(1)} %pad_maximum_fusion.4), channel_id=1, source_target_pairs={{0,6},{1,7},{2,4},{3,5},{4,2},{5,3},{6,0},{7,1},{8,14},{9,15},{10,... | collective-permute-start | bytes 2359304 | tf_op jit(solution)/shard_map/ppermute | solution.py:52
  64.9 33.5 %collective-permute-start.12 = (bf16[6,256,256]{2,1,0:T(8,128)(2,1)S(1)}, bf16[6,256,256]{2,1,0:T(8,128)(2,1)S(1)}, u32[]{:S(2)}, u32[]{:S(2)}) collective-permute-start(bf16[6,256,256]{2,1,0:T(8,128)(2,1)S(1)} %pad_maximum_fusion.5), channel_id=1, source_target_pairs={{0,5},{1,4},{2,7},{3,6},{4,1},{5,0},{6,3},{7,2},{8,13},{9,12},{10,... | collective-permute-start | bytes 2359304 | tf_op jit(solution)/shard_map/ppermute | solution.py:52
  65.8 49.5 %collective-permute-start.13 = (bf16[6,256,256]{2,1,0:T(8,128)(2,1)S(1)}, bf16[6,256,256]{2,1,0:T(8,128)(2,1)S(1)}, u32[]{:S(2)}, u32[]{:S(2)}) collective-permute-start(bf16[6,256,256]{2,1,0:T(8,128)(2,1)S(1)} %pad_maximum_fusion.6), channel_id=1, source_target_pairs={{0,4},{1,5},{2,6},{3,7},{4,0},{5,1},{6,2},{7,3},{8,12},{9,13},{10,... | collective-permute-start | bytes 2359304 | tf_op jit(solution)/shard_map/ppermute | solution.py:52
  67.2 49.0 %collective-permute-start.14 = (bf16[6,256,256]{2,1,0:T(8,128)(2,1)S(1)}, bf16[6,256,256]{2,1,0:T(8,128)(2,1)S(1)}, u32[]{:S(2)}, u32[]{:S(2)}) collective-permute-start(bf16[6,256,256]{2,1,0:T(8,128)(2,1)S(1)} %pad_maximum_fusion.7), channel_id=1, source_target_pairs={{0,3},{1,2},{2,1},{3,0},{4,7},{5,6},{6,5},{7,4},{8,11},{9,10},{10,... | collective-permute-start | bytes 2359304 | tf_op jit(solution)/shard_map/ppermute | solution.py:52
  68.1 49.0 %collective-permute-start.15 = (bf16[6,256,256]{2,1,0:T(8,128)(2,1)S(1)}, bf16[6,256,256]{2,1,0:T(8,128)(2,1)S(1)}, u32[]{:S(2)}, u32[]{:S(2)}) collective-permute-start(bf16[6,256,256]{2,1,0:T(8,128)(2,1)S(1)} %pad_maximum_fusion.8), channel_id=1, source_target_pairs={{0,2},{1,3},{2,0},{3,1},{4,6},{5,7},{6,4},{7,5},{8,10},{9,11},{10,... | collective-permute-start | bytes 2359304 | tf_op jit(solution)/shard_map/ppermute | solution.py:52
  80.9 37.3 %collective-permute-start.16 = (bf16[6,256,256]{2,1,0:T(8,128)(2,1)S(1)}, bf16[6,256,256]{2,1,0:T(8,128)(2,1)S(1)}, u32[]{:S(2)}, u32[]{:S(2)}) collective-permute-start(bf16[6,256,256]{2,1,0:T(8,128)(2,1)S(1)} %pad_maximum_fusion.9), channel_id=1, source_target_pairs={{0,1},{1,0},{2,3},{3,2},{4,5},{5,4},{6,7},{7,6},{8,9},{9,8},{10,11... | collective-permute-start | bytes 2359304 | tf_op jit(solution)/shard_map/ppermute | solution.py:52
  120.0 31.0 %collective-permute-start.17 = (bf16[96,2048]{1,0:T(8,128)(2,1)S(1)}, bf16[96,2048]{1,0:T(8,128)(2,1)S(1)}, u32[]{:S(2)}, u32[]{:S(2)}) collective-permute-start(bf16[96,2048]{1,0:T(8,128)(2,1)S(1)} %pad_maximum_fusion.11.refs_1_.refs_9_), channel_id=1, source_target_pairs={{0,2},{1,3},{2,0},{3,1},{4,6},{5,7},{6,4},{7,5},{8,10},{9,11},{10,... | collective-permute-start | bytes 1179656 | tf_op jit(solution)/shard_map/ppermute | solution.py:52
  121.3 29.8 %collective-permute-start.18 = (bf16[96,2048]{1,0:T(8,128)(2,1)S(1)}, bf16[96,2048]{1,0:T(8,128)(2,1)}, u32[]{:S(2)}, u32[]{:S(2)}) collective-permute-start(bf16[96,2048]{1,0:T(8,128)(2,1)S(1)} %pad_maximum_fusion.11.refs_1_.refs_9_), channel_id=1, source_target_pairs={{0,4},{1,5},{2,6},{3,7},{4,0},{5,1},{6,2},{7,3},{8,12},{9,13},{10,... | collective-permute-start | bytes 1179656 | tf_op jit(solution)/shard_map/ppermute | solution.py:52
  122.1 28.9 %collective-permute-start.19 = (bf16[96,2048]{1,0:T(8,128)(2,1)S(1)}, bf16[96,2048]{1,0:T(8,128)(2,1)}, u32[]{:S(2)}, u32[]{:S(2)}) collective-permute-start(bf16[96,2048]{1,0:T(8,128)(2,1)S(1)} %pad_maximum_fusion.11.refs_1_.refs_9_), channel_id=1, source_target_pairs={{0,6},{1,7},{2,4},{3,5},{4,2},{5,3},{6,0},{7,1},{8,14},{9,15},{10,... | collective-permute-start | bytes 1179656 | tf_op jit(solution)/shard_map/ppermute | solution.py:52
  155.0 39.3 %collective-permute-start.24 = (bf16[128,2048]{1,0:T(8,128)(2,1)S(1)}, bf16[128,2048]{1,0:T(8,128)(2,1)}, u32[]{:S(2)}, u32[]{:S(2)}) collective-permute-start(bf16[128,2048]{1,0:T(8,128)(2,1)S(1)} %copy-done.9), channel_id=1, source_target_pairs={{0,2},{1,3},{2,0},{3,1},{4,6},{5,7},{6,4},{7,5},{8,10},{9,11},{10,... | collective-permute-start | bytes 1572872 | tf_op jit(solution)/shard_map/ppermute | solution.py:52
  156.3 38.0 %collective-permute-start.25 = (bf16[128,2048]{1,0:T(8,128)(2,1)S(1)}, bf16[128,2048]{1,0:T(8,128)(2,1)}, u32[]{:S(2)}, u32[]{:S(2)}) collective-permute-start(bf16[128,2048]{1,0:T(8,128)(2,1)S(1)} %copy-done.9), channel_id=1, source_target_pairs={{0,4},{1,5},{2,6},{3,7},{4,0},{5,1},{6,2},{7,3},{8,12},{9,13},{10,... | collective-permute-start | bytes 1572872 | tf_op jit(solution)/shard_map/ppermute | solution.py:52
  157.1 37.1 %collective-permute-start.26 = (bf16[128,2048]{1,0:T(8,128)(2,1)S(1)}, bf16[128,2048]{1,0:T(8,128)(2,1)}, u32[]{:S(2)}, u32[]{:S(2)}) collective-permute-start(bf16[128,2048]{1,0:T(8,128)(2,1)S(1)} %copy-done.9), channel_id=1, source_target_pairs={{0,6},{1,7},{2,4},{3,5},{4,2},{5,3},{6,0},{7,1},{8,14},{9,15},{10,... | collective-permute-start | bytes 1572872 | tf_op jit(solution)/shard_map/ppermute | solution.py:52
  204.1 27.6 %collective-permute-start.32 = (bf16[128,2048]{1,0:T(8,128)(2,1)}, bf16[128,2048]{1,0:T(8,128)(2,1)}, u32[]{:S(2)}, u32[]{:S(2)}) collective-permute-start(bf16[128,2048]{1,0:T(8,128)(2,1)} %get-tuple-element.175), channel_id=1, source_target_pairs={{0,2},{1,3},{2,0},{3,1},{4,6},{5,7},{6,4},{7,5},{8,10},{9,11},{10,... | collective-permute-start | bytes 1572872 | tf_op jit(solution)/shard_map/ppermute | solution.py:52
  234.5 29.2 %collective-permute-start.36 = (bf16[128,2048]{1,0:T(8,128)(2,1)S(1)}, bf16[128,2048]{1,0:T(8,128)(2,1)S(1)}, u32[]{:S(2)}, u32[]{:S(2)}) collective-permute-start(bf16[128,2048]{1,0:T(8,128)(2,1)S(1)} %multiply_convert_fusion.refs_1_), channel_id=1, source_target_pairs={{0,2},{1,3},{2,0},{3,1},{4,6},{5,7},{6,4},{7,5},{8,10},{9,11},{10,... | collective-permute-start | bytes 1572872 | tf_op jit(solution)/shard_map/ppermute | solution.py:52
  235.9 28.4 %collective-permute-start.38 = (bf16[128,2048]{1,0:T(8,128)(2,1)S(1)}, bf16[128,2048]{1,0:T(8,128)(2,1)}, u32[]{:S(2)}, u32[]{:S(2)}) collective-permute-start(bf16[128,2048]{1,0:T(8,128)(2,1)S(1)} %multiply_convert_fusion.refs_1_), channel_id=1, source_target_pairs={{0,4},{1,5},{2,6},{3,7},{4,0},{5,1},{6,2},{7,3},{8,12},{9,13},{10,... | collective-permute-start | bytes 1572872 | tf_op jit(solution)/shard_map/ppermute | solution.py:52
  236.7 27.7 %collective-permute-start.40 = (bf16[128,2048]{1,0:T(8,128)(2,1)S(1)}, bf16[128,2048]{1,0:T(8,128)(2,1)}, u32[]{:S(2)}, u32[]{:S(2)}) collective-permute-start(bf16[128,2048]{1,0:T(8,128)(2,1)S(1)} %multiply_convert_fusion.refs_1_), channel_id=1, source_target_pairs={{0,6},{1,7},{2,4},{3,5},{4,2},{5,3},{6,0},{7,1},{8,14},{9,15},{10,... | collective-permute-start | bytes 1572872 | tf_op jit(solution)/shard_map/ppermute | solution.py:52
  360.5 34.3 %collective-permute-start.47 = (bf16[128,2048]{1,0:T(8,128)(2,1)}, bf16[128,2048]{1,0:T(8,128)(2,1)}, u32[]{:S(2)}, u32[]{:S(2)}) collective-permute-start(bf16[128,2048]{1,0:T(8,128)(2,1)} %get-tuple-element.186), channel_id=1, source_target_pairs={{0,2},{1,3},{2,0},{3,1},{4,6},{5,7},{6,4},{7,5},{8,10},{9,11},{10,... | collective-permute-start | bytes 1572872 | tf_op jit(solution)/shard_map/ppermute | solution.py:52
  361.2 33.7 %collective-permute-start.48 = (bf16[128,2048]{1,0:T(8,128)(2,1)}, bf16[128,2048]{1,0:T(8,128)(2,1)}, u32[]{:S(2)}, u32[]{:S(2)}) collective-permute-start(bf16[128,2048]{1,0:T(8,128)(2,1)} %get-tuple-element.187), channel_id=1, source_target_pairs={{0,4},{1,5},{2,6},{3,7},{4,0},{5,1},{6,2},{7,3},{8,12},{9,13},{10,... | collective-permute-start | bytes 1572872 | tf_op jit(solution)/shard_map/ppermute | solution.py:52
  362.4 32.5 %collective-permute-start.49 = (bf16[128,2048]{1,0:T(8,128)(2,1)}, bf16[128,2048]{1,0:T(8,128)(2,1)}, u32[]{:S(2)}, u32[]{:S(2)}) collective-permute-start(bf16[128,2048]{1,0:T(8,128)(2,1)} %get-tuple-element.188), channel_id=1, source_target_pairs={{0,6},{1,7},{2,4},{3,5},{4,2},{5,3},{6,0},{7,1},{8,14},{9,15},{10,... | collective-permute-start | bytes 1572872 | tf_op jit(solution)/shard_map/ppermute | solution.py:52
  364.3 30.2 %collective-permute-start.52 = (f32[8,2560]{1,0:T(8,128)S(1)}, f32[8,2560]{1,0:T(8,128)S(1)}, u32[]{:S(2)}, u32[]{:S(2)}) collective-permute-start(f32[8,2560]{1,0:T(8,128)S(1)} %add.362), channel_id=1, source_target_pairs={{0,4},{1,5},{2,6},{3,7},{4,0},{5,1},{6,2},{7,3},{8,12},{9,13},{10,... | collective-permute-start | bytes 245768 | tf_op jit(solution)/shard_map/ppermute | solution.py:52
  432.7 223.0 %all-gather.7.cloned.1.call-start = ((), (), s32[]{:S(2)}) async-start(), calls=%async_computation.1 | async-start | bytes 1474560 | tf_op jit(solution)/shard_map/all_gather | solution.py:1099
  464.9 29.6 %collective-permute-start.68 = (bf16[9,48,256]{2,1,0:T(8,128)(2,1)}, bf16[9,48,256]{2,1,0:T(8,128)(2,1)S(1)}, u32[]{:S(2)}, u32[]{:S(2)}) collective-permute-start(bf16[9,48,256]{2,1,0:T(8,128)(2,1)} %fusion.34), channel_id=1, source_target_pairs={{0,8},{8,0},{16,24},{24,16},{1,9},{9,1},{17,25},{25,17},{2,10},{10... | collective-permute-start | bytes 663560 | tf_op jit(solution)/shard_map/ppermute | solution.py:997
  466.5 28.5 %collective-permute-start.69 = (bf16[9,48,256]{2,1,0:T(8,128)(2,1)}, bf16[9,48,256]{2,1,0:T(8,128)(2,1)S(1)}, u32[]{:S(2)}, u32[]{:S(2)}) collective-permute-start(bf16[9,48,256]{2,1,0:T(8,128)(2,1)} %fusion.34), channel_id=1, source_target_pairs={{0,16},{8,24},{16,0},{24,8},{1,17},{9,25},{17,1},{25,9},{2,18},{10... | collective-permute-start | bytes 663560 | tf_op jit(solution)/shard_map/ppermute | solution.py:997
  469.1 29.4 %collective-permute-start.70 = (bf16[9,48,256]{2,1,0:T(8,128)(2,1)}, bf16[9,48,256]{2,1,0:T(8,128)(2,1)S(1)}, u32[]{:S(2)}, u32[]{:S(2)}) collective-permute-start(bf16[9,48,256]{2,1,0:T(8,128)(2,1)} %fusion.34), channel_id=1, source_target_pairs={{0,24},{8,16},{16,8},{24,0},{1,25},{9,17},{17,9},{25,1},{2,26},{10... | collective-permute-start | bytes 663560 | tf_op jit(solution)/shard_map/ppermute | solution.py:997
  527.9 27.5 %collective-permute-start.72 = (bf16[16,4864]{1,0:T(8,128)(2,1)S(1)}, bf16[16,4864]{1,0:T(8,128)(2,1)S(1)}, u32[]{:S(2)}, u32[]{:S(2)}) collective-permute-start(bf16[16,4864]{1,0:T(8,128)(2,1)S(1)} %fusion.99), channel_id=1, source_target_pairs={{0,2},{1,3},{2,0},{3,1},{4,6},{5,7},{6,4},{7,5},{8,10},{9,11},{10,... | collective-permute-start | bytes 466952 | tf_op jit(solution)/shard_map/ppermute | solution.py:52
  555.5 53.8 %collective-permute-start.78 = (bf16[4,128,2048]{2,1,0:T(8,128)(2,1)}, bf16[4,128,2048]{2,1,0:T(8,128)(2,1)}, u32[]{:S(2)}, u32[]{:S(2)}) collective-permute-start(bf16[4,128,2048]{2,1,0:T(8,128)(2,1)} %get-tuple-element.243), channel_id=1, source_target_pairs={{0,1},{1,0},{2,3},{3,2},{4,5},{5,4},{6,7},{7,6},{8,9},{9,8},{10,11... | collective-permute-start | bytes 6291464 | tf_op jit(solution)/shard_map/ppermute | solution.py:52
  556.4 102.8 %collective-permute-start.65 = (bf16[128,2048]{1,0:T(8,128)(2,1)}, bf16[128,2048]{1,0:T(8,128)(2,1)}, u32[]{:S(2)}, u32[]{:S(2)}) collective-permute-start(bf16[128,2048]{1,0:T(8,128)(2,1)} %get-tuple-element.209), channel_id=1, source_target_pairs={{0,2},{1,3},{2,0},{3,1},{4,6},{5,7},{6,4},{7,5},{8,10},{9,11},{10,... | collective-permute-start | bytes 1572872 | tf_op jit(solution)/shard_map/ppermute | solution.py:52
  557.7 101.5 %collective-permute-start.66 = (bf16[128,2048]{1,0:T(8,128)(2,1)}, bf16[128,2048]{1,0:T(8,128)(2,1)}, u32[]{:S(2)}, u32[]{:S(2)}) collective-permute-start(bf16[128,2048]{1,0:T(8,128)(2,1)} %get-tuple-element.210), channel_id=1, source_target_pairs={{0,4},{1,5},{2,6},{3,7},{4,0},{5,1},{6,2},{7,3},{8,12},{9,13},{10,... | collective-permute-start | bytes 1572872 | tf_op jit(solution)/shard_map/ppermute | solution.py:52
  558.9 100.3 %collective-permute-start.67 = (bf16[128,2048]{1,0:T(8,128)(2,1)}, bf16[128,2048]{1,0:T(8,128)(2,1)}, u32[]{:S(2)}, u32[]{:S(2)}) collective-permute-start(bf16[128,2048]{1,0:T(8,128)(2,1)} %get-tuple-element.211), channel_id=1, source_target_pairs={{0,6},{1,7},{2,4},{3,5},{4,2},{5,3},{6,0},{7,1},{8,14},{9,15},{10,... | collective-permute-start | bytes 1572872 | tf_op jit(solution)/shard_map/ppermute | solution.py:52
  (138 other events, 1716.8 us)
Sparse Core Ops, SparseCore 0:
  432.8 88.8 all-gather.4
  560.1 29.1 all-gather.6

commit v4 on v3

--- a/solution.py
+++ b/solution.py
@@ -69,14 +69,6 @@
     mine = jnp.stack(list(across(x, n).values()))
     mask = jnp.arange(n) ^ me
     return jnp.concatenate([mine, swap(mine, n, 1)])[mask // 2 + mask % 2 * (n // 2)]
-
-
-def sum_small(x, n):
-    d = 1
-    while d < n:
-        x = x + swap(x, n, d)
-        d *= 2
-    return x
 
 
 def halve(near, far, n):
@@ -941,13 +933,17 @@
     own_lo = (own_a - lax.reduce_precision(own_a, 8, 7)).astype(BF16)
     spare = jnp.stack([routes.astype(BF16).reshape(-1), own_hi.reshape(-1), own_lo.reshape(-1)])
     first = jnp.concatenate([pack_maps(attn_small[0, : EXPERTS + 2], n, spare), normed_own])
+    def send(g):
+        return [lax.ppermute(g, "rep", [(i, i ^ d) for i in range(reps)]) if d else g for d in range(reps)]
+
     weights = [attention_query_weight, key_value_weight]
+    picks_sent = send(docs)
     if n == 8:
         cut = (first.shape[0] // 2 + 15) // 16 * 16
         y0, x1 = swap(first[:cut], n, 4), swap(first[cut:], n, 2)
         y1, x0 = swap(first[cut:], n, 4), swap(first[:cut], n, 2)
         y0, x1, *weights = tie(y0, x1, *weights)
-        d0, d1 = swap(y0, n, 2), swap(x1, n, 4)
+        d0, d1, *picks_sent = tie(swap(y0, n, 2), swap(x1, n, 4), *picks_sent)
         chips = {0: first}
         for m, p in ((2, (x0, x1)), (4, (y0, y1)), (6, (d0, d1))):
             chips[m] = jnp.concatenate(p)
@@ -993,9 +989,6 @@
 
     select_a, select_f = slot_select(slot_a), slot_select(slot_f)
 
-    def send(g):
-        return [lax.ppermute(g, "rep", [(i, i ^ d) for i in range(reps)]) if d else g for d in range(reps)]
-
     share_ae = share_a.transpose(1, 0, 2)
     q, kv, rank_q, rank_kv, rows_a_own, normed_own_columns = qkv(
         me_ref, pieces, key_a, select_tok, table_hi, table_lo, w_in, b_in
@@ -1012,6 +1005,11 @@
     grads_out_all = from_sibling(dict(zip(cotangent_chips, sent)), n)
     *attn_low, key_late = tie(*attn_low, key_f)
 
+    def slot_row(share, slot):
+        hot = slot[:, :, None, :] == jnp.arange(CAP, dtype=jnp.int32)[None, None, :, None]
+        row = jnp.sum(jnp.where(hot, share[:, :, None, :], 0.0), axis=-1)
+        return row.transpose(1, 0, 2).reshape(EXPERTS, 1, slots)
+
     w_feed = jnp.swapaxes(feed_expert_weight, 2, 3)
     grad_inner, back_down, rows_g_own = feed_back_down(
         me_ref, grads_out_all, maps, groups, EXPERTS + 2, 3, key_late, select_tok, w_feed, hidden_small
@@ -1019,7 +1017,10 @@
     attn_total, grad_inner = tie(attn_total, grad_inner)
     attended = x + collect(attn_total, attn_low, n)
     normed_two_own = rms_norm(gain_two, attended).astype(BF16)
-    normed_two = from_sibling(across(normed_two_own, n), n)
+    chips = across(normed_two_own, n)
+    scaled_a = select_a * slot_row(share_a, slot_a)
+    select_a, select_f, scaled_a, *sent = tie(select_a, select_f, scaled_a, *chips.values())
+    normed_two = from_sibling(dict(zip(chips, sent)), n)
     own_f = own_shares(normed_two_own, feed_router_weight, routes_f_own)
     share_f = gather_small(own_f, me, n)
     share_fe = share_f.transpose(1, 0, 2)
@@ -1029,20 +1030,26 @@
     )
     near, far = near.reshape(n // 2, tok, wide), far.reshape(n // 2, tok, wide)
     two_total, two_low = halve(near, far, n)
+    dshare_f = dshare_f[:1]
+    dshare_f = dshare_f + swap(dshare_f, n, 1)
     *two_low, inner, dshare_f, live_f, live_o = tie(*two_low, inner, dshare_f, live_f, live_o)
     live_f = jnp.concatenate([live_f, live_o])
     live_f = live_f + swap(live_f, n, 1)
     near, far, unused = project_out(
         "feed_out", me_ref, inner, key_f, share_fe, select_tok, hidden_small, w_feed, maps, groups, EXPERTS + 2, 3, 2
     )
-    grad_two_own = collect(two_total, two_low, n)
+    two_got = [swap(part, n, 2 * i + 2) for i, part in enumerate(two_low)]
+    near, far, *two_got = tie(near, far, *two_got)
+    grad_two_own = added([two_total] + two_got)
 
     def own_tokens(slot, dshare):
         mine = lax.dynamic_slice_in_dim(dshare.reshape(EXPERTS, n, CAP), me, 1, 1)[:, 0]
         hot = lax.dynamic_slice_in_dim(slot, me, 1, 0)[0][:, None, :] == jnp.arange(CAP)[None, :, None]
         return jnp.sum(jnp.where(hot, mine[:, :, None], 0.0), axis=1)
 
-    dshare_f = sum_small(dshare_f, n)[:1]
+    d = 2
+    while d < n:
+        dshare_f, d = dshare_f + swap(dshare_f, n, d), 2 * d
     grad_two_own = grad_two_own + route_back(own_f, own_tokens(slot_f, dshare_f), feed_router_weight)
     grad_attended = cotangent.astype(F32) + rms_back(attended, gain_two, grad_two_own)
 
@@ -1059,6 +1066,10 @@
     )
     grad_mixed, *sent = tie(grad_mixed, *live_f_sent, *out_low)
     live_f_sent, out_low = sent[: n // 2], sent[n // 2 :]
+    gq, gk, gv = attend_back(slot_a, begin[:, None], q, grad_mixed, mixed, lse, kv[0], kv[1])
+    out_got = [swap(part, n, 2 * i + 2) for i, part in enumerate(out_low)]
+    gq, *sent = tie(gq, *live_f_sent, *out_got)
+    live_f_sent, out_got = sent[: n // 2], sent[n // 2 :]
     live_f = added(live_f_sent)
     live_f, live_o = live_f[: 3 * RANK], live_f[3 * RANK :]
 
@@ -1071,11 +1082,6 @@
 
     def grads(rank, rows):
         return ein("eks,esw->ekw", rank, rows).astype(BF16)
-
-    def slot_row(share, slot):
-        hot = slot[:, :, None, :] == jnp.arange(CAP, dtype=jnp.int32)[None, None, :, None]
-        row = jnp.sum(jnp.where(hot, share[:, :, None, :], 0.0), axis=-1)
-        return row.transpose(1, 0, 2).reshape(EXPERTS, 1, slots)
 
     def by_stream(sent):
         out = jnp.zeros((reps,) + sent[0].shape, sent[0].dtype)
@@ -1083,7 +1089,7 @@
             out = lax.dynamic_update_slice_in_dim(out, got[None], lax.axis_index("rep") ^ d, 0)
         return out
 
-    scaled_f, scaled_a = select_f * slot_row(share_f, slot_f), select_a * slot_row(share_a, slot_a)
+    scaled_f = select_f * slot_row(share_f, slot_f)
     width_grad = jnp.stack(
         [
             grads(spread(of_slots(live_f[:RANK]), select_f), rows_f_own),
@@ -1093,14 +1099,8 @@
         axis=1,
     )
     b_out_grad = grads(spread(of_slots(live_o), scaled_a), rows_ga_own)
-    noted = jnp.zeros((1, k, own), BF16).at[0, 0, :doc_count].set(docs.astype(BF16))
-    early_grad = jnp.concatenate([a_out_grad, b_out_grad, noted])
-    width_grad, early_grad, lse_late = tie(width_grad, early_grad, lse)
-    hidden_all, width_all = lax.all_gather(hidden_grad, "rep"), lax.all_gather(width_grad, "rep")
-    early_sent = send(early_grad)
-    gq, gk, gv = attend_back(slot_a, begin[:, None], q, grad_mixed, mixed, lse_late, kv[0], kv[1])
-    gq, *early_sent = tie(gq, *early_sent)
-    layer_out = attended + collect(out_total, out_low, n)
+    early_grad = jnp.concatenate([a_out_grad, b_out_grad])
+    layer_out = attended + added([out_total] + out_got)
     gq, gkv, back_q, back_kv, live_in, b_in_grad = qkv_rank(
         key_a, select_tok, table_hi, table_lo, b_in, gq, gk, gv, rank_q, rank_kv
     )
@@ -1108,11 +1108,13 @@
     spare = -dshare_a.shape[1] % 128
     live_in = jnp.concatenate([live_in, jnp.pad(dshare_a, ((0, 0), (0, spare)))], axis=1)
     live_in = live_in + swap(live_in, n, 1)
-    gq, live_in, b_in_grad = tie(gq, live_in, b_in_grad)
+    gq, live_in, b_in_grad, early_grad, width_grad = tie(gq, live_in, b_in_grad, early_grad, width_grad)
+    hidden_all, width_all = lax.all_gather(hidden_grad, "rep"), lax.all_gather(width_grad, "rep")
+    early_sent = send(early_grad)
     live_sent, late_b_sent = list(across(live_in, n).values()), send(b_in_grad)
     near, far = qkv_back(me_ref, pieces, key_a, w_in, gq, gkv, back_q, back_kv)
-    near, far, *sent = tie(near, far, *live_sent, *late_b_sent)
-    live_sent, late_b_sent = sent[: n // 2], sent[n // 2 :]
+    near, far, *sent = tie(near, far, *live_sent, *early_sent)
+    live_sent, early_sent = sent[: n // 2], sent[n // 2 :]
     in_total, in_low = (quarter if n == 8 else halve)(near, far, n)
     *in_low, first_sent = tie(*in_low, live_sent[0])
     in_got = [swap(part, n, 2 * i + 2) for i, part in enumerate(in_low)]
@@ -1126,19 +1128,20 @@
             ein("pks,sw->pkw", spread(live_kv, select_row), normed_own_columns).astype(BF16),
         ]
     )
-    a_in_grad, hidden_all, *in_got = tie(a_in_grad, hidden_all, *in_got)
+    a_in_grad, hidden_all, *sent = tie(a_in_grad, hidden_all, *late_b_sent, *in_got)
+    late_b_sent, in_got = sent[:reps], sent[reps:]
     late_a_sent = send(a_in_grad)
     grad_normed = collect_quarters(in_total, in_got, n) if n == 8 else added([in_total] + in_got)
     grad_normed = grad_normed + route_back(own_a, own_tokens(slot_a, dshare_a), attention_router_weight)
     grad_normed, width_all = tie(grad_normed, width_all)
     grad_in = grad_attended + rms_back(x, gain_one, grad_normed)
 
+    picks = jax.vmap(one_hot)(jnp.stack(picks_sent)[jnp.arange(reps) ^ lax.axis_index("rep")])
     early = by_stream(early_sent)
-    picks = jax.vmap(one_hot)(early[:, 2 * EXPERTS, 0, :doc_count].astype(jnp.int32))
     hidden_out = ein("rpekf,rkc->pecf", hidden_all, picks)
     width_out = ein("rpmkw,rkc->pmwc", width_all, picks)
     late_b, late_a = by_stream(late_b_sent), by_stream(late_a_sent)
-    attn = jnp.concatenate([late_a, early[:, :EXPERTS], late_b, early[:, EXPERTS : 2 * EXPERTS]], axis=1)
+    attn = jnp.concatenate([late_a, early[:, :EXPERTS], late_b, early[:, EXPERTS:]], axis=1)
     attn = attn.reshape(reps, 2, -1, k, own)
     attn_out = ein("rpmkw,rkc->pmwc", attn, picks)
     return (layer_out, grad_in, attn_out, width_out, hidden_out)

time: 679 us -> 616 us (0.907)
  local copies, waits for them, and re-layouts: 93.1 us -> 51.4 us
  starting transfers between devices: 91.1 us -> 80.9 us
  waiting for transfers between devices: 136 us -> 128 us
    dynamic_update_slice x12, local copies, waits for them, and re-layouts: 44.9 us -> 3.87 us  [by_stream(): lax.dynamic_update_slice_in_dim(out, got[None], lax.axis_index('rep') ^ d...]
    ppermute x9 -> x12, starting transfers between devices: 27.5 us -> 19.9 us  [send(): lax.ppermute(g, 'rep', [(i, i ^ d) for i in range(reps)])]
  transfers between devices with their start and end apart: 88 -> 91, of which waited for: 24 -> 20; matrix products, arithmetic and copies ran while one was open for 21% -> 15% of each run, Pallas kernels for 27% -> 30%
where the time goes in v4:
time: 616 us; the launch traced here: 608 us
  Pallas kernels  261 us (42%)
  waiting for transfers between devices  128 us (21%)
  starting transfers between devices  80.9 us (13%)
  local copies, waits for them, and re-layouts  51.4 us (8%)
  other arithmetic  49.7 us (8%)
  matrix products  20.6 us (3%)
  between operations  16.8 us (3%)
    pallas_call x10, Pallas kernels, run(): return call(*args)  261 us
    ppermute x77, waiting for transfers between devices, swap(): return lax.ppermute(x, 'shard', [(i, i ^ d) for i in range(n)])  124 us
    ppermute x77, starting transfers between devices, swap(): return lax.ppermute(x, 'shard', [(i, i ^ d) for i in range(n)])  61 us
    ppermute x12, starting transfers between devices, send(): lax.ppermute(g, 'rep', [(i, i ^ d) for i in range(reps)])  19.9 us
    dot_general x16, matrix products, ein(): return jnp.einsum(spec, a, b, preferred_element_type=F32)  19.3 us
  transfers between devices with their start and end apart: 91, of which 20 were waited for; matrix products, arithmetic and copies ran while one was open for 15% of the time, Pallas kernels for 30%

profile of v4, /device:TPU:0, one launch (start us, length us, event | category | flops | bytes accessed | tf_op | source)
XLA Modules:
  0.0 608.3 jit_solution(7005902506992695708)
XLA Ops:
  27.7 4.7 collective-permute-done.3
  32.4 3.6 collective-permute-start.11
  48.2 36.6 %collective-permute-done.8 = bf16[80,2048]{1,0:T(8,128)(2,1)S(1)} collective-permute-done((bf16[80,2048]{1,0:T(8,128)(2,1)S(1)}, bf16[80,2048]{1,0:T(8,128)(2,1)S(1)}, u32[]{:S(2)}, u32[]{:S(2)}) %collective-permute-start.8) | collective-permute-done | bytes 327712 | tf_op jit(solution)/shard_map/ppermute | solution.py:52
  94.2 10.5 %collective-permute-done.15 = bf16[6,256,256]{2,1,0:T(8,128)(2,1)S(1)} collective-permute-done((bf16[6,256,256]{2,1,0:T(8,128)(2,1)S(1)}, bf16[6,256,256]{2,1,0:T(8,128)(2,1)S(1)}, u32[]{:S(2)}, u32[]{:S(2)}) %collective-permute-start.15) | collective-permute-done | bytes 786464 | tf_op jit(solution)/shard_map/ppermute | solution.py:52
  105.7 11.7 %collective-permute-done.16 = bf16[6,256,256]{2,1,0:T(8,128)(2,1)S(1)} collective-permute-done((bf16[6,256,256]{2,1,0:T(8,128)(2,1)S(1)}, bf16[6,256,256]{2,1,0:T(8,128)(2,1)S(1)}, u32[]{:S(2)}, u32[]{:S(2)}) %collective-permute-start.16) | collective-permute-done | bytes 786464 | tf_op jit(solution)/shard_map/ppermute | solution.py:52
  119.2 4.7 collective-permute-done.18
  133.1 24.3 %qkv.1 = (bf16[4,640,256]{2,1,0:T(8,128)(2,1)}, bf16[2,1024,256]{2,1,0:T(8,128)(2,1)}, bf16[4,640,48]{2,1,0:T(8,128)(2,1)}, bf16[2,1024,48]{2,1,0:T(8,128)(2,1)}...) custom-call(s32[1]{0:T(128)} %bitcast.refs_0_, bf16[176,2048]{1,0:T(8,128)(2,1)} %copy-done.25, ...), custom_call_target="tpu_custom_call" | custom-call | flops 7247757312 | bytes 33554432 | tf_op jit(solution)/shard_map/qkv/pallas_call | solution.py:638
  165.3 17.8 %attend.1 = (bf16[4,8,80,256]{3,2,1,0:T(8,128)(2,1)}, f32[4,8,80,256]{3,2,1,0:T(8,128)}) custom-call(s32[8,4,128]{2,1,0:T(4,128)} %copy.136.key, s32[8,1,128]{2,1,0:T(1,128)} %bitcast.451, bf16[4,8,80,256]{3,2,1,0:T(8,128)(2,1)} %bitcast.474, bf16[1024,256]{1,0:T(8,128)(2,1)} %get-tuple-element.359.k, bf16[1024,256]{1,0:T(8,128)(2,1)} %get-tuple-element.358.v), custom_call_target="tpu_custom_call" | custom-call | flops 2013265920 | bytes 33554432 | tf_op jit(solution)/shard_map/attend/pallas_call | solution.py:638
  183.2 18.1 %attend_out.1 = (bf16[4,128,2048]{2,1,0:T(8,128)(2,1)}, bf16[4,128,2048]{2,1,0:T(8,128)(2,1)}, bf16[16,2560]{1,0:T(8,128)(2,1)}) custom-call(s32[1]{0:T(128)} %bitcast.refs_0_, bf16[96,2048]{1,0:T(8,128)(2,1)} %copy-done.12, bf16[96,2048]{1,0:T(8,128)(2,1)} %copy-done.19, bf16[96,2048]{1,0:T(8,128)(2,1)} %copy-done.18, bf16[96,2048]{1,0:T(8,128)(2,1)} %copy-done.20, ...), custom_call_target="tpu_custom_call" | custom-call | flops 4026531840 | bytes 33554432 | tf_op jit(solution)/shard_map/attend_out/pallas_call | solution.py:638
  201.4 3.6 fusion.refs_20_.refs_22_.refs_13_
  206.2 3.4 and_reduce_fusion
  210.8 3.1 convert_add_fusion.3
  219.4 22.0 %feed_down_back.1 = (f32[4,640,704]{2,1,0:T(8,128)}, bf16[4,640,48]{2,1,0:T(8,128)(2,1)}, bf16[4,640,256]{2,1,0:T(8,128)(2,1)}) custom-call(s32[1]{0:T(128)} %bitcast.refs_0_, bf16[128,2048]{1,0:T(8,128)(2,1)} %refs_1_, bf16[128,2048]{1,0:T(8,128)(2,1)} %copy-done.27, bf16[128,2048]{1,0:T(8,128)(2,1)} %collective-permute-done.27.refs_3_, ...), custom_call_target="tpu_custom_call" | custom-call | flops 9596567552 | bytes 33554432 | tf_op jit(solution)/shard_map/feed_down_back/pallas_call | solution.py:638
  254.8 10.5 %collective-permute-done.38.refs_3_ = bf16[128,2048]{1,0:T(8,128)(2,1)S(1)} collective-permute-done((bf16[128,2048]{1,0:T(8,128)(2,1)S(1)}, bf16[128,2048]{1,0:T(8,128)(2,1)S(1)}, u32[]{:S(2)}, u32[]{:S(2)}) %collective-permute-start.38) | collective-permute-done | bytes 524320 | tf_op jit(solution)/shard_map/ppermute | solution.py:52
  265.3 9.8 %collective-permute-done.40.refs_7_ = bf16[128,2048]{1,0:T(8,128)(2,1)} collective-permute-done((bf16[128,2048]{1,0:T(8,128)(2,1)S(1)}, bf16[128,2048]{1,0:T(8,128)(2,1)}, u32[]{:S(2)}, u32[]{:S(2)}) %collective-permute-start.40) | collective-permute-done | bytes 524320 | tf_op jit(solution)/shard_map/ppermute | solution.py:52
  279.6 79.1 %feed.1 = (bf16[512,2048]{1,0:T(8,128)(2,1)}, bf16[512,2048]{1,0:T(8,128)(2,1)}, bf16[4,640,704]{2,1,0:T(8,128)(2,1)}, bf16[48,2560]{1,0:T(8,128)(2,1)}, f32[8,2...) custom-call(s32[1]{0:T(128)} %bitcast.refs_0_, bf16[128,2048]{1,0:T(8,128)(2,1)} %copy-done.17, ...), custom_call_target="tpu_custom_call" | custom-call | flops 38386270208 | bytes 33554432 | tf_op jit(solution)/shard_map/feed/pallas_call | solution.py:638
  363.9 5.2 convert_add_fusion
  376.2 28.8 %feed_out.1 = (bf16[4,128,2048]{2,1,0:T(8,128)(2,1)}, bf16[4,128,2048]{2,1,0:T(8,128)(2,1)}, bf16[16,2560]{1,0:T(8,128)(2,1)}) custom-call(s32[1]{0:T(128)} %bitcast.refs_0_, bf16[96,2048]{1,0:T(8,128)(2,1)} %copy-done.12, bf16[96,2048]{1,0:T(8,128)(2,1)} %copy-done.19, bf16[96,2048]{1,0:T(8,128)(2,1)} %copy-done.18, bf16[96,2048]{1,0:T(8,128)(2,1)} %copy-done.20, ...), custom_call_target="tpu_custom_call" | custom-call | flops 11072962560 | bytes 33554432 | tf_op jit(solution)/shard_map/feed_out/pallas_call | solution.py:638
  416.9 7.5 %collective-permute-done.57.refs_3_ = bf16[128,2048]{1,0:T(8,128)(2,1)S(1)} collective-permute-done((bf16[128,2048]{1,0:T(8,128)(2,1)S(1)}, bf16[128,2048]{1,0:T(8,128)(2,1)S(1)}, u32[]{:S(2)}, u32[]{:S(2)}) %collective-permute-start.57) | collective-permute-done | bytes 524320 | tf_op jit(solution)/shard_map/ppermute | solution.py:52
  424.5 10.8 %collective-permute-done.59.refs_7_ = bf16[128,2048]{1,0:T(8,128)(2,1)} collective-permute-done((bf16[128,2048]{1,0:T(8,128)(2,1)S(1)}, bf16[128,2048]{1,0:T(8,128)(2,1)}, u32[]{:S(2)}, u32[]{:S(2)}) %collective-permute-start.59) | collective-permute-done | bytes 524320 | tf_op jit(solution)/shard_map/ppermute | solution.py:52
  443.3 16.4 %mixed_back.1 = (bf16[4,640,256]{2,1,0:T(8,128)(2,1)}, bf16[4,48,256]{2,1,0:T(8,128)(2,1)}, f32[8,2560]{1,0:T(8,128)}, bf16[4,640,256]{2,1,0:T(8,128)(2,1)}) custom-call(s32[1]{0:T(128)} %bitcast.refs_0_, bf16[128,2048]{1,0:T(8,128)(2,1)} %copy-done.31, bf16[128,2048]{1,0:T(8,128)(2,1)} %collective-permute-done.60.refs_2_, bf16[128,2048]{1,0:T(8,128)(2,1)} %copy-done.94, ...), custom_call_target="tpu_custom_call" | custom-call | flops 4026531840 | bytes 33554432 | tf_op jit(solution)/shard_map/mixed_back/pallas_call | solution.py:638
  465.7 24.2 %attend_back.1 = (f32[4,8,80,256]{3,2,1,0:T(8,128)}, f32[1024,256]{1,0:T(8,128)}, f32[1024,256]{1,0:T(8,128)}) custom-call(s32[8,4,128]{2,1,0:T(4,128)} %copy.136.key, s32[8,1,128]{2,1,0:T(1,128)} %bitcast.452, bf16[4,8,80,256]{3,2,1,0:T(8,128)(2,1)} %bitcast.475, bf16[4,8,80,256]{3,2,1,0:T(8,128)(2,1)} %bitcast.478, ...), custom_call_target="tpu_custom_call" | custom-call | flops 4697620480 | bytes 33554432 | tf_op jit(solution)/shard_map/attend_back/pallas_call | solution.py:638
  492.7 9.0 %qkv_rank.1 = (bf16[4,640,256]{2,1,0:T(8,128)(2,1)}, bf16[2,1024,256]{2,1,0:T(8,128)(2,1)}, bf16[4,640,48]{2,1,0:T(8,128)(2,1)}, bf16[2,1024,48]{2,1,0:T(8,128)(...) custom-call(s32[4,8,128]{2,1,0:T(8,128)} %get-tuple-element.404.refs_9_.refs_10_.refs_17_.key, ...), custom_call_target="tpu_custom_call" | custom-call | flops 226492416 | bytes 33554432 | tf_op jit(solution)/shard_map/qkv_rank/pallas_call | solution.py:638
  511.0 4.1 collective-permute-start.77
  517.3 21.5 %qkv_back.1 = (bf16[4,128,2048]{2,1,0:T(8,128)(2,1)}, bf16[4,128,2048]{2,1,0:T(8,128)(2,1)}) custom-call(s32[1]{0:T(128)} %bitcast.refs_0_, bf16[176,2048]{1,0:T(8,128)(2,1)} %copy-done.25, bf16[176,2048]{1,0:T(8,128)(2,1)} %copy-done.89, bf16[176,2048]{1,0:T(8,128)(2,1)} %copy-done.37, bf16[176,2048]{1,0:T(8,128)(2,1)} %copy-done.90, ...), custom_call_target="tpu_custom_call" | custom-call | flops 7247757312 | bytes 33554432 | tf_op jit(solution)/shard_map/qkv_back/pallas_call | solution.py:638
  543.8 4.2 collective-permute-start.81
  549.2 5.2 convert_add_fusion.1
  560.8 9.5 %collective-permute-done.82 = bf16[2,64,2048]{2,1,0:T(8,128)(2,1)S(1)} collective-permute-done((bf16[2,64,2048]{2,1,0:T(8,128)(2,1)}, bf16[2,64,2048]{2,1,0:T(8,128)(2,1)S(1)}, u32[]{:S(2)}, u32[]{:S(2)}) %collective-permute-start.82) | collective-permute-done | bytes 524320 | tf_op jit(solution)/shard_map/ppermute | solution.py:52
  572.3 3.5 collective-permute-start.88
  580.8 4.0 convolution_bitcast_fusion
  594.5 3.2 convolution_bitcast_fusion.2
  598.1 3.2 fusion.10
  (597 shorter events, 167.6 us)
Async XLA Ops:
  7.2 553.5 %all-gather.5.cloned.1.call-start = ((), (), s32[]{:S(2)}) async-start(), calls=%async_computation | async-start | bytes 4423680 | tf_op jit(solution)/shard_map/all_gather | solution.py:1112
  17.7 25.3 %collective-permute-start.10 = (s32[3]{0:T(128)}, s32[3]{0:T(128)}, u32[]{:S(2)}, u32[]{:S(2)}) collective-permute-start(s32[3]{0:T(128)} %bitcast.1), channel_id=1, source_target_pairs={{0,16},{8,24},{16,0},{24,8},{1,17},{9,25},{17,1},{25,9},{2,18},{10... | collective-permute-start | bytes 44 | tf_op jit(solution)/shard_map/ppermute | solution.py:937
  39.4 45.5 %collective-permute-start.7 = (bf16[96,2048]{1,0:T(8,128)(2,1)S(1)}, bf16[96,2048]{1,0:T(8,128)(2,1)S(1)}, u32[]{:S(2)}, u32[]{:S(2)}) collective-permute-start(bf16[96,2048]{1,0:T(8,128)(2,1)S(1)} %collective-permute-done.2), channel_id=1, source_target_pairs={{0,2},{1,3},{2,0},{3,1},{4,6},{5,7},{6,4},{7,5},{8,10},{9,11},{10,... | collective-permute-start | bytes 1179656 | tf_op jit(solution)/shard_map/ppermute | solution.py:52
  41.2 43.6 %collective-permute-start.8 = (bf16[80,2048]{1,0:T(8,128)(2,1)S(1)}, bf16[80,2048]{1,0:T(8,128)(2,1)S(1)}, u32[]{:S(2)}, u32[]{:S(2)}) collective-permute-start(bf16[80,2048]{1,0:T(8,128)(2,1)S(1)} %collective-permute-done.3), channel_id=1, source_target_pairs={{0,4},{1,5},{2,6},{3,7},{4,0},{5,1},{6,2},{7,3},{8,12},{9,13},{10,... | collective-permute-start | bytes 983048 | tf_op jit(solution)/shard_map/ppermute | solution.py:52
  42.8 42.1 %collective-permute-start.4 = (bf16[176,2048]{1,0:T(8,128)(2,1)S(1)}, bf16[176,2048]{1,0:T(8,128)(2,1)S(1)}, u32[]{:S(2)}, u32[]{:S(2)}) collective-permute-start(bf16[176,2048]{1,0:T(8,128)(2,1)S(1)} %constant_dynamic-update-slice_fusion.7.refs_3_), channel_id=1, source_target_pairs={{0,1},{1,0},{2,3},{3,2},{4,5},{5,4},{6,7},{7,6},{8,9},{9,8},{10,11... | collective-permute-start | bytes 2162696 | tf_op jit(solution)/shard_map/ppermute | solution.py:52
  43.7 44.3 %collective-permute-start.13 = (bf16[6,256,256]{2,1,0:T(8,128)(2,1)S(1)}, bf16[6,256,256]{2,1,0:T(8,128)(2,1)S(1)}, u32[]{:S(2)}, u32[]{:S(2)}) collective-permute-start(bf16[6,256,256]{2,1,0:T(8,128)(2,1)S(1)} %pad_maximum_fusion.3), channel_id=1, source_target_pairs={{0,7},{1,6},{2,5},{3,4},{4,3},{5,2},{6,1},{7,0},{8,15},{9,14},{10,... | collective-permute-start | bytes 2359304 | tf_op jit(solution)/shard_map/ppermute | solution.py:52
  46.7 42.2 %collective-permute-start.14 = (bf16[6,256,256]{2,1,0:T(8,128)(2,1)S(1)}, bf16[6,256,256]{2,1,0:T(8,128)(2,1)S(1)}, u32[]{:S(2)}, u32[]{:S(2)}) collective-permute-start(bf16[6,256,256]{2,1,0:T(8,128)(2,1)S(1)} %pad_maximum_fusion.4), channel_id=1, source_target_pairs={{0,6},{1,7},{2,4},{3,5},{4,2},{5,3},{6,0},{7,1},{8,14},{9,15},{10,... | collective-permute-start | bytes 2359304 | tf_op jit(solution)/shard_map/ppermute | solution.py:52
  84.9 32.4 %collective-permute-start.16 = (bf16[6,256,256]{2,1,0:T(8,128)(2,1)S(1)}, bf16[6,256,256]{2,1,0:T(8,128)(2,1)S(1)}, u32[]{:S(2)}, u32[]{:S(2)}) collective-permute-start(bf16[6,256,256]{2,1,0:T(8,128)(2,1)S(1)} %pad_maximum_fusion.6), channel_id=1, source_target_pairs={{0,4},{1,5},{2,6},{3,7},{4,0},{5,1},{6,2},{7,3},{8,12},{9,13},{10,... | collective-permute-start | bytes 2359304 | tf_op jit(solution)/shard_map/ppermute | solution.py:52
  87.2 31.1 %collective-permute-start.17 = (bf16[6,256,256]{2,1,0:T(8,128)(2,1)S(1)}, bf16[6,256,256]{2,1,0:T(8,128)(2,1)S(1)}, u32[]{:S(2)}, u32[]{:S(2)}) collective-permute-start(bf16[6,256,256]{2,1,0:T(8,128)(2,1)S(1)} %pad_maximum_fusion.7), channel_id=1, source_target_pairs={{0,3},{1,2},{2,1},{3,0},{4,7},{5,6},{6,5},{7,4},{8,11},{9,10},{10,... | collective-permute-start | bytes 2359304 | tf_op jit(solution)/shard_map/ppermute | solution.py:52
  88.0 35.9 %collective-permute-start.18 = (bf16[6,256,256]{2,1,0:T(8,128)(2,1)S(1)}, bf16[6,256,256]{2,1,0:T(8,128)(2,1)S(1)}, u32[]{:S(2)}, u32[]{:S(2)}) collective-permute-start(bf16[6,256,256]{2,1,0:T(8,128)(2,1)S(1)} %pad_maximum_fusion.8), channel_id=1, source_target_pairs={{0,2},{1,3},{2,0},{3,1},{4,6},{5,7},{6,4},{7,5},{8,10},{9,11},{10,... | collective-permute-start | bytes 2359304 | tf_op jit(solution)/shard_map/ppermute | solution.py:52
  88.9 36.0 %collective-permute-start.19 = (bf16[6,256,256]{2,1,0:T(8,128)(2,1)S(1)}, bf16[6,256,256]{2,1,0:T(8,128)(2,1)S(1)}, u32[]{:S(2)}, u32[]{:S(2)}) collective-permute-start(bf16[6,256,256]{2,1,0:T(8,128)(2,1)S(1)} %pad_maximum_fusion.9), channel_id=1, source_target_pairs={{0,1},{1,0},{2,3},{3,2},{4,5},{5,4},{6,7},{7,6},{8,9},{9,8},{10,11... | collective-permute-start | bytes 2359304 | tf_op jit(solution)/shard_map/ppermute | solution.py:52
  104.7 25.5 %collective-permute-start.12 = (bf16[176,2048]{1,0:T(8,128)(2,1)S(1)}, bf16[176,2048]{1,0:T(8,128)(2,1)S(1)}, u32[]{:S(2)}, u32[]{:S(2)}) collective-permute-start(bf16[176,2048]{1,0:T(8,128)(2,1)S(1)} %constant_dynamic-update-slice_fusion.11.refs_7_), channel_id=1, source_target_pairs={{0,1},{1,0},{2,3},{3,2},{4,5},{5,4},{6,7},{7,6},{8,9},{9,8},{10,11... | collective-permute-start | bytes 2162696 | tf_op jit(solution)/shard_map/ppermute | solution.py:52
  126.7 30.8 %collective-permute-start.20 = (bf16[96,2048]{1,0:T(8,128)(2,1)S(1)}, bf16[96,2048]{1,0:T(8,128)(2,1)S(1)}, u32[]{:S(2)}, u32[]{:S(2)}) collective-permute-start(bf16[96,2048]{1,0:T(8,128)(2,1)S(1)} %pad_maximum_fusion.11.refs_1_.refs_9_), channel_id=1, source_target_pairs={{0,2},{1,3},{2,0},{3,1},{4,6},{5,7},{6,4},{7,5},{8,10},{9,11},{10,... | collective-permute-start | bytes 1179656 | tf_op jit(solution)/shard_map/ppermute | solution.py:52
  126.7 30.8 %collective-permute-start.21 = (bf16[96,2048]{1,0:T(8,128)(2,1)S(1)}, bf16[96,2048]{1,0:T(8,128)(2,1)}, u32[]{:S(2)}, u32[]{:S(2)}) collective-permute-start(bf16[96,2048]{1,0:T(8,128)(2,1)S(1)} %pad_maximum_fusion.11.refs_1_.refs_9_), channel_id=1, source_target_pairs={{0,4},{1,5},{2,6},{3,7},{4,0},{5,1},{6,2},{7,3},{8,12},{9,13},{10,... | collective-permute-start | bytes 1179656 | tf_op jit(solution)/shard_map/ppermute | solution.py:52
  128.6 28.9 %collective-permute-start.22 = (bf16[96,2048]{1,0:T(8,128)(2,1)S(1)}, bf16[96,2048]{1,0:T(8,128)(2,1)}, u32[]{:S(2)}, u32[]{:S(2)}) collective-permute-start(bf16[96,2048]{1,0:T(8,128)(2,1)S(1)} %pad_maximum_fusion.11.refs_1_.refs_9_), channel_id=1, source_target_pairs={{0,6},{1,7},{2,4},{3,5},{4,2},{5,3},{6,0},{7,1},{8,14},{9,15},{10,... | collective-permute-start | bytes 1179656 | tf_op jit(solution)/shard_map/ppermute | solution.py:52
  161.4 39.8 %collective-permute-start.27 = (bf16[128,2048]{1,0:T(8,128)(2,1)S(1)}, bf16[128,2048]{1,0:T(8,128)(2,1)}, u32[]{:S(2)}, u32[]{:S(2)}) collective-permute-start(bf16[128,2048]{1,0:T(8,128)(2,1)S(1)} %copy-done.8), channel_id=1, source_target_pairs={{0,2},{1,3},{2,0},{3,1},{4,6},{5,7},{6,4},{7,5},{8,10},{9,11},{10,... | collective-permute-start | bytes 1572872 | tf_op jit(solution)/shard_map/ppermute | solution.py:52
  161.6 39.6 %collective-permute-start.28 = (bf16[128,2048]{1,0:T(8,128)(2,1)S(1)}, bf16[128,2048]{1,0:T(8,128)(2,1)}, u32[]{:S(2)}, u32[]{:S(2)}) collective-permute-start(bf16[128,2048]{1,0:T(8,128)(2,1)S(1)} %copy-done.8), channel_id=1, source_target_pairs={{0,4},{1,5},{2,6},{3,7},{4,0},{5,1},{6,2},{7,3},{8,12},{9,13},{10,... | collective-permute-start | bytes 1572872 | tf_op jit(solution)/shard_map/ppermute | solution.py:52
  163.4 37.9 %collective-permute-start.29 = (bf16[128,2048]{1,0:T(8,128)(2,1)S(1)}, bf16[128,2048]{1,0:T(8,128)(2,1)}, u32[]{:S(2)}, u32[]{:S(2)}) collective-permute-start(bf16[128,2048]{1,0:T(8,128)(2,1)S(1)} %copy-done.8), channel_id=1, source_target_pairs={{0,6},{1,7},{2,4},{3,5},{4,2},{5,3},{6,0},{7,1},{8,14},{9,15},{10,... | collective-permute-start | bytes 1572872 | tf_op jit(solution)/shard_map/ppermute | solution.py:52
  215.1 27.6 %collective-permute-start.35 = (bf16[128,2048]{1,0:T(8,128)(2,1)}, bf16[128,2048]{1,0:T(8,128)(2,1)}, u32[]{:S(2)}, u32[]{:S(2)}) collective-permute-start(bf16[128,2048]{1,0:T(8,128)(2,1)} %get-tuple-element.189), channel_id=1, source_target_pairs={{0,2},{1,3},{2,0},{3,1},{4,6},{5,7},{6,4},{7,5},{8,10},{9,11},{10,... | collective-permute-start | bytes 1572872 | tf_op jit(solution)/shard_map/ppermute | solution.py:52
  216.5 26.3 %collective-permute-start.36 = (bf16[128,2048]{1,0:T(8,128)(2,1)}, bf16[128,2048]{1,0:T(8,128)(2,1)S(1)}, u32[]{:S(2)}, u32[]{:S(2)}) collective-permute-start(bf16[128,2048]{1,0:T(8,128)(2,1)} %get-tuple-element.190), channel_id=1, source_target_pairs={{0,4},{1,5},{2,6},{3,7},{4,0},{5,1},{6,2},{7,3},{8,12},{9,13},{10,... | collective-permute-start | bytes 1572872 | tf_op jit(solution)/shard_map/ppermute | solution.py:52
  217.6 26.0 %collective-permute-start.37 = (bf16[128,2048]{1,0:T(8,128)(2,1)}, bf16[128,2048]{1,0:T(8,128)(2,1)}, u32[]{:S(2)}, u32[]{:S(2)}) collective-permute-start(bf16[128,2048]{1,0:T(8,128)(2,1)} %get-tuple-element.191), channel_id=1, source_target_pairs={{0,6},{1,7},{2,4},{3,5},{4,2},{5,3},{6,0},{7,1},{8,14},{9,15},{10,... | collective-permute-start | bytes 1572872 | tf_op jit(solution)/shard_map/ppermute | solution.py:52
  371.3 34.6 %collective-permute-start.51 = (bf16[128,2048]{1,0:T(8,128)(2,1)}, bf16[128,2048]{1,0:T(8,128)(2,1)}, u32[]{:S(2)}, u32[]{:S(2)}) collective-permute-start(bf16[128,2048]{1,0:T(8,128)(2,1)} %get-tuple-element.207), channel_id=1, source_target_pairs={{0,2},{1,3},{2,0},{3,1},{4,6},{5,7},{6,4},{7,5},{8,10},{9,11},{10,... | collective-permute-start | bytes 1572872 | tf_op jit(solution)/shard_map/ppermute | solution.py:52
  372.3 33.6 %collective-permute-start.52 = (bf16[128,2048]{1,0:T(8,128)(2,1)}, bf16[128,2048]{1,0:T(8,128)(2,1)}, u32[]{:S(2)}, u32[]{:S(2)}) collective-permute-start(bf16[128,2048]{1,0:T(8,128)(2,1)} %get-tuple-element.208), channel_id=1, source_target_pairs={{0,4},{1,5},{2,6},{3,7},{4,0},{5,1},{6,2},{7,3},{8,12},{9,13},{10,... | collective-permute-start | bytes 1572872 | tf_op jit(solution)/shard_map/ppermute | solution.py:52
  373.0 33.0 %collective-permute-start.53 = (bf16[128,2048]{1,0:T(8,128)(2,1)}, bf16[128,2048]{1,0:T(8,128)(2,1)}, u32[]{:S(2)}, u32[]{:S(2)}) collective-permute-start(bf16[128,2048]{1,0:T(8,128)(2,1)} %get-tuple-element.209), channel_id=1, source_target_pairs={{0,6},{1,7},{2,4},{3,5},{4,2},{5,3},{6,0},{7,1},{8,14},{9,15},{10,... | collective-permute-start | bytes 1572872 | tf_op jit(solution)/shard_map/ppermute | solution.py:52
  374.8 30.2 %collective-permute-start.55 = (f32[1,2560]{1,0:T(1,128)S(1)}, f32[1,2560]{1,0:T(1,128)S(1)}, u32[]{:S(2)}, u32[]{:S(2)}) collective-permute-start(f32[1,2560]{1,0:T(1,128)S(1)} %add.368), channel_id=1, source_target_pairs={{0,4},{1,5},{2,6},{3,7},{4,0},{5,1},{6,2},{7,3},{8,12},{9,13},{10,... | collective-permute-start | bytes 30728 | tf_op jit(solution)/shard_map/ppermute | solution.py:52
  439.1 155.3 %all-gather.7.cloned.1.call-start = ((), (), s32[]{:S(2)}) async-start(), calls=%async_computation.1 | async-start | bytes 1474560 | tf_op jit(solution)/shard_map/all_gather | solution.py:1112
  461.2 28.7 %collective-permute-start.68 = (bf16[128,2048]{1,0:T(8,128)(2,1)}, bf16[128,2048]{1,0:T(8,128)(2,1)S(1)}, u32[]{:S(2)}, u32[]{:S(2)}) collective-permute-start(bf16[128,2048]{1,0:T(8,128)(2,1)} %get-tuple-element.239), channel_id=1, source_target_pairs={{0,2},{1,3},{2,0},{3,1},{4,6},{5,7},{6,4},{7,5},{8,10},{9,11},{10,... | collective-permute-start | bytes 1572872 | tf_op jit(solution)/shard_map/ppermute | solution.py:52
  462.9 27.0 %collective-permute-start.69 = (bf16[128,2048]{1,0:T(8,128)(2,1)}, bf16[128,2048]{1,0:T(8,128)(2,1)}, u32[]{:S(2)}, u32[]{:S(2)}) collective-permute-start(bf16[128,2048]{1,0:T(8,128)(2,1)} %get-tuple-element.240), channel_id=1, source_target_pairs={{0,4},{1,5},{2,6},{3,7},{4,0},{5,1},{6,2},{7,3},{8,12},{9,13},{10,... | collective-permute-start | bytes 1572872 | tf_op jit(solution)/shard_map/ppermute | solution.py:52
  463.6 26.3 %collective-permute-start.70 = (bf16[128,2048]{1,0:T(8,128)(2,1)}, bf16[128,2048]{1,0:T(8,128)(2,1)}, u32[]{:S(2)}, u32[]{:S(2)}) collective-permute-start(bf16[128,2048]{1,0:T(8,128)(2,1)} %get-tuple-element.241), channel_id=1, source_target_pairs={{0,6},{1,7},{2,4},{3,5},{4,2},{5,3},{6,0},{7,1},{8,14},{9,15},{10,... | collective-permute-start | bytes 1572872 | tf_op jit(solution)/shard_map/ppermute | solution.py:52
  510.7 28.1 %collective-permute-start.75 = (bf16[8,48,256]{2,1,0:T(8,128)(2,1)S(1)}, bf16[8,48,256]{2,1,0:T(8,128)(2,1)S(1)}, u32[]{:S(2)}, u32[]{:S(2)}) collective-permute-start(bf16[8,48,256]{2,1,0:T(8,128)(2,1)S(1)} %pad_maximum_fusion.13), channel_id=1, source_target_pairs={{0,8},{8,0},{16,24},{24,16},{1,9},{9,1},{17,25},{25,17},{2,10},{10... | collective-permute-start | bytes 589832 | tf_op jit(solution)/shard_map/ppermute | solution.py:937
  510.7 28.1 %collective-permute-start.76 = (bf16[8,48,256]{2,1,0:T(8,128)(2,1)S(1)}, bf16[8,48,256]{2,1,0:T(8,128)(2,1)S(1)}, u32[]{:S(2)}, u32[]{:S(2)}) collective-permute-start(bf16[8,48,256]{2,1,0:T(8,128)(2,1)S(1)} %pad_maximum_fusion.13), channel_id=1, source_target_pairs={{0,16},{8,24},{16,0},{24,8},{1,17},{9,25},{17,1},{25,9},{2,18},{10... | collective-permute-start | bytes 589832 | tf_op jit(solution)/shard_map/ppermute | solution.py:937
  511.0 27.9 %collective-permute-start.77 = (bf16[8,48,256]{2,1,0:T(8,128)(2,1)S(1)}, bf16[8,48,256]{2,1,0:T(8,128)(2,1)S(1)}, u32[]{:S(2)}, u32[]{:S(2)}) collective-permute-start(bf16[8,48,256]{2,1,0:T(8,128)(2,1)S(1)} %pad_maximum_fusion.13), channel_id=1, source_target_pairs={{0,24},{8,16},{16,8},{24,0},{1,25},{9,17},{17,9},{25,1},{2,26},{10... | collective-permute-start | bytes 589832 | tf_op jit(solution)/shard_map/ppermute | solution.py:937
  (155 other events, 1880.5 us)
Sparse Core Ops, SparseCore 0:
  439.2 67.7 all-gather.4
  548.1 40.4 all-gather.6

commit v5 on v4

--- a/solution.py
+++ b/solution.py
@@ -72,8 +72,9 @@
 
 
 def halve(near, far, n):
-    q = near.astype(F32) + swap(far, n, 1).astype(F32)
-    return q[0], [q[i].astype(BF16) for i in range(1, n // 2)]
+    got = swap(far, n, 1)
+    sums = [near[i].astype(F32) + got[i].astype(F32) for i in range(n // 2)]
+    return sums[0], [one.astype(BF16) for one in sums[1:]]
 
 
 def added(parts):
@@ -81,11 +82,15 @@
 
 
 def quarter(near, far, n):
-    q = near.astype(F32) + swap(far, n, 1).astype(F32)
-    cut = q.shape[1] // 2
-    qa, qb = q[:, :cut], q[:, cut:]
-    sent = [jnp.stack([qa[1], qa[3]]).astype(BF16), jnp.stack([qb[2], qb[3]]).astype(BF16)]
-    return [qa[0], qa[2], qb[0], qb[1]], sent
+    got = swap(far, n, 1)
+    cut = near.shape[1] // 2
+
+    def total(i, at):
+        return near[i, at].astype(F32) + got[i, at].astype(F32)
+
+    top, low = slice(0, cut), slice(cut, None)
+    sent = [jnp.stack([total(i, at).astype(BF16) for i in pair]) for at, pair in ((top, (1, 3)), (low, (2, 3)))]
+    return [total(0, top), total(2, top), total(0, low), total(1, low)], sent
 
 
 def collect_quarters(kept, got, n):
@@ -937,18 +942,17 @@
         return [lax.ppermute(g, "rep", [(i, i ^ d) for i in range(reps)]) if d else g for d in range(reps)]
 
     weights = [attention_query_weight, key_value_weight]
-    picks_sent = send(docs)
     if n == 8:
         cut = (first.shape[0] // 2 + 15) // 16 * 16
         y0, x1 = swap(first[:cut], n, 4), swap(first[cut:], n, 2)
         y1, x0 = swap(first[cut:], n, 4), swap(first[:cut], n, 2)
-        y0, x1, *weights = tie(y0, x1, *weights)
-        d0, d1, *picks_sent = tie(swap(y0, n, 2), swap(x1, n, 4), *picks_sent)
+        y0, x1, docs_sent, *weights = tie(y0, x1, docs, *weights)
+        d0, d1 = swap(y0, n, 2), swap(x1, n, 4)
         chips = {0: first}
         for m, p in ((2, (x0, x1)), (4, (y0, y1)), (6, (d0, d1))):
             chips[m] = jnp.concatenate(p)
     else:
-        chips = across(first, n)
+        chips, docs_sent = across(first, n), docs
     pieces = from_sibling(chips, n)
     w_in = reshard(weights, me, n)
 
@@ -959,8 +963,6 @@
 
     second = jnp.concatenate([attn_small[1, EXPERTS + 2 :], width_small.reshape(-1, k, own)])
     groups = -(-second.shape[0] // n)
-    second, w_in = tie(pack_maps(second, n), w_in)
-    map_chips = across(second, n)
 
     begins = jnp.sum((segments[None, :] < jnp.arange(doc_count)[:, None]).astype(jnp.int32), axis=1)
     doc = segments.reshape(n, tok)
@@ -989,6 +991,15 @@
 
     select_a, select_f = slot_select(slot_a), slot_select(slot_f)
 
+    def slot_row(share, slot):
+        hot = slot[:, :, None, :] == jnp.arange(CAP, dtype=jnp.int32)[None, None, :, None]
+        row = jnp.sum(jnp.where(hot, share[:, :, None, :], 0.0), axis=-1)
+        return row.transpose(1, 0, 2).reshape(EXPERTS, 1, slots)
+
+    picks_sent = send(docs_sent)
+    second, w_in, hidden_small, *picks_sent = tie(pack_maps(second, n), w_in, hidden_small, *picks_sent)
+    map_chips = across(second, n)
+
     share_ae = share_a.transpose(1, 0, 2)
     q, kv, rank_q, rank_kv, rows_a_own, normed_own_columns = qkv(
         me_ref, pieces, key_a, select_tok, table_hi, table_lo, w_in, b_in
@@ -1004,11 +1015,6 @@
     attn_total, attn_low = halve(near, far, n)
     grads_out_all = from_sibling(dict(zip(cotangent_chips, sent)), n)
     *attn_low, key_late = tie(*attn_low, key_f)
-
-    def slot_row(share, slot):
-        hot = slot[:, :, None, :] == jnp.arange(CAP, dtype=jnp.int32)[None, None, :, None]
-        row = jnp.sum(jnp.where(hot, share[:, :, None, :], 0.0), axis=-1)
-        return row.transpose(1, 0, 2).reshape(EXPERTS, 1, slots)
 
     w_feed = jnp.swapaxes(feed_expert_weight, 2, 3)
     grad_inner, back_down, rows_g_own = feed_back_down(

time: 616 us -> 608 us (0.987)
    add x3 -> x1, other arithmetic: 13.5 us -> 3.49 us  [halve(): sums = [near[i].astype(F32) + got[i].astype(F32) for i in range(n // 2)]]
    convert_element_type x0 -> x3, other arithmetic: none -> 7.43 us  [the longest x2 5.48 us: halve(): return (sums[0], [one.astype(BF16) for one in sums[1:]])]
  transfers between devices with their start and end apart: 91 -> 91, of which waited for: 20 -> 21; matrix products, arithmetic and copies ran while one was open for 15% -> 15% of each run, Pallas kernels for 30% -> 30%
where the time goes in v5:
time: 608 us; the launch traced here: 600 us
  Pallas kernels  261 us (43%)
  waiting for transfers between devices  127 us (21%)
  starting transfers between devices  79.5 us (13%)
  other arithmetic  47.9 us (8%)
  local copies, waits for them, and re-layouts  46.8 us (8%)
  matrix products  20.5 us (3%)
  between operations  16.7 us (3%)
    pallas_call x10, Pallas kernels, run(): return call(*args)  261 us
    ppermute x77, waiting for transfers between devices, swap(): return lax.ppermute(x, 'shard', [(i, i ^ d) for i in range(n)])  120 us
    ppermute x77, starting transfers between devices, swap(): return lax.ppermute(x, 'shard', [(i, i ^ d) for i in range(n)])  61.9 us
    dot_general x16, matrix products, ein(): return jnp.einsum(spec, a, b, preferred_element_type=F32)  19.2 us
    ppermute x12, starting transfers between devices, send(): lax.ppermute(g, 'rep', [(i, i ^ d) for i in range(reps)])  17.5 us
  transfers between devices with their start and end apart: 91, of which 21 were waited for; matrix products, arithmetic and copies ran while one was open for 15% of the time, Pallas kernels for 30%

profile of v5, /device:TPU:0, one launch (start us, length us, event | category | flops | bytes accessed | tf_op | source)
XLA Modules:
  0.0 599.8 jit_solution(9935779000940362310)
XLA Ops:
  11.7 3.0 collective-permute-start.2
  24.4 3.5 fusion.refs_20_.refs_22_.refs_13_
  28.0 4.5 collective-permute-done.3
  45.5 19.0 %collective-permute-done.7 = bf16[96,2048]{1,0:T(8,128)(2,1)S(1)} collective-permute-done((bf16[96,2048]{1,0:T(8,128)(2,1)S(1)}, bf16[96,2048]{1,0:T(8,128)(2,1)S(1)}, u32[]{:S(2)}, u32[]{:S(2)}) %collective-permute-start.7) | collective-permute-done | bytes 393248 | tf_op jit(solution)/shard_map/ppermute | solution.py:52
  68.6 11.9 %collective-permute-done.11 = bf16[6,256,256]{2,1,0:T(8,128)(2,1)S(1)} collective-permute-done((bf16[6,256,256]{2,1,0:T(8,128)(2,1)S(1)}, bf16[6,256,256]{2,1,0:T(8,128)(2,1)S(1)}, u32[]{:S(2)}, u32[]{:S(2)}) %collective-permute-start.11) | collective-permute-done | bytes 786464 | tf_op jit(solution)/shard_map/ppermute | solution.py:52
  82.0 3.1 broadcast_in_dim.102
  86.9 11.1 %collective-permute-done.12 = bf16[6,256,256]{2,1,0:T(8,128)(2,1)S(1)} collective-permute-done((bf16[6,256,256]{2,1,0:T(8,128)(2,1)S(1)}, bf16[6,256,256]{2,1,0:T(8,128)(2,1)S(1)}, u32[]{:S(2)}, u32[]{:S(2)}) %collective-permute-start.12) | collective-permute-done | bytes 786464 | tf_op jit(solution)/shard_map/ppermute | solution.py:52
  99.1 15.8 %collective-permute-done.13 = bf16[6,256,256]{2,1,0:T(8,128)(2,1)S(1)} collective-permute-done((bf16[6,256,256]{2,1,0:T(8,128)(2,1)S(1)}, bf16[6,256,256]{2,1,0:T(8,128)(2,1)S(1)}, u32[]{:S(2)}, u32[]{:S(2)}) %collective-permute-start.13) | collective-permute-done | bytes 786464 | tf_op jit(solution)/shard_map/ppermute | solution.py:52
  132.8 24.3 %qkv.1 = (bf16[4,640,256]{2,1,0:T(8,128)(2,1)}, bf16[2,1024,256]{2,1,0:T(8,128)(2,1)}, bf16[4,640,48]{2,1,0:T(8,128)(2,1)}, bf16[2,1024,48]{2,1,0:T(8,128)(2,1)}...) custom-call(s32[1]{0:T(128)} %bitcast.refs_0_, bf16[176,2048]{1,0:T(8,128)(2,1)} %copy-done.24, ...), custom_call_target="tpu_custom_call" | custom-call | flops 7247757312 | bytes 33554432 | tf_op jit(solution)/shard_map/qkv/pallas_call | solution.py:643
  164.9 17.8 %attend.1 = (bf16[4,8,80,256]{3,2,1,0:T(8,128)(2,1)}, f32[4,8,80,256]{3,2,1,0:T(8,128)}) custom-call(s32[8,4,128]{2,1,0:T(4,128)} %copy.136.key, s32[8,1,128]{2,1,0:T(1,128)} %bitcast.452, bf16[4,8,80,256]{3,2,1,0:T(8,128)(2,1)} %bitcast.479, bf16[1024,256]{1,0:T(8,128)(2,1)} %get-tuple-element.355.k, bf16[1024,256]{1,0:T(8,128)(2,1)} %get-tuple-element.354.v), custom_call_target="tpu_custom_call" | custom-call | flops 2013265920 | bytes 33554432 | tf_op jit(solution)/shard_map/attend/pallas_call | solution.py:643
  182.7 18.1 %attend_out.1 = (bf16[4,128,2048]{2,1,0:T(8,128)(2,1)}, bf16[4,128,2048]{2,1,0:T(8,128)(2,1)}, bf16[16,2560]{1,0:T(8,128)(2,1)}) custom-call(s32[1]{0:T(128)} %bitcast.refs_0_, bf16[96,2048]{1,0:T(8,128)(2,1)} %copy-done.13, bf16[96,2048]{1,0:T(8,128)(2,1)} %copy-done.18, bf16[96,2048]{1,0:T(8,128)(2,1)} %copy-done.17, bf16[96,2048]{1,0:T(8,128)(2,1)} %copy-done.19, ...), custom_call_target="tpu_custom_call" | custom-call | flops 4026531840 | bytes 33554432 | tf_op jit(solution)/shard_map/attend_out/pallas_call | solution.py:643
  202.1 3.4 and_reduce_fusion
  206.7 3.5 add_bitcast_fusion.1
  214.5 22.0 %feed_down_back.1 = (f32[4,640,704]{2,1,0:T(8,128)}, bf16[4,640,48]{2,1,0:T(8,128)(2,1)}, bf16[4,640,256]{2,1,0:T(8,128)(2,1)}) custom-call(s32[1]{0:T(128)} %bitcast.refs_0_, bf16[128,2048]{1,0:T(8,128)(2,1)} %refs_1_, bf16[128,2048]{1,0:T(8,128)(2,1)} %copy-done.26, bf16[128,2048]{1,0:T(8,128)(2,1)} %collective-permute-done.27.refs_3_, ...), custom_call_target="tpu_custom_call" | custom-call | flops 9596567552 | bytes 33554432 | tf_op jit(solution)/shard_map/feed_down_back/pallas_call | solution.py:643
  250.0 10.5 %collective-permute-done.38.refs_3_ = bf16[128,2048]{1,0:T(8,128)(2,1)S(1)} collective-permute-done((bf16[128,2048]{1,0:T(8,128)(2,1)S(1)}, bf16[128,2048]{1,0:T(8,128)(2,1)S(1)}, u32[]{:S(2)}, u32[]{:S(2)}) %collective-permute-start.38) | collective-permute-done | bytes 524320 | tf_op jit(solution)/shard_map/ppermute | solution.py:52
  260.5 9.4 %collective-permute-done.39.refs_5_ = bf16[128,2048]{1,0:T(8,128)(2,1)} collective-permute-done((bf16[128,2048]{1,0:T(8,128)(2,1)S(1)}, bf16[128,2048]{1,0:T(8,128)(2,1)}, u32[]{:S(2)}, u32[]{:S(2)}) %collective-permute-start.39) | collective-permute-done | bytes 524320 | tf_op jit(solution)/shard_map/ppermute | solution.py:52
  274.4 79.0 %feed.1 = (bf16[512,2048]{1,0:T(8,128)(2,1)}, bf16[512,2048]{1,0:T(8,128)(2,1)}, bf16[4,640,704]{2,1,0:T(8,128)(2,1)}, bf16[48,2560]{1,0:T(8,128)(2,1)}, f32[8,2...) custom-call(s32[1]{0:T(128)} %bitcast.refs_0_, bf16[128,2048]{1,0:T(8,128)(2,1)} %copy-done.16, ...), custom_call_target="tpu_custom_call" | custom-call | flops 38386270208 | bytes 33554432 | tf_op jit(solution)/shard_map/feed/pallas_call | solution.py:643
  354.9 2.8 collective-permute-done.50
  358.5 3.3 fusion.15
  367.5 28.8 %feed_out.1 = (bf16[4,128,2048]{2,1,0:T(8,128)(2,1)}, bf16[4,128,2048]{2,1,0:T(8,128)(2,1)}, bf16[16,2560]{1,0:T(8,128)(2,1)}) custom-call(s32[1]{0:T(128)} %bitcast.refs_0_, bf16[96,2048]{1,0:T(8,128)(2,1)} %copy-done.13, bf16[96,2048]{1,0:T(8,128)(2,1)} %copy-done.18, bf16[96,2048]{1,0:T(8,128)(2,1)} %copy-done.17, bf16[96,2048]{1,0:T(8,128)(2,1)} %copy-done.19, ...), custom_call_target="tpu_custom_call" | custom-call | flops 11072962560 | bytes 33554432 | tf_op jit(solution)/shard_map/feed_out/pallas_call | solution.py:643
  407.1 8.7 %collective-permute-done.57.refs_3_ = bf16[128,2048]{1,0:T(8,128)(2,1)S(1)} collective-permute-done((bf16[128,2048]{1,0:T(8,128)(2,1)S(1)}, bf16[128,2048]{1,0:T(8,128)(2,1)S(1)}, u32[]{:S(2)}, u32[]{:S(2)}) %collective-permute-start.57) | collective-permute-done | bytes 524320 | tf_op jit(solution)/shard_map/ppermute | solution.py:52
  415.8 11.8 %collective-permute-done.58.refs_5_ = bf16[128,2048]{1,0:T(8,128)(2,1)} collective-permute-done((bf16[128,2048]{1,0:T(8,128)(2,1)S(1)}, bf16[128,2048]{1,0:T(8,128)(2,1)}, u32[]{:S(2)}, u32[]{:S(2)}) %collective-permute-start.58) | collective-permute-done | bytes 524320 | tf_op jit(solution)/shard_map/ppermute | solution.py:52
  435.6 16.5 %mixed_back.1 = (bf16[4,640,256]{2,1,0:T(8,128)(2,1)}, bf16[4,48,256]{2,1,0:T(8,128)(2,1)}, f32[8,2560]{1,0:T(8,128)}, bf16[4,640,256]{2,1,0:T(8,128)(2,1)}) custom-call(s32[1]{0:T(128)} %bitcast.refs_0_, bf16[128,2048]{1,0:T(8,128)(2,1)} %copy-done.30, bf16[128,2048]{1,0:T(8,128)(2,1)} %collective-permute-done.60.refs_2_, bf16[128,2048]{1,0:T(8,128)(2,1)} %copy-done.92, ...), custom_call_target="tpu_custom_call" | custom-call | flops 4026531840 | bytes 33554432 | tf_op jit(solution)/shard_map/mixed_back/pallas_call | solution.py:643
  458.1 24.2 %attend_back.1 = (f32[4,8,80,256]{3,2,1,0:T(8,128)}, f32[1024,256]{1,0:T(8,128)}, f32[1024,256]{1,0:T(8,128)}) custom-call(s32[8,4,128]{2,1,0:T(4,128)} %copy.136.key, s32[8,1,128]{2,1,0:T(1,128)} %bitcast.453, bf16[4,8,80,256]{3,2,1,0:T(8,128)(2,1)} %bitcast.480, bf16[4,8,80,256]{3,2,1,0:T(8,128)(2,1)} %bitcast.483, ...), custom_call_target="tpu_custom_call" | custom-call | flops 4697620480 | bytes 33554432 | tf_op jit(solution)/shard_map/attend_back/pallas_call | solution.py:643
  485.0 9.0 %qkv_rank.1 = (bf16[4,640,256]{2,1,0:T(8,128)(2,1)}, bf16[2,1024,256]{2,1,0:T(8,128)(2,1)}, bf16[4,640,48]{2,1,0:T(8,128)(2,1)}, bf16[2,1024,48]{2,1,0:T(8,128)(...) custom-call(s32[4,8,128]{2,1,0:T(8,128)} %get-tuple-element.400.refs_9_.refs_10_.refs_17_.key, ...), custom_call_target="tpu_custom_call" | custom-call | flops 226492416 | bytes 33554432 | tf_op jit(solution)/shard_map/qkv_rank/pallas_call | solution.py:643
  503.7 2.8 collective-permute-start.77
  509.4 21.5 %qkv_back.1 = (bf16[4,128,2048]{2,1,0:T(8,128)(2,1)}, bf16[4,128,2048]{2,1,0:T(8,128)(2,1)}) custom-call(s32[1]{0:T(128)} %bitcast.refs_0_, bf16[176,2048]{1,0:T(8,128)(2,1)} %copy-done.24, bf16[176,2048]{1,0:T(8,128)(2,1)} %collective-permute-done.refs_2_, bf16[176,2048]{1,0:T(8,128)(2,1)} %copy-done.36, bf16[176,2048]{1,0:T(8,128)(2,1)} %copy-done.88, ...), custom_call_target="tpu_custom_call" | custom-call | flops 7247757312 | bytes 33554432 | tf_op jit(solution)/shard_map/qkv_back/pallas_call | solution.py:643
  549.7 9.6 %collective-permute-done.82 = bf16[2,64,2048]{2,1,0:T(8,128)(2,1)S(1)} collective-permute-done((bf16[2,64,2048]{2,1,0:T(8,128)(2,1)}, bf16[2,64,2048]{2,1,0:T(8,128)(2,1)S(1)}, u32[]{:S(2)}, u32[]{:S(2)}) %collective-permute-start.82) | collective-permute-done | bytes 524320 | tf_op jit(solution)/shard_map/ppermute | solution.py:52
  569.2 4.0 convolution_bitcast_fusion
  576.1 4.9 collective-permute-done.87
  585.9 3.2 convolution_bitcast_fusion.2
  589.5 3.2 fusion.10
  (587 shorter events, 169.1 us)
Async XLA Ops:
  7.2 542.4 %all-gather.5.cloned.1.call-start = ((), (), s32[]{:S(2)}) async-start(), calls=%async_computation | async-start | bytes 4423680 | tf_op jit(solution)/shard_map/all_gather | solution.py:1118
  17.5 25.9 %collective-permute-start = (bf16[176,2048]{1,0:T(8,128)(2,1)S(1)}, bf16[176,2048]{1,0:T(8,128)(2,1)}, u32[]{:S(2)}, u32[]{:S(2)}) collective-permute-start(bf16[176,2048]{1,0:T(8,128)(2,1)S(1)} %pad_maximum_fusion.2.refs_1_), channel_id=1, source_target_pairs={{0,1},{1,0},{2,3},{3,2},{4,5},{5,4},{6,7},{7,6},{8,9},{9,8},{10,11... | collective-permute-start | bytes 2162696 | tf_op jit(solution)/shard_map/ppermute | solution.py:52
  36.0 32.3 %collective-permute-start.10 = (bf16[6,256,256]{2,1,0:T(8,128)(2,1)S(1)}, bf16[6,256,256]{2,1,0:T(8,128)(2,1)S(1)}, u32[]{:S(2)}, u32[]{:S(2)}) collective-permute-start(bf16[6,256,256]{2,1,0:T(8,128)(2,1)S(1)} %pad_maximum_fusion.3), channel_id=1, source_target_pairs={{0,7},{1,6},{2,5},{3,4},{4,3},{5,2},{6,1},{7,0},{8,15},{9,14},{10,... | collective-permute-start | bytes 2359304 | tf_op jit(solution)/shard_map/ppermute | solution.py:52
  36.1 28.4 %collective-permute-start.8 = (bf16[80,2048]{1,0:T(8,128)(2,1)}, bf16[80,2048]{1,0:T(8,128)(2,1)S(1)}, u32[]{:S(2)}, u32[]{:S(2)}) collective-permute-start(bf16[80,2048]{1,0:T(8,128)(2,1)} %collective-permute-done.3), channel_id=1, source_target_pairs={{0,4},{1,5},{2,6},{3,7},{4,0},{5,1},{6,2},{7,3},{8,12},{9,13},{10,... | collective-permute-start | bytes 983048 | tf_op jit(solution)/shard_map/ppermute | solution.py:52
  40.8 39.7 %collective-permute-start.11 = (bf16[6,256,256]{2,1,0:T(8,128)(2,1)S(1)}, bf16[6,256,256]{2,1,0:T(8,128)(2,1)S(1)}, u32[]{:S(2)}, u32[]{:S(2)}) collective-permute-start(bf16[6,256,256]{2,1,0:T(8,128)(2,1)S(1)} %pad_maximum_fusion.4), channel_id=1, source_target_pairs={{0,6},{1,7},{2,4},{3,5},{4,2},{5,3},{6,0},{7,1},{8,14},{9,15},{10,... | collective-permute-start | bytes 2359304 | tf_op jit(solution)/shard_map/ppermute | solution.py:52
  64.5 33.5 %collective-permute-start.12 = (bf16[6,256,256]{2,1,0:T(8,128)(2,1)S(1)}, bf16[6,256,256]{2,1,0:T(8,128)(2,1)S(1)}, u32[]{:S(2)}, u32[]{:S(2)}) collective-permute-start(bf16[6,256,256]{2,1,0:T(8,128)(2,1)S(1)} %pad_maximum_fusion.5), channel_id=1, source_target_pairs={{0,5},{1,4},{2,7},{3,6},{4,1},{5,0},{6,3},{7,2},{8,13},{9,12},{10,... | collective-permute-start | bytes 2359304 | tf_op jit(solution)/shard_map/ppermute | solution.py:52
  65.4 49.5 %collective-permute-start.13 = (bf16[6,256,256]{2,1,0:T(8,128)(2,1)S(1)}, bf16[6,256,256]{2,1,0:T(8,128)(2,1)S(1)}, u32[]{:S(2)}, u32[]{:S(2)}) collective-permute-start(bf16[6,256,256]{2,1,0:T(8,128)(2,1)S(1)} %pad_maximum_fusion.6), channel_id=1, source_target_pairs={{0,4},{1,5},{2,6},{3,7},{4,0},{5,1},{6,2},{7,3},{8,12},{9,13},{10,... | collective-permute-start | bytes 2359304 | tf_op jit(solution)/shard_map/ppermute | solution.py:52
  66.8 50.6 %collective-permute-start.14 = (bf16[6,256,256]{2,1,0:T(8,128)(2,1)S(1)}, bf16[6,256,256]{2,1,0:T(8,128)(2,1)S(1)}, u32[]{:S(2)}, u32[]{:S(2)}) collective-permute-start(bf16[6,256,256]{2,1,0:T(8,128)(2,1)S(1)} %pad_maximum_fusion.7), channel_id=1, source_target_pairs={{0,3},{1,2},{2,1},{3,0},{4,7},{5,6},{6,5},{7,4},{8,11},{9,10},{10,... | collective-permute-start | bytes 2359304 | tf_op jit(solution)/shard_map/ppermute | solution.py:52
  68.3 52.7 %collective-permute-start.15 = (bf16[6,256,256]{2,1,0:T(8,128)(2,1)S(1)}, bf16[6,256,256]{2,1,0:T(8,128)(2,1)S(1)}, u32[]{:S(2)}, u32[]{:S(2)}) collective-permute-start(bf16[6,256,256]{2,1,0:T(8,128)(2,1)S(1)} %pad_maximum_fusion.8), channel_id=1, source_target_pairs={{0,2},{1,3},{2,0},{3,1},{4,6},{5,7},{6,4},{7,5},{8,10},{9,11},{10,... | collective-permute-start | bytes 2359304 | tf_op jit(solution)/shard_map/ppermute | solution.py:52
  80.4 41.8 %collective-permute-start.16 = (bf16[6,256,256]{2,1,0:T(8,128)(2,1)S(1)}, bf16[6,256,256]{2,1,0:T(8,128)(2,1)S(1)}, u32[]{:S(2)}, u32[]{:S(2)}) collective-permute-start(bf16[6,256,256]{2,1,0:T(8,128)(2,1)S(1)} %pad_maximum_fusion.9), channel_id=1, source_target_pairs={{0,1},{1,0},{2,3},{3,2},{4,5},{5,4},{6,7},{7,6},{8,9},{9,8},{10,11... | collective-permute-start | bytes 2359304 | tf_op jit(solution)/shard_map/ppermute | solution.py:52
  98.0 31.8 %collective-permute-start.9 = (bf16[176,2048]{1,0:T(8,128)(2,1)S(1)}, bf16[176,2048]{1,0:T(8,128)(2,1)S(1)}, u32[]{:S(2)}, u32[]{:S(2)}) collective-permute-start(bf16[176,2048]{1,0:T(8,128)(2,1)S(1)} %constant_dynamic-update-slice_fusion.11.refs_7_), channel_id=1, source_target_pairs={{0,1},{1,0},{2,3},{3,2},{4,5},{5,4},{6,7},{7,6},{8,9},{9,8},{10,11... | collective-permute-start | bytes 2162696 | tf_op jit(solution)/shard_map/ppermute | solution.py:52
  126.4 30.8 %collective-permute-start.20 = (bf16[96,2048]{1,0:T(8,128)(2,1)S(1)}, bf16[96,2048]{1,0:T(8,128)(2,1)S(1)}, u32[]{:S(2)}, u32[]{:S(2)}) collective-permute-start(bf16[96,2048]{1,0:T(8,128)(2,1)S(1)} %pad_maximum_fusion.12.refs_1_.refs_9_), channel_id=1, source_target_pairs={{0,2},{1,3},{2,0},{3,1},{4,6},{5,7},{6,4},{7,5},{8,10},{9,11},{10,... | collective-permute-start | bytes 1179656 | tf_op jit(solution)/shard_map/ppermute | solution.py:52
  127.6 29.5 %collective-permute-start.21 = (bf16[96,2048]{1,0:T(8,128)(2,1)S(1)}, bf16[96,2048]{1,0:T(8,128)(2,1)}, u32[]{:S(2)}, u32[]{:S(2)}) collective-permute-start(bf16[96,2048]{1,0:T(8,128)(2,1)S(1)} %pad_maximum_fusion.12.refs_1_.refs_9_), channel_id=1, source_target_pairs={{0,4},{1,5},{2,6},{3,7},{4,0},{5,1},{6,2},{7,3},{8,12},{9,13},{10,... | collective-permute-start | bytes 1179656 | tf_op jit(solution)/shard_map/ppermute | solution.py:52
  128.5 28.7 %collective-permute-start.22 = (bf16[96,2048]{1,0:T(8,128)(2,1)S(1)}, bf16[96,2048]{1,0:T(8,128)(2,1)}, u32[]{:S(2)}, u32[]{:S(2)}) collective-permute-start(bf16[96,2048]{1,0:T(8,128)(2,1)S(1)} %pad_maximum_fusion.12.refs_1_.refs_9_), channel_id=1, source_target_pairs={{0,6},{1,7},{2,4},{3,5},{4,2},{5,3},{6,0},{7,1},{8,14},{9,15},{10,... | collective-permute-start | bytes 1179656 | tf_op jit(solution)/shard_map/ppermute | solution.py:52
  161.2 39.6 %collective-permute-start.27 = (bf16[128,2048]{1,0:T(8,128)(2,1)S(1)}, bf16[128,2048]{1,0:T(8,128)(2,1)}, u32[]{:S(2)}, u32[]{:S(2)}) collective-permute-start(bf16[128,2048]{1,0:T(8,128)(2,1)S(1)} %copy-done.8), channel_id=1, source_target_pairs={{0,2},{1,3},{2,0},{3,1},{4,6},{5,7},{6,4},{7,5},{8,10},{9,11},{10,... | collective-permute-start | bytes 1572872 | tf_op jit(solution)/shard_map/ppermute | solution.py:52
  162.5 38.3 %collective-permute-start.28 = (bf16[128,2048]{1,0:T(8,128)(2,1)S(1)}, bf16[128,2048]{1,0:T(8,128)(2,1)}, u32[]{:S(2)}, u32[]{:S(2)}) collective-permute-start(bf16[128,2048]{1,0:T(8,128)(2,1)S(1)} %copy-done.8), channel_id=1, source_target_pairs={{0,4},{1,5},{2,6},{3,7},{4,0},{5,1},{6,2},{7,3},{8,12},{9,13},{10,... | collective-permute-start | bytes 1572872 | tf_op jit(solution)/shard_map/ppermute | solution.py:52
  163.4 37.5 %collective-permute-start.29 = (bf16[128,2048]{1,0:T(8,128)(2,1)S(1)}, bf16[128,2048]{1,0:T(8,128)(2,1)}, u32[]{:S(2)}, u32[]{:S(2)}) collective-permute-start(bf16[128,2048]{1,0:T(8,128)(2,1)S(1)} %copy-done.8), channel_id=1, source_target_pairs={{0,6},{1,7},{2,4},{3,5},{4,2},{5,3},{6,0},{7,1},{8,14},{9,15},{10,... | collective-permute-start | bytes 1572872 | tf_op jit(solution)/shard_map/ppermute | solution.py:52
  210.2 26.3 %collective-permute-start.35 = (bf16[128,2048]{1,0:T(8,128)(2,1)}, bf16[128,2048]{1,0:T(8,128)(2,1)}, u32[]{:S(2)}, u32[]{:S(2)}) collective-permute-start(bf16[128,2048]{1,0:T(8,128)(2,1)} %get-tuple-element.189), channel_id=1, source_target_pairs={{0,2},{1,3},{2,0},{3,1},{4,6},{5,7},{6,4},{7,5},{8,10},{9,11},{10,... | collective-permute-start | bytes 1572872 | tf_op jit(solution)/shard_map/ppermute | solution.py:52
  212.2 25.4 %collective-permute-start.36 = (bf16[128,2048]{1,0:T(8,128)(2,1)}, bf16[128,2048]{1,0:T(8,128)(2,1)S(1)}, u32[]{:S(2)}, u32[]{:S(2)}) collective-permute-start(bf16[128,2048]{1,0:T(8,128)(2,1)} %get-tuple-element.190), channel_id=1, source_target_pairs={{0,4},{1,5},{2,6},{3,7},{4,0},{5,1},{6,2},{7,3},{8,12},{9,13},{10,... | collective-permute-start | bytes 1572872 | tf_op jit(solution)/shard_map/ppermute | solution.py:52
  213.1 25.4 %collective-permute-start.37 = (bf16[128,2048]{1,0:T(8,128)(2,1)}, bf16[128,2048]{1,0:T(8,128)(2,1)}, u32[]{:S(2)}, u32[]{:S(2)}) collective-permute-start(bf16[128,2048]{1,0:T(8,128)(2,1)} %get-tuple-element.191), channel_id=1, source_target_pairs={{0,6},{1,7},{2,4},{3,5},{4,2},{5,3},{6,0},{7,1},{8,14},{9,15},{10,... | collective-permute-start | bytes 1572872 | tf_op jit(solution)/shard_map/ppermute | solution.py:52
  363.1 34.2 %collective-permute-start.51 = (bf16[128,2048]{1,0:T(8,128)(2,1)}, bf16[128,2048]{1,0:T(8,128)(2,1)}, u32[]{:S(2)}, u32[]{:S(2)}) collective-permute-start(bf16[128,2048]{1,0:T(8,128)(2,1)} %get-tuple-element.207), channel_id=1, source_target_pairs={{0,2},{1,3},{2,0},{3,1},{4,6},{5,7},{6,4},{7,5},{8,10},{9,11},{10,... | collective-permute-start | bytes 1572872 | tf_op jit(solution)/shard_map/ppermute | solution.py:52
  363.9 33.4 %collective-permute-start.52 = (bf16[128,2048]{1,0:T(8,128)(2,1)}, bf16[128,2048]{1,0:T(8,128)(2,1)}, u32[]{:S(2)}, u32[]{:S(2)}) collective-permute-start(bf16[128,2048]{1,0:T(8,128)(2,1)} %get-tuple-element.208), channel_id=1, source_target_pairs={{0,4},{1,5},{2,6},{3,7},{4,0},{5,1},{6,2},{7,3},{8,12},{9,13},{10,... | collective-permute-start | bytes 1572872 | tf_op jit(solution)/shard_map/ppermute | solution.py:52
  365.2 32.1 %collective-permute-start.53 = (bf16[128,2048]{1,0:T(8,128)(2,1)}, bf16[128,2048]{1,0:T(8,128)(2,1)}, u32[]{:S(2)}, u32[]{:S(2)}) collective-permute-start(bf16[128,2048]{1,0:T(8,128)(2,1)} %get-tuple-element.209), channel_id=1, source_target_pairs={{0,6},{1,7},{2,4},{3,5},{4,2},{5,3},{6,0},{7,1},{8,14},{9,15},{10,... | collective-permute-start | bytes 1572872 | tf_op jit(solution)/shard_map/ppermute | solution.py:52
  366.6 29.7 %collective-permute-start.55 = (f32[1,2560]{1,0:T(1,128)S(1)}, f32[1,2560]{1,0:T(1,128)S(1)}, u32[]{:S(2)}, u32[]{:S(2)}) collective-permute-start(f32[1,2560]{1,0:T(1,128)S(1)} %add.443), channel_id=1, source_target_pairs={{0,4},{1,5},{2,6},{3,7},{4,0},{5,1},{6,2},{7,3},{8,12},{9,13},{10,... | collective-permute-start | bytes 30728 | tf_op jit(solution)/shard_map/ppermute | solution.py:52
  402.3 25.3 %collective-permute-start.58 = (bf16[128,2048]{1,0:T(8,128)(2,1)S(1)}, bf16[128,2048]{1,0:T(8,128)(2,1)}, u32[]{:S(2)}, u32[]{:S(2)}) collective-permute-start(bf16[128,2048]{1,0:T(8,128)(2,1)S(1)} %fusion.105.refs_1_), channel_id=1, source_target_pairs={{0,4},{1,5},{2,6},{3,7},{4,0},{5,1},{6,2},{7,3},{8,12},{9,13},{10,... | collective-permute-start | bytes 1572872 | tf_op jit(solution)/shard_map/ppermute | solution.py:52
  431.4 154.4 %all-gather.7.cloned.1.call-start = ((), (), s32[]{:S(2)}) async-start(), calls=%async_computation.1 | async-start | bytes 1474560 | tf_op jit(solution)/shard_map/all_gather | solution.py:1118
  453.6 28.7 %collective-permute-start.68 = (bf16[128,2048]{1,0:T(8,128)(2,1)}, bf16[128,2048]{1,0:T(8,128)(2,1)S(1)}, u32[]{:S(2)}, u32[]{:S(2)}) collective-permute-start(bf16[128,2048]{1,0:T(8,128)(2,1)} %get-tuple-element.239), channel_id=1, source_target_pairs={{0,2},{1,3},{2,0},{3,1},{4,6},{5,7},{6,4},{7,5},{8,10},{9,11},{10,... | collective-permute-start | bytes 1572872 | tf_op jit(solution)/shard_map/ppermute | solution.py:52
  454.2 28.0 %collective-permute-start.69 = (bf16[128,2048]{1,0:T(8,128)(2,1)}, bf16[128,2048]{1,0:T(8,128)(2,1)}, u32[]{:S(2)}, u32[]{:S(2)}) collective-permute-start(bf16[128,2048]{1,0:T(8,128)(2,1)} %get-tuple-element.240), channel_id=1, source_target_pairs={{0,4},{1,5},{2,6},{3,7},{4,0},{5,1},{6,2},{7,3},{8,12},{9,13},{10,... | collective-permute-start | bytes 1572872 | tf_op jit(solution)/shard_map/ppermute | solution.py:52
  455.4 26.9 %collective-permute-start.70 = (bf16[128,2048]{1,0:T(8,128)(2,1)}, bf16[128,2048]{1,0:T(8,128)(2,1)}, u32[]{:S(2)}, u32[]{:S(2)}) collective-permute-start(bf16[128,2048]{1,0:T(8,128)(2,1)} %get-tuple-element.241), channel_id=1, source_target_pairs={{0,6},{1,7},{2,4},{3,5},{4,2},{5,3},{6,0},{7,1},{8,14},{9,15},{10,... | collective-permute-start | bytes 1572872 | tf_op jit(solution)/shard_map/ppermute | solution.py:52
  502.1 28.8 %collective-permute-start.75 = (bf16[8,48,256]{2,1,0:T(8,128)(2,1)S(1)}, bf16[8,48,256]{2,1,0:T(8,128)(2,1)S(1)}, u32[]{:S(2)}, u32[]{:S(2)}) collective-permute-start(bf16[8,48,256]{2,1,0:T(8,128)(2,1)S(1)} %pad_maximum_fusion.14), channel_id=1, source_target_pairs={{0,8},{8,0},{16,24},{24,16},{1,9},{9,1},{17,25},{25,17},{2,10},{10... | collective-permute-start | bytes 589832 | tf_op jit(solution)/shard_map/ppermute | solution.py:942
  502.1 28.8 %collective-permute-start.76 = (bf16[8,48,256]{2,1,0:T(8,128)(2,1)S(1)}, bf16[8,48,256]{2,1,0:T(8,128)(2,1)S(1)}, u32[]{:S(2)}, u32[]{:S(2)}) collective-permute-start(bf16[8,48,256]{2,1,0:T(8,128)(2,1)S(1)} %pad_maximum_fusion.14), channel_id=1, source_target_pairs={{0,16},{8,24},{16,0},{24,8},{1,17},{9,25},{17,1},{25,9},{2,18},{10... | collective-permute-start | bytes 589832 | tf_op jit(solution)/shard_map/ppermute | solution.py:942
  503.7 27.2 %collective-permute-start.77 = (bf16[8,48,256]{2,1,0:T(8,128)(2,1)S(1)}, bf16[8,48,256]{2,1,0:T(8,128)(2,1)S(1)}, u32[]{:S(2)}, u32[]{:S(2)}) collective-permute-start(bf16[8,48,256]{2,1,0:T(8,128)(2,1)S(1)} %pad_maximum_fusion.14), channel_id=1, source_target_pairs={{0,24},{8,16},{16,8},{24,0},{1,25},{9,17},{17,9},{25,1},{2,26},{10... | collective-permute-start | bytes 589832 | tf_op jit(solution)/shard_map/ppermute | solution.py:942
  (153 other events, 1856.2 us)
Sparse Core Ops, SparseCore 0:
  431.5 68.1 all-gather.4
  539.4 41.8 all-gather.6

commit v6 on v5

--- a/solution.py
+++ b/solution.py
@@ -1116,8 +1116,8 @@
     live_in = live_in + swap(live_in, n, 1)
     gq, live_in, b_in_grad, early_grad, width_grad = tie(gq, live_in, b_in_grad, early_grad, width_grad)
     hidden_all, width_all = lax.all_gather(hidden_grad, "rep"), lax.all_gather(width_grad, "rep")
-    early_sent = send(early_grad)
-    live_sent, late_b_sent = list(across(live_in, n).values()), send(b_in_grad)
+    early_sent = send(jnp.concatenate([early_grad, b_in_grad]))
+    live_sent = list(across(live_in, n).values())
     near, far = qkv_back(me_ref, pieces, key_a, w_in, gq, gkv, back_q, back_kv)
     near, far, *sent = tie(near, far, *live_sent, *early_sent)
     live_sent, early_sent = sent[: n // 2], sent[n // 2 :]
@@ -1134,8 +1134,7 @@
             ein("pks,sw->pkw", spread(live_kv, select_row), normed_own_columns).astype(BF16),
         ]
     )
-    a_in_grad, hidden_all, *sent = tie(a_in_grad, hidden_all, *late_b_sent, *in_got)
-    late_b_sent, in_got = sent[:reps], sent[reps:]
+    a_in_grad, hidden_all, *in_got = tie(a_in_grad, hidden_all, *in_got)
     late_a_sent = send(a_in_grad)
     grad_normed = collect_quarters(in_total, in_got, n) if n == 8 else added([in_total] + in_got)
     grad_normed = grad_normed + route_back(own_a, own_tokens(slot_a, dshare_a), attention_router_weight)
@@ -1146,8 +1145,9 @@
     early = by_stream(early_sent)
     hidden_out = ein("rpekf,rkc->pecf", hidden_all, picks)
     width_out = ein("rpmkw,rkc->pmwc", width_all, picks)
-    late_b, late_a = by_stream(late_b_sent), by_stream(late_a_sent)
-    attn = jnp.concatenate([late_a, early[:, :EXPERTS], late_b, early[:, EXPERTS:]], axis=1)
+    late = by_stream(late_a_sent)
+    first, second, third = jnp.split(early, [EXPERTS, 2 * EXPERTS], axis=1)
+    attn = jnp.concatenate([late, first, third, second], axis=1)
     attn = attn.reshape(reps, 2, -1, k, own)
     attn_out = ein("rpmkw,rkc->pmwc", attn, picks)
     return (layer_out, grad_in, attn_out, width_out, hidden_out)

time: 608 us -> 604 us (level)
    ppermute x12 -> x9, starting transfers between devices: 17.5 us -> 17.1 us  [send(): lax.ppermute(g, 'rep', [(i, i ^ d) for i in range(reps)])]
  transfers between devices with their start and end apart: 91 -> 88, of which waited for: 21 -> 22; matrix products, arithmetic and copies ran while one was open for 15% -> 15% of each run, Pallas kernels for 30% -> 31%
where the time goes in v6:
time: 604 us; the launch traced here: 595 us
  Pallas kernels  261 us (43%)
  waiting for transfers between devices  125 us (21%)
  starting transfers between devices  78.4 us (13%)
  other arithmetic  48.9 us (8%)
  local copies, waits for them, and re-layouts  43 us (7%)
  matrix products  21.8 us (4%)
  between operations  16.5 us (3%)
    pallas_call x10, Pallas kernels, run(): return call(*args)  261 us
    ppermute x77, waiting for transfers between devices, swap(): return lax.ppermute(x, 'shard', [(i, i ^ d) for i in range(n)])  119 us
    ppermute x77, starting transfers between devices, swap(): return lax.ppermute(x, 'shard', [(i, i ^ d) for i in range(n)])  61.2 us
    dot_general x16, matrix products, ein(): return jnp.einsum(spec, a, b, preferred_element_type=F32)  20.5 us
    ppermute x9, starting transfers between devices, send(): lax.ppermute(g, 'rep', [(i, i ^ d) for i in range(reps)])  17.1 us
  transfers between devices with their start and end apart: 88, of which 22 were waited for; matrix products, arithmetic and copies ran while one was open for 15% of the time, Pallas kernels for 31%

profile of v6, /device:TPU:0, one launch (start us, length us, event | category | flops | bytes accessed | tf_op | source)
XLA Modules:
  0.0 595.1 jit_solution(4738869147071015913)
XLA Ops:
  11.7 3.0 collective-permute-start.2
  24.5 3.5 fusion.refs_20_.refs_22_.refs_13_
  28.1 4.5 collective-permute-done.3
  45.5 19.0 %collective-permute-done.7 = bf16[96,2048]{1,0:T(8,128)(2,1)S(1)} collective-permute-done((bf16[96,2048]{1,0:T(8,128)(2,1)S(1)}, bf16[96,2048]{1,0:T(8,128)(2,1)S(1)}, u32[]{:S(2)}, u32[]{:S(2)}) %collective-permute-start.7) | collective-permute-done | bytes 393248 | tf_op jit(solution)/shard_map/ppermute | solution.py:52
  68.6 11.8 %collective-permute-done.11 = bf16[6,256,256]{2,1,0:T(8,128)(2,1)S(1)} collective-permute-done((bf16[6,256,256]{2,1,0:T(8,128)(2,1)S(1)}, bf16[6,256,256]{2,1,0:T(8,128)(2,1)S(1)}, u32[]{:S(2)}, u32[]{:S(2)}) %collective-permute-start.11) | collective-permute-done | bytes 786464 | tf_op jit(solution)/shard_map/ppermute | solution.py:52
  82.0 3.1 broadcast_in_dim.96
  87.0 11.0 %collective-permute-done.12 = bf16[6,256,256]{2,1,0:T(8,128)(2,1)S(1)} collective-permute-done((bf16[6,256,256]{2,1,0:T(8,128)(2,1)S(1)}, bf16[6,256,256]{2,1,0:T(8,128)(2,1)S(1)}, u32[]{:S(2)}, u32[]{:S(2)}) %collective-permute-start.12) | collective-permute-done | bytes 786464 | tf_op jit(solution)/shard_map/ppermute | solution.py:52
  99.1 15.9 %collective-permute-done.13 = bf16[6,256,256]{2,1,0:T(8,128)(2,1)S(1)} collective-permute-done((bf16[6,256,256]{2,1,0:T(8,128)(2,1)S(1)}, bf16[6,256,256]{2,1,0:T(8,128)(2,1)S(1)}, u32[]{:S(2)}, u32[]{:S(2)}) %collective-permute-start.13) | collective-permute-done | bytes 786464 | tf_op jit(solution)/shard_map/ppermute | solution.py:52
  132.9 24.3 %qkv.1 = (bf16[4,640,256]{2,1,0:T(8,128)(2,1)}, bf16[2,1024,256]{2,1,0:T(8,128)(2,1)}, bf16[4,640,48]{2,1,0:T(8,128)(2,1)}, bf16[2,1024,48]{2,1,0:T(8,128)(2,1)}...) custom-call(s32[1]{0:T(128)} %bitcast.refs_0_, bf16[176,2048]{1,0:T(8,128)(2,1)} %copy-done.23, ...), custom_call_target="tpu_custom_call" | custom-call | flops 7247757312 | bytes 33554432 | tf_op jit(solution)/shard_map/qkv/pallas_call | solution.py:643
  164.9 17.8 %attend.1 = (bf16[4,8,80,256]{3,2,1,0:T(8,128)(2,1)}, f32[4,8,80,256]{3,2,1,0:T(8,128)}) custom-call(s32[8,4,128]{2,1,0:T(4,128)} %copy.124.key, s32[8,1,128]{2,1,0:T(1,128)} %bitcast.444, bf16[4,8,80,256]{3,2,1,0:T(8,128)(2,1)} %bitcast.471, bf16[1024,256]{1,0:T(8,128)(2,1)} %get-tuple-element.349.k, bf16[1024,256]{1,0:T(8,128)(2,1)} %get-tuple-element.348.v), custom_call_target="tpu_custom_call" | custom-call | flops 2013265920 | bytes 33554432 | tf_op jit(solution)/shard_map/attend/pallas_call | solution.py:643
  182.7 18.1 %attend_out.1 = (bf16[4,128,2048]{2,1,0:T(8,128)(2,1)}, bf16[4,128,2048]{2,1,0:T(8,128)(2,1)}, bf16[16,2560]{1,0:T(8,128)(2,1)}) custom-call(s32[1]{0:T(128)} %bitcast.refs_0_, bf16[96,2048]{1,0:T(8,128)(2,1)} %copy-done.13, bf16[96,2048]{1,0:T(8,128)(2,1)} %copy-done.18, bf16[96,2048]{1,0:T(8,128)(2,1)} %copy-done.17, bf16[96,2048]{1,0:T(8,128)(2,1)} %copy-done.19, ...), custom_call_target="tpu_custom_call" | custom-call | flops 4026531840 | bytes 33554432 | tf_op jit(solution)/shard_map/attend_out/pallas_call | solution.py:643
  202.1 3.4 and_reduce_fusion
  206.7 3.5 add_bitcast_fusion.1
  214.6 22.2 %feed_down_back.1 = (f32[4,640,704]{2,1,0:T(8,128)}, bf16[4,640,48]{2,1,0:T(8,128)(2,1)}, bf16[4,640,256]{2,1,0:T(8,128)(2,1)}) custom-call(s32[1]{0:T(128)} %bitcast.refs_0_, bf16[128,2048]{1,0:T(8,128)(2,1)} %refs_1_, bf16[128,2048]{1,0:T(8,128)(2,1)} %copy-done.25, bf16[128,2048]{1,0:T(8,128)(2,1)} %collective-permute-done.27.refs_3_, ...), custom_call_target="tpu_custom_call" | custom-call | flops 9596567552 | bytes 33554432 | tf_op jit(solution)/shard_map/feed_down_back/pallas_call | solution.py:643
  250.0 10.5 %collective-permute-done.38.refs_3_ = bf16[128,2048]{1,0:T(8,128)(2,1)S(1)} collective-permute-done((bf16[128,2048]{1,0:T(8,128)(2,1)S(1)}, bf16[128,2048]{1,0:T(8,128)(2,1)S(1)}, u32[]{:S(2)}, u32[]{:S(2)}) %collective-permute-start.38) | collective-permute-done | bytes 524320 | tf_op jit(solution)/shard_map/ppermute | solution.py:52
  260.4 9.5 %collective-permute-done.39.refs_5_ = bf16[128,2048]{1,0:T(8,128)(2,1)} collective-permute-done((bf16[128,2048]{1,0:T(8,128)(2,1)S(1)}, bf16[128,2048]{1,0:T(8,128)(2,1)}, u32[]{:S(2)}, u32[]{:S(2)}) %collective-permute-start.39) | collective-permute-done | bytes 524320 | tf_op jit(solution)/shard_map/ppermute | solution.py:52
  274.4 79.0 %feed.1 = (bf16[512,2048]{1,0:T(8,128)(2,1)}, bf16[512,2048]{1,0:T(8,128)(2,1)}, bf16[4,640,704]{2,1,0:T(8,128)(2,1)}, bf16[48,2560]{1,0:T(8,128)(2,1)}, f32[8,2...) custom-call(s32[1]{0:T(128)} %bitcast.refs_0_, bf16[128,2048]{1,0:T(8,128)(2,1)} %copy-done.16, ...), custom_call_target="tpu_custom_call" | custom-call | flops 38386270208 | bytes 33554432 | tf_op jit(solution)/shard_map/feed/pallas_call | solution.py:643
  358.6 3.3 fusion.15
  367.5 28.7 %feed_out.1 = (bf16[4,128,2048]{2,1,0:T(8,128)(2,1)}, bf16[4,128,2048]{2,1,0:T(8,128)(2,1)}, bf16[16,2560]{1,0:T(8,128)(2,1)}) custom-call(s32[1]{0:T(128)} %bitcast.refs_0_, bf16[96,2048]{1,0:T(8,128)(2,1)} %copy-done.13, bf16[96,2048]{1,0:T(8,128)(2,1)} %copy-done.18, bf16[96,2048]{1,0:T(8,128)(2,1)} %copy-done.17, bf16[96,2048]{1,0:T(8,128)(2,1)} %copy-done.19, ...), custom_call_target="tpu_custom_call" | custom-call | flops 11072962560 | bytes 33554432 | tf_op jit(solution)/shard_map/feed_out/pallas_call | solution.py:643
  405.1 4.2 fusion.28
  409.3 6.8 %collective-permute-done.57.refs_3_ = bf16[128,2048]{1,0:T(8,128)(2,1)S(1)} collective-permute-done((bf16[128,2048]{1,0:T(8,128)(2,1)S(1)}, bf16[128,2048]{1,0:T(8,128)(2,1)S(1)}, u32[]{:S(2)}, u32[]{:S(2)}) %collective-permute-start.57) | collective-permute-done | bytes 524320 | tf_op jit(solution)/shard_map/ppermute | solution.py:52
  416.1 11.9 %collective-permute-done.58.refs_5_ = bf16[128,2048]{1,0:T(8,128)(2,1)} collective-permute-done((bf16[128,2048]{1,0:T(8,128)(2,1)S(1)}, bf16[128,2048]{1,0:T(8,128)(2,1)}, u32[]{:S(2)}, u32[]{:S(2)}) %collective-permute-start.58) | collective-permute-done | bytes 524320 | tf_op jit(solution)/shard_map/ppermute | solution.py:52
  436.0 16.5 %mixed_back.1 = (bf16[4,640,256]{2,1,0:T(8,128)(2,1)}, bf16[4,48,256]{2,1,0:T(8,128)(2,1)}, f32[8,2560]{1,0:T(8,128)}, bf16[4,640,256]{2,1,0:T(8,128)(2,1)}) custom-call(s32[1]{0:T(128)} %bitcast.refs_0_, bf16[128,2048]{1,0:T(8,128)(2,1)} %copy-done.29, bf16[128,2048]{1,0:T(8,128)(2,1)} %collective-permute-done.60.refs_2_, bf16[128,2048]{1,0:T(8,128)(2,1)} %copy-done.75, ...), custom_call_target="tpu_custom_call" | custom-call | flops 4026531840 | bytes 33554432 | tf_op jit(solution)/shard_map/mixed_back/pallas_call | solution.py:643
  459.1 24.1 %attend_back.1 = (f32[4,8,80,256]{3,2,1,0:T(8,128)}, f32[1024,256]{1,0:T(8,128)}, f32[1024,256]{1,0:T(8,128)}) custom-call(s32[8,4,128]{2,1,0:T(4,128)} %copy.124.key, s32[8,1,128]{2,1,0:T(1,128)} %bitcast.445, bf16[4,8,80,256]{3,2,1,0:T(8,128)(2,1)} %bitcast.472, bf16[4,8,80,256]{3,2,1,0:T(8,128)(2,1)} %bitcast.475, ...), custom_call_target="tpu_custom_call" | custom-call | flops 4697620480 | bytes 33554432 | tf_op jit(solution)/shard_map/attend_back/pallas_call | solution.py:643
  486.1 9.0 %qkv_rank.1 = (bf16[4,640,256]{2,1,0:T(8,128)(2,1)}, bf16[2,1024,256]{2,1,0:T(8,128)(2,1)}, bf16[4,640,48]{2,1,0:T(8,128)(2,1)}, bf16[2,1024,48]{2,1,0:T(8,128)(...) custom-call(s32[4,8,128]{2,1,0:T(8,128)} %get-tuple-element.392.refs_9_.refs_10_.refs_17_.key, ...), custom_call_target="tpu_custom_call" | custom-call | flops 226492416 | bytes 33554432 | tf_op jit(solution)/shard_map/qkv_rank/pallas_call | solution.py:643
  510.5 21.5 %qkv_back.1 = (bf16[4,128,2048]{2,1,0:T(8,128)(2,1)}, bf16[4,128,2048]{2,1,0:T(8,128)(2,1)}) custom-call(s32[1]{0:T(128)} %bitcast.refs_0_, bf16[176,2048]{1,0:T(8,128)(2,1)} %copy-done.23, bf16[176,2048]{1,0:T(8,128)(2,1)} %collective-permute-done.refs_2_, bf16[176,2048]{1,0:T(8,128)(2,1)} %copy-done.35, bf16[176,2048]{1,0:T(8,128)(2,1)} %copy-done.72, ...), custom_call_target="tpu_custom_call" | custom-call | flops 7247757312 | bytes 33554432 | tf_op jit(solution)/shard_map/qkv_back/pallas_call | solution.py:643
  546.5 8.9 %collective-permute-done.79 = bf16[2,64,2048]{2,1,0:T(8,128)(2,1)S(1)} collective-permute-done((bf16[2,64,2048]{2,1,0:T(8,128)(2,1)}, bf16[2,64,2048]{2,1,0:T(8,128)(2,1)S(1)}, u32[]{:S(2)}, u32[]{:S(2)}) %collective-permute-start.79) | collective-permute-done | bytes 524320 | tf_op jit(solution)/shard_map/ppermute | solution.py:52
  555.9 5.9 collective-permute-start.83
  568.6 4.0 convolution_bitcast_fusion
  572.7 3.7 collective-permute-done.84
  581.3 3.2 convolution_bitcast_fusion.2
  584.9 3.2 fusion.10
  (545 shorter events, 163.5 us)
Async XLA Ops:
  7.2 539.2 %all-gather.5.cloned.1.call-start = ((), (), s32[]{:S(2)}) async-start(), calls=%async_computation | async-start | bytes 4423680 | tf_op jit(solution)/shard_map/all_gather | solution.py:1118
  17.5 25.9 %collective-permute-start = (bf16[176,2048]{1,0:T(8,128)(2,1)S(1)}, bf16[176,2048]{1,0:T(8,128)(2,1)}, u32[]{:S(2)}, u32[]{:S(2)}) collective-permute-start(bf16[176,2048]{1,0:T(8,128)(2,1)S(1)} %pad_maximum_fusion.2.refs_1_), channel_id=1, source_target_pairs={{0,1},{1,0},{2,3},{3,2},{4,5},{5,4},{6,7},{7,6},{8,9},{9,8},{10,11... | collective-permute-start | bytes 2162696 | tf_op jit(solution)/shard_map/ppermute | solution.py:52
  36.1 32.3 %collective-permute-start.10 = (bf16[6,256,256]{2,1,0:T(8,128)(2,1)S(1)}, bf16[6,256,256]{2,1,0:T(8,128)(2,1)S(1)}, u32[]{:S(2)}, u32[]{:S(2)}) collective-permute-start(bf16[6,256,256]{2,1,0:T(8,128)(2,1)S(1)} %pad_maximum_fusion.3), channel_id=1, source_target_pairs={{0,7},{1,6},{2,5},{3,4},{4,3},{5,2},{6,1},{7,0},{8,15},{9,14},{10,... | collective-permute-start | bytes 2359304 | tf_op jit(solution)/shard_map/ppermute | solution.py:52
  36.1 28.4 %collective-permute-start.8 = (bf16[80,2048]{1,0:T(8,128)(2,1)}, bf16[80,2048]{1,0:T(8,128)(2,1)S(1)}, u32[]{:S(2)}, u32[]{:S(2)}) collective-permute-start(bf16[80,2048]{1,0:T(8,128)(2,1)} %collective-permute-done.3), channel_id=1, source_target_pairs={{0,4},{1,5},{2,6},{3,7},{4,0},{5,1},{6,2},{7,3},{8,12},{9,13},{10,... | collective-permute-start | bytes 983048 | tf_op jit(solution)/shard_map/ppermute | solution.py:52
  40.8 39.7 %collective-permute-start.11 = (bf16[6,256,256]{2,1,0:T(8,128)(2,1)S(1)}, bf16[6,256,256]{2,1,0:T(8,128)(2,1)S(1)}, u32[]{:S(2)}, u32[]{:S(2)}) collective-permute-start(bf16[6,256,256]{2,1,0:T(8,128)(2,1)S(1)} %pad_maximum_fusion.4), channel_id=1, source_target_pairs={{0,6},{1,7},{2,4},{3,5},{4,2},{5,3},{6,0},{7,1},{8,14},{9,15},{10,... | collective-permute-start | bytes 2359304 | tf_op jit(solution)/shard_map/ppermute | solution.py:52
  64.5 33.5 %collective-permute-start.12 = (bf16[6,256,256]{2,1,0:T(8,128)(2,1)S(1)}, bf16[6,256,256]{2,1,0:T(8,128)(2,1)S(1)}, u32[]{:S(2)}, u32[]{:S(2)}) collective-permute-start(bf16[6,256,256]{2,1,0:T(8,128)(2,1)S(1)} %pad_maximum_fusion.5), channel_id=1, source_target_pairs={{0,5},{1,4},{2,7},{3,6},{4,1},{5,0},{6,3},{7,2},{8,13},{9,12},{10,... | collective-permute-start | bytes 2359304 | tf_op jit(solution)/shard_map/ppermute | solution.py:52
  65.5 49.5 %collective-permute-start.13 = (bf16[6,256,256]{2,1,0:T(8,128)(2,1)S(1)}, bf16[6,256,256]{2,1,0:T(8,128)(2,1)S(1)}, u32[]{:S(2)}, u32[]{:S(2)}) collective-permute-start(bf16[6,256,256]{2,1,0:T(8,128)(2,1)S(1)} %pad_maximum_fusion.6), channel_id=1, source_target_pairs={{0,4},{1,5},{2,6},{3,7},{4,0},{5,1},{6,2},{7,3},{8,12},{9,13},{10,... | collective-permute-start | bytes 2359304 | tf_op jit(solution)/shard_map/ppermute | solution.py:52
  66.9 50.7 %collective-permute-start.14 = (bf16[6,256,256]{2,1,0:T(8,128)(2,1)S(1)}, bf16[6,256,256]{2,1,0:T(8,128)(2,1)S(1)}, u32[]{:S(2)}, u32[]{:S(2)}) collective-permute-start(bf16[6,256,256]{2,1,0:T(8,128)(2,1)S(1)} %pad_maximum_fusion.7), channel_id=1, source_target_pairs={{0,3},{1,2},{2,1},{3,0},{4,7},{5,6},{6,5},{7,4},{8,11},{9,10},{10,... | collective-permute-start | bytes 2359304 | tf_op jit(solution)/shard_map/ppermute | solution.py:52
  68.3 52.8 %collective-permute-start.15 = (bf16[6,256,256]{2,1,0:T(8,128)(2,1)S(1)}, bf16[6,256,256]{2,1,0:T(8,128)(2,1)S(1)}, u32[]{:S(2)}, u32[]{:S(2)}) collective-permute-start(bf16[6,256,256]{2,1,0:T(8,128)(2,1)S(1)} %pad_maximum_fusion.8), channel_id=1, source_target_pairs={{0,2},{1,3},{2,0},{3,1},{4,6},{5,7},{6,4},{7,5},{8,10},{9,11},{10,... | collective-permute-start | bytes 2359304 | tf_op jit(solution)/shard_map/ppermute | solution.py:52
  80.5 41.8 %collective-permute-start.16 = (bf16[6,256,256]{2,1,0:T(8,128)(2,1)S(1)}, bf16[6,256,256]{2,1,0:T(8,128)(2,1)S(1)}, u32[]{:S(2)}, u32[]{:S(2)}) collective-permute-start(bf16[6,256,256]{2,1,0:T(8,128)(2,1)S(1)} %pad_maximum_fusion.9), channel_id=1, source_target_pairs={{0,1},{1,0},{2,3},{3,2},{4,5},{5,4},{6,7},{7,6},{8,9},{9,8},{10,11... | collective-permute-start | bytes 2359304 | tf_op jit(solution)/shard_map/ppermute | solution.py:52
  98.1 31.9 %collective-permute-start.9 = (bf16[176,2048]{1,0:T(8,128)(2,1)S(1)}, bf16[176,2048]{1,0:T(8,128)(2,1)S(1)}, u32[]{:S(2)}, u32[]{:S(2)}) collective-permute-start(bf16[176,2048]{1,0:T(8,128)(2,1)S(1)} %constant_dynamic-update-slice_fusion.11.refs_7_), channel_id=1, source_target_pairs={{0,1},{1,0},{2,3},{3,2},{4,5},{5,4},{6,7},{7,6},{8,9},{9,8},{10,11... | collective-permute-start | bytes 2162696 | tf_op jit(solution)/shard_map/ppermute | solution.py:52
  126.5 30.8 %collective-permute-start.20 = (bf16[96,2048]{1,0:T(8,128)(2,1)S(1)}, bf16[96,2048]{1,0:T(8,128)(2,1)S(1)}, u32[]{:S(2)}, u32[]{:S(2)}) collective-permute-start(bf16[96,2048]{1,0:T(8,128)(2,1)S(1)} %pad_maximum_fusion.12.refs_1_.refs_9_), channel_id=1, source_target_pairs={{0,2},{1,3},{2,0},{3,1},{4,6},{5,7},{6,4},{7,5},{8,10},{9,11},{10,... | collective-permute-start | bytes 1179656 | tf_op jit(solution)/shard_map/ppermute | solution.py:52
  127.6 29.6 %collective-permute-start.21 = (bf16[96,2048]{1,0:T(8,128)(2,1)S(1)}, bf16[96,2048]{1,0:T(8,128)(2,1)}, u32[]{:S(2)}, u32[]{:S(2)}) collective-permute-start(bf16[96,2048]{1,0:T(8,128)(2,1)S(1)} %pad_maximum_fusion.12.refs_1_.refs_9_), channel_id=1, source_target_pairs={{0,4},{1,5},{2,6},{3,7},{4,0},{5,1},{6,2},{7,3},{8,12},{9,13},{10,... | collective-permute-start | bytes 1179656 | tf_op jit(solution)/shard_map/ppermute | solution.py:52
  128.4 28.8 %collective-permute-start.22 = (bf16[96,2048]{1,0:T(8,128)(2,1)S(1)}, bf16[96,2048]{1,0:T(8,128)(2,1)}, u32[]{:S(2)}, u32[]{:S(2)}) collective-permute-start(bf16[96,2048]{1,0:T(8,128)(2,1)S(1)} %pad_maximum_fusion.12.refs_1_.refs_9_), channel_id=1, source_target_pairs={{0,6},{1,7},{2,4},{3,5},{4,2},{5,3},{6,0},{7,1},{8,14},{9,15},{10,... | collective-permute-start | bytes 1179656 | tf_op jit(solution)/shard_map/ppermute | solution.py:52
  161.2 39.6 %collective-permute-start.27 = (bf16[128,2048]{1,0:T(8,128)(2,1)S(1)}, bf16[128,2048]{1,0:T(8,128)(2,1)}, u32[]{:S(2)}, u32[]{:S(2)}) collective-permute-start(bf16[128,2048]{1,0:T(8,128)(2,1)S(1)} %copy-done.8), channel_id=1, source_target_pairs={{0,2},{1,3},{2,0},{3,1},{4,6},{5,7},{6,4},{7,5},{8,10},{9,11},{10,... | collective-permute-start | bytes 1572872 | tf_op jit(solution)/shard_map/ppermute | solution.py:52
  162.4 38.4 %collective-permute-start.28 = (bf16[128,2048]{1,0:T(8,128)(2,1)S(1)}, bf16[128,2048]{1,0:T(8,128)(2,1)}, u32[]{:S(2)}, u32[]{:S(2)}) collective-permute-start(bf16[128,2048]{1,0:T(8,128)(2,1)S(1)} %copy-done.8), channel_id=1, source_target_pairs={{0,4},{1,5},{2,6},{3,7},{4,0},{5,1},{6,2},{7,3},{8,12},{9,13},{10,... | collective-permute-start | bytes 1572872 | tf_op jit(solution)/shard_map/ppermute | solution.py:52
  163.3 37.5 %collective-permute-start.29 = (bf16[128,2048]{1,0:T(8,128)(2,1)S(1)}, bf16[128,2048]{1,0:T(8,128)(2,1)}, u32[]{:S(2)}, u32[]{:S(2)}) collective-permute-start(bf16[128,2048]{1,0:T(8,128)(2,1)S(1)} %copy-done.8), channel_id=1, source_target_pairs={{0,6},{1,7},{2,4},{3,5},{4,2},{5,3},{6,0},{7,1},{8,14},{9,15},{10,... | collective-permute-start | bytes 1572872 | tf_op jit(solution)/shard_map/ppermute | solution.py:52
  210.3 26.5 %collective-permute-start.35 = (bf16[128,2048]{1,0:T(8,128)(2,1)}, bf16[128,2048]{1,0:T(8,128)(2,1)}, u32[]{:S(2)}, u32[]{:S(2)}) collective-permute-start(bf16[128,2048]{1,0:T(8,128)(2,1)} %get-tuple-element.185), channel_id=1, source_target_pairs={{0,2},{1,3},{2,0},{3,1},{4,6},{5,7},{6,4},{7,5},{8,10},{9,11},{10,... | collective-permute-start | bytes 1572872 | tf_op jit(solution)/shard_map/ppermute | solution.py:52
  212.2 25.4 %collective-permute-start.36 = (bf16[128,2048]{1,0:T(8,128)(2,1)}, bf16[128,2048]{1,0:T(8,128)(2,1)S(1)}, u32[]{:S(2)}, u32[]{:S(2)}) collective-permute-start(bf16[128,2048]{1,0:T(8,128)(2,1)} %get-tuple-element.186), channel_id=1, source_target_pairs={{0,4},{1,5},{2,6},{3,7},{4,0},{5,1},{6,2},{7,3},{8,12},{9,13},{10,... | collective-permute-start | bytes 1572872 | tf_op jit(solution)/shard_map/ppermute | solution.py:52
  213.1 25.4 %collective-permute-start.37 = (bf16[128,2048]{1,0:T(8,128)(2,1)}, bf16[128,2048]{1,0:T(8,128)(2,1)}, u32[]{:S(2)}, u32[]{:S(2)}) collective-permute-start(bf16[128,2048]{1,0:T(8,128)(2,1)} %get-tuple-element.187), channel_id=1, source_target_pairs={{0,6},{1,7},{2,4},{3,5},{4,2},{5,3},{6,0},{7,1},{8,14},{9,15},{10,... | collective-permute-start | bytes 1572872 | tf_op jit(solution)/shard_map/ppermute | solution.py:52
  363.0 34.2 %collective-permute-start.51 = (bf16[128,2048]{1,0:T(8,128)(2,1)}, bf16[128,2048]{1,0:T(8,128)(2,1)}, u32[]{:S(2)}, u32[]{:S(2)}) collective-permute-start(bf16[128,2048]{1,0:T(8,128)(2,1)} %get-tuple-element.203), channel_id=1, source_target_pairs={{0,2},{1,3},{2,0},{3,1},{4,6},{5,7},{6,4},{7,5},{8,10},{9,11},{10,... | collective-permute-start | bytes 1572872 | tf_op jit(solution)/shard_map/ppermute | solution.py:52
  364.0 33.2 %collective-permute-start.52 = (bf16[128,2048]{1,0:T(8,128)(2,1)}, bf16[128,2048]{1,0:T(8,128)(2,1)}, u32[]{:S(2)}, u32[]{:S(2)}) collective-permute-start(bf16[128,2048]{1,0:T(8,128)(2,1)} %get-tuple-element.204), channel_id=1, source_target_pairs={{0,4},{1,5},{2,6},{3,7},{4,0},{5,1},{6,2},{7,3},{8,12},{9,13},{10,... | collective-permute-start | bytes 1572872 | tf_op jit(solution)/shard_map/ppermute | solution.py:52
  365.2 31.9 %collective-permute-start.53 = (bf16[128,2048]{1,0:T(8,128)(2,1)}, bf16[128,2048]{1,0:T(8,128)(2,1)}, u32[]{:S(2)}, u32[]{:S(2)}) collective-permute-start(bf16[128,2048]{1,0:T(8,128)(2,1)} %get-tuple-element.205), channel_id=1, source_target_pairs={{0,6},{1,7},{2,4},{3,5},{4,2},{5,3},{6,0},{7,1},{8,14},{9,15},{10,... | collective-permute-start | bytes 1572872 | tf_op jit(solution)/shard_map/ppermute | solution.py:52
  366.5 29.7 %collective-permute-start.55 = (f32[1,2560]{1,0:T(1,128)S(1)}, f32[1,2560]{1,0:T(1,128)S(1)}, u32[]{:S(2)}, u32[]{:S(2)}) collective-permute-start(f32[1,2560]{1,0:T(1,128)S(1)} %add.439), channel_id=1, source_target_pairs={{0,4},{1,5},{2,6},{3,7},{4,0},{5,1},{6,2},{7,3},{8,12},{9,13},{10,... | collective-permute-start | bytes 30728 | tf_op jit(solution)/shard_map/ppermute | solution.py:52
  402.7 25.3 %collective-permute-start.58 = (bf16[128,2048]{1,0:T(8,128)(2,1)S(1)}, bf16[128,2048]{1,0:T(8,128)(2,1)}, u32[]{:S(2)}, u32[]{:S(2)}) collective-permute-start(bf16[128,2048]{1,0:T(8,128)(2,1)S(1)} %fusion.105.refs_1_), channel_id=1, source_target_pairs={{0,4},{1,5},{2,6},{3,7},{4,0},{5,1},{6,2},{7,3},{8,12},{9,13},{10,... | collective-permute-start | bytes 1572872 | tf_op jit(solution)/shard_map/ppermute | solution.py:52
  431.8 149.4 %all-gather.7.cloned.1.call-start = ((), (), s32[]{:S(2)}) async-start(), calls=%async_computation.1 | async-start | bytes 1474560 | tf_op jit(solution)/shard_map/all_gather | solution.py:1118
  454.0 29.3 %collective-permute-start.68 = (bf16[128,2048]{1,0:T(8,128)(2,1)}, bf16[128,2048]{1,0:T(8,128)(2,1)S(1)}, u32[]{:S(2)}, u32[]{:S(2)}) collective-permute-start(bf16[128,2048]{1,0:T(8,128)(2,1)} %get-tuple-element.235), channel_id=1, source_target_pairs={{0,2},{1,3},{2,0},{3,1},{4,6},{5,7},{6,4},{7,5},{8,10},{9,11},{10,... | collective-permute-start | bytes 1572872 | tf_op jit(solution)/shard_map/ppermute | solution.py:52
  454.6 28.6 %collective-permute-start.69 = (bf16[128,2048]{1,0:T(8,128)(2,1)}, bf16[128,2048]{1,0:T(8,128)(2,1)}, u32[]{:S(2)}, u32[]{:S(2)}) collective-permute-start(bf16[128,2048]{1,0:T(8,128)(2,1)} %get-tuple-element.236), channel_id=1, source_target_pairs={{0,4},{1,5},{2,6},{3,7},{4,0},{5,1},{6,2},{7,3},{8,12},{9,13},{10,... | collective-permute-start | bytes 1572872 | tf_op jit(solution)/shard_map/ppermute | solution.py:52
  455.6 27.6 %collective-permute-start.70 = (bf16[128,2048]{1,0:T(8,128)(2,1)}, bf16[128,2048]{1,0:T(8,128)(2,1)}, u32[]{:S(2)}, u32[]{:S(2)}) collective-permute-start(bf16[128,2048]{1,0:T(8,128)(2,1)} %get-tuple-element.237), channel_id=1, source_target_pairs={{0,6},{1,7},{2,4},{3,5},{4,2},{5,3},{6,0},{7,1},{8,14},{9,15},{10,... | collective-permute-start | bytes 1572872 | tf_op jit(solution)/shard_map/ppermute | solution.py:52
  503.1 28.9 %collective-permute-start.75 = (bf16[14,48,256]{2,1,0:T(8,128)(2,1)S(1)}, bf16[14,48,256]{2,1,0:T(8,128)(2,1)S(1)}, u32[]{:S(2)}, u32[]{:S(2)}) collective-permute-start(bf16[14,48,256]{2,1,0:T(8,128)(2,1)S(1)} %constant_dynamic-update-slice_fusion.44), channel_id=1, source_target_pairs={{0,8},{8,0},{16,24},{24,16},{1,9},{9,1},{17,25},{25,17},{2,10},{10... | collective-permute-start | bytes 1032200 | tf_op jit(solution)/shard_map/ppermute | solution.py:942
  503.2 28.8 %collective-permute-start.76 = (bf16[14,48,256]{2,1,0:T(8,128)(2,1)S(1)}, bf16[14,48,256]{2,1,0:T(8,128)(2,1)S(1)}, u32[]{:S(2)}, u32[]{:S(2)}) collective-permute-start(bf16[14,48,256]{2,1,0:T(8,128)(2,1)S(1)} %constant_dynamic-update-slice_fusion.44), channel_id=1, source_target_pairs={{0,16},{8,24},{16,0},{24,8},{1,17},{9,25},{17,1},{25,9},{2,18},{10... | collective-permute-start | bytes 1032200 | tf_op jit(solution)/shard_map/ppermute | solution.py:942
  504.7 27.3 %collective-permute-start.77 = (bf16[14,48,256]{2,1,0:T(8,128)(2,1)S(1)}, bf16[14,48,256]{2,1,0:T(8,128)(2,1)}, u32[]{:S(2)}, u32[]{:S(2)}) collective-permute-start(bf16[14,48,256]{2,1,0:T(8,128)(2,1)S(1)} %constant_dynamic-update-slice_fusion.44), channel_id=1, source_target_pairs={{0,24},{8,16},{16,8},{24,0},{1,25},{9,17},{17,9},{25,1},{2,26},{10... | collective-permute-start | bytes 1032200 | tf_op jit(solution)/shard_map/ppermute | solution.py:942
  (133 other events, 1731.4 us)
Sparse Core Ops, SparseCore 0:
  432.0 68.1 all-gather.4
  533.2 34.4 all-gather.6
